TPU v7x, 32 devices: a whole 2x2x4 slice. The times are simulated.
32 devices in a mesh: row: 4 (over y, x), col: 8 (over z, core).
Axes of the slice: x: 2, y: 2, z: 4, core: 2. Of those that a mesh axis runs over, the one named last changes fastest.
Arguments:
- sensitivity: bfloat16 [32, 4, 2, 256, 128], P(('row', 'col')), may hold values from -0.3984375 to 0.3984375
- tile_ids: int32 [32, 4, 2], P(('row', 'col')), may hold values from 0 to 31, as said below
- counts: int32 [32, 4], P(('row', 'col')), may hold values from 0 to 2, as said below
- weight_class: int32 [32, 256], P(('row', 'col')), may hold values from 0 to 3
Outputs:
- normal_matrix: float32 [16384, 16384], P('row', 'col')
Inputs may be any that keep to these rules, and one draw needn't show every extreme that they name: `tile_ids`: within one station block and one row owner the 2 slots name distinct tiles. `counts`: slots at or beyond the count are padding; in every draw some station block uses all 2 slots of every row owner.
All inputs are finite; a program needn't handle non-finite values.
Results may differ from a plain program's by a relative error of at most 0.0003.
Values may be sent and summed in bfloat16 or wider, within the bound.
No kernel may reach another device: no remote copies, remote signals or barrier semaphores. Data moves between devices by JAX's collectives and lax.ppermute only.
A program may use at most 128 MiB of HBM per device.

v0:
```python
import jax
import jax.numpy as jnp
from jax import lax
from jax.sharding import PartitionSpec as P

TILES = 128


def station_scale(weight_class):
    levels = jnp.array([1.0, 0.5, 0.25, 0.125], jnp.float32)
    hits = weight_class[..., None] == jnp.arange(4, dtype=jnp.int32)
    return jnp.sum(jnp.where(hits, levels, jnp.float32(0.0)), axis=-1)


def local(sensitivity, tile_ids, counts, weight_class):
    row_devices = lax.axis_size("row")
    col_devices = lax.axis_size("col")
    blocks, _, slots, rows, width = sensitivity.shape
    per_row = TILES // row_devices
    per_col = TILES // col_devices
    ratio = col_devices // row_devices
    live = jnp.arange(slots, dtype=jnp.int32)[None, None, :] < counts[:, :, None]
    factor = station_scale(weight_class)[:, None, None, :, None] * live[:, :, :, None, None].astype(
        jnp.float32
    )
    weighted = (sensitivity.astype(jnp.float32) * factor).astype(jnp.bfloat16)
    left_ids = jnp.where(live, tile_ids, -1)
    owned_data, owned_ids = (
        lax.all_to_all(weighted, "row", split_axis=1, concat_axis=0, tiled=True),
        lax.all_to_all(left_ids, "row", split_axis=1, concat_axis=0, tiled=True),
    )
    left_data, left_tiles = (
        lax.all_gather(owned_data, "col", axis=1, tiled=True),
        lax.all_gather(owned_ids, "col", axis=1, tiled=True),
    )
    stations = row_devices * col_devices * blocks
    left_data = left_data.reshape(stations, slots, rows, width)
    left_tiles = left_tiles.reshape(stations, slots)
    picked = jnp.repeat(weighted, ratio, axis=1)
    picked_ids = jnp.repeat(left_ids, ratio, axis=1)
    offsets = (jnp.arange(col_devices, dtype=jnp.int32) % ratio * per_col)[None, :, None]
    inside = (picked_ids >= offsets) & (picked_ids < offsets + per_col)
    chosen_ids = jnp.where(inside, picked_ids - offsets, -1)
    sorted_data, sorted_ids = (
        lax.all_to_all(picked, "col", split_axis=1, concat_axis=0, tiled=True),
        lax.all_to_all(chosen_ids, "col", split_axis=1, concat_axis=0, tiled=True),
    )
    right_data, right_tiles = (
        lax.all_gather(sorted_data, "row", axis=0, tiled=True),
        lax.all_gather(sorted_ids, "row", axis=0, tiled=True),
    )
    right_data = right_data.reshape(stations, slots, rows, width)
    right_tiles = right_tiles.reshape(stations, slots)
    group = min(stations, 32)

    def accumulate(index, normal):
        start = index * group
        left_part = lax.dynamic_slice_in_dim(left_data, start, group, 0)
        left_part_ids = lax.dynamic_slice_in_dim(left_tiles, start, group, 0)
        right_part = lax.dynamic_slice_in_dim(right_data, start, group, 0)
        right_part_ids = lax.dynamic_slice_in_dim(right_tiles, start, group, 0)
        gram = jnp.einsum(
            "girk,gjrn->gijkn", left_part, right_part, preferred_element_type=jnp.float32
        )
        left_place = jnp.where(left_part_ids >= 0, left_part_ids, per_row)
        right_place = jnp.where(right_part_ids >= 0, right_part_ids, per_col)
        return normal.at[left_place[:, :, None], :, right_place[:, None, :], :].add(
            gram, mode="drop"
        )

    normal = jnp.zeros((per_row, width, per_col, width), jnp.float32)
    normal = lax.fori_loop(0, stations // group, accumulate, normal)
    return normal.reshape(per_row * width, per_col * width)


def solution(mesh):
    in_specs = (
        P(("row", "col"), None, None, None, None),
        P(("row", "col"), None, None),
        P(("row", "col"), None),
        P(("row", "col"), None),
    )
    out_specs = P("row", "col")
    return jax.shard_map(local, mesh=mesh, in_specs=in_specs, out_specs=out_specs, check_vma=False)
```

profile of v0, /device:TPU:0, one launch (start us, length us, event | category | flops | bytes accessed | tf_op | source)
XLA Modules:
  0.0 256.6 jit_solution(9188043475256037133)
XLA Ops:
  6.5 0.8 fusion.5
  7.3 0.8 select_reduce_fusion
  8.2 1.4 multiply_convert_fusion
  9.6 13.6 %all_to_all.48 = bf16[1,4,2,256,128]{4,3,2,0,1:T(8,128)(2,1)} all-to-all(bf16[1,4,2,256,128]{4,3,2,0,1:T(8,128)(2,1)S(1)} %multiply_convert_fusion), channel_id=1, replica_groups=mesh['row'=4,'col'=8] {'row'}, dimensions={1} | all-to-all | bytes 1048576 | tf_op jit(solution)/shard_map/all_to_all | solution.py:29
  23.2 1.4 fusion.9
  24.6 0.2 copy.39
  24.9 57.5 %all_to_all.49 = bf16[1,8,2,256,128]{3,4,2,0,1:T(8,128)(2,1)S(1)} all-to-all(bf16[1,8,2,256,128]{3,4,2,0,1:T(8,128)(2,1)S(1)} %bitcast.43), channel_id=1, replica_groups=mesh['row'=4,'col'=8] {'col'}, dimensions={1} | all-to-all | bytes 2097152 | tf_op jit(solution)/shard_map/all_to_all | solution.py:45
  82.5 1.3 copy.40
  83.9 0.7 compare_select_fusion.2
  84.5 3.2 %all-to-all-start = ((s32[1,4,2]{2,0,1:T(1,128)}), s32[1,4,2]{2,0,1:T(1,128)S(1)}, u32[]{:S(2)}, u32[]{:S(2)}) async-start(s32[1,4,2]{2,0,1:T(1,128)} %compare_select_fusion.2), calls=%async_computation | async-start | bytes 4096 | tf_op jit(solution)/shard_map/all_to_all | solution.py:30
  87.7 0.8 copy.33
  88.7 0.7 copy.34
  89.4 3.0 %all-to-all-done = s32[1,4,2]{2,0,1:T(1,128)S(1)} async-done(((s32[1,4,2]{2,0,1:T(1,128)}), s32[1,4,2]{2,0,1:T(1,128)S(1)}, u32[]{:S(2)}, u32[]{:S(2)}) %all-to-all-start) | async-done | bytes 64 | tf_op jit(solution)/shard_map/all_to_all | solution.py:30
  92.3 3.3 %all-to-all-start.1 = ((s32[1,8,2]{2,0,1:T(1,128)}), s32[1,8,2]{2,0,1:T(1,128)S(1)}, u32[]{:S(2)}, u32[]{:S(2)}) async-start(s32[1,8,2]{2,0,1:T(1,128)} %copy.34), calls=%async_computation.1 | async-start | bytes 8192 | tf_op jit(solution)/shard_map/all_to_all | solution.py:46
  95.8 12.1 %all-gather = s32[1,4,16]{1,0,2:T(1,128)S(1)} all-gather(s32[1,4,2]{1,0,2:T(1,128)S(1)} %copy.31), channel_id=2, replica_groups=mesh['row'=4,'col'=8] {'col'}, dimensions={2}, use_global_device_ids=true | all-gather | bytes 288 | tf_op jit(solution)/shard_map/all_gather | solution.py:34
  108.1 7.3 %all-gather.1 = s32[1,32,2]{2,0,1:T(1,128)S(1)} all-gather(s32[1,8,2]{2,0,1:T(1,128)S(1)} %all-to-all-done.1), channel_id=3, replica_groups=mesh['row'=4,'col'=8] {'row'}, dimensions={1}, use_global_device_ids=true | all-gather | bytes 320 | tf_op jit(solution)/shard_map/all_gather | solution.py:50
  115.7 0.1 reshape.326
  115.9 27.7 %all-gather.7.cloned.1.call-done = bf16[1,32,2,256,128]{4,3,2,0,1:T(8,128)(2,1)} async-done(((bf16[1,8,2,256,128]{4,3,2,0,1:T(8,128)(2,1)}), bf16[1,32,2,256,128]{4,3,2,0,1:T(8,128)(2,1)}) %all-gather.7.cloned.1.call-update) | async-done | bytes 4194320 | tf_op jit(solution)/shard_map/all_gather | solution.py:49
  143.6 8.2 %fusion.2 = f32[32,2,2,128,128]{3,4,1,2,0:T(8,128)} fusion(bf16[32,2,256,128,1]{3,2,1,4,0:T(8,128)(2,1)} %bitcast.44, bf16[1,32,2,256,128]{4,3,2,0,1:T(8,128)(2,1)} %all-gather.7.cloned.1.call-done), kind=kOutput, calls=%fused_computation.4 | convolution fusion | flops 1073741824 | bytes 16777216 | tf_op jit(solution)/shard_map/while/body/eval_jaxpr/girk,gjrn->gijkn/dot_general | solution.py:62
  151.7 9.0 %copy.42 = f32[32,2,2,128,128]{4,3,2,1,0:T(8,128)} copy(f32[32,2,2,128,128]{3,4,1,2,0:T(8,128)} %fusion.2) | data formatting | bytes 16777216 | tf_op jit(solution)/shard_map/while/body/eval_jaxpr/girk,gjrn->gijkn/transpose | solution.py:62
  160.7 11.5 %broadcast_in_dim.67 = f32[32,128,16,128]{3,1,2,0:T(8,128)} broadcast(f32[]{:T(128)} %constant.18.clone.1), dimensions={} | broadcast | bytes 33554436 | tf_op jit(solution)/shard_map/broadcast_in_dim | solution.py:71
  172.2 28.1 %scatter_fusion = f32[32,128,16,128]{3,1,2,0:T(8,128)} fusion(f32[32,128,16,128]{3,1,2,0:T(8,128)} %broadcast_in_dim.67, s32[128]{0:T(128)S(1)} %reshape.326, f32[128,128,128]{2,1,0:T(8,128)} %bitcast.42), kind=kCustom, calls=%fused_computation | custom fusion | flops 2097152 | bytes 25166848 | tf_op jit(solution)/shard_map/while/body/eval_jaxpr/scatter-add | solution.py:67
  200.3 28.8 %copy.43 = f32[32,128,16,128]{3,2,1,0:T(8,128)S(1)} copy(f32[32,128,16,128]{3,1,2,0:T(8,128)} %scatter_fusion) | data formatting | bytes 67108864 | tf_op jit(solution)/shard_map/while/body/eval_jaxpr/scatter-add | solution.py:67
  229.1 20.7 %copy.48 = f32[512,8,16,128]{3,1,2,0:T(8,128)} copy(f32[512,8,16,128]{3,2,1,0:T(8,128)S(1)} %bitcast.41) | data formatting | bytes 67108864
  (28 shorter events, 1.2 us)
Async XLA Ops:
  6.5 77.3 %copy-start = (s32[1,4]{1,0:T(1,128)S(1)}, s32[1,4]{1,0:T(1,128)}, u32[]{:S(2)}) copy-start(s32[1,4]{1,0:T(1,128)} %param.7) | copy-start | bytes 52
  6.5 77.2 %copy-start.1 = (s32[1,4,2]{1,2,0:T(2,128)S(1)}, s32[1,4,2]{1,2,0:T(2,128)}, u32[]{:S(2)}) copy-start(s32[1,4,2]{1,2,0:T(2,128)} %param.6) | copy-start | bytes 100
  6.5 109.3 %all-gather.9.cloned.1.call-start = ((), (), s32[]{:S(2)}) async-start(), calls=%async_computation.5 | async-start | bytes 4718592 | tf_op jit(solution)/shard_map/all_gather | solution.py:33
  23.2 120.4 %all-gather.7.cloned.1.call-start = ((), (), s32[]{:S(2)}) async-start(), calls=%async_computation.4 | async-start | bytes 5242880 | tf_op jit(solution)/shard_map/all_gather | solution.py:49
  84.5 7.8 %all-to-all-start = ((s32[1,4,2]{2,0,1:T(1,128)}), s32[1,4,2]{2,0,1:T(1,128)S(1)}, u32[]{:S(2)}, u32[]{:S(2)}) async-start(s32[1,4,2]{2,0,1:T(1,128)} %compare_select_fusion.2), calls=%async_computation | async-start | bytes 4096 | tf_op jit(solution)/shard_map/all_to_all | solution.py:30
  92.3 15.8 %all-to-all-start.1 = ((s32[1,8,2]{2,0,1:T(1,128)}), s32[1,8,2]{2,0,1:T(1,128)S(1)}, u32[]{:S(2)}, u32[]{:S(2)}) async-start(s32[1,8,2]{2,0,1:T(1,128)} %copy.34), calls=%async_computation.1 | async-start | bytes 8192 | tf_op jit(solution)/shard_map/all_to_all | solution.py:46
Sparse Core Ops, SparseCore 0:
  23.3 68.1 all-gather.8
  93.4 50.1 all-gather.6
where the time goes:
time: 257 us
  blocking collectives  90.5 us (35%)
  local copies, waits for them, and re-layouts  73.8 us (29%)
  other arithmetic  33.4 us (13%)
  waiting for transfers between devices  30.7 us (12%)
  between operations  13.5 us (5%)
  matrix products  8.17 us (3%)
  starting transfers between devices  6.53 us (3%)
    all_to_all x1, blocking collectives, local(): lax.all_to_all(picked, 'col', split_axis=1, concat_axis=0, tiled=True)  57.5 us
    scatter-add x1, local copies, waits for them, and re-layouts, accumulate(): normal.at[left_place[:, :, None], :, right_place[:, None, :], :]  28.8 us
    scatter-add x1, other arithmetic, accumulate(): normal.at[left_place[:, :, None], :, right_place[:, None, :], :]  28.1 us
    all_gather x1, waiting for transfers between devices, local(): lax.all_gather(sorted_data, 'row', axis=0, tiled=True)  27.7 us
    unnamed x6, local copies, waits for them, and re-layouts  20.8 us
    all_to_all x1, blocking collectives, local(): lax.all_to_all(weighted, 'row', split_axis=1, concat_axis=0, tiled=True)  13.6 us
    all_gather x1, blocking collectives, local(): lax.all_gather(owned_ids, 'col', axis=1, tiled=True)  12.1 us
    broadcast_in_dim x1, local copies, waits for them, and re-layouts, local(): normal = jnp.zeros((per_row, width, per_col, width), jnp.float32)  11.5 us
  transfers between devices with their start and end apart: 4, of which 2 were waited for; matrix products, arithmetic and copies ran while one was open for 2% of the time, Pallas kernels for 0%

commit v1 on v0

v1 whole, which is shorter than its diff:
```python
import functools

import jax
import jax.numpy as jnp
from jax import lax
from jax.experimental import pallas as pl
from jax.experimental.pallas import tpu as pltpu
from jax.sharding import PartitionSpec as P

TILES = 128
CORES = 2
META_ROWS = 8


def accumulate_kernel(
    n_row, n_chip, slots, per_row, per_col, width,
    place_ref, weight_ref, *refs,
):
    chunks = CORES * (n_chip + n_row)
    sources = refs[:chunks]
    out_ref = refs[chunks + 1]
    acc, left_buf, right_buf, gram_buf, touches, done, load_sem, store_sem = refs[chunks + 2 :]
    n_left = CORES * n_chip

    def load(index):
        target = left_buf.at[index] if index < n_left else right_buf.at[index - n_left]
        return pltpu.make_async_copy(sources[index], target, load_sem.at[index])

    for index in range(chunks):
        load(index).start()

    tiles = per_row * per_col
    stations = CORES * n_row * n_chip

    def clear(index, carry):
        touches[index] = 0
        done[index] = 0
        return carry

    lax.fori_loop(0, tiles + 1, clear, 0)

    def tile_of(station, i, j):
        left = place_ref[station, i]
        right = place_ref[station, slots + j]
        inside = jnp.logical_and(left >= 0, right >= 0)
        return jnp.where(inside, left * per_col + right, tiles)

    def count(station, carry):
        for i in range(slots):
            for j in range(slots):
                tile = tile_of(station, i, j)
                touches[tile] = touches[tile] + 1
        return carry

    lax.fori_loop(0, stations, count, 0)

    for index in range(chunks):
        load(index).wait()

    def store(tile):
        rows = pl.ds(pl.multiple_of(lax.div(tile, per_col) * width, width), width)
        columns = pl.ds(pl.multiple_of(lax.rem(tile, per_col) * width, width), width)
        return pltpu.make_async_copy(acc.at[tile], out_ref.at[rows, columns], store_sem)

    def station_step(station, stored):
        row = lax.rem(station, n_row)
        core_chip = lax.div(station, n_row)
        core = lax.div(core_chip, n_chip)
        chip = lax.rem(core_chip, n_chip)
        weights = weight_ref[pl.ds(station, 1), :]
        left = jnp.concatenate([left_buf[core_chip, row, i].T for i in range(slots)], axis=0)
        left = (left.astype(jnp.float32) * weights).astype(jnp.bfloat16)
        right = jnp.concatenate(
            [right_buf[core * n_row + row, chip, j] for j in range(slots)], axis=1
        )
        gram_buf[...] = jnp.dot(left, right, preferred_element_type=jnp.float32)
        for i in range(slots):
            for j in range(slots):
                tile = tile_of(station, i, j)
                seen = done[tile]
                gram = gram_buf[i * width : (i + 1) * width, j * width : (j + 1) * width]
                acc[tile] = jnp.where(seen == 0, gram, acc[tile] + gram)
                done[tile] = seen + 1
                last = jnp.logical_and(seen + 1 == touches[tile], tile < tiles)

                @pl.when(last)
                def _():
                    store(tile).start()

                stored = stored + last.astype(jnp.int32)
        return stored

    stored = lax.fori_loop(0, stations, station_step, 0)

    def drain(index, carry):
        store(0).wait()
        return carry

    lax.fori_loop(0, stored, drain, 0)


def accumulate(place, weights, left, right, zeros, per_row, per_col):
    n_chip = len(left) // CORES
    n_row = len(right) // CORES
    _, slots, rows, width = left[0].shape
    chunks = len(left) + len(right)
    tiles = per_row * per_col
    anywhere = pl.BlockSpec(memory_space=pl.ANY)
    return pl.pallas_call(
        functools.partial(accumulate_kernel, n_row, n_chip, slots, per_row, per_col, width),
        out_shape=jax.ShapeDtypeStruct(zeros.shape, zeros.dtype),
        in_specs=[
            pl.BlockSpec(memory_space=pltpu.SMEM),
            pl.BlockSpec(memory_space=pltpu.VMEM),
            *[anywhere] * (chunks + 1),
        ],
        out_specs=anywhere,
        scratch_shapes=[
            pltpu.VMEM((tiles + 1, width, width), jnp.float32),
            pltpu.VMEM((len(left), n_row, slots, rows, width), jnp.bfloat16),
            pltpu.VMEM((len(right), n_chip, slots, rows, width), jnp.bfloat16),
            pltpu.VMEM((slots * width, slots * width), jnp.float32),
            pltpu.SMEM((tiles + 1,), jnp.int32),
            pltpu.SMEM((tiles + 1,), jnp.int32),
            pltpu.SemaphoreType.DMA((chunks,)),
            pltpu.SemaphoreType.DMA,
        ],
        input_output_aliases={2 + chunks: 0},
        compiler_params=pltpu.CompilerParams(vmem_limit_bytes=56 * 1024 * 1024),
        cost_estimate=pl.CostEstimate(flops=10**9, bytes_accessed=16 * 2**20, transcendentals=0),
    )(place, weights, *left, *right, zeros)


def zero_kernel(out_ref, block, sem):
    block[...] = jnp.zeros_like(block)
    height = block.shape[0]
    copies = [
        pltpu.make_async_copy(block, out_ref.at[pl.ds(index * height, height)], sem.at[index])
        for index in range(out_ref.shape[0] // height)
    ]
    for copy in copies:
        copy.start()
    for copy in copies:
        copy.wait()


def zero_fill(height, width):
    step = 128
    return pl.pallas_call(
        zero_kernel,
        out_shape=jax.ShapeDtypeStruct((height, width), jnp.float32),
        out_specs=pl.BlockSpec(memory_space=pl.ANY),
        scratch_shapes=[
            pltpu.VMEM((step, width), jnp.float32),
            pltpu.SemaphoreType.DMA((height // step,)),
        ],
        cost_estimate=pl.CostEstimate(
            flops=0, bytes_accessed=height * width * 4, transcendentals=0
        ),
    )()


def local(sensitivity, tile_ids, counts, weight_class):
    n_row = lax.axis_size("row")
    n_col = lax.axis_size("col")
    n_chip = n_col // CORES
    r = lax.axis_index("row")
    c = lax.axis_index("col")
    z, core = c // CORES, c % CORES
    _, _, slots, rows, width = sensitivity.shape
    per_row = TILES // n_row
    per_col = TILES // n_col
    owned = sensitivity[0]

    def part(owner):
        return lax.dynamic_index_in_dim(owned, owner, 0, keepdims=False)

    def flip_row(value, j):
        return lax.ppermute(value, "row", [(i, i ^ j) for i in range(n_row)])

    def shift_chip(value, s):
        pairs = [(i, (i + CORES * s) % n_col) for i in range(n_col)]
        return lax.ppermute(value, "col", pairs)

    def flip_core(value):
        return lax.ppermute(value, "col", [(i, i ^ 1) for i in range(n_col)])

    live = jnp.arange(slots, dtype=jnp.int32) < counts[0, :, None]
    ids = jnp.where(live, tile_ids[0], -1).reshape(-1)
    ids = jnp.pad(ids, (0, width - n_row * slots)).reshape(1, width)
    own_meta = jnp.concatenate(
        [weight_class.reshape(rows // width, width), ids], axis=0
    )
    own_meta = jnp.pad(own_meta, ((0, META_ROWS - rows // width - 1), (0, 0)))
    meta = lax.all_gather(own_meta, ("row", "col"), axis=0, tiled=False)

    left = [jnp.stack([part(r)] + [flip_row(part(r ^ j), j) for j in range(1, n_row)])]
    right = jnp.stack(
        [part(z)] + [shift_chip(part((z + s) % n_chip), s) for s in range(1, n_chip)]
    )
    right = [right] + [flip_row(right, j) for j in range(1, n_row)]
    for s in range(1, n_chip):
        left.append(shift_chip(left[-1], 1))
    left = left + [flip_core(x) for x in left]
    right = right + [flip_core(x) for x in right]

    rel_core = jnp.arange(CORES, dtype=jnp.int32)[:, None, None]
    rel_chip = jnp.arange(n_chip, dtype=jnp.int32)[None, :, None]
    rel_row = jnp.arange(n_row, dtype=jnp.int32)[None, None, :]
    station = (
        (r ^ rel_row) * n_col + (z - rel_chip) % n_chip * CORES + (core ^ rel_core)
    ).reshape(-1)
    meta = meta[station]
    classes = meta[:, : rows // width].reshape(-1, rows)
    weights = jnp.where(
        classes == 0, 1.0, jnp.where(classes == 1, 0.25, jnp.where(classes == 2, 0.0625, 0.015625))
    ).astype(jnp.float32)
    ids = meta[:, rows // width, : n_row * slots].reshape(-1, n_row, slots)
    left_ids = lax.dynamic_index_in_dim(ids, r, 1, keepdims=False)
    right_ids = lax.dynamic_index_in_dim(ids, z, 1, keepdims=False) - core * per_col
    right_ids = jnp.where((right_ids >= 0) & (right_ids < per_col), right_ids, -1)
    place = jnp.concatenate([left_ids, right_ids], axis=1)

    zeros = zero_fill(per_row * width, per_col * width)
    return accumulate(place, weights, left, right, zeros, per_row, per_col)


def solution(mesh):
    in_specs = (
        P(("row", "col"), None, None, None, None),
        P(("row", "col"), None, None),
        P(("row", "col"), None),
        P(("row", "col"), None),
    )
    return jax.shard_map(
        local, mesh=mesh, in_specs=in_specs, out_specs=P("row", "col"), check_vma=False
    )
```

time: 257 us -> 123 us (0.48)
  local copies, waits for them, and re-layouts: 73.8 us -> 4.41 us
  blocking collectives: 90.5 us -> 40.6 us
  other arithmetic: 33.4 us -> 1.09 us
  Pallas kernels: 0 us -> 24.6 us
  between operations: 13.5 us -> 0.17 us
  starting transfers between devices: 6.53 us -> 17.2 us
  matrix products: 8.17 us -> 0 us
  waiting for transfers between devices: 30.7 us -> 34.1 us
    all_to_all x2 -> x0, blocking collectives: 71.1 us -> none  [the longest x1 57.5 us: local(): lax.all_to_all(picked, 'col', split_axis=1, concat_axis=0, tiled=True)]
    ppermute x0 -> x20, waiting for transfers between devices: none -> 34.1 us  [the longest x6 19.5 us: shift_chip(): return lax.ppermute(value, 'col', pairs)]
    scatter-add x1 -> x0, local copies, waits for them, and re-layouts: 28.8 us -> none  [accumulate(): normal.at[left_place[:, :, None], :, right_place[:, None, :], :]]
    scatter-add x1 -> x0, other arithmetic: 28.1 us -> none  [accumulate(): normal.at[left_place[:, :, None], :, right_place[:, None, :], :]]
    all_gather x2 -> x0, waiting for transfers between devices: 27.7 us -> none  [the longest x1 27.7 us: local(): lax.all_gather(sorted_data, 'row', axis=0, tiled=True)]
    pallas_call x0 -> x2, Pallas kernels: none -> 24.6 us  [the longest x1 13.3 us: accumulate(): pl.pallas_call(functools.partial(accumulate_kernel, n_row, n_chip, slots,...]
    all_gather x2 -> x1, blocking collectives: 19.4 us -> 40.6 us  [local(): meta = lax.all_gather(own_meta, ('row', 'col'), axis=0, tiled=False)]
    unnamed x6 -> x16, local copies, waits for them, and re-layouts: 20.8 us -> 1.4 us
  transfers between devices with their start and end apart: 4 -> 20, of which waited for: 2 -> 6; matrix products, arithmetic and copies ran while one was open for 2% -> 3% of each run, Pallas kernels for 0% -> 9%
where the time goes in v1:
time: 123 us; the launch traced here: 122 us
  blocking collectives  40.6 us (33%)
  waiting for transfers between devices  34.1 us (28%)
  Pallas kernels  24.6 us (20%)
  starting transfers between devices  17.2 us (14%)
  local copies, waits for them, and re-layouts  4.41 us (4%)
    all_gather x1, blocking collectives, local(): meta = lax.all_gather(own_meta, ('row', 'col'), axis=0, tiled=False)  40.6 us
    ppermute x6, waiting for transfers between devices, shift_chip(): return lax.ppermute(value, 'col', pairs)  19.5 us
    pallas_call x1, Pallas kernels, accumulate(): pl.pallas_call(functools.partial(accumulate_kernel, n_row, n_chip, slots,...  13.3 us
    ppermute x6, waiting for transfers between devices, flip_row(): return lax.ppermute(value, 'row', [(i, i ^ j) for i in range(n_row)])  12 us
    pallas_call x1, Pallas kernels, zero_fill(): pl.pallas_call(zero_kernel, out_shape=jax.ShapeDtypeStruct((height, width...  11.2 us
    ppermute x6, starting transfers between devices, flip_row(): return lax.ppermute(value, 'row', [(i, i ^ j) for i in range(n_row)])  8.15 us
    ppermute x6, starting transfers between devices, shift_chip(): return lax.ppermute(value, 'col', pairs)  7.58 us
    ppermute x8, waiting for transfers between devices, flip_core(): return lax.ppermute(value, 'col', [(i, i ^ 1) for i in range(n_col)])  2.53 us
  transfers between devices with their start and end apart: 20, of which 6 were waited for; matrix products, arithmetic and copies ran while one was open for 3% of the time, Pallas kernels for 9%

profile of v1, /device:TPU:0, one launch (start us, length us, event | category | flops | bytes accessed | tf_op | source)
XLA Modules:
  0.0 122.0 jit_solution(10608533185068357263)
XLA Ops:
  0.0 1.4 %dynamic-slice_bitcast_fusion.3 = (bf16[1,2,256,128]{3,2,1,0:T(8,128)(2,1)S(1)}, bf16[2,256,128]{2,1,0:T(8,128)(2,1)S(1)}, bf16[2,256,128]{2,1,0:T(8,128)(2,1)S(...) fusion(bf16[1,4,2,256,128]{4,3,2,1,0:T(8,128)(2,1)} %param.4, ...), kind=kLoop, calls=%fused_computation.6 | loop fusion | bytes 2097184 | tf_op jit(solution)/shard_map/jit(dynamic_index_in_dim)/dynamic_slice | solution.py:176
  1.4 4.0 %collective-permute-start.2 = (bf16[2,256,128]{2,1,0:T(8,128)(2,1)S(1)}, bf16[2,256,128]{2,1,0:T(8,128)(2,1)S(1)}, u32[]{:S(2)}, u32[]{:S(2)}) collective-permute-start(bf16[2,256,128]{2,1,0:T(8,128)(2,1)S(1)} %get-tuple-element.7), channel_id=1, source_target_pairs={{0,24},{8,16},{16,8},{24,0},{1,25},{9,17},{17,9},{25,1},{2,26},{10... | collective-permute-start | bytes 393224 | tf_op jit(solution)/shard_map/ppermute | solution.py:179
  5.4 0.5 collective-permute-start.1
  6.0 2.0 %collective-permute-start.10 = (bf16[2,256,128]{2,1,0:T(8,128)(2,1)S(1)}, bf16[2,256,128]{2,1,0:T(8,128)(2,1)S(1)}, u32[]{:S(2)}, u32[]{:S(2)}) collective-permute-start(bf16[2,256,128]{2,1,0:T(8,128)(2,1)S(1)} %get-tuple-element.6), channel_id=1, source_target_pairs={{0,2},{1,3},{2,4},{3,5},{4,6},{5,7},{6,0},{7,1},{8,10},{9,11},{10,... | collective-permute-start | bytes 393224 | tf_op jit(solution)/shard_map/ppermute | solution.py:183
  8.0 2.0 %collective-permute-start.12 = (bf16[2,256,128]{2,1,0:T(8,128)(2,1)S(1)}, bf16[2,256,128]{2,1,0:T(8,128)(2,1)S(1)}, u32[]{:S(2)}, u32[]{:S(2)}) collective-permute-start(bf16[2,256,128]{2,1,0:T(8,128)(2,1)S(1)} %get-tuple-element.11), channel_id=1, source_target_pairs={{0,6},{1,7},{2,0},{3,1},{4,2},{5,3},{6,4},{7,5},{8,14},{9,15},{10,... | collective-permute-start | bytes 393224 | tf_op jit(solution)/shard_map/ppermute | solution.py:183
  10.0 1.9 %collective-permute-start.11 = (bf16[2,256,128]{2,1,0:T(8,128)(2,1)S(1)}, bf16[2,256,128]{2,1,0:T(8,128)(2,1)S(1)}, u32[]{:S(2)}, u32[]{:S(2)}) collective-permute-start(bf16[2,256,128]{2,1,0:T(8,128)(2,1)S(1)} %get-tuple-element.12), channel_id=1, source_target_pairs={{0,4},{1,5},{2,6},{3,7},{4,0},{5,1},{6,2},{7,3},{8,12},{9,13},{10,... | collective-permute-start | bytes 393224 | tf_op jit(solution)/shard_map/ppermute | solution.py:183
  12.0 1.6 %collective-permute-start.3 = (bf16[4,2,256,128]{3,2,1,0:T(8,128)(2,1)S(1)}, bf16[4,2,256,128]{3,2,1,0:T(8,128)(2,1)S(1)}, u32[]{:S(2)}, u32[]{:S(2)}) collective-permute-start(bf16[4,2,256,128]{3,2,1,0:T(8,128)(2,1)S(1)} %pad_maximum_fusion.refs_0_), channel_id=1, source_target_pairs={{0,2},{1,3},{2,4},{3,5},{4,6},{5,7},{6,0},{7,1},{8,10},{9,11},{10,... | collective-permute-start | bytes 1572872 | tf_op jit(solution)/shard_map/ppermute | solution.py:183
  13.7 0.7 iota_compare_fusion
  14.5 0.8 copy.18
  15.4 16.9 %collective-permute-done.11 = bf16[2,256,128]{2,1,0:T(8,128)(2,1)S(1)} collective-permute-done((bf16[2,256,128]{2,1,0:T(8,128)(2,1)S(1)}, bf16[2,256,128]{2,1,0:T(8,128)(2,1)S(1)}, u32[]{:S(2)}, u32[]{:S(2)}) %collective-permute-start.11) | collective-permute-done | bytes 131104 | tf_op jit(solution)/shard_map/ppermute | solution.py:183
  32.5 2.5 %collective-permute-start.15 = (bf16[4,2,256,128]{3,2,1,0:T(8,128)(2,1)S(1)}, bf16[4,2,256,128]{3,2,1,0:T(8,128)(2,1)S(1)}, u32[]{:S(2)}, u32[]{:S(2)}) collective-permute-start(bf16[4,2,256,128]{3,2,1,0:T(8,128)(2,1)S(1)} %pad_maximum_fusion.1.refs_8_), channel_id=1, source_target_pairs={{0,24},{8,16},{16,8},{24,0},{1,25},{9,17},{17,9},{25,1},{2,26},{10... | collective-permute-start | bytes 1572872 | tf_op jit(solution)/shard_map/ppermute | solution.py:179
  35.2 0.5 collective-permute-start.14
  35.7 0.5 collective-permute-start.13
  36.2 12.0 %collective-permute-done.15.refs_11_ = bf16[4,2,256,128]{3,2,1,0:T(8,128)(2,1)S(1)} collective-permute-done((bf16[4,2,256,128]{3,2,1,0:T(8,128)(2,1)S(1)}, bf16[4,2,256,128]{3,2,1,0:T(8,128)(2,1)S(1)}, u32[]{:S(2)}, u32[]{:S(2)}) %collective-permute-start.15) | collective-permute-done | bytes 524320 | tf_op jit(solution)/shard_map/ppermute | solution.py:179
  48.2 2.6 %collective-permute-done.4.refs_2_ = bf16[4,2,256,128]{3,2,1,0:T(8,128)(2,1)S(1)} collective-permute-done((bf16[4,2,256,128]{3,2,1,0:T(8,128)(2,1)S(1)}, bf16[4,2,256,128]{3,2,1,0:T(8,128)(2,1)S(1)}, u32[]{:S(2)}, u32[]{:S(2)}) %collective-permute-start.4) | collective-permute-done | bytes 524320 | tf_op jit(solution)/shard_map/ppermute | solution.py:183
  50.8 11.2 %shard_map.46.refs_16_ = f32[4096,2048]{1,0:T(8,128)} custom-call(), custom_call_target="tpu_custom_call" | custom-call | bytes 33554432 | tf_op jit(solution)/shard_map/pallas_call | solution.py:149
  62.1 40.6 %all-gather = s32[256,128]{1,0:T(8,128)S(1)} all-gather(s32[8,128]{1,0:T(8,128)S(1)} %pad.9), channel_id=2, replica_groups=mesh['row'=4,'col'=8] {'row','col'}, dimensions={0}, use_global_device_ids=true | all-gather | bytes 135168 | tf_op jit(solution)/shard_map/all_gather | solution.py:195
  102.7 0.6 gather_fusion
  104.8 0.6 copy.23
  105.5 0.7 copy.20.place_ref
  106.1 1.0 collective-permute-done.18.refs_14_
  107.1 0.8 collective-permute-done.17.refs_13_
  107.9 0.7 collective-permute-done.9.refs_7_
  108.7 13.3 %shard_map.47 = f32[4096,2048]{1,0:T(8,128)} custom-call(s32[32,4]{1,0:T(8,128)} %copy.20.place_ref, f32[32,256]{1,0:T(8,128)} %bitcast.41, bf16[4,2,256,128]{3,2,1,0:T(8,128)(2,1)} %copy-done, bf16[4,2,256,128]{3,2,1,0:T(8,128)(2,1)} %copy-done.2, bf16[4,2,256,128]{3,2,1,0:T(8,128)(2,1)} %copy-done.5, ...), custom_call_target="tpu_custom_call", output_to_operand_aliasing={{}: (18, {})} | custom-call | flops 1000000000 | bytes 16777216 | tf_op jit(solution)/shard_map/pallas_call | solution.py:109
  (60 shorter events, 2.4 us)
Async XLA Ops:
  1.4 8.6 %collective-permute-start.2 = (bf16[2,256,128]{2,1,0:T(8,128)(2,1)S(1)}, bf16[2,256,128]{2,1,0:T(8,128)(2,1)S(1)}, u32[]{:S(2)}, u32[]{:S(2)}) collective-permute-start(bf16[2,256,128]{2,1,0:T(8,128)(2,1)S(1)} %get-tuple-element.7), channel_id=1, source_target_pairs={{0,24},{8,16},{16,8},{24,0},{1,25},{9,17},{17,9},{25,1},{2,26},{10... | collective-permute-start | bytes 393224 | tf_op jit(solution)/shard_map/ppermute | solution.py:179
  5.4 6.6 %collective-permute-start.1 = (bf16[2,256,128]{2,1,0:T(8,128)(2,1)S(1)}, bf16[2,256,128]{2,1,0:T(8,128)(2,1)S(1)}, u32[]{:S(2)}, u32[]{:S(2)}) collective-permute-start(bf16[2,256,128]{2,1,0:T(8,128)(2,1)S(1)} %get-tuple-element.8), channel_id=1, source_target_pairs={{0,16},{8,24},{16,0},{24,8},{1,17},{9,25},{17,1},{25,9},{2,18},{10... | collective-permute-start | bytes 393224 | tf_op jit(solution)/shard_map/ppermute | solution.py:179
  5.9 6.1 %collective-permute-start = (bf16[2,256,128]{2,1,0:T(8,128)(2,1)S(1)}, bf16[2,256,128]{2,1,0:T(8,128)(2,1)S(1)}, u32[]{:S(2)}, u32[]{:S(2)}) collective-permute-start(bf16[2,256,128]{2,1,0:T(8,128)(2,1)S(1)} %get-tuple-element.9), channel_id=1, source_target_pairs={{0,8},{8,0},{16,24},{24,16},{1,9},{9,1},{17,25},{25,17},{2,10},{10... | collective-permute-start | bytes 393224 | tf_op jit(solution)/shard_map/ppermute | solution.py:179
  6.0 9.4 %collective-permute-start.10 = (bf16[2,256,128]{2,1,0:T(8,128)(2,1)S(1)}, bf16[2,256,128]{2,1,0:T(8,128)(2,1)S(1)}, u32[]{:S(2)}, u32[]{:S(2)}) collective-permute-start(bf16[2,256,128]{2,1,0:T(8,128)(2,1)S(1)} %get-tuple-element.6), channel_id=1, source_target_pairs={{0,2},{1,3},{2,4},{3,5},{4,6},{5,7},{6,0},{7,1},{8,10},{9,11},{10,... | collective-permute-start | bytes 393224 | tf_op jit(solution)/shard_map/ppermute | solution.py:183
  8.0 7.4 %collective-permute-start.12 = (bf16[2,256,128]{2,1,0:T(8,128)(2,1)S(1)}, bf16[2,256,128]{2,1,0:T(8,128)(2,1)S(1)}, u32[]{:S(2)}, u32[]{:S(2)}) collective-permute-start(bf16[2,256,128]{2,1,0:T(8,128)(2,1)S(1)} %get-tuple-element.11), channel_id=1, source_target_pairs={{0,6},{1,7},{2,0},{3,1},{4,2},{5,3},{6,4},{7,5},{8,14},{9,15},{10,... | collective-permute-start | bytes 393224 | tf_op jit(solution)/shard_map/ppermute | solution.py:183
  10.0 22.3 %collective-permute-start.11 = (bf16[2,256,128]{2,1,0:T(8,128)(2,1)S(1)}, bf16[2,256,128]{2,1,0:T(8,128)(2,1)S(1)}, u32[]{:S(2)}, u32[]{:S(2)}) collective-permute-start(bf16[2,256,128]{2,1,0:T(8,128)(2,1)S(1)} %get-tuple-element.12), channel_id=1, source_target_pairs={{0,4},{1,5},{2,6},{3,7},{4,0},{5,1},{6,2},{7,3},{8,12},{9,13},{10,... | collective-permute-start | bytes 393224 | tf_op jit(solution)/shard_map/ppermute | solution.py:183
  12.0 96.6 %copy-start = (bf16[4,2,256,128]{3,2,1,0:T(8,128)(2,1)}, bf16[4,2,256,128]{3,2,1,0:T(8,128)(2,1)S(1)}, u32[]{:S(2)}) copy-start(bf16[4,2,256,128]{3,2,1,0:T(8,128)(2,1)S(1)} %pad_maximum_fusion.refs_0_) | copy-start | bytes 1572868
  12.0 22.9 %collective-permute-start.3 = (bf16[4,2,256,128]{3,2,1,0:T(8,128)(2,1)S(1)}, bf16[4,2,256,128]{3,2,1,0:T(8,128)(2,1)S(1)}, u32[]{:S(2)}, u32[]{:S(2)}) collective-permute-start(bf16[4,2,256,128]{3,2,1,0:T(8,128)(2,1)S(1)} %pad_maximum_fusion.refs_0_), channel_id=1, source_target_pairs={{0,2},{1,3},{2,4},{3,5},{4,6},{5,7},{6,0},{7,1},{8,10},{9,11},{10,... | collective-permute-start | bytes 1572872 | tf_op jit(solution)/shard_map/ppermute | solution.py:183
  32.4 76.3 %copy-start.1 = (bf16[4,2,256,128]{3,2,1,0:T(8,128)(2,1)}, bf16[4,2,256,128]{3,2,1,0:T(8,128)(2,1)S(1)}, u32[]{:S(2)}) copy-start(bf16[4,2,256,128]{3,2,1,0:T(8,128)(2,1)S(1)} %pad_maximum_fusion.1.refs_8_) | copy-start | bytes 1572868
  32.4 3.8 %collective-permute-start.16 = (bf16[4,2,256,128]{3,2,1,0:T(8,128)(2,1)S(1)}, bf16[4,2,256,128]{3,2,1,0:T(8,128)(2,1)S(1)}, u32[]{:S(2)}, u32[]{:S(2)}) collective-permute-start(bf16[4,2,256,128]{3,2,1,0:T(8,128)(2,1)S(1)} %pad_maximum_fusion.1.refs_8_), channel_id=1, source_target_pairs={{0,1},{1,0},{2,3},{3,2},{4,5},{5,4},{6,7},{7,6},{8,9},{9,8},{10,11... | collective-permute-start | bytes 1572872 | tf_op jit(solution)/shard_map/ppermute | solution.py:186
  32.5 15.7 %collective-permute-start.15 = (bf16[4,2,256,128]{3,2,1,0:T(8,128)(2,1)S(1)}, bf16[4,2,256,128]{3,2,1,0:T(8,128)(2,1)S(1)}, u32[]{:S(2)}, u32[]{:S(2)}) collective-permute-start(bf16[4,2,256,128]{3,2,1,0:T(8,128)(2,1)S(1)} %pad_maximum_fusion.1.refs_8_), channel_id=1, source_target_pairs={{0,24},{8,16},{16,8},{24,0},{1,25},{9,17},{17,9},{25,1},{2,26},{10... | collective-permute-start | bytes 1572872 | tf_op jit(solution)/shard_map/ppermute | solution.py:179
  35.0 73.7 %copy-start.2 = (bf16[4,2,256,128]{3,2,1,0:T(8,128)(2,1)}, bf16[4,2,256,128]{3,2,1,0:T(8,128)(2,1)S(1)}, u32[]{:S(2)}) copy-start(bf16[4,2,256,128]{3,2,1,0:T(8,128)(2,1)S(1)} %collective-permute-done.3.refs_1_) | copy-start | bytes 1572868
  35.0 15.8 %collective-permute-start.4 = (bf16[4,2,256,128]{3,2,1,0:T(8,128)(2,1)S(1)}, bf16[4,2,256,128]{3,2,1,0:T(8,128)(2,1)S(1)}, u32[]{:S(2)}, u32[]{:S(2)}) collective-permute-start(bf16[4,2,256,128]{3,2,1,0:T(8,128)(2,1)S(1)} %collective-permute-done.3.refs_1_), channel_id=1, source_target_pairs={{0,2},{1,3},{2,4},{3,5},{4,6},{5,7},{6,0},{7,1},{8,10},{9,11},{10,... | collective-permute-start | bytes 1572872 | tf_op jit(solution)/shard_map/ppermute | solution.py:183
  35.2 68.2 %collective-permute-start.14 = (bf16[4,2,256,128]{3,2,1,0:T(8,128)(2,1)S(1)}, bf16[4,2,256,128]{3,2,1,0:T(8,128)(2,1)}, u32[]{:S(2)}, u32[]{:S(2)}) collective-permute-start(bf16[4,2,256,128]{3,2,1,0:T(8,128)(2,1)S(1)} %pad_maximum_fusion.1.refs_8_), channel_id=1, source_target_pairs={{0,16},{8,24},{16,0},{24,8},{1,17},{9,25},{17,1},{25,9},{2,18},{10... | collective-permute-start | bytes 1572872 | tf_op jit(solution)/shard_map/ppermute | solution.py:179
  35.7 68.1 %collective-permute-start.13 = (bf16[4,2,256,128]{3,2,1,0:T(8,128)(2,1)S(1)}, bf16[4,2,256,128]{3,2,1,0:T(8,128)(2,1)}, u32[]{:S(2)}, u32[]{:S(2)}) collective-permute-start(bf16[4,2,256,128]{3,2,1,0:T(8,128)(2,1)S(1)} %pad_maximum_fusion.1.refs_8_), channel_id=1, source_target_pairs={{0,8},{8,0},{16,24},{24,16},{1,9},{9,1},{17,25},{25,17},{2,10},{10... | collective-permute-start | bytes 1572872 | tf_op jit(solution)/shard_map/ppermute | solution.py:179
  36.2 72.5 %copy-start.3 = (bf16[4,2,256,128]{3,2,1,0:T(8,128)(2,1)}, bf16[4,2,256,128]{3,2,1,0:T(8,128)(2,1)S(1)}, u32[]{:S(2)}) copy-start(bf16[4,2,256,128]{3,2,1,0:T(8,128)(2,1)S(1)} %collective-permute-done.16.refs_12_) | copy-start | bytes 1572868
  36.2 67.7 %collective-permute-start.6 = (bf16[4,2,256,128]{3,2,1,0:T(8,128)(2,1)S(1)}, bf16[4,2,256,128]{3,2,1,0:T(8,128)(2,1)}, u32[]{:S(2)}, u32[]{:S(2)}) collective-permute-start(bf16[4,2,256,128]{3,2,1,0:T(8,128)(2,1)S(1)} %pad_maximum_fusion.refs_0_), channel_id=1, source_target_pairs={{0,1},{1,0},{2,3},{3,2},{4,5},{5,4},{6,7},{7,6},{8,9},{9,8},{10,11... | collective-permute-start | bytes 1572872 | tf_op jit(solution)/shard_map/ppermute | solution.py:186
  48.2 56.1 %collective-permute-start.19 = (bf16[4,2,256,128]{3,2,1,0:T(8,128)(2,1)S(1)}, bf16[4,2,256,128]{3,2,1,0:T(8,128)(2,1)}, u32[]{:S(2)}, u32[]{:S(2)}) collective-permute-start(bf16[4,2,256,128]{3,2,1,0:T(8,128)(2,1)S(1)} %collective-permute-done.15.refs_11_), channel_id=1, source_target_pairs={{0,1},{1,0},{2,3},{3,2},{4,5},{5,4},{6,7},{7,6},{8,9},{9,8},{10,11... | collective-permute-start | bytes 1572872 | tf_op jit(solution)/shard_map/ppermute | solution.py:186
  50.8 53.7 %collective-permute-start.5 = (bf16[4,2,256,128]{3,2,1,0:T(8,128)(2,1)S(1)}, bf16[4,2,256,128]{3,2,1,0:T(8,128)(2,1)}, u32[]{:S(2)}, u32[]{:S(2)}) collective-permute-start(bf16[4,2,256,128]{3,2,1,0:T(8,128)(2,1)S(1)} %collective-permute-done.4.refs_2_), channel_id=1, source_target_pairs={{0,2},{1,3},{2,4},{3,5},{4,6},{5,7},{6,0},{7,1},{8,10},{9,11},{10,... | collective-permute-start | bytes 1572872 | tf_op jit(solution)/shard_map/ppermute | solution.py:183
  103.4 4.5 %collective-permute-start.7 = (bf16[4,2,256,128]{3,2,1,0:T(8,128)(2,1)S(1)}, bf16[4,2,256,128]{3,2,1,0:T(8,128)(2,1)}, u32[]{:S(2)}, u32[]{:S(2)}) collective-permute-start(bf16[4,2,256,128]{3,2,1,0:T(8,128)(2,1)S(1)} %collective-permute-done.3.refs_1_), channel_id=1, source_target_pairs={{0,1},{1,0},{2,3},{3,2},{4,5},{5,4},{6,7},{7,6},{8,9},{9,8},{10,11... | collective-permute-start | bytes 1572872 | tf_op jit(solution)/shard_map/ppermute | solution.py:186
  103.8 3.4 %collective-permute-start.18 = (bf16[4,2,256,128]{3,2,1,0:T(8,128)(2,1)}, bf16[4,2,256,128]{3,2,1,0:T(8,128)(2,1)}, u32[]{:S(2)}, u32[]{:S(2)}) collective-permute-start(bf16[4,2,256,128]{3,2,1,0:T(8,128)(2,1)} %collective-permute-done.14.refs_10_), channel_id=1, source_target_pairs={{0,1},{1,0},{2,3},{3,2},{4,5},{5,4},{6,7},{7,6},{8,9},{9,8},{10,11... | collective-permute-start | bytes 1572872 | tf_op jit(solution)/shard_map/ppermute | solution.py:186
  103.9 4.0 %collective-permute-start.17 = (bf16[4,2,256,128]{3,2,1,0:T(8,128)(2,1)}, bf16[4,2,256,128]{3,2,1,0:T(8,128)(2,1)}, u32[]{:S(2)}, u32[]{:S(2)}) collective-permute-start(bf16[4,2,256,128]{3,2,1,0:T(8,128)(2,1)} %collective-permute-done.13.refs_9_), channel_id=1, source_target_pairs={{0,1},{1,0},{2,3},{3,2},{4,5},{5,4},{6,7},{7,6},{8,9},{9,8},{10,11... | collective-permute-start | bytes 1572872 | tf_op jit(solution)/shard_map/ppermute | solution.py:186
  104.3 3.6 %collective-permute-start.8 = (bf16[4,2,256,128]{3,2,1,0:T(8,128)(2,1)S(1)}, bf16[4,2,256,128]{3,2,1,0:T(8,128)(2,1)}, u32[]{:S(2)}, u32[]{:S(2)}) collective-permute-start(bf16[4,2,256,128]{3,2,1,0:T(8,128)(2,1)S(1)} %collective-permute-done.4.refs_2_), channel_id=1, source_target_pairs={{0,1},{1,0},{2,3},{3,2},{4,5},{5,4},{6,7},{7,6},{8,9},{9,8},{10,11... | collective-permute-start | bytes 1572872 | tf_op jit(solution)/shard_map/ppermute | solution.py:186
  104.4 4.2 %collective-permute-start.9 = (bf16[4,2,256,128]{3,2,1,0:T(8,128)(2,1)}, bf16[4,2,256,128]{3,2,1,0:T(8,128)(2,1)}, u32[]{:S(2)}, u32[]{:S(2)}) collective-permute-start(bf16[4,2,256,128]{3,2,1,0:T(8,128)(2,1)} %collective-permute-done.5.refs_3_), channel_id=1, source_target_pairs={{0,1},{1,0},{2,3},{3,2},{4,5},{5,4},{6,7},{7,6},{8,9},{9,8},{10,11... | collective-permute-start | bytes 1572872 | tf_op jit(solution)/shard_map/ppermute | solution.py:186
  (3 other events, 180.5 us)

commit v2 on v1

v2 whole, which is shorter than its diff:
```python
import functools

import jax
import jax.numpy as jnp
from jax import lax
from jax.experimental import pallas as pl
from jax.experimental.pallas import tpu as pltpu
from jax.sharding import PartitionSpec as P

TILES = 128
CORES = 2
STREAMS = 2
META = 16
MIB = 1024 * 1024


def pack_kernel(n_row, n_chip, slots, sens_ref, class_ref, ids_ref, counts_ref, *outs):
    r = lax.axis_index("row")
    z = lax.div(lax.axis_index("col"), CORES)
    rows, width = sens_ref.shape[2:]
    classes = class_ref[...]
    scale = jnp.where(
        classes == 0, 1.0, jnp.where(classes == 1, 0.5, jnp.where(classes == 2, 0.25, 0.125))
    ).astype(jnp.float32)
    scale = jnp.broadcast_to(scale, (width, rows)).T

    def tile(owner, slot):
        return (sens_ref[owner, slot].astype(jnp.float32) * scale).astype(jnp.bfloat16)

    for j in range(n_row):
        owner = r ^ j
        for i in range(slots):
            outs[j][i] = tile(owner, i)

    lane = lax.broadcasted_iota(jnp.int32, (META, width), 1)
    meta = jnp.zeros((META, width), jnp.float32)
    for q in range(n_row):
        for i in range(slots):
            place = jnp.where(i < counts_ref[q], ids_ref[q, i], -1)
            meta = jnp.where(lane == q * slots + i, place.astype(jnp.float32), meta)
    meta = meta.astype(jnp.bfloat16)
    for s in range(n_chip):
        owner = lax.rem(z + s, n_chip)
        out = outs[n_row + s]
        for i in range(slots):
            out[i * rows : (i + 1) * rows] = tile(owner, i)
        out[slots * rows :] = meta


def pack(sensitivity, weight_class, tile_ids, counts, n_chip):
    n_row, slots, rows, width = sensitivity.shape
    vmem = pl.BlockSpec(memory_space=pltpu.VMEM)
    smem = pl.BlockSpec(memory_space=pltpu.SMEM)
    return pl.pallas_call(
        functools.partial(pack_kernel, n_row, n_chip, slots),
        out_shape=[jax.ShapeDtypeStruct((slots, rows, width), jnp.bfloat16)] * n_row
        + [jax.ShapeDtypeStruct((slots * rows + META, width), jnp.bfloat16)] * n_chip,
        in_specs=[vmem, vmem, smem, smem],
        out_specs=[vmem] * (n_row + n_chip),
    )(sensitivity, weight_class, tile_ids, counts)


def tile_of(place, station, r, z, core, i, j, slots, per_col, none):
    left = place[station, r * slots + i]
    right = place[station, z * slots + j] - core * per_col
    inside = (left >= 0) & (right >= 0) & (right < per_col)
    return jnp.where(inside, left * per_col + right, none)


def block_of(out_ref, tile, per_col, width):
    rows = pl.ds(pl.multiple_of(lax.div(tile, per_col) * width, width), width)
    columns = pl.ds(pl.multiple_of(lax.rem(tile, per_col) * width, width), width)
    return out_ref.at[rows, columns]


def gram_of(left, right, slots):
    a = jnp.concatenate([left(i).T for i in range(slots)], axis=0)
    b = jnp.concatenate([right(j) for j in range(slots)], axis=1)
    return jnp.dot(a, b, preferred_element_type=jnp.float32)


def main_kernel(n_row, n_chip, slots, per_row, per_col, *refs):
    last = n_chip - 1
    n_left = last * STREAMS * CORES
    n_right = n_row * CORES
    sources = refs[: n_left + n_right]
    out_ref, carry_ref, right_ref, slot_ref, tile_ref = refs[n_left + n_right + 1 :][:5]
    (acc, left_buf, right_buf, gram_buf, meta_buf, place, touches, done, owner,
     load_sem, meta_sem, right_sem, store_sem) = refs[n_left + n_right + 6 :]
    r = lax.axis_index("row")
    c = lax.axis_index("col")
    z, core = lax.div(c, CORES), lax.rem(c, CORES)
    rows, width = left_buf.shape[-2:]
    half = n_row // STREAMS
    tiles = per_row * per_col
    pairs = [(i, j) for i in range(slots) for j in range(slots)]

    def load(index):
        target = left_buf.at[index] if index < n_left else right_buf.at[index - n_left]
        return pltpu.make_async_copy(sources[index], target, load_sem.at[index])

    for index in [*range(n_left, n_left + n_right), *range(n_left)]:
        load(index).start()

    def clear(index, carry):
        touches[index] = 0
        done[index] = 0
        owner[index] = -1
        return carry

    lax.fori_loop(0, tiles + 1, clear, 0)

    for index in range(n_right):
        load(n_left + index).wait()
        for s in range(n_chip):
            meta = right_buf[index, s, slots * rows :].astype(jnp.float32)
            meta_buf[index * n_chip + s : index * n_chip + s + 1, :] = meta[:1].astype(jnp.int32)
    to_smem = pltpu.make_async_copy(meta_buf, place, meta_sem)
    to_smem.start()
    right_out = [
        pltpu.make_async_copy(
            right_buf.at[index, last, pl.ds(0, slots * rows)],
            right_ref.at[index],
            right_sem.at[index],
        )
        for index in range(n_right)
    ]
    for copy in right_out:
        copy.start()
    to_smem.wait()

    def find(station, i, j, none):
        return tile_of(place, station, r, z, core, i, j, slots, per_col, none)

    def number(index, used):
        for n, (i, j) in enumerate(pairs):
            tile = find(index * n_chip + last, i, j, tiles)
            held = owner[tile]
            fresh = (held < 0) & (tile < tiles)
            spot = jnp.where(tile == tiles, len(pairs) * n_right, jnp.where(fresh, used, held))
            slot_ref[index * len(pairs) + n] = 2 * spot + fresh.astype(jnp.int32)
            owner[tile] = jnp.where(tile == tiles, -1, spot)
            tile_ref[jnp.where(fresh, used, len(pairs) * n_right)] = tile
            used = used + fresh.astype(jnp.int32)
        return used

    used = lax.fori_loop(0, n_right, number, 0)
    tile_ref[len(pairs) * n_right] = used

    def station_of(step):
        s = lax.div(step, n_right)
        index = lax.rem(step, n_right)
        return s, index, index * n_chip + s

    def count(step, carry):
        _, _, station = station_of(step)
        for i, j in pairs:
            tile = find(station, i, j, tiles)
            touches[tile] = touches[tile] + 1
        return carry

    lax.fori_loop(0, last * n_right, count, 0)

    def store(tile):
        return pltpu.make_async_copy(
            acc.at[tile], block_of(out_ref, tile, per_col, width), store_sem
        )

    for index in range(n_left):
        load(index).wait()

    def add(step, stored):
        s, index, station = station_of(step)
        other, j_row = lax.div(index, n_row), lax.rem(index, n_row)
        stream, place_in = lax.div(j_row, half), lax.rem(j_row, half)
        source = (s * STREAMS + stream) * CORES + other
        gram_buf[...] = gram_of(
            lambda i: left_buf[source, place_in, i],
            lambda j: right_buf[index, s, j * rows : (j + 1) * rows],
            slots,
        )
        for i, j in pairs:
            tile = find(station, i, j, tiles)
            seen = done[tile]
            gram = gram_buf[i * width : (i + 1) * width, j * width : (j + 1) * width]
            acc[tile] = jnp.where(seen == 0, gram, acc[tile] + gram)
            done[tile] = seen + 1
            ready = (seen + 1 == touches[tile]) & (tile < tiles) & (owner[tile] < 0)

            @pl.when(ready)
            def _():
                store(tile).start()

            stored = stored + ready.astype(jnp.int32)
        return stored

    stored = lax.fori_loop(0, last * n_right, add, 0)

    def hand_on(spot, carry):
        tile = tile_ref[spot]
        carry_ref[spot] = jnp.where(done[tile] == 0, 0.0, acc[tile])
        return carry

    lax.fori_loop(0, used, hand_on, 0)

    def drain(index, carry):
        store(0).wait()
        return carry

    lax.fori_loop(0, stored, drain, 0)
    for copy in right_out:
        copy.wait()


def main_part(left, right, zeros, per_row, per_col):
    last, n_chip = len(left), len(left) + 1
    n_row = len(right) // CORES
    _, slots, rows, width = left[0][0][0].shape
    flat = [x for chip in left for stream in chip for x in stream]
    chunks = len(flat) + len(right)
    tiles = per_row * per_col
    pairs = slots * slots * len(right)
    stations = n_chip * len(right)
    anywhere = pl.BlockSpec(memory_space=pl.ANY)
    vmem = pl.BlockSpec(memory_space=pltpu.VMEM)
    smem = pl.BlockSpec(memory_space=pltpu.SMEM)
    return pl.pallas_call(
        functools.partial(main_kernel, n_row, n_chip, slots, per_row, per_col),
        out_shape=[
            jax.ShapeDtypeStruct(zeros.shape, zeros.dtype),
            jax.ShapeDtypeStruct((pairs + 1, width, width), jnp.float32),
            jax.ShapeDtypeStruct((len(right), slots * rows, width), jnp.bfloat16),
            jax.ShapeDtypeStruct((pairs,), jnp.int32),
            jax.ShapeDtypeStruct((pairs + 1,), jnp.int32),
        ],
        in_specs=[anywhere] * (chunks + 1),
        out_specs=[anywhere, vmem, anywhere, smem, smem],
        scratch_shapes=[
            pltpu.VMEM((tiles + 1, width, width), jnp.float32),
            pltpu.VMEM((len(flat), n_row // STREAMS, slots, rows, width), jnp.bfloat16),
            pltpu.VMEM((len(right), n_chip, slots * rows + META, width), jnp.bfloat16),
            pltpu.VMEM((slots * width, slots * width), jnp.float32),
            pltpu.VMEM((stations, width), jnp.int32),
            pltpu.SMEM((stations, width), jnp.int32),
            pltpu.SMEM((tiles + 1,), jnp.int32),
            pltpu.SMEM((tiles + 1,), jnp.int32),
            pltpu.SMEM((tiles + 1,), jnp.int32),
            pltpu.SemaphoreType.DMA((chunks,)),
            pltpu.SemaphoreType.DMA,
            pltpu.SemaphoreType.DMA((len(right),)),
            pltpu.SemaphoreType.DMA,
        ],
        input_output_aliases={chunks: 0},
        compiler_params=pltpu.CompilerParams(vmem_limit_bytes=52 * MIB),
        cost_estimate=pl.CostEstimate(flops=10**9, bytes_accessed=16 * MIB, transcendentals=0),
    )(*flat, *right, zeros)


def tail_kernel(n_row, slots, per_col, slot_ref, tile_ref, *refs):
    lefts = refs[: STREAMS * CORES]
    carry_ref, right_ref = refs[STREAMS * CORES : STREAMS * CORES + 2]
    out_ref, acc, gram_buf, store_sem = refs[STREAMS * CORES + 3 :]
    rows, width = lefts[0].shape[-2:]
    half = n_row // STREAMS
    pairs = [(i, j) for i in range(slots) for j in range(slots)]

    for other in range(CORES):
        for stream in range(STREAMS):
            left = lefts[stream * CORES + other]

            def add(place_in, carry, left=left, base=other * n_row + stream * half):
                index = base + place_in
                gram_buf[...] = gram_of(
                    lambda i: left[place_in, i],
                    lambda j: right_ref[index, j * rows : (j + 1) * rows],
                    slots,
                )
                for n, (i, j) in enumerate(pairs):
                    code = slot_ref[index * len(pairs) + n]
                    spot, fresh = lax.shift_right_logical(code, 1), code & 1
                    gram = gram_buf[i * width : (i + 1) * width, j * width : (j + 1) * width]
                    acc[spot] = jnp.where(fresh == 1, carry_ref[spot], acc[spot]) + gram
                return carry

            lax.fori_loop(0, half, add, 0)

    def store(spot):
        return pltpu.make_async_copy(
            acc.at[spot], block_of(out_ref, tile_ref[spot], per_col, width), store_sem
        )

    def start(spot, carry):
        store(spot).start()
        return carry

    def drain(spot, carry):
        store(spot).wait()
        return carry

    used = tile_ref[len(pairs) * CORES * n_row]
    lax.fori_loop(0, used, start, 0)
    lax.fori_loop(0, used, drain, 0)


def tail_part(left, carried, right, slot, tile, out, per_col):
    flat = [x for stream in left for x in stream]
    half, slots, _, width = flat[0].shape
    anywhere = pl.BlockSpec(memory_space=pl.ANY)
    vmem = pl.BlockSpec(memory_space=pltpu.VMEM)
    smem = pl.BlockSpec(memory_space=pltpu.SMEM)
    return pl.pallas_call(
        functools.partial(tail_kernel, half * STREAMS, slots, per_col),
        out_shape=jax.ShapeDtypeStruct(out.shape, out.dtype),
        in_specs=[smem, smem] + [vmem] * (len(flat) + 2) + [anywhere],
        out_specs=anywhere,
        scratch_shapes=[
            pltpu.VMEM(carried.shape, jnp.float32),
            pltpu.VMEM((slots * width, slots * width), jnp.float32),
            pltpu.SemaphoreType.DMA,
        ],
        input_output_aliases={len(flat) + 4: 0},
        compiler_params=pltpu.CompilerParams(vmem_limit_bytes=32 * MIB),
        cost_estimate=pl.CostEstimate(flops=3 * 10**8, bytes_accessed=8 * MIB, transcendentals=0),
    )(slot, tile, *flat, carried, right, out)


def zero_kernel(out_ref, block, sem):
    block[...] = jnp.zeros_like(block)
    height = block.shape[0]
    copies = [
        pltpu.make_async_copy(block, out_ref.at[pl.ds(index * height, height)], sem.at[index])
        for index in range(out_ref.shape[0] // height)
    ]
    for copy in copies:
        copy.start()
    for copy in copies:
        copy.wait()


def zero_fill(height, width):
    step = 128
    return pl.pallas_call(
        zero_kernel,
        out_shape=jax.ShapeDtypeStruct((height, width), jnp.float32),
        out_specs=pl.BlockSpec(memory_space=pl.ANY),
        scratch_shapes=[
            pltpu.VMEM((step, width), jnp.float32),
            pltpu.SemaphoreType.DMA((height // step,)),
        ],
        cost_estimate=pl.CostEstimate(
            flops=0, bytes_accessed=height * width * 4, transcendentals=0
        ),
    )()


def local(sensitivity, tile_ids, counts, weight_class):
    n_row = lax.axis_size("row")
    n_col = lax.axis_size("col")
    n_chip = n_col // CORES
    per_row = TILES // n_row
    per_col = TILES // n_col

    def flip_row(value, j):
        return lax.ppermute(value, "row", [(i, i ^ j) for i in range(n_row)])

    def shift_chip(value, s):
        pairs = [(i, (i + CORES * s) % n_col) for i in range(n_col)]
        return lax.ppermute(value, "col", pairs)

    def flip_core(value):
        return lax.ppermute(value, "col", [(i, i ^ 1) for i in range(n_col)])

    parts = pack(sensitivity[0], weight_class, tile_ids[0], counts[0], n_chip)
    to_row, to_chip = parts[:n_row], parts[n_row:]
    right = jnp.stack([to_chip[0]] + [shift_chip(to_chip[s], s) for s in range(1, n_chip)])
    plane = [to_row[0]] + [flip_row(to_row[j], j) for j in range(1, n_row)]
    half = n_row // STREAMS
    left = [[jnp.stack(plane[k * half : (k + 1) * half]) for k in range(STREAMS)]]
    for _ in range(1, n_chip):
        left.append([shift_chip(x, 1) for x in left[-1]])
    right = [right] + [flip_row(right, j) for j in range(1, n_row)]
    right = right + [flip_core(x) for x in right]
    left = [[[x, flip_core(x)] for x in chip] for chip in left]

    width = sensitivity.shape[-1]
    zeros = zero_fill(per_row * width, per_col * width)
    out, carried, right, slot, tile = main_part(left[:-1], right, zeros, per_row, per_col)
    return tail_part(left[-1], carried, right, slot, tile, out, per_col)


def solution(mesh):
    in_specs = (
        P(("row", "col"), None, None, None, None),
        P(("row", "col"), None, None),
        P(("row", "col"), None),
        P(("row", "col"), None),
    )
    return jax.shard_map(
        local, mesh=mesh, in_specs=in_specs, out_specs=P("row", "col"), check_vma=False
    )
```

time: 123 us -> 116 us (0.943)
  blocking collectives: 40.6 us -> 0 us
  waiting for transfers between devices: 34.1 us -> 55.8 us
  Pallas kernels: 24.6 us -> 30.2 us
  starting transfers between devices: 17.2 us -> 22.5 us
    all_gather x1 -> x0, blocking collectives: 40.6 us -> none  [local(): meta = lax.all_gather(own_meta, ('row', 'col'), axis=0, tiled=False)]
    ppermute x6 -> x9, waiting for transfers between devices: 19.5 us -> 33.5 us  [shift_chip(): return lax.ppermute(value, 'col', pairs)]
    ppermute x6, waiting for transfers between devices: 12 us -> 20.5 us  [flip_row(): return lax.ppermute(value, 'row', [(i, i ^ j) for i in range(n_row)])]
    pallas_call x1 -> x3, Pallas kernels: 13.3 us -> 19 us  [the longest x1 13.5 us: main_part(): pl.pallas_call(functools.partial(main_kernel, n_row, n_chip, slots, per_r...]
    ppermute x6 -> x9, starting transfers between devices: 7.58 us -> 11.4 us  [shift_chip(): return lax.ppermute(value, 'col', pairs)]
    unnamed x16, local copies, waits for them, and re-layouts: 1.4 us -> 3.57 us
    another operation x2 -> x3, other arithmetic: 0.14 us -> 1.93 us  [the longest x1 0.97 us: local(): jnp.stack([to_chip[0]] + [shift_chip(to_chip[s], s) for s in range(1, n_c...]
    ppermute x6, starting transfers between devices: 8.15 us -> 9.85 us  [flip_row(): return lax.ppermute(value, 'row', [(i, i ^ j) for i in range(n_row)])]
  transfers between devices with their start and end apart: 20 -> 27, of which waited for: 6 -> 12; matrix products, arithmetic and copies ran while one was open for 3% -> 2% of each run, Pallas kernels for 9% -> 21%
where the time goes in v2:
time: 116 us
  waiting for transfers between devices  55.8 us (48%)
  Pallas kernels  30.2 us (26%)
  starting transfers between devices  22.5 us (19%)
  local copies, waits for them, and re-layouts  4.9 us (4%)
  other arithmetic  1.93 us (2%)
    ppermute x9, waiting for transfers between devices, shift_chip(): return lax.ppermute(value, 'col', pairs)  33.5 us
    ppermute x6, waiting for transfers between devices, flip_row(): return lax.ppermute(value, 'row', [(i, i ^ j) for i in range(n_row)])  20.5 us
    pallas_call x1, Pallas kernels, main_part(): pl.pallas_call(functools.partial(main_kernel, n_row, n_chip, slots, per_r...  13.5 us
    ppermute x9, starting transfers between devices, shift_chip(): return lax.ppermute(value, 'col', pairs)  11.4 us
    pallas_call x1, Pallas kernels, zero_fill(): pl.pallas_call(zero_kernel, out_shape=jax.ShapeDtypeStruct((height, width...  11.2 us
    ppermute x6, starting transfers between devices, flip_row(): return lax.ppermute(value, 'row', [(i, i ^ j) for i in range(n_row)])  9.85 us
    unnamed x16, local copies, waits for them, and re-layouts  3.57 us
    pallas_call x1, Pallas kernels, tail_part(): pl.pallas_call(functools.partial(tail_kernel, half * STREAMS, slots, per_...  3.18 us
  transfers between devices with their start and end apart: 27, of which 12 were waited for; matrix products, arithmetic and copies ran while one was open for 2% of the time, Pallas kernels for 21%

profile of v2, /device:TPU:0, one launch (start us, length us, event | category | flops | bytes accessed | tf_op | source)
XLA Modules:
  0.0 115.5 jit_solution(11108685496099608112)
XLA Ops:
  1.3 2.3 %shard_map.46 = (bf16[2,256,128]{2,1,0:T(8,128)(2,1)}, bf16[2,256,128]{2,1,0:T(8,128)(2,1)}, bf16[2,256,128]{2,1,0:T(8,128)(2,1)}, bf16[2,256,128]{2,1,0:T(8,128...) custom-call(bf16[4,2,256,128]{3,2,1,0:T(8,128)(2,1)} %bitcast.11, ...), custom_call_target="tpu_custom_call" | custom-call | tf_op jit(solution)/shard_map/pallas_call | solution.py:54
  3.6 3.0 %collective-permute-start.2 = (bf16[2,256,128]{2,1,0:T(8,128)(2,1)}, bf16[2,256,128]{2,1,0:T(8,128)(2,1)S(1)}, u32[]{:S(2)}, u32[]{:S(2)}) collective-permute-start(bf16[2,256,128]{2,1,0:T(8,128)(2,1)} %get-tuple-element.20), channel_id=1, source_target_pairs={{0,16},{8,24},{16,0},{24,8},{1,17},{9,25},{17,1},{25,9},{2,18},{10... | collective-permute-start | bytes 393224 | tf_op jit(solution)/shard_map/ppermute | solution.py:364
  8.1 4.4 %collective-permute-done.2 = bf16[2,256,128]{2,1,0:T(8,128)(2,1)S(1)} collective-permute-done((bf16[2,256,128]{2,1,0:T(8,128)(2,1)}, bf16[2,256,128]{2,1,0:T(8,128)(2,1)S(1)}, u32[]{:S(2)}, u32[]{:S(2)}) %collective-permute-start.2) | collective-permute-done | bytes 131104 | tf_op jit(solution)/shard_map/ppermute | solution.py:364
  12.5 1.6 %collective-permute-done.3 = bf16[2,256,128]{2,1,0:T(8,128)(2,1)S(1)} collective-permute-done((bf16[2,256,128]{2,1,0:T(8,128)(2,1)}, bf16[2,256,128]{2,1,0:T(8,128)(2,1)S(1)}, u32[]{:S(2)}, u32[]{:S(2)}) %collective-permute-start.3) | collective-permute-done | bytes 131104 | tf_op jit(solution)/shard_map/ppermute | solution.py:364
  14.1 1.6 %collective-permute-start.7 = (bf16[2,2,256,128]{3,2,1,0:T(8,128)(2,1)S(1)}, bf16[2,2,256,128]{3,2,1,0:T(8,128)(2,1)S(1)}, u32[]{:S(2)}, u32[]{:S(2)}) collective-permute-start(bf16[2,2,256,128]{3,2,1,0:T(8,128)(2,1)S(1)} %pad_maximum_fusion.2.refs_2_), channel_id=1, source_target_pairs={{0,2},{1,3},{2,4},{3,5},{4,6},{5,7},{6,0},{7,1},{8,10},{9,11},{10,... | collective-permute-start | bytes 786440 | tf_op jit(solution)/shard_map/ppermute | solution.py:368
  16.7 1.6 %collective-permute-start.5 = (bf16[2,2,256,128]{3,2,1,0:T(8,128)(2,1)S(1)}, bf16[2,2,256,128]{3,2,1,0:T(8,128)(2,1)S(1)}, u32[]{:S(2)}, u32[]{:S(2)}) collective-permute-start(bf16[2,2,256,128]{3,2,1,0:T(8,128)(2,1)S(1)} %pad_maximum_fusion.1.refs_0_), channel_id=1, source_target_pairs={{0,2},{1,3},{2,4},{3,5},{4,6},{5,7},{6,0},{7,1},{8,10},{9,11},{10,... | collective-permute-start | bytes 786440 | tf_op jit(solution)/shard_map/ppermute | solution.py:368
  18.3 2.2 %collective-permute-start.15 = (bf16[528,128]{1,0:T(8,128)(2,1)}, bf16[528,128]{1,0:T(8,128)(2,1)S(1)}, u32[]{:S(2)}, u32[]{:S(2)}) collective-permute-start(bf16[528,128]{1,0:T(8,128)(2,1)} %get-tuple-element.25), channel_id=1, source_target_pairs={{0,6},{1,7},{2,0},{3,1},{4,2},{5,3},{6,4},{7,5},{8,14},{9,15},{10,... | collective-permute-start | bytes 405512 | tf_op jit(solution)/shard_map/ppermute | solution.py:368
  21.7 9.6 %collective-permute-done.15 = bf16[528,128]{1,0:T(8,128)(2,1)S(1)} collective-permute-done((bf16[528,128]{1,0:T(8,128)(2,1)}, bf16[528,128]{1,0:T(8,128)(2,1)S(1)}, u32[]{:S(2)}, u32[]{:S(2)}) %collective-permute-start.15) | collective-permute-done | bytes 135200 | tf_op jit(solution)/shard_map/ppermute | solution.py:368
  31.3 3.3 %collective-permute-done.13 = bf16[528,128]{1,0:T(8,128)(2,1)S(1)} collective-permute-done((bf16[528,128]{1,0:T(8,128)(2,1)}, bf16[528,128]{1,0:T(8,128)(2,1)S(1)}, u32[]{:S(2)}, u32[]{:S(2)}) %collective-permute-start.13) | collective-permute-done | bytes 135200 | tf_op jit(solution)/shard_map/ppermute | solution.py:368
  34.6 1.6 %collective-permute-start.11 = (bf16[2,2,256,128]{3,2,1,0:T(8,128)(2,1)S(1)}, bf16[2,2,256,128]{3,2,1,0:T(8,128)(2,1)S(1)}, u32[]{:S(2)}, u32[]{:S(2)}) collective-permute-start(bf16[2,2,256,128]{3,2,1,0:T(8,128)(2,1)S(1)} %collective-permute-done.7.refs_6_), channel_id=1, source_target_pairs={{0,2},{1,3},{2,4},{3,5},{4,6},{5,7},{6,0},{7,1},{8,10},{9,11},{10,... | collective-permute-start | bytes 786440 | tf_op jit(solution)/shard_map/ppermute | solution.py:368
  36.2 2.4 %collective-permute-start.9 = (bf16[2,2,256,128]{3,2,1,0:T(8,128)(2,1)S(1)}, bf16[2,2,256,128]{3,2,1,0:T(8,128)(2,1)S(1)}, u32[]{:S(2)}, u32[]{:S(2)}) collective-permute-start(bf16[2,2,256,128]{3,2,1,0:T(8,128)(2,1)S(1)} %collective-permute-done.5.refs_4_), channel_id=1, source_target_pairs={{0,2},{1,3},{2,4},{3,5},{4,6},{5,7},{6,0},{7,1},{8,10},{9,11},{10,... | collective-permute-start | bytes 786440 | tf_op jit(solution)/shard_map/ppermute | solution.py:368
  41.3 1.6 %collective-permute-start.17 = (bf16[4,528,128]{2,1,0:T(8,128)(2,1)S(1)}, bf16[4,528,128]{2,1,0:T(8,128)(2,1)}, u32[]{:S(2)}, u32[]{:S(2)}) collective-permute-start(bf16[4,528,128]{2,1,0:T(8,128)(2,1)S(1)} %pad_maximum_fusion.refs_12_), channel_id=1, source_target_pairs={{0,16},{8,24},{16,0},{24,8},{1,17},{9,25},{17,1},{25,9},{2,18},{10... | collective-permute-start | bytes 1622024 | tf_op jit(solution)/shard_map/ppermute | solution.py:364
  42.9 2.6 %collective-permute-done.11.refs_10_ = bf16[2,2,256,128]{3,2,1,0:T(8,128)(2,1)S(1)} collective-permute-done((bf16[2,2,256,128]{3,2,1,0:T(8,128)(2,1)S(1)}, bf16[2,2,256,128]{3,2,1,0:T(8,128)(2,1)S(1)}, u32[]{:S(2)}, u32[]{:S(2)}) %collective-permute-start.11) | collective-permute-done | bytes 262176 | tf_op jit(solution)/shard_map/ppermute | solution.py:368
  45.5 2.3 %collective-permute-start.18 = (bf16[4,528,128]{2,1,0:T(8,128)(2,1)S(1)}, bf16[4,528,128]{2,1,0:T(8,128)(2,1)}, u32[]{:S(2)}, u32[]{:S(2)}) collective-permute-start(bf16[4,528,128]{2,1,0:T(8,128)(2,1)S(1)} %pad_maximum_fusion.refs_12_), channel_id=1, source_target_pairs={{0,24},{8,16},{16,8},{24,0},{1,25},{9,17},{17,9},{25,1},{2,26},{10... | collective-permute-start | bytes 1622024 | tf_op jit(solution)/shard_map/ppermute | solution.py:364
  47.8 2.9 %collective-permute-done.9.refs_8_ = bf16[2,2,256,128]{3,2,1,0:T(8,128)(2,1)S(1)} collective-permute-done((bf16[2,2,256,128]{3,2,1,0:T(8,128)(2,1)S(1)}, bf16[2,2,256,128]{3,2,1,0:T(8,128)(2,1)S(1)}, u32[]{:S(2)}, u32[]{:S(2)}) %collective-permute-start.9) | collective-permute-done | bytes 262176 | tf_op jit(solution)/shard_map/ppermute | solution.py:368
  51.2 1.8 %collective-permute-done.6.refs_5_ = bf16[2,2,256,128]{3,2,1,0:T(8,128)(2,1)S(1)} collective-permute-done((bf16[2,2,256,128]{3,2,1,0:T(8,128)(2,1)S(1)}, bf16[2,2,256,128]{3,2,1,0:T(8,128)(2,1)S(1)}, u32[]{:S(2)}, u32[]{:S(2)}) %collective-permute-start.6) | collective-permute-done | bytes 262176 | tf_op jit(solution)/shard_map/ppermute | solution.py:371
  53.2 1.9 %collective-permute-done.16.refs_13_ = bf16[4,528,128]{2,1,0:T(8,128)(2,1)} collective-permute-done((bf16[4,528,128]{2,1,0:T(8,128)(2,1)S(1)}, bf16[4,528,128]{2,1,0:T(8,128)(2,1)}, u32[]{:S(2)}, u32[]{:S(2)}) %collective-permute-start.16) | collective-permute-done | bytes 540704 | tf_op jit(solution)/shard_map/ppermute | solution.py:364
  55.1 12.6 %collective-permute-done.17.refs_14_ = bf16[4,528,128]{2,1,0:T(8,128)(2,1)} collective-permute-done((bf16[4,528,128]{2,1,0:T(8,128)(2,1)S(1)}, bf16[4,528,128]{2,1,0:T(8,128)(2,1)}, u32[]{:S(2)}, u32[]{:S(2)}) %collective-permute-start.17) | collective-permute-done | bytes 540704 | tf_op jit(solution)/shard_map/ppermute | solution.py:364
  69.7 10.2 %collective-permute-done.25.refs_2_ = bf16[2,2,256,128]{3,2,1,0:T(8,128)(2,1)S(1)} collective-permute-done((bf16[2,2,256,128]{3,2,1,0:T(8,128)(2,1)S(1)}, bf16[2,2,256,128]{3,2,1,0:T(8,128)(2,1)S(1)}, u32[]{:S(2)}, u32[]{:S(2)}) %collective-permute-start.25) | collective-permute-done | bytes 262176 | tf_op jit(solution)/shard_map/ppermute | solution.py:368
  79.9 4.7 %collective-permute-done.23.refs_0_ = bf16[2,2,256,128]{3,2,1,0:T(8,128)(2,1)S(1)} collective-permute-done((bf16[2,2,256,128]{3,2,1,0:T(8,128)(2,1)S(1)}, bf16[2,2,256,128]{3,2,1,0:T(8,128)(2,1)S(1)}, u32[]{:S(2)}, u32[]{:S(2)}) %collective-permute-start.23) | collective-permute-done | bytes 262176 | tf_op jit(solution)/shard_map/ppermute | solution.py:368
  84.7 11.2 %shard_map.47.refs_20_ = f32[4096,2048]{1,0:T(8,128)} custom-call(), custom_call_target="tpu_custom_call" | custom-call | bytes 33554432 | tf_op jit(solution)/shard_map/pallas_call | solution.py:342
  95.9 13.5 %shard_map.48 = (f32[4096,2048]{1,0:T(8,128)}, f32[33,128,128]{2,1,0:T(8,128)}, bf16[8,512,128]{2,1,0:T(8,128)(2,1)}, s32[32]{0:T(128)S(1)}, s32[33]{0:T(128)S(1)}) custom-call(bf16[2,2,256,128]{3,2,1,0:T(8,128)(2,1)S(1)} %pad_maximum_fusion.1.refs_0_, bf16[2,2,256,128]{3,2,1,0:T(8,128)(2,1)S(1)} %collective-permute-done.1.refs_1_, ...), custom_call_target="tpu_custom_call", output_to_operand_aliasing={{0}: (20, {})} | custom-call | flops 1000000000 | bytes 16777216 | tf_op jit(solution)/shard_map/pallas_call | solution.py:227
  109.5 1.6 %copy-done = f32[33,128,128]{2,1,0:T(8,128)S(1)} copy-done((f32[33,128,128]{2,1,0:T(8,128)S(1)}, f32[33,128,128]{2,1,0:T(8,128)}, u32[]{:S(2)}) %copy-start) | copy-done | bytes 2162712
  112.3 3.2 %shard_map.49 = f32[4096,2048]{1,0:T(8,128)} custom-call(s32[32]{0:T(128)S(1)} %get-tuple-element.26.slot_ref, s32[33]{0:T(128)S(1)} %get-tuple-element.27.tile_ref, bf16[2,2,256,128]{3,2,1,0:T(8,128)(2,1)S(1)} %collective-permute-done.23.refs_0_, bf16[2,2,256,128]{3,2,1,0:T(8,128)(2,1)S(1)} %collective-permute-done.24.refs_1_, ...), custom_call_target="tpu_custom_call", output_to_operand_aliasing={{}: (8, {})} | custom-call | flops 300000000 | bytes 8388608 | tf_op jit(solution)/shard_map/pallas_call | solution.py:311
  (54 shorter events, 11.7 us)
Async XLA Ops:
  3.6 8.8 %collective-permute-start.2 = (bf16[2,256,128]{2,1,0:T(8,128)(2,1)}, bf16[2,256,128]{2,1,0:T(8,128)(2,1)S(1)}, u32[]{:S(2)}, u32[]{:S(2)}) collective-permute-start(bf16[2,256,128]{2,1,0:T(8,128)(2,1)} %get-tuple-element.20), channel_id=1, source_target_pairs={{0,16},{8,24},{16,0},{24,8},{1,17},{9,25},{17,1},{25,9},{2,18},{10... | collective-permute-start | bytes 393224 | tf_op jit(solution)/shard_map/ppermute | solution.py:364
  8.0 7.7 %collective-permute-start = (bf16[2,256,128]{2,1,0:T(8,128)(2,1)}, bf16[2,256,128]{2,1,0:T(8,128)(2,1)S(1)}, u32[]{:S(2)}, u32[]{:S(2)}) collective-permute-start(bf16[2,256,128]{2,1,0:T(8,128)(2,1)} %get-tuple-element.19), channel_id=1, source_target_pairs={{0,8},{8,0},{16,24},{24,16},{1,9},{9,1},{17,25},{25,17},{2,10},{10... | collective-permute-start | bytes 393224 | tf_op jit(solution)/shard_map/ppermute | solution.py:364
  14.1 20.4 %collective-permute-start.7 = (bf16[2,2,256,128]{3,2,1,0:T(8,128)(2,1)S(1)}, bf16[2,2,256,128]{3,2,1,0:T(8,128)(2,1)S(1)}, u32[]{:S(2)}, u32[]{:S(2)}) collective-permute-start(bf16[2,2,256,128]{3,2,1,0:T(8,128)(2,1)S(1)} %pad_maximum_fusion.2.refs_2_), channel_id=1, source_target_pairs={{0,2},{1,3},{2,4},{3,5},{4,6},{5,7},{6,0},{7,1},{8,10},{9,11},{10,... | collective-permute-start | bytes 786440 | tf_op jit(solution)/shard_map/ppermute | solution.py:368
  16.7 19.5 %collective-permute-start.5 = (bf16[2,2,256,128]{3,2,1,0:T(8,128)(2,1)S(1)}, bf16[2,2,256,128]{3,2,1,0:T(8,128)(2,1)S(1)}, u32[]{:S(2)}, u32[]{:S(2)}) collective-permute-start(bf16[2,2,256,128]{3,2,1,0:T(8,128)(2,1)S(1)} %pad_maximum_fusion.1.refs_0_), channel_id=1, source_target_pairs={{0,2},{1,3},{2,4},{3,5},{4,6},{5,7},{6,0},{7,1},{8,10},{9,11},{10,... | collective-permute-start | bytes 786440 | tf_op jit(solution)/shard_map/ppermute | solution.py:368
  18.3 13.0 %collective-permute-start.15 = (bf16[528,128]{1,0:T(8,128)(2,1)}, bf16[528,128]{1,0:T(8,128)(2,1)S(1)}, u32[]{:S(2)}, u32[]{:S(2)}) collective-permute-start(bf16[528,128]{1,0:T(8,128)(2,1)} %get-tuple-element.25), channel_id=1, source_target_pairs={{0,6},{1,7},{2,0},{3,1},{4,2},{5,3},{6,4},{7,5},{8,14},{9,15},{10,... | collective-permute-start | bytes 405512 | tf_op jit(solution)/shard_map/ppermute | solution.py:368
  20.6 14.0 %collective-permute-start.13 = (bf16[528,128]{1,0:T(8,128)(2,1)}, bf16[528,128]{1,0:T(8,128)(2,1)S(1)}, u32[]{:S(2)}, u32[]{:S(2)}) collective-permute-start(bf16[528,128]{1,0:T(8,128)(2,1)} %get-tuple-element.23), channel_id=1, source_target_pairs={{0,2},{1,3},{2,4},{3,5},{4,6},{5,7},{6,0},{7,1},{8,10},{9,11},{10,... | collective-permute-start | bytes 405512 | tf_op jit(solution)/shard_map/ppermute | solution.py:368
  20.6 18.2 %collective-permute-start.14 = (bf16[528,128]{1,0:T(8,128)(2,1)}, bf16[528,128]{1,0:T(8,128)(2,1)S(1)}, u32[]{:S(2)}, u32[]{:S(2)}) collective-permute-start(bf16[528,128]{1,0:T(8,128)(2,1)} %get-tuple-element.24), channel_id=1, source_target_pairs={{0,4},{1,5},{2,6},{3,7},{4,0},{5,1},{6,2},{7,3},{8,12},{9,13},{10,... | collective-permute-start | bytes 405512 | tf_op jit(solution)/shard_map/ppermute | solution.py:368
  31.3 10.0 %collective-permute-start.4 = (bf16[2,2,256,128]{3,2,1,0:T(8,128)(2,1)S(1)}, bf16[2,2,256,128]{3,2,1,0:T(8,128)(2,1)S(1)}, u32[]{:S(2)}, u32[]{:S(2)}) collective-permute-start(bf16[2,2,256,128]{3,2,1,0:T(8,128)(2,1)S(1)} %pad_maximum_fusion.2.refs_2_), channel_id=1, source_target_pairs={{0,1},{1,0},{2,3},{3,2},{4,5},{5,4},{6,7},{7,6},{8,9},{9,8},{10,11... | collective-permute-start | bytes 786440 | tf_op jit(solution)/shard_map/ppermute | solution.py:371
  34.6 10.9 %collective-permute-start.11 = (bf16[2,2,256,128]{3,2,1,0:T(8,128)(2,1)S(1)}, bf16[2,2,256,128]{3,2,1,0:T(8,128)(2,1)S(1)}, u32[]{:S(2)}, u32[]{:S(2)}) collective-permute-start(bf16[2,2,256,128]{3,2,1,0:T(8,128)(2,1)S(1)} %collective-permute-done.7.refs_6_), channel_id=1, source_target_pairs={{0,2},{1,3},{2,4},{3,5},{4,6},{5,7},{6,0},{7,1},{8,10},{9,11},{10,... | collective-permute-start | bytes 786440 | tf_op jit(solution)/shard_map/ppermute | solution.py:368
  36.2 14.5 %collective-permute-start.9 = (bf16[2,2,256,128]{3,2,1,0:T(8,128)(2,1)S(1)}, bf16[2,2,256,128]{3,2,1,0:T(8,128)(2,1)S(1)}, u32[]{:S(2)}, u32[]{:S(2)}) collective-permute-start(bf16[2,2,256,128]{3,2,1,0:T(8,128)(2,1)S(1)} %collective-permute-done.5.refs_4_), channel_id=1, source_target_pairs={{0,2},{1,3},{2,4},{3,5},{4,6},{5,7},{6,0},{7,1},{8,10},{9,11},{10,... | collective-permute-start | bytes 786440 | tf_op jit(solution)/shard_map/ppermute | solution.py:368
  39.8 15.3 %collective-permute-start.16 = (bf16[4,528,128]{2,1,0:T(8,128)(2,1)S(1)}, bf16[4,528,128]{2,1,0:T(8,128)(2,1)}, u32[]{:S(2)}, u32[]{:S(2)}) collective-permute-start(bf16[4,528,128]{2,1,0:T(8,128)(2,1)S(1)} %pad_maximum_fusion.refs_12_), channel_id=1, source_target_pairs={{0,8},{8,0},{16,24},{24,16},{1,9},{9,1},{17,25},{25,17},{2,10},{10... | collective-permute-start | bytes 1622024 | tf_op jit(solution)/shard_map/ppermute | solution.py:364
  41.2 9.5 %collective-permute-start.8 = (bf16[2,2,256,128]{3,2,1,0:T(8,128)(2,1)S(1)}, bf16[2,2,256,128]{3,2,1,0:T(8,128)(2,1)}, u32[]{:S(2)}, u32[]{:S(2)}) collective-permute-start(bf16[2,2,256,128]{3,2,1,0:T(8,128)(2,1)S(1)} %collective-permute-done.7.refs_6_), channel_id=1, source_target_pairs={{0,1},{1,0},{2,3},{3,2},{4,5},{5,4},{6,7},{7,6},{8,9},{9,8},{10,11... | collective-permute-start | bytes 786440 | tf_op jit(solution)/shard_map/ppermute | solution.py:371
  41.3 26.4 %collective-permute-start.17 = (bf16[4,528,128]{2,1,0:T(8,128)(2,1)S(1)}, bf16[4,528,128]{2,1,0:T(8,128)(2,1)}, u32[]{:S(2)}, u32[]{:S(2)}) collective-permute-start(bf16[4,528,128]{2,1,0:T(8,128)(2,1)S(1)} %pad_maximum_fusion.refs_12_), channel_id=1, source_target_pairs={{0,16},{8,24},{16,0},{24,8},{1,17},{9,25},{17,1},{25,9},{2,18},{10... | collective-permute-start | bytes 1622024 | tf_op jit(solution)/shard_map/ppermute | solution.py:364
  45.5 22.2 %collective-permute-start.18 = (bf16[4,528,128]{2,1,0:T(8,128)(2,1)S(1)}, bf16[4,528,128]{2,1,0:T(8,128)(2,1)}, u32[]{:S(2)}, u32[]{:S(2)}) collective-permute-start(bf16[4,528,128]{2,1,0:T(8,128)(2,1)S(1)} %pad_maximum_fusion.refs_12_), channel_id=1, source_target_pairs={{0,24},{8,16},{16,8},{24,0},{1,25},{9,17},{17,9},{25,1},{2,26},{10... | collective-permute-start | bytes 1622024 | tf_op jit(solution)/shard_map/ppermute | solution.py:364
  50.7 17.4 %collective-permute-start.19 = (bf16[4,528,128]{2,1,0:T(8,128)(2,1)S(1)}, bf16[4,528,128]{2,1,0:T(8,128)(2,1)S(1)}, u32[]{:S(2)}, u32[]{:S(2)}) collective-permute-start(bf16[4,528,128]{2,1,0:T(8,128)(2,1)S(1)} %pad_maximum_fusion.refs_12_), channel_id=1, source_target_pairs={{0,1},{1,0},{2,3},{3,2},{4,5},{5,4},{6,7},{7,6},{8,9},{9,8},{10,11... | collective-permute-start | bytes 1622024 | tf_op jit(solution)/shard_map/ppermute | solution.py:371
  53.0 15.9 %collective-permute-start.12 = (bf16[2,2,256,128]{3,2,1,0:T(8,128)(2,1)S(1)}, bf16[2,2,256,128]{3,2,1,0:T(8,128)(2,1)S(1)}, u32[]{:S(2)}, u32[]{:S(2)}) collective-permute-start(bf16[2,2,256,128]{3,2,1,0:T(8,128)(2,1)S(1)} %collective-permute-done.11.refs_10_), channel_id=1, source_target_pairs={{0,1},{1,0},{2,3},{3,2},{4,5},{5,4},{6,7},{7,6},{8,9},{9,8},{10,11... | collective-permute-start | bytes 786440 | tf_op jit(solution)/shard_map/ppermute | solution.py:371
  55.1 13.9 %collective-permute-start.10 = (bf16[2,2,256,128]{3,2,1,0:T(8,128)(2,1)S(1)}, bf16[2,2,256,128]{3,2,1,0:T(8,128)(2,1)S(1)}, u32[]{:S(2)}, u32[]{:S(2)}) collective-permute-start(bf16[2,2,256,128]{3,2,1,0:T(8,128)(2,1)S(1)} %collective-permute-done.9.refs_8_), channel_id=1, source_target_pairs={{0,1},{1,0},{2,3},{3,2},{4,5},{5,4},{6,7},{7,6},{8,9},{9,8},{10,11... | collective-permute-start | bytes 786440 | tf_op jit(solution)/shard_map/ppermute | solution.py:371
  67.6 28.3 %collective-permute-start.20 = (bf16[4,528,128]{2,1,0:T(8,128)(2,1)}, bf16[4,528,128]{2,1,0:T(8,128)(2,1)}, u32[]{:S(2)}, u32[]{:S(2)}) collective-permute-start(bf16[4,528,128]{2,1,0:T(8,128)(2,1)} %collective-permute-done.16.refs_13_), channel_id=1, source_target_pairs={{0,1},{1,0},{2,3},{3,2},{4,5},{5,4},{6,7},{7,6},{8,9},{9,8},{10,11... | collective-permute-start | bytes 1622024 | tf_op jit(solution)/shard_map/ppermute | solution.py:371
  67.6 28.3 %collective-permute-start.21 = (bf16[4,528,128]{2,1,0:T(8,128)(2,1)}, bf16[4,528,128]{2,1,0:T(8,128)(2,1)}, u32[]{:S(2)}, u32[]{:S(2)}) collective-permute-start(bf16[4,528,128]{2,1,0:T(8,128)(2,1)} %collective-permute-done.17.refs_14_), channel_id=1, source_target_pairs={{0,1},{1,0},{2,3},{3,2},{4,5},{5,4},{6,7},{7,6},{8,9},{9,8},{10,11... | collective-permute-start | bytes 1622024 | tf_op jit(solution)/shard_map/ppermute | solution.py:371
  68.1 27.8 %collective-permute-start.22 = (bf16[4,528,128]{2,1,0:T(8,128)(2,1)}, bf16[4,528,128]{2,1,0:T(8,128)(2,1)}, u32[]{:S(2)}, u32[]{:S(2)}) collective-permute-start(bf16[4,528,128]{2,1,0:T(8,128)(2,1)} %collective-permute-done.18.refs_15_), channel_id=1, source_target_pairs={{0,1},{1,0},{2,3},{3,2},{4,5},{5,4},{6,7},{7,6},{8,9},{9,8},{10,11... | collective-permute-start | bytes 1622024 | tf_op jit(solution)/shard_map/ppermute | solution.py:371
  69.0 11.0 %collective-permute-start.25 = (bf16[2,2,256,128]{3,2,1,0:T(8,128)(2,1)S(1)}, bf16[2,2,256,128]{3,2,1,0:T(8,128)(2,1)S(1)}, u32[]{:S(2)}, u32[]{:S(2)}) collective-permute-start(bf16[2,2,256,128]{3,2,1,0:T(8,128)(2,1)S(1)} %collective-permute-done.11.refs_10_), channel_id=1, source_target_pairs={{0,2},{1,3},{2,4},{3,5},{4,6},{5,7},{6,0},{7,1},{8,10},{9,11},{10,... | collective-permute-start | bytes 786440 | tf_op jit(solution)/shard_map/ppermute | solution.py:368
  69.0 15.6 %collective-permute-start.23 = (bf16[2,2,256,128]{3,2,1,0:T(8,128)(2,1)S(1)}, bf16[2,2,256,128]{3,2,1,0:T(8,128)(2,1)S(1)}, u32[]{:S(2)}, u32[]{:S(2)}) collective-permute-start(bf16[2,2,256,128]{3,2,1,0:T(8,128)(2,1)S(1)} %collective-permute-done.9.refs_8_), channel_id=1, source_target_pairs={{0,2},{1,3},{2,4},{3,5},{4,6},{5,7},{6,0},{7,1},{8,10},{9,11},{10,... | collective-permute-start | bytes 786440 | tf_op jit(solution)/shard_map/ppermute | solution.py:368
  79.9 29.6 %collective-permute-start.26 = (bf16[2,2,256,128]{3,2,1,0:T(8,128)(2,1)S(1)}, bf16[2,2,256,128]{3,2,1,0:T(8,128)(2,1)S(1)}, u32[]{:S(2)}, u32[]{:S(2)}) collective-permute-start(bf16[2,2,256,128]{3,2,1,0:T(8,128)(2,1)S(1)} %collective-permute-done.25.refs_2_), channel_id=1, source_target_pairs={{0,1},{1,0},{2,3},{3,2},{4,5},{5,4},{6,7},{7,6},{8,9},{9,8},{10,11... | collective-permute-start | bytes 786440 | tf_op jit(solution)/shard_map/ppermute | solution.py:371
  84.6 24.9 %collective-permute-start.24 = (bf16[2,2,256,128]{3,2,1,0:T(8,128)(2,1)S(1)}, bf16[2,2,256,128]{3,2,1,0:T(8,128)(2,1)S(1)}, u32[]{:S(2)}, u32[]{:S(2)}) collective-permute-start(bf16[2,2,256,128]{3,2,1,0:T(8,128)(2,1)S(1)} %collective-permute-done.23.refs_0_), channel_id=1, source_target_pairs={{0,1},{1,0},{2,3},{3,2},{4,5},{5,4},{6,7},{7,6},{8,9},{9,8},{10,11... | collective-permute-start | bytes 786440 | tf_op jit(solution)/shard_map/ppermute | solution.py:371
  (11 other events, 165.7 us)

commit v3 on v2

v3 whole, which is shorter than its diff:
```python
import functools

import jax
import jax.numpy as jnp
from jax import lax
from jax.experimental import pallas as pl
from jax.experimental.pallas import tpu as pltpu
from jax.sharding import PartitionSpec as P

TILES = 128
CORES = 2
STREAMS = 2
META = 16
FACTS = 3
MIB = 1024 * 1024


def scale_of(class_ref):
    classes = class_ref[...]
    return jnp.where(
        classes == 0, 1.0, jnp.where(classes == 1, 0.5, jnp.where(classes == 2, 0.25, 0.125))
    ).astype(jnp.float32)


def pack_right_kernel(n_chip, slots, sens_ref, class_ref, ids_ref, counts_ref, *refs):
    outs, meta_ref = refs[:n_chip], refs[n_chip]
    z = lax.div(lax.axis_index("col"), CORES)
    n_row, _, rows, width = sens_ref.shape
    scale = jnp.broadcast_to(scale_of(class_ref), (width, rows)).T
    meta_ref[...] = jnp.zeros_like(meta_ref)
    for q in range(n_row):
        meta_ref[q : q + 1, :slots] = ids_ref[q].astype(jnp.float32)
    meta_ref[n_row : n_row + 1, :n_row] = counts_ref[...].astype(jnp.float32)
    meta = meta_ref[...].astype(jnp.bfloat16)
    for s in range(n_chip):
        owner = lax.rem(z + s, n_chip)
        for i in range(slots):
            tile = sens_ref[owner, i].astype(jnp.float32) * scale
            outs[s][i * rows : (i + 1) * rows] = tile.astype(jnp.bfloat16)
        outs[s][slots * rows :] = meta


def pack_left_kernel(n_row, slots, sens_ref, class_ref, after_ref, *outs):
    r = lax.axis_index("row")
    width = sens_ref.shape[-1]
    scale = scale_of(class_ref)
    for j in range(n_row):
        for i in range(slots):
            tile = sens_ref[r ^ j, i].T.astype(jnp.float32) * scale
            outs[j][i * width : (i + 1) * width] = tile.astype(jnp.bfloat16)


def pack_right(sensitivity, weight_class, tile_ids, counts, n_chip):
    n_row, slots, rows, width = sensitivity.shape
    vmem = pl.BlockSpec(memory_space=pltpu.VMEM)
    return pl.pallas_call(
        functools.partial(pack_right_kernel, n_chip, slots),
        out_shape=[jax.ShapeDtypeStruct((slots * rows + META, width), jnp.bfloat16)] * n_chip,
        in_specs=[vmem] * 4,
        out_specs=[vmem] * n_chip,
        scratch_shapes=[pltpu.VMEM((META, width), jnp.float32)],
    )(sensitivity, weight_class, tile_ids, counts)


def pack_left(sensitivity, weight_class, after):
    n_row, slots, rows, width = sensitivity.shape
    vmem = pl.BlockSpec(memory_space=pltpu.VMEM)
    return pl.pallas_call(
        functools.partial(pack_left_kernel, n_row, slots),
        out_shape=[jax.ShapeDtypeStruct((slots * width, rows), jnp.bfloat16)] * n_row,
        in_specs=[vmem, vmem, pl.BlockSpec(memory_space=pl.ANY)],
        out_specs=[vmem] * n_row,
    )(sensitivity, weight_class, after)


def tile_of(place, station, r, z, core, i, j, per_col, none):
    left = place[FACTS * station, i]
    right = place[FACTS * station + 1, j] - core * per_col
    used = (i < place[FACTS * station + 2, r]) & (j < place[FACTS * station + 2, z])
    inside = used & (right >= 0) & (right < per_col)
    return jnp.where(inside, left * per_col + right, none)


def block_of(out_ref, tile, per_col, width):
    rows = pl.ds(pl.multiple_of(lax.div(tile, per_col) * width, width), width)
    columns = pl.ds(pl.multiple_of(lax.rem(tile, per_col) * width, width), width)
    return out_ref.at[rows, columns]


def main_kernel(n_row, n_chip, slots, per_row, per_col, *refs):
    last = n_chip - 1
    n_left = last * STREAMS * CORES
    n_right = n_row * CORES
    sources = refs[: n_left + n_right]
    out_ref, carry_ref, right_ref, slot_ref, tile_ref = refs[n_left + n_right + 2 :][:5]
    (acc, left_buf, right_buf, meta_buf, fact_buf, zero_buf, place, touches, owner, plan, has,
     load_sem, fact_sem, zero_sem, store_sem) = refs[n_left + n_right + 7 :]
    r = lax.axis_index("row")
    c = lax.axis_index("col")
    z, core = lax.div(c, CORES), lax.rem(c, CORES)
    width = acc.shape[-1]
    rows = left_buf.shape[-1]
    half = n_row // STREAMS
    tiles = per_row * per_col
    pairs = [(i, j) for i in range(slots) for j in range(slots)]

    def load(index):
        target = left_buf.at[index] if index < n_left else right_buf.at[index - n_left]
        return pltpu.make_async_copy(sources[index], target, load_sem.at[index])

    for index in [*range(n_left, n_left + n_right), *range(n_left)]:
        load(index).start()
    zero_buf[...] = jnp.zeros_like(zero_buf)
    clears = [
        pltpu.make_async_copy(zero_buf, touches, zero_sem.at[0]),
        pltpu.make_async_copy(zero_buf, owner, zero_sem.at[1]),
    ]
    for copy in clears:
        copy.start()

    for index in range(n_right):
        load(n_left + index).wait()
        for s in range(n_chip):
            station = index * n_chip + s
            meta_buf[station] = right_buf[index, s, slots * rows :].astype(jnp.float32)
            for n, fact in enumerate((r, z, n_row)):
                row = meta_buf[station, pl.ds(fact, 1), :].astype(jnp.int32)
                fact_buf[FACTS * station + n : FACTS * station + n + 1, :] = row
    to_smem = pltpu.make_async_copy(fact_buf, place, fact_sem)
    to_smem.start()
    for index in range(n_right):
        right_ref[index] = right_buf[index, last, : slots * rows]
    for copy in clears:
        copy.wait()
    to_smem.wait()

    def at(tile):
        return lax.div(tile, width), lax.rem(tile, width)

    def find(station, i, j):
        return tile_of(place, station, r, z, core, i, j, per_col, tiles)

    def count(index, carry):
        for s in range(last):
            for n, (i, j) in enumerate(pairs):
                tile = find(index * n_chip + s, i, j)
                before = touches[at(tile)]
                touches[at(tile)] = before + 1
                code = 2 * tile + (before == 0).astype(jnp.int32)
                plan[(index * last + s) * len(pairs) + n] = code
        return carry

    lax.fori_loop(0, n_right, count, 0)

    none = len(pairs) * n_right

    def number(index, used):
        for n, (i, j) in enumerate(pairs):
            tile = find(index * n_chip + last, i, j)
            held = owner[at(tile)]
            fresh = (held == 0) & (tile < tiles)
            spot = jnp.where(tile == tiles, none, jnp.where(fresh, used, held - 1))
            slot_ref[index * len(pairs) + n] = 2 * spot + fresh.astype(jnp.int32)
            owner[at(tile)] = jnp.where(tile == tiles, 0, spot + 1)
            tile_ref[jnp.where(fresh, used, none)] = tile
            has[spot] = touches[at(tile)]
            used = used + fresh.astype(jnp.int32)
        return used

    used = lax.fori_loop(0, n_right, number, 0)
    tile_ref[none] = used

    for index in range(n_left):
        load(index).wait()

    def store(tile):
        return pltpu.make_async_copy(
            acc.at[tile], block_of(out_ref, tile, per_col, width), store_sem
        )

    def add(index, stored):
        other, j_row = lax.div(index, n_row), lax.rem(index, n_row)
        stream, place_in = lax.div(j_row, half), lax.rem(j_row, half)
        for s in range(last):
            left = left_buf[(s * STREAMS + stream) * CORES + other, place_in]
            right = jnp.concatenate(
                [right_buf[index, s, j * rows : (j + 1) * rows] for j in range(slots)], axis=1
            )
            gram = jnp.dot(left, right, preferred_element_type=jnp.float32)
            for n, (i, j) in enumerate(pairs):
                code = plan[(index * last + s) * len(pairs) + n]
                tile, fresh = lax.shift_right_logical(code, 1), code & 1
                part = gram[i * width : (i + 1) * width, j * width : (j + 1) * width]
                acc[tile] = jnp.where(fresh == 1, part, acc[tile] + part)
        for n in range(last * len(pairs)):
            tile = lax.shift_right_logical(plan[index * last * len(pairs) + n], 1)
            rest = touches[at(tile)] - 1
            touches[at(tile)] = rest
            ready = (rest == 0) & (tile < tiles) & (owner[at(tile)] == 0)

            @pl.when(ready)
            def _():
                store(tile).start()

            stored = stored + ready.astype(jnp.int32)
        return stored

    stored = lax.fori_loop(0, n_right, add, 0)

    def hand_on(spot, carry):
        carry_ref[spot] = jnp.where(has[spot] == 0, 0.0, acc[tile_ref[spot]])
        return carry

    lax.fori_loop(0, used, hand_on, 0)

    def drain(index, carry):
        store(0).wait()
        return carry

    lax.fori_loop(0, stored, drain, 0)


def main_part(left, right, zeros, token, per_row, per_col):
    last, n_chip = len(left), len(left) + 1
    n_row = len(right) // CORES
    half, height, rows = left[0][0][0].shape
    width = right[0].shape[-1]
    slots = height // width
    flat = [x for chip in left for stream in chip for x in stream]
    chunks = len(flat) + len(right)
    tiles = per_row * per_col
    pairs = slots * slots * len(right)
    stations = n_chip * len(right)
    state = (tiles // width + 1, width)
    held = (
        (tiles + pairs + 2) * width * width * 4
        + len(flat) * half * height * rows * 2
        + len(right) * (n_chip + 1) * (slots * rows + META) * width * 2
        + stations * (META + 2 * FACTS) * width * 4
    )
    anywhere = pl.BlockSpec(memory_space=pl.ANY)
    vmem = pl.BlockSpec(memory_space=pltpu.VMEM)
    smem = pl.BlockSpec(memory_space=pltpu.SMEM)
    return pl.pallas_call(
        functools.partial(main_kernel, n_row, n_chip, slots, per_row, per_col),
        out_shape=[
            jax.ShapeDtypeStruct(zeros.shape, zeros.dtype),
            jax.ShapeDtypeStruct((pairs + 1, width, width), jnp.float32),
            jax.ShapeDtypeStruct((len(right), slots * rows, width), jnp.bfloat16),
            jax.ShapeDtypeStruct((pairs,), jnp.int32),
            jax.ShapeDtypeStruct((pairs + 1,), jnp.int32),
        ],
        in_specs=[anywhere] * (chunks + 2),
        out_specs=[anywhere, vmem, vmem, smem, smem],
        scratch_shapes=[
            pltpu.VMEM((tiles + 1, width, width), jnp.float32),
            pltpu.VMEM((len(flat), half, height, rows), jnp.bfloat16),
            pltpu.VMEM((len(right), n_chip, slots * rows + META, width), jnp.bfloat16),
            pltpu.VMEM((stations, META, width), jnp.float32),
            pltpu.VMEM((FACTS * stations, width), jnp.int32),
            pltpu.VMEM(state, jnp.int32),
            pltpu.SMEM((FACTS * stations, width), jnp.int32),
            pltpu.SMEM(state, jnp.int32),
            pltpu.SMEM(state, jnp.int32),
            pltpu.SMEM((pairs * last,), jnp.int32),
            pltpu.SMEM((pairs + 1,), jnp.int32),
            pltpu.SemaphoreType.DMA((chunks,)),
            pltpu.SemaphoreType.DMA,
            pltpu.SemaphoreType.DMA((2,)),
            pltpu.SemaphoreType.DMA,
        ],
        input_output_aliases={chunks: 0},
        compiler_params=pltpu.CompilerParams(vmem_limit_bytes=held + 3 * MIB),
        cost_estimate=pl.CostEstimate(flops=0, bytes_accessed=0, transcendentals=0),
    )(*flat, *right, zeros, token)


def tail_kernel(n_row, slots, per_col, slot_ref, tile_ref, *refs):
    lefts = refs[: STREAMS * CORES]
    carry_ref, right_ref = refs[STREAMS * CORES : STREAMS * CORES + 2]
    out_ref, acc, store_sem = refs[STREAMS * CORES + 3 :]
    rows, width = lefts[0].shape[-1], acc.shape[-1]
    half = n_row // STREAMS
    pairs = [(i, j) for i in range(slots) for j in range(slots)]

    for index in range(CORES * n_row):
        other, j_row = index // n_row, index % n_row
        left = lefts[j_row // half * CORES + other][j_row % half]
        right = jnp.concatenate(
            [right_ref[index, j * rows : (j + 1) * rows] for j in range(slots)], axis=1
        )
        gram = jnp.dot(left, right, preferred_element_type=jnp.float32)
        for n, (i, j) in enumerate(pairs):
            code = slot_ref[index * len(pairs) + n]
            spot, fresh = lax.shift_right_logical(code, 1), code & 1
            part = gram[i * width : (i + 1) * width, j * width : (j + 1) * width]
            acc[spot] = jnp.where(fresh == 1, carry_ref[spot], acc[spot]) + part

    def store(spot):
        return pltpu.make_async_copy(
            acc.at[spot], block_of(out_ref, tile_ref[spot], per_col, width), store_sem
        )

    def start(spot, carry):
        store(spot).start()
        return carry

    def drain(spot, carry):
        store(spot).wait()
        return carry

    used = tile_ref[len(pairs) * CORES * n_row]
    lax.fori_loop(0, used, start, 0)
    lax.fori_loop(0, used, drain, 0)


def tail_part(left, carried, right, slot, tile, out, per_col):
    flat = [x for stream in left for x in stream]
    half, height, _ = flat[0].shape
    width = carried.shape[-1]
    anywhere = pl.BlockSpec(memory_space=pl.ANY)
    vmem = pl.BlockSpec(memory_space=pltpu.VMEM)
    smem = pl.BlockSpec(memory_space=pltpu.SMEM)
    return pl.pallas_call(
        functools.partial(tail_kernel, half * STREAMS, height // width, per_col),
        out_shape=jax.ShapeDtypeStruct(out.shape, out.dtype),
        in_specs=[smem, smem] + [vmem] * (len(flat) + 2) + [anywhere],
        out_specs=anywhere,
        scratch_shapes=[
            pltpu.VMEM(carried.shape, jnp.float32),
            pltpu.SemaphoreType.DMA,
        ],
        input_output_aliases={len(flat) + 4: 0},
        compiler_params=pltpu.CompilerParams(vmem_limit_bytes=24 * MIB),
        cost_estimate=pl.CostEstimate(flops=3 * 10**8, bytes_accessed=8 * MIB, transcendentals=0),
    )(slot, tile, *flat, carried, right, out)


def zero_kernel(first, count, *refs):
    out_ref, token_ref, block, sem = refs[-4:]
    block[...] = jnp.zeros_like(block)
    token_ref[...] = jnp.zeros_like(token_ref)
    height = block.shape[0]
    copies = [
        pltpu.make_async_copy(
            block, out_ref.at[pl.ds((first + index) * height, height)], sem.at[index]
        )
        for index in range(count)
    ]
    for copy in copies:
        copy.start()
    for copy in copies:
        copy.wait()


def zero_fill(height, width, half, after, out=None):
    step = 128
    count = height // step // 2
    inputs = [after] if out is None else [after, out]
    anywhere = pl.BlockSpec(memory_space=pl.ANY)
    return pl.pallas_call(
        functools.partial(zero_kernel, half * count, count),
        out_shape=[
            jax.ShapeDtypeStruct((height, width), jnp.float32),
            jax.ShapeDtypeStruct((8, 128), jnp.float32),
        ],
        in_specs=[anywhere] * len(inputs),
        out_specs=[anywhere, pl.BlockSpec(memory_space=pltpu.VMEM)],
        scratch_shapes=[
            pltpu.VMEM((step, width), jnp.float32),
            pltpu.SemaphoreType.DMA((count,)),
        ],
        input_output_aliases={} if out is None else {1: 0},
        cost_estimate=pl.CostEstimate(flops=0, bytes_accessed=0, transcendentals=0),
    )(*inputs)


def local(sensitivity, tile_ids, counts, weight_class):
    n_row = lax.axis_size("row")
    n_col = lax.axis_size("col")
    n_chip = n_col // CORES
    width = sensitivity.shape[-1]
    per_row = TILES // n_row
    per_col = TILES // n_col
    height, breadth = per_row * width, per_col * width

    def flip_row(value, j):
        return lax.ppermute(value, "row", [(i, i ^ j) for i in range(n_row)])

    def shift_chip(value, s):
        pairs = [(i, (i + CORES * s) % n_col) for i in range(n_col)]
        return lax.ppermute(value, "col", pairs)

    def flip_core(value):
        return lax.ppermute(value, "col", [(i, i ^ 1) for i in range(n_col)])

    after = lax.optimization_barrier

    ids = jnp.transpose(tile_ids, (1, 0, 2))
    to_chip = pack_right(sensitivity[0], weight_class, ids, counts, n_chip)
    to_row = pack_left(sensitivity[0], weight_class, to_chip[0])
    from_chip = [to_chip[0]] + [shift_chip(to_chip[s], s) for s in range(1, n_chip)]
    plane = [to_row[0]] + [flip_row(to_row[j], j) for j in range(1, n_row)]
    zeros, token = zero_fill(height, breadth, 0, to_row[0])
    from_chip, plane, token = after((from_chip, plane, token))

    half = n_row // STREAMS
    ring = [[jnp.stack(plane[k * half : (k + 1) * half]) for k in range(STREAMS)]]
    right = [jnp.stack(from_chip)]
    right += [flip_row(right[0], j) for j in range(1, n_row)]
    zeros, token = zero_fill(height, breadth, 1, token, zeros)
    for s in range(1, n_chip):
        ring.append([shift_chip(x, 1) for x in ring[-1]])
        if s == 1:
            ring[1], token = after((ring[1], token))
    left = [[[x, flip_core(x)] for x in chip] for chip in ring[:-1]]
    swapped = [flip_core(right[0])]
    others, before = after((right[1:], ring[-2]))
    left[-1] = [[x, flip_core(x)] for x in before]
    right = [right[0], *others, swapped[0], *(flip_core(x) for x in others)]

    out, carried, right, slot, tile = main_part(left, right, zeros, token, per_row, per_col)
    final, slot = after((ring[-1], slot))
    final = [[x, flip_core(x)] for x in final]
    return tail_part(final, carried, right, slot, tile, out, per_col)


def solution(mesh):
    in_specs = (
        P(("row", "col"), None, None, None, None),
        P(("row", "col"), None, None),
        P(("row", "col"), None),
        P(("row", "col"), None),
    )
    return jax.shard_map(
        local, mesh=mesh, in_specs=in_specs, out_specs=P("row", "col"), check_vma=False
    )
```

time: 116 us -> 78.9 us (0.68)
  waiting for transfers between devices: 55.8 us -> 21.7 us
  Pallas kernels: 30.2 us -> 28.4 us
  local copies, waits for them, and re-layouts: 4.9 us -> 3.62 us
    ppermute x6, waiting for transfers between devices: 20.5 us -> 1.17 us  [flip_row(): return lax.ppermute(value, 'row', [(i, i ^ j) for i in range(n_row)])]
    ppermute x9, waiting for transfers between devices: 33.5 us -> 16.4 us  [shift_chip(): return lax.ppermute(value, 'col', pairs)]
    pallas_call x1, Pallas kernels: 13.5 us -> 9.28 us  [main_part(): pl.pallas_call(functools.partial(main_kernel, n_row, n_chip, slots, per_r...]
    pallas_call x3 -> x5, Pallas kernels: 16.7 us -> 19.2 us  [the longest x2 13.2 us: zero_fill(): pl.pallas_call(functools.partial(zero_kernel, half * count, count), out_s...]
    ppermute x12, waiting for transfers between devices: 1.82 us -> 4.18 us  [flip_core(): return lax.ppermute(value, 'col', [(i, i ^ 1) for i in range(n_col)])]
    ppermute x6, starting transfers between devices: 9.85 us -> 8.49 us  [flip_row(): return lax.ppermute(value, 'row', [(i, i ^ j) for i in range(n_row)])]
    transpose x0 -> x1, local copies, waits for them, and re-layouts: none -> 1.34 us  [local(): ids = jnp.transpose(tile_ids, (1, 0, 2))]
    squeeze x1 -> x0, local copies, waits for them, and re-layouts: 1.33 us -> none  [local(): parts = pack(sensitivity[0], weight_class, tile_ids[0], counts[0], n_chip)]
  transfers between devices with their start and end apart: 27 -> 27, of which waited for: 12 -> 9; matrix products, arithmetic and copies ran while one was open for 2% -> 2% of each run, Pallas kernels for 21% -> 29%
where the time goes in v3:
time: 78.9 us; the launch traced here: 78.7 us
  Pallas kernels  28.4 us (36%)
  starting transfers between devices  22.9 us (29%)
  waiting for transfers between devices  21.7 us (28%)
  local copies, waits for them, and re-layouts  3.62 us (5%)
  other arithmetic  1.93 us (2%)
    ppermute x9, waiting for transfers between devices, shift_chip(): return lax.ppermute(value, 'col', pairs)  16.4 us
    pallas_call x2, Pallas kernels, zero_fill(): pl.pallas_call(functools.partial(zero_kernel, half * count, count), out_s...  13.2 us
    ppermute x9, starting transfers between devices, shift_chip(): return lax.ppermute(value, 'col', pairs)  11.7 us
    pallas_call x1, Pallas kernels, main_part(): pl.pallas_call(functools.partial(main_kernel, n_row, n_chip, slots, per_r...  9.28 us
    ppermute x6, starting transfers between devices, flip_row(): return lax.ppermute(value, 'row', [(i, i ^ j) for i in range(n_row)])  8.49 us
    ppermute x12, waiting for transfers between devices, flip_core(): return lax.ppermute(value, 'col', [(i, i ^ 1) for i in range(n_col)])  4.18 us
    ppermute x12, starting transfers between devices, flip_core(): return lax.ppermute(value, 'col', [(i, i ^ 1) for i in range(n_col)])  2.63 us
    unnamed x4, local copies, waits for them, and re-layouts  2.29 us
  transfers between devices with their start and end apart: 27, of which 9 were waited for; matrix products, arithmetic and copies ran while one was open for 2% of the time, Pallas kernels for 29%

profile of v3, /device:TPU:0, one launch (start us, length us, event | category | flops | bytes accessed | tf_op | source)
XLA Modules:
  0.0 78.7 jit_solution(13979593335015507314)
XLA Ops:
  0.0 1.3 %copy.8.ids_ref = s32[4,1,2]{2,1,0:T(1,128)} copy(s32[4,1,2]{0,2,1:T(2,128)} %bitcast.20) | data formatting | bytes 64 | tf_op jit(solution)/shard_map/transpose | solution.py:399
  1.3 2.0 %shard_map.46 = (bf16[528,128]{1,0:T(8,128)(2,1)}, bf16[528,128]{1,0:T(8,128)(2,1)}, bf16[528,128]{1,0:T(8,128)(2,1)}, bf16[528,128]{1,0:T(8,128)(2,1)}) custom-call(bf16[4,2,256,128]{3,2,1,0:T(8,128)(2,1)} %bitcast.10, s32[1,256]{1,0:T(1,128)} %class_ref.3, s32[4,1,2]{2,1,0:T(1,128)} %copy.8.ids_ref, s32[1,4]{1,0:T(1,128)} %counts_ref.1), custom_call_target="tpu_custom_call" | custom-call | tf_op jit(solution)/shard_map/pallas_call | solution.py:56
  3.4 1.9 %shard_map.47 = (bf16[256,256]{1,0:T(8,128)(2,1)}, bf16[256,256]{1,0:T(8,128)(2,1)}, bf16[256,256]{1,0:T(8,128)(2,1)}, bf16[256,256]{1,0:T(8,128)(2,1)}) custom-call(bf16[4,2,256,128]{3,2,1,0:T(8,128)(2,1)} %bitcast.11, s32[1,256]{1,0:T(1,128)} %class_ref.3, bf16[528,128]{1,0:T(8,128)(2,1)} %get-tuple-element.60.after_ref), custom_call_target="tpu_custom_call" | custom-call | tf_op jit(solution)/shard_map/pallas_call | solution.py:68
  5.3 2.9 %collective-permute-start.3 = (bf16[256,256]{1,0:T(8,128)(2,1)}, bf16[256,256]{1,0:T(8,128)(2,1)S(1)}, u32[]{:S(2)}, u32[]{:S(2)}) collective-permute-start(bf16[256,256]{1,0:T(8,128)(2,1)} %get-tuple-element.47), channel_id=1, source_target_pairs={{0,8},{8,0},{16,24},{24,16},{1,9},{9,1},{17,25},{25,17},{2,10},{10... | collective-permute-start | bytes 393224 | tf_op jit(solution)/shard_map/ppermute | solution.py:388
  8.2 1.6 %collective-permute-start = (bf16[528,128]{1,0:T(8,128)(2,1)}, bf16[528,128]{1,0:T(8,128)(2,1)S(1)}, u32[]{:S(2)}, u32[]{:S(2)}) collective-permute-start(bf16[528,128]{1,0:T(8,128)(2,1)} %get-tuple-element.43), channel_id=1, source_target_pairs={{0,2},{1,3},{2,4},{3,5},{4,6},{5,7},{6,0},{7,1},{8,10},{9,11},{10,... | collective-permute-start | bytes 405512 | tf_op jit(solution)/shard_map/ppermute | solution.py:392
  9.8 2.6 %collective-permute-start.1 = (bf16[528,128]{1,0:T(8,128)(2,1)}, bf16[528,128]{1,0:T(8,128)(2,1)S(1)}, u32[]{:S(2)}, u32[]{:S(2)}) collective-permute-start(bf16[528,128]{1,0:T(8,128)(2,1)} %get-tuple-element.44), channel_id=1, source_target_pairs={{0,4},{1,5},{2,6},{3,7},{4,0},{5,1},{6,2},{7,3},{8,12},{9,13},{10,... | collective-permute-start | bytes 405512 | tf_op jit(solution)/shard_map/ppermute | solution.py:392
  12.4 1.3 %collective-permute-start.2 = (bf16[528,128]{1,0:T(8,128)(2,1)}, bf16[528,128]{1,0:T(8,128)(2,1)S(1)}, u32[]{:S(2)}, u32[]{:S(2)}) collective-permute-start(bf16[528,128]{1,0:T(8,128)(2,1)} %get-tuple-element.45), channel_id=1, source_target_pairs={{0,6},{1,7},{2,0},{3,1},{4,2},{5,3},{6,4},{7,5},{8,14},{9,15},{10,... | collective-permute-start | bytes 405512 | tf_op jit(solution)/shard_map/ppermute | solution.py:392
  13.7 1.5 %collective-permute-start.4 = (bf16[256,256]{1,0:T(8,128)(2,1)}, bf16[256,256]{1,0:T(8,128)(2,1)S(1)}, u32[]{:S(2)}, u32[]{:S(2)}) collective-permute-start(bf16[256,256]{1,0:T(8,128)(2,1)} %get-tuple-element.48), channel_id=1, source_target_pairs={{0,16},{8,24},{16,0},{24,8},{1,17},{9,25},{17,1},{25,9},{2,18},{10... | collective-permute-start | bytes 393224 | tf_op jit(solution)/shard_map/ppermute | solution.py:388
  15.7 6.6 %shard_map.48 = (f32[4096,2048]{1,0:T(8,128)}, f32[8,128]{1,0:T(8,128)}) custom-call(bf16[256,256]{1,0:T(8,128)(2,1)} %get-tuple-element.51.refs_0_), custom_call_target="tpu_custom_call" | custom-call | tf_op jit(solution)/shard_map/pallas_call | solution.py:361
  22.5 2.2 %collective-permute-start.7 = (bf16[2,256,256]{2,1,0:T(8,128)(2,1)S(1)}, bf16[2,256,256]{2,1,0:T(8,128)(2,1)S(1)}, u32[]{:S(2)}, u32[]{:S(2)}) collective-permute-start(bf16[2,256,256]{2,1,0:T(8,128)(2,1)S(1)} %pad_maximum_fusion.2.refs_2_), channel_id=1, source_target_pairs={{0,2},{1,3},{2,4},{3,5},{4,6},{5,7},{6,0},{7,1},{8,10},{9,11},{10,... | collective-permute-start | bytes 786440 | tf_op jit(solution)/shard_map/ppermute | solution.py:392
  25.7 1.0 %pad_maximum_fusion.refs_12_ = bf16[4,528,128]{2,1,0:T(8,128)(2,1)S(1)} fusion(bf16[1,528,128]{2,1,0:T(8,128)(2,1)S(1)} %bitcast.16, bf16[1,528,128]{2,1,0:T(8,128)(2,1)S(1)} %bitcast.15, bf16[1,528,128]{2,1,0:T(8,128)(2,1)S(1)} %bitcast.14, bf16[1,528,128]{2,1,0:T(8,128)(2,1)} %bitcast.12), kind=kLoop, calls=%fused_computation | loop fusion | flops 811008 | bytes 1081344 | tf_op jit(solution)/shard_map/stack | solution.py:409
  27.3 1.5 %collective-permute-start.17 = (bf16[4,528,128]{2,1,0:T(8,128)(2,1)S(1)}, bf16[4,528,128]{2,1,0:T(8,128)(2,1)S(1)}, u32[]{:S(2)}, u32[]{:S(2)}) collective-permute-start(bf16[4,528,128]{2,1,0:T(8,128)(2,1)S(1)} %pad_maximum_fusion.refs_12_), channel_id=1, source_target_pairs={{0,16},{8,24},{16,0},{24,8},{1,17},{9,25},{17,1},{25,9},{2,18},{10... | collective-permute-start | bytes 1622024 | tf_op jit(solution)/shard_map/ppermute | solution.py:388
  28.8 1.4 %collective-permute-start.18 = (bf16[4,528,128]{2,1,0:T(8,128)(2,1)S(1)}, bf16[4,528,128]{2,1,0:T(8,128)(2,1)S(1)}, u32[]{:S(2)}, u32[]{:S(2)}) collective-permute-start(bf16[4,528,128]{2,1,0:T(8,128)(2,1)S(1)} %pad_maximum_fusion.refs_12_), channel_id=1, source_target_pairs={{0,24},{8,16},{16,8},{24,0},{1,25},{9,17},{17,9},{25,1},{2,26},{10... | collective-permute-start | bytes 1622024 | tf_op jit(solution)/shard_map/ppermute | solution.py:388
  30.2 6.6 %shard_map.49 = (f32[4096,2048]{1,0:T(8,128)}, f32[8,128]{1,0:T(8,128)}) custom-call(f32[8,128]{1,0:T(8,128)} %get-tuple-element.55.refs_0_, f32[4096,2048]{1,0:T(8,128)} %get-tuple-element.56.refs_1_), custom_call_target="tpu_custom_call", output_to_operand_aliasing={{0}: (1, {})} | custom-call | tf_op jit(solution)/shard_map/pallas_call | solution.py:361
  36.9 2.2 %collective-permute-start.10 = (bf16[2,256,256]{2,1,0:T(8,128)(2,1)S(1)}, bf16[2,256,256]{2,1,0:T(8,128)(2,1)S(1)}, u32[]{:S(2)}, u32[]{:S(2)}) collective-permute-start(bf16[2,256,256]{2,1,0:T(8,128)(2,1)S(1)} %collective-permute-done.7.refs_6_), channel_id=1, source_target_pairs={{0,2},{1,3},{2,4},{3,5},{4,6},{5,7},{6,0},{7,1},{8,10},{9,11},{10,... | collective-permute-start | bytes 786440 | tf_op jit(solution)/shard_map/ppermute | solution.py:392
  39.7 8.3 %collective-permute-done.10.refs_10_ = bf16[2,256,256]{2,1,0:T(8,128)(2,1)S(1)} collective-permute-done((bf16[2,256,256]{2,1,0:T(8,128)(2,1)S(1)}, bf16[2,256,256]{2,1,0:T(8,128)(2,1)S(1)}, u32[]{:S(2)}, u32[]{:S(2)}) %collective-permute-start.10) | collective-permute-done | bytes 262176 | tf_op jit(solution)/shard_map/ppermute | solution.py:392
  48.0 3.5 %collective-permute-done.8.refs_8_ = bf16[2,256,256]{2,1,0:T(8,128)(2,1)S(1)} collective-permute-done((bf16[2,256,256]{2,1,0:T(8,128)(2,1)S(1)}, bf16[2,256,256]{2,1,0:T(8,128)(2,1)S(1)}, u32[]{:S(2)}, u32[]{:S(2)}) %collective-permute-start.8) | collective-permute-done | bytes 262176 | tf_op jit(solution)/shard_map/ppermute | solution.py:392
  52.0 1.2 %collective-permute-done.18.refs_15_ = bf16[4,528,128]{2,1,0:T(8,128)(2,1)S(1)} collective-permute-done((bf16[4,528,128]{2,1,0:T(8,128)(2,1)S(1)}, bf16[4,528,128]{2,1,0:T(8,128)(2,1)S(1)}, u32[]{:S(2)}, u32[]{:S(2)}) %collective-permute-start.18) | collective-permute-done | bytes 540704 | tf_op jit(solution)/shard_map/ppermute | solution.py:388
  55.2 2.2 %collective-permute-done.19.refs_9_ = bf16[2,256,256]{2,1,0:T(8,128)(2,1)S(1)} collective-permute-done((bf16[2,256,256]{2,1,0:T(8,128)(2,1)S(1)}, bf16[2,256,256]{2,1,0:T(8,128)(2,1)S(1)}, u32[]{:S(2)}, u32[]{:S(2)}) %collective-permute-start.19) | collective-permute-done | bytes 262176 | tf_op jit(solution)/shard_map/ppermute | solution.py:395
  59.3 9.3 %shard_map.50 = (f32[4096,2048]{1,0:T(8,128)}, f32[33,128,128]{2,1,0:T(8,128)}, bf16[8,512,128]{2,1,0:T(8,128)(2,1)S(1)}, s32[32]{0:T(128)S(1)}, s32[33]{0:T(128)S(1)}) custom-call(bf16[2,256,256]{2,1,0:T(8,128)(2,1)S(1)} %pad_maximum_fusion.1.refs_0_, bf16[2,256,256]{2,1,0:T(8,128)(2,1)S(1)} %collective-permute-done.12.refs_1_, ...), custom_call_target="tpu_custom_call", output_to_operand_aliasing={{0}: (20, {})} | custom-call | tf_op jit(solution)/shard_map/pallas_call | solution.py:244
  68.6 4.6 %collective-permute-done.9.refs_0_ = bf16[2,256,256]{2,1,0:T(8,128)(2,1)S(1)} collective-permute-done((bf16[2,256,256]{2,1,0:T(8,128)(2,1)S(1)}, bf16[2,256,256]{2,1,0:T(8,128)(2,1)S(1)}, u32[]{:S(2)}, u32[]{:S(2)}) %collective-permute-start.9) | collective-permute-done | bytes 262176 | tf_op jit(solution)/shard_map/ppermute | solution.py:392
  73.7 1.0 %collective-permute-done.25.refs_1_ = bf16[2,256,256]{2,1,0:T(8,128)(2,1)S(1)} collective-permute-done((bf16[2,256,256]{2,1,0:T(8,128)(2,1)S(1)}, bf16[2,256,256]{2,1,0:T(8,128)(2,1)S(1)}, u32[]{:S(2)}, u32[]{:S(2)}) %collective-permute-start.25) | collective-permute-done | bytes 262176 | tf_op jit(solution)/shard_map/ppermute | solution.py:395
  75.1 1.6 %copy-done = f32[33,128,128]{2,1,0:T(8,128)S(1)} copy-done((f32[33,128,128]{2,1,0:T(8,128)S(1)}, f32[33,128,128]{2,1,0:T(8,128)}, u32[]{:S(2)}) %copy-start) | copy-done | bytes 2162712
  76.7 2.0 %shard_map.51 = f32[4096,2048]{1,0:T(8,128)} custom-call(s32[32]{0:T(128)S(1)} %get-tuple-element.72.slot_ref, s32[33]{0:T(128)S(1)} %get-tuple-element.73.tile_ref, bf16[2,256,256]{2,1,0:T(8,128)(2,1)S(1)} %collective-permute-done.9.refs_0_, bf16[2,256,256]{2,1,0:T(8,128)(2,1)S(1)} %collective-permute-done.25.refs_1_, ...), custom_call_target="tpu_custom_call", output_to_operand_aliasing={{}: (8, {})} | custom-call | flops 300000000 | bytes 8388608 | tf_op jit(solution)/shard_map/pallas_call | solution.py:324
  (44 shorter events, 8.1 us)
Async XLA Ops:
  5.3 10.0 %collective-permute-start.3 = (bf16[256,256]{1,0:T(8,128)(2,1)}, bf16[256,256]{1,0:T(8,128)(2,1)S(1)}, u32[]{:S(2)}, u32[]{:S(2)}) collective-permute-start(bf16[256,256]{1,0:T(8,128)(2,1)} %get-tuple-element.47), channel_id=1, source_target_pairs={{0,8},{8,0},{16,24},{24,16},{1,9},{9,1},{17,25},{25,17},{2,10},{10... | collective-permute-start | bytes 393224 | tf_op jit(solution)/shard_map/ppermute | solution.py:388
  8.2 14.2 %collective-permute-start = (bf16[528,128]{1,0:T(8,128)(2,1)}, bf16[528,128]{1,0:T(8,128)(2,1)S(1)}, u32[]{:S(2)}, u32[]{:S(2)}) collective-permute-start(bf16[528,128]{1,0:T(8,128)(2,1)} %get-tuple-element.43), channel_id=1, source_target_pairs={{0,2},{1,3},{2,4},{3,5},{4,6},{5,7},{6,0},{7,1},{8,10},{9,11},{10,... | collective-permute-start | bytes 405512 | tf_op jit(solution)/shard_map/ppermute | solution.py:392
  9.8 12.6 %collective-permute-start.1 = (bf16[528,128]{1,0:T(8,128)(2,1)}, bf16[528,128]{1,0:T(8,128)(2,1)S(1)}, u32[]{:S(2)}, u32[]{:S(2)}) collective-permute-start(bf16[528,128]{1,0:T(8,128)(2,1)} %get-tuple-element.44), channel_id=1, source_target_pairs={{0,4},{1,5},{2,6},{3,7},{4,0},{5,1},{6,2},{7,3},{8,12},{9,13},{10,... | collective-permute-start | bytes 405512 | tf_op jit(solution)/shard_map/ppermute | solution.py:392
  12.4 10.0 %collective-permute-start.2 = (bf16[528,128]{1,0:T(8,128)(2,1)}, bf16[528,128]{1,0:T(8,128)(2,1)S(1)}, u32[]{:S(2)}, u32[]{:S(2)}) collective-permute-start(bf16[528,128]{1,0:T(8,128)(2,1)} %get-tuple-element.45), channel_id=1, source_target_pairs={{0,6},{1,7},{2,0},{3,1},{4,2},{5,3},{6,4},{7,5},{8,14},{9,15},{10,... | collective-permute-start | bytes 405512 | tf_op jit(solution)/shard_map/ppermute | solution.py:392
  13.7 8.6 %collective-permute-start.4 = (bf16[256,256]{1,0:T(8,128)(2,1)}, bf16[256,256]{1,0:T(8,128)(2,1)S(1)}, u32[]{:S(2)}, u32[]{:S(2)}) collective-permute-start(bf16[256,256]{1,0:T(8,128)(2,1)} %get-tuple-element.48), channel_id=1, source_target_pairs={{0,16},{8,24},{16,0},{24,8},{1,17},{9,25},{17,1},{25,9},{2,18},{10... | collective-permute-start | bytes 393224 | tf_op jit(solution)/shard_map/ppermute | solution.py:388
  15.3 7.1 %collective-permute-start.5 = (bf16[256,256]{1,0:T(8,128)(2,1)}, bf16[256,256]{1,0:T(8,128)(2,1)S(1)}, u32[]{:S(2)}, u32[]{:S(2)}) collective-permute-start(bf16[256,256]{1,0:T(8,128)(2,1)} %get-tuple-element.49), channel_id=1, source_target_pairs={{0,24},{8,16},{16,8},{24,0},{1,25},{9,17},{17,9},{25,1},{2,26},{10... | collective-permute-start | bytes 393224 | tf_op jit(solution)/shard_map/ppermute | solution.py:388
  22.5 14.4 %collective-permute-start.7 = (bf16[2,256,256]{2,1,0:T(8,128)(2,1)S(1)}, bf16[2,256,256]{2,1,0:T(8,128)(2,1)S(1)}, u32[]{:S(2)}, u32[]{:S(2)}) collective-permute-start(bf16[2,256,256]{2,1,0:T(8,128)(2,1)S(1)} %pad_maximum_fusion.2.refs_2_), channel_id=1, source_target_pairs={{0,2},{1,3},{2,4},{3,5},{4,6},{5,7},{6,0},{7,1},{8,10},{9,11},{10,... | collective-permute-start | bytes 786440 | tf_op jit(solution)/shard_map/ppermute | solution.py:392
  25.6 11.3 %collective-permute-start.6 = (bf16[2,256,256]{2,1,0:T(8,128)(2,1)S(1)}, bf16[2,256,256]{2,1,0:T(8,128)(2,1)S(1)}, u32[]{:S(2)}, u32[]{:S(2)}) collective-permute-start(bf16[2,256,256]{2,1,0:T(8,128)(2,1)S(1)} %pad_maximum_fusion.1.refs_0_), channel_id=1, source_target_pairs={{0,2},{1,3},{2,4},{3,5},{4,6},{5,7},{6,0},{7,1},{8,10},{9,11},{10,... | collective-permute-start | bytes 786440 | tf_op jit(solution)/shard_map/ppermute | solution.py:392
  26.7 24.8 %collective-permute-start.16 = (bf16[4,528,128]{2,1,0:T(8,128)(2,1)S(1)}, bf16[4,528,128]{2,1,0:T(8,128)(2,1)S(1)}, u32[]{:S(2)}, u32[]{:S(2)}) collective-permute-start(bf16[4,528,128]{2,1,0:T(8,128)(2,1)S(1)} %pad_maximum_fusion.refs_12_), channel_id=1, source_target_pairs={{0,8},{8,0},{16,24},{24,16},{1,9},{9,1},{17,25},{25,17},{2,10},{10... | collective-permute-start | bytes 1622024 | tf_op jit(solution)/shard_map/ppermute | solution.py:388
  27.3 24.7 %collective-permute-start.17 = (bf16[4,528,128]{2,1,0:T(8,128)(2,1)S(1)}, bf16[4,528,128]{2,1,0:T(8,128)(2,1)S(1)}, u32[]{:S(2)}, u32[]{:S(2)}) collective-permute-start(bf16[4,528,128]{2,1,0:T(8,128)(2,1)S(1)} %pad_maximum_fusion.refs_12_), channel_id=1, source_target_pairs={{0,16},{8,24},{16,0},{24,8},{1,17},{9,25},{17,1},{25,9},{2,18},{10... | collective-permute-start | bytes 1622024 | tf_op jit(solution)/shard_map/ppermute | solution.py:388
  28.8 24.4 %collective-permute-start.18 = (bf16[4,528,128]{2,1,0:T(8,128)(2,1)S(1)}, bf16[4,528,128]{2,1,0:T(8,128)(2,1)S(1)}, u32[]{:S(2)}, u32[]{:S(2)}) collective-permute-start(bf16[4,528,128]{2,1,0:T(8,128)(2,1)S(1)} %pad_maximum_fusion.refs_12_), channel_id=1, source_target_pairs={{0,24},{8,16},{16,8},{24,0},{1,25},{9,17},{17,9},{25,1},{2,26},{10... | collective-permute-start | bytes 1622024 | tf_op jit(solution)/shard_map/ppermute | solution.py:388
  36.9 11.1 %collective-permute-start.10 = (bf16[2,256,256]{2,1,0:T(8,128)(2,1)S(1)}, bf16[2,256,256]{2,1,0:T(8,128)(2,1)S(1)}, u32[]{:S(2)}, u32[]{:S(2)}) collective-permute-start(bf16[2,256,256]{2,1,0:T(8,128)(2,1)S(1)} %collective-permute-done.7.refs_6_), channel_id=1, source_target_pairs={{0,2},{1,3},{2,4},{3,5},{4,6},{5,7},{6,0},{7,1},{8,10},{9,11},{10,... | collective-permute-start | bytes 786440 | tf_op jit(solution)/shard_map/ppermute | solution.py:392
  39.1 12.4 %collective-permute-start.8 = (bf16[2,256,256]{2,1,0:T(8,128)(2,1)S(1)}, bf16[2,256,256]{2,1,0:T(8,128)(2,1)S(1)}, u32[]{:S(2)}, u32[]{:S(2)}) collective-permute-start(bf16[2,256,256]{2,1,0:T(8,128)(2,1)S(1)} %collective-permute-done.6.refs_4_), channel_id=1, source_target_pairs={{0,2},{1,3},{2,4},{3,5},{4,6},{5,7},{6,0},{7,1},{8,10},{9,11},{10,... | collective-permute-start | bytes 786440 | tf_op jit(solution)/shard_map/ppermute | solution.py:392
  48.0 6.9 %collective-permute-start.21 = (bf16[4,528,128]{2,1,0:T(8,128)(2,1)S(1)}, bf16[4,528,128]{2,1,0:T(8,128)(2,1)S(1)}, u32[]{:S(2)}, u32[]{:S(2)}) collective-permute-start(bf16[4,528,128]{2,1,0:T(8,128)(2,1)S(1)} %pad_maximum_fusion.refs_12_), channel_id=1, source_target_pairs={{0,1},{1,0},{2,3},{3,2},{4,5},{5,4},{6,7},{7,6},{8,9},{9,8},{10,11... | collective-permute-start | bytes 1622024 | tf_op jit(solution)/shard_map/ppermute | solution.py:395
  51.5 2.3 %collective-permute-start.12 = (bf16[2,256,256]{2,1,0:T(8,128)(2,1)S(1)}, bf16[2,256,256]{2,1,0:T(8,128)(2,1)S(1)}, u32[]{:S(2)}, u32[]{:S(2)}) collective-permute-start(bf16[2,256,256]{2,1,0:T(8,128)(2,1)S(1)} %pad_maximum_fusion.1.refs_0_), channel_id=1, source_target_pairs={{0,1},{1,0},{2,3},{3,2},{4,5},{5,4},{6,7},{7,6},{8,9},{9,8},{10,11... | collective-permute-start | bytes 786440 | tf_op jit(solution)/shard_map/ppermute | solution.py:395
  52.0 1.8 %collective-permute-start.14 = (bf16[2,256,256]{2,1,0:T(8,128)(2,1)S(1)}, bf16[2,256,256]{2,1,0:T(8,128)(2,1)S(1)}, u32[]{:S(2)}, u32[]{:S(2)}) collective-permute-start(bf16[2,256,256]{2,1,0:T(8,128)(2,1)S(1)} %collective-permute-done.6.refs_4_), channel_id=1, source_target_pairs={{0,1},{1,0},{2,3},{3,2},{4,5},{5,4},{6,7},{7,6},{8,9},{9,8},{10,11... | collective-permute-start | bytes 786440 | tf_op jit(solution)/shard_map/ppermute | solution.py:395
  53.2 5.4 %collective-permute-start.22 = (bf16[4,528,128]{2,1,0:T(8,128)(2,1)S(1)}, bf16[4,528,128]{2,1,0:T(8,128)(2,1)S(1)}, u32[]{:S(2)}, u32[]{:S(2)}) collective-permute-start(bf16[4,528,128]{2,1,0:T(8,128)(2,1)S(1)} %collective-permute-done.16.refs_13_), channel_id=1, source_target_pairs={{0,1},{1,0},{2,3},{3,2},{4,5},{5,4},{6,7},{7,6},{8,9},{9,8},{10,11... | collective-permute-start | bytes 1622024 | tf_op jit(solution)/shard_map/ppermute | solution.py:395
  53.7 4.9 %collective-permute-start.23 = (bf16[4,528,128]{2,1,0:T(8,128)(2,1)S(1)}, bf16[4,528,128]{2,1,0:T(8,128)(2,1)S(1)}, u32[]{:S(2)}, u32[]{:S(2)}) collective-permute-start(bf16[4,528,128]{2,1,0:T(8,128)(2,1)S(1)} %collective-permute-done.17.refs_14_), channel_id=1, source_target_pairs={{0,1},{1,0},{2,3},{3,2},{4,5},{5,4},{6,7},{7,6},{8,9},{9,8},{10,11... | collective-permute-start | bytes 1622024 | tf_op jit(solution)/shard_map/ppermute | solution.py:395
  53.8 4.9 %collective-permute-start.24 = (bf16[4,528,128]{2,1,0:T(8,128)(2,1)S(1)}, bf16[4,528,128]{2,1,0:T(8,128)(2,1)S(1)}, u32[]{:S(2)}, u32[]{:S(2)}) collective-permute-start(bf16[4,528,128]{2,1,0:T(8,128)(2,1)S(1)} %collective-permute-done.18.refs_15_), channel_id=1, source_target_pairs={{0,1},{1,0},{2,3},{3,2},{4,5},{5,4},{6,7},{7,6},{8,9},{9,8},{10,11... | collective-permute-start | bytes 1622024 | tf_op jit(solution)/shard_map/ppermute | solution.py:395
  54.7 2.7 %collective-permute-start.19 = (bf16[2,256,256]{2,1,0:T(8,128)(2,1)S(1)}, bf16[2,256,256]{2,1,0:T(8,128)(2,1)S(1)}, u32[]{:S(2)}, u32[]{:S(2)}) collective-permute-start(bf16[2,256,256]{2,1,0:T(8,128)(2,1)S(1)} %collective-permute-done.8.refs_8_), channel_id=1, source_target_pairs={{0,1},{1,0},{2,3},{3,2},{4,5},{5,4},{6,7},{7,6},{8,9},{9,8},{10,11... | collective-permute-start | bytes 786440 | tf_op jit(solution)/shard_map/ppermute | solution.py:395
  54.9 2.9 %collective-permute-start.20 = (bf16[2,256,256]{2,1,0:T(8,128)(2,1)S(1)}, bf16[2,256,256]{2,1,0:T(8,128)(2,1)S(1)}, u32[]{:S(2)}, u32[]{:S(2)}) collective-permute-start(bf16[2,256,256]{2,1,0:T(8,128)(2,1)S(1)} %collective-permute-done.10.refs_10_), channel_id=1, source_target_pairs={{0,1},{1,0},{2,3},{3,2},{4,5},{5,4},{6,7},{7,6},{8,9},{9,8},{10,11... | collective-permute-start | bytes 786440 | tf_op jit(solution)/shard_map/ppermute | solution.py:395
  57.4 11.2 %collective-permute-start.11 = (bf16[2,256,256]{2,1,0:T(8,128)(2,1)S(1)}, bf16[2,256,256]{2,1,0:T(8,128)(2,1)S(1)}, u32[]{:S(2)}, u32[]{:S(2)}) collective-permute-start(bf16[2,256,256]{2,1,0:T(8,128)(2,1)S(1)} %collective-permute-done.10.refs_10_), channel_id=1, source_target_pairs={{0,2},{1,3},{2,4},{3,5},{4,6},{5,7},{6,0},{7,1},{8,10},{9,11},{10,... | collective-permute-start | bytes 786440 | tf_op jit(solution)/shard_map/ppermute | solution.py:392
  57.8 15.4 %collective-permute-start.9 = (bf16[2,256,256]{2,1,0:T(8,128)(2,1)S(1)}, bf16[2,256,256]{2,1,0:T(8,128)(2,1)S(1)}, u32[]{:S(2)}, u32[]{:S(2)}) collective-permute-start(bf16[2,256,256]{2,1,0:T(8,128)(2,1)S(1)} %collective-permute-done.8.refs_8_), channel_id=1, source_target_pairs={{0,2},{1,3},{2,4},{3,5},{4,6},{5,7},{6,0},{7,1},{8,10},{9,11},{10,... | collective-permute-start | bytes 786440 | tf_op jit(solution)/shard_map/ppermute | solution.py:392
  73.2 1.9 %collective-permute-start.26 = (bf16[2,256,256]{2,1,0:T(8,128)(2,1)S(1)}, bf16[2,256,256]{2,1,0:T(8,128)(2,1)S(1)}, u32[]{:S(2)}, u32[]{:S(2)}) collective-permute-start(bf16[2,256,256]{2,1,0:T(8,128)(2,1)S(1)} %collective-permute-done.11.refs_2_), channel_id=1, source_target_pairs={{0,1},{1,0},{2,3},{3,2},{4,5},{5,4},{6,7},{7,6},{8,9},{9,8},{10,11... | collective-permute-start | bytes 786440 | tf_op jit(solution)/shard_map/ppermute | solution.py:395
  (5 other events, 7.1 us)

commit v4 on v3

v4 whole, which is shorter than its diff:
```python
import functools

import jax
import jax.numpy as jnp
from jax import lax
from jax.experimental import pallas as pl
from jax.experimental.pallas import tpu as pltpu
from jax.sharding import PartitionSpec as P

TILES = 128
CORES = 2
META = 16
EXTRA = 48
MIB = 1024 * 1024


def scale_of(class_ref):
    classes = class_ref[...]
    return jnp.where(
        classes == 0, 1.0, jnp.where(classes == 1, 0.5, jnp.where(classes == 2, 0.25, 0.125))
    ).astype(jnp.float32)


def pack_kernel(n_row, n_chip, slots, sens_ref, class_ref, ids_ref, counts_ref, *refs):
    outs, meta_ref = refs[:-1], refs[-1]
    r = lax.axis_index("row")
    z = lax.div(lax.axis_index("col"), CORES)
    rows, width = sens_ref.shape[2:]
    scale = scale_of(class_ref)
    for j in range(n_row):
        for i in range(slots):
            tile = sens_ref[r ^ j, i].T.astype(jnp.float32) * scale
            outs[j][i * width : (i + 1) * width] = tile.astype(jnp.bfloat16)
    scale = jnp.broadcast_to(scale, (width, rows)).T
    meta_ref[...] = jnp.zeros_like(meta_ref)
    meta_ref[:slots, :n_row] = ids_ref[...].astype(jnp.float32)
    meta_ref[slots : slots + 1, :n_row] = counts_ref[...].astype(jnp.float32)
    meta = meta_ref[...].astype(jnp.bfloat16)
    for s in range(n_chip):
        owner = lax.rem(z + s, n_chip)
        out = outs[n_row + s]
        for i in range(slots):
            tile = sens_ref[owner, i].astype(jnp.float32) * scale
            out[i * rows : (i + 1) * rows] = tile.astype(jnp.bfloat16)
        out[slots * rows :] = meta


def pack(sensitivity, weight_class, ids, counts, n_chip):
    n_row, slots, rows, width = sensitivity.shape
    vmem = pl.BlockSpec(memory_space=pltpu.VMEM)
    return pl.pallas_call(
        functools.partial(pack_kernel, n_row, n_chip, slots),
        out_shape=[jax.ShapeDtypeStruct((slots * width, rows), jnp.bfloat16)] * n_row
        + [jax.ShapeDtypeStruct((slots * rows + META, width), jnp.bfloat16)] * n_chip,
        in_specs=[vmem] * 4,
        out_specs=[vmem] * (n_row + n_chip),
        scratch_shapes=[pltpu.VMEM((META, width), jnp.float32)],
        cost_estimate=pl.CostEstimate(flops=0, bytes_accessed=0, transcendentals=0),
    )(sensitivity, weight_class, ids, counts)


def tile_of(place, station, r, z, core, i, j, slots, per_col, none):
    base = (slots + 1) * station
    left = place[base + i, r]
    right = place[base + j, z] - core * per_col
    used = (i < place[base + slots, r]) & (j < place[base + slots, z])
    inside = used & (right >= 0) & (right < per_col)
    return jnp.where(inside, left * per_col + right, none)


def block_of(out_ref, tile, per_col, width):
    rows = pl.ds(pl.multiple_of(lax.div(tile, per_col) * width, width), width)
    columns = pl.ds(pl.multiple_of(lax.rem(tile, per_col) * width, width), width)
    return out_ref.at[rows, columns]


def main_kernel(n_row, n_chip, slots, per_row, per_col, pieces, *refs):
    last = n_chip // 2
    others = [s for s in range(n_chip) if s != last]
    n_left = len(others) * CORES
    n_right = n_row * CORES
    n_source = n_left + len(pieces)
    sources = refs[:n_source]
    out_ref, right_ref, slot_ref, tile_ref = refs[n_source + 1 :][:4]
    (acc, left_buf, right_buf, fact_buf, zero_buf, blank, place, touches, owner, plan,
     load_sem, fact_sem, zero_sem, blank_sem, store_sem) = refs[n_source + 5 :]
    r = lax.axis_index("row")
    c = lax.axis_index("col")
    z, core = lax.div(c, CORES), lax.rem(c, CORES)
    width = acc.shape[-1]
    rows = left_buf.shape[-1]
    tiles = per_row * per_col
    facts = slots + 1
    pairs = [(i, j) for i in range(slots) for j in range(slots)]

    def load(index):
        if index < n_left:
            target = left_buf.at[index]
            source = sources[index].at[pl.ds(0, target.shape[0])]
        else:
            which, first, number = pieces[index - n_left]
            target = right_buf.at[which, pl.ds(first, number)]
            source = sources[index]
        return pltpu.make_async_copy(source, target, load_sem.at[index])

    for index in [*range(n_left, n_source), *range(n_left)]:
        load(index).start()
    zero_buf[...] = jnp.zeros_like(zero_buf)
    clears = [
        pltpu.make_async_copy(zero_buf, touches, zero_sem.at[0]),
        pltpu.make_async_copy(zero_buf, owner, zero_sem.at[1]),
    ]
    for copy in clears:
        copy.start()
    blank[...] = jnp.zeros_like(blank)
    step = blank.shape[0]
    top = out_ref.shape[0] // 2
    blanks = [
        pltpu.make_async_copy(blank, out_ref.at[pl.ds(top + n * step, step)], blank_sem.at[n])
        for n in range(top // step)
    ]
    for copy in blanks:
        copy.start()

    for index, (which, first, number) in enumerate(pieces):
        load(n_left + index).wait()
        for s in range(first, first + number):
            base = (which * n_chip + s) * facts
            meta = right_buf[which, s, slots * rows :].astype(jnp.float32)
            fact_buf[base : base + facts, :] = meta[:facts].astype(jnp.int32)
    to_smem = pltpu.make_async_copy(fact_buf, place, fact_sem)
    to_smem.start()
    for index in range(n_right):
        right_ref[index] = right_buf[index, last, : slots * rows]
    for copy in clears:
        copy.wait()
    to_smem.wait()

    def at(tile):
        return lax.div(tile, width), lax.rem(tile, width)

    def find(station, i, j):
        return tile_of(place, station, r, z, core, i, j, slots, per_col, tiles)

    none = len(pairs) * n_right

    def number_step(index, used):
        for n, (i, j) in enumerate(pairs):
            tile = find(index * n_chip + last, i, j)
            held = owner[at(tile)]
            fresh = (held == 0) & (tile < tiles)
            spot = jnp.where(tile == tiles, none, jnp.where(fresh, used, held - 1))
            slot_ref[index * len(pairs) + n] = 2 * spot + fresh.astype(jnp.int32)
            owner[at(tile)] = jnp.where(tile == tiles, 0, spot + 1)
            tile_ref[jnp.where(fresh, used, none)] = tile
            used = used + fresh.astype(jnp.int32)
        return used

    used = lax.fori_loop(0, n_right, number_step, 0)
    tile_ref[none] = used

    def plan_step(index, stored):
        for m, s in enumerate(others):
            for n, (i, j) in enumerate(pairs):
                tile = find(index * n_chip + s, i, j)
                fresh = touches[at(tile)] == 0
                touches[at(tile)] = 1
                own = fresh & (tile < tiles)
                code = 4 * tile + 2 * own.astype(jnp.int32) + fresh.astype(jnp.int32)
                plan[(index * len(others) + m) * len(pairs) + n] = code
                stored = stored + own.astype(jnp.int32)
        return stored

    stored = lax.fori_loop(0, n_right, plan_step, 0)

    for index in range(n_left):
        load(index).wait()

    def add(index, carry):
        other, j_row = lax.div(index, n_row), lax.rem(index, n_row)
        for m, s in enumerate(others):
            left = left_buf[m * CORES + other, pl.ds(j_row * slots * width, slots * width)]
            right = jnp.concatenate(
                [right_buf[index, s, j * rows : (j + 1) * rows] for j in range(slots)], axis=1
            )
            gram = jnp.dot(left, right, preferred_element_type=jnp.float32)
            for n, (i, j) in enumerate(pairs):
                code = plan[(index * len(others) + m) * len(pairs) + n]
                tile, fresh = lax.shift_right_logical(code, 2), code & 1
                part = gram[i * width : (i + 1) * width, j * width : (j + 1) * width]
                acc[tile] = jnp.where(fresh == 1, part, acc[tile] + part)
        return carry

    lax.fori_loop(0, n_right, add, 0)

    for copy in blanks:
        copy.wait()

    def store(tile):
        return pltpu.make_async_copy(
            acc.at[tile], block_of(out_ref, tile, per_col, width), store_sem
        )

    def store_step(index, carry):
        for n in range(len(others) * len(pairs)):
            code = plan[index * len(others) * len(pairs) + n]

            @pl.when(code & 2 != 0)
            def _():
                store(lax.shift_right_logical(code, 2)).start()

        return carry

    lax.fori_loop(0, n_right, store_step, 0)

    def drain_store(index, carry):
        store(0).wait()
        return carry

    lax.fori_loop(0, stored, drain_store, 0)


def main_part(left, right, pieces, zeros, n_row, per_row, per_col):
    n_chip = len(left) + 1
    n_right = n_row * CORES
    rows = left[0][0].shape[1]
    width = right[0].shape[-1]
    slots = right[0].shape[1] // rows
    height = n_row * slots * width
    flat = [x for chip in left for x in chip]
    chunks = len(flat) + len(right)
    tiles = per_row * per_col
    pairs = slots * slots * n_right
    facts = (n_chip * n_right * (slots + 1), width)
    state = (tiles // width + 1, width)
    step = width
    held = (
        (tiles + 1) * width * width * 4
        + len(flat) * height * rows * 2
        + n_right * (n_chip + 1) * (slots * rows + META) * width * 2
        + facts[0] * width * 4
        + step * zeros.shape[1] * 4
    )
    anywhere = pl.BlockSpec(memory_space=pl.ANY)
    vmem = pl.BlockSpec(memory_space=pltpu.VMEM)
    smem = pl.BlockSpec(memory_space=pltpu.SMEM)
    return pl.pallas_call(
        functools.partial(main_kernel, n_row, n_chip, slots, per_row, per_col, pieces),
        out_shape=[
            jax.ShapeDtypeStruct(zeros.shape, zeros.dtype),
            jax.ShapeDtypeStruct((n_right, slots * rows, width), jnp.bfloat16),
            jax.ShapeDtypeStruct((pairs,), jnp.int32),
            jax.ShapeDtypeStruct((pairs + 1,), jnp.int32),
        ],
        in_specs=[anywhere] * (chunks + 1),
        out_specs=[anywhere, vmem, smem, smem],
        scratch_shapes=[
            pltpu.VMEM((tiles + 1, width, width), jnp.float32),
            pltpu.VMEM((len(flat), height, rows), jnp.bfloat16),
            pltpu.VMEM((n_right, n_chip, slots * rows + META, width), jnp.bfloat16),
            pltpu.VMEM(facts, jnp.int32),
            pltpu.VMEM(state, jnp.int32),
            pltpu.VMEM((step, zeros.shape[1]), jnp.float32),
            pltpu.SMEM(facts, jnp.int32),
            pltpu.SMEM(state, jnp.int32),
            pltpu.SMEM(state, jnp.int32),
            pltpu.SMEM((pairs * len(left),), jnp.int32),
            pltpu.SemaphoreType.DMA((chunks,)),
            pltpu.SemaphoreType.DMA,
            pltpu.SemaphoreType.DMA((2,)),
            pltpu.SemaphoreType.DMA((zeros.shape[0] // 2 // step,)),
            pltpu.SemaphoreType.DMA,
        ],
        input_output_aliases={chunks: 0},
        compiler_params=pltpu.CompilerParams(vmem_limit_bytes=held + 3 * MIB),
        cost_estimate=pl.CostEstimate(flops=0, bytes_accessed=0, transcendentals=0),
    )(*flat, *right, zeros)


def tail_kernel(n_row, slots, per_col, slot_ref, tile_ref, *refs):
    lefts, right_ref = refs[:CORES], refs[CORES]
    out_ref, held, acc, load_sem, store_sem = refs[CORES + 2 :]
    rows, width = lefts[0].shape[-1], acc.shape[-1]
    pairs = [(i, j) for i in range(slots) for j in range(slots)]
    used = tile_ref[len(pairs) * CORES * n_row]

    def load(spot):
        tile = block_of(out_ref, tile_ref[spot], per_col, width)
        return pltpu.make_async_copy(tile, held.at[spot], load_sem)

    def store(spot):
        tile = block_of(out_ref, tile_ref[spot], per_col, width)
        return pltpu.make_async_copy(acc.at[spot], tile, store_sem)

    def each(act):
        def step(spot, carry):
            act(spot)
            return carry

        lax.fori_loop(0, used, step, 0)

    def gram_of(index):
        first = index % n_row * slots * width
        left = lefts[index // n_row][first : first + slots * width]
        right = jnp.concatenate(
            [right_ref[index, j * rows : (j + 1) * rows] for j in range(slots)], axis=1
        )
        return jnp.dot(left, right, preferred_element_type=jnp.float32)

    each(lambda spot: load(spot).start())
    for index in range(CORES * n_row):
        gram = gram_of(index)
        for n, (i, j) in enumerate(pairs):
            code = slot_ref[index * len(pairs) + n]
            spot, fresh = lax.shift_right_logical(code, 1), code & 1
            part = gram[i * width : (i + 1) * width, j * width : (j + 1) * width]
            acc[spot] = jnp.where(fresh == 1, part, acc[spot] + part)
    each(lambda spot: load(spot).wait())

    def add_store(spot):
        acc[spot] = acc[spot] + held[spot]
        store(spot).start()

    each(add_store)
    each(lambda spot: store(spot).wait())


def tail_part(left, right, slot, tile, out, per_col):
    rows = left[0].shape[1]
    n_row = right.shape[0] // CORES
    slots, width = right.shape[1] // rows, right.shape[2]
    spots = (slot.shape[0] + 1, width, width)
    anywhere = pl.BlockSpec(memory_space=pl.ANY)
    vmem = pl.BlockSpec(memory_space=pltpu.VMEM)
    smem = pl.BlockSpec(memory_space=pltpu.SMEM)
    return pl.pallas_call(
        functools.partial(tail_kernel, n_row, slots, per_col),
        out_shape=jax.ShapeDtypeStruct(out.shape, out.dtype),
        in_specs=[smem, smem] + [vmem] * (len(left) + 1) + [anywhere],
        out_specs=anywhere,
        scratch_shapes=[
            pltpu.VMEM(spots, jnp.float32),
            pltpu.VMEM(spots, jnp.float32),
            pltpu.SemaphoreType.DMA,
            pltpu.SemaphoreType.DMA,
        ],
        input_output_aliases={len(left) + 3: 0},
        compiler_params=pltpu.CompilerParams(vmem_limit_bytes=24 * MIB),
        cost_estimate=pl.CostEstimate(flops=0, bytes_accessed=0, transcendentals=0),
    )(slot, tile, *left, right, out)


def zero_kernel(after_ref, out_ref, block, sem):
    block[...] = jnp.zeros_like(block)
    height = block.shape[0]
    copies = [
        pltpu.make_async_copy(block, out_ref.at[pl.ds(n * height, height)], sem.at[n])
        for n in range(out_ref.shape[0] // 2 // height)
    ]
    for copy in copies:
        copy.start()
    for copy in copies:
        copy.wait()


def zero_upper(height, width, after):
    step = 128
    anywhere = pl.BlockSpec(memory_space=pl.ANY)
    return pl.pallas_call(
        zero_kernel,
        out_shape=jax.ShapeDtypeStruct((height, width), jnp.float32),
        in_specs=[anywhere],
        out_specs=anywhere,
        scratch_shapes=[
            pltpu.VMEM((step, width), jnp.float32),
            pltpu.SemaphoreType.DMA((height // 2 // step,)),
        ],
        cost_estimate=pl.CostEstimate(
            flops=0, bytes_accessed=height * width * 2, transcendentals=0
        ),
    )(after)


def local(sensitivity, tile_ids, counts, weight_class):
    n_row = lax.axis_size("row")
    n_col = lax.axis_size("col")
    n_chip = n_col // CORES
    width = sensitivity.shape[-1]
    per_row = TILES // n_row
    per_col = TILES // n_col
    middle = n_chip // 2

    def flip_row(value, j):
        return lax.ppermute(value, "row", [(i, i ^ j) for i in range(n_row)])

    def shift_chip(value, s):
        pairs = [(i, (i + CORES * s) % n_col) for i in range(n_col)]
        return lax.ppermute(value, "col", pairs)

    def flip_core(value):
        return lax.ppermute(value, "col", [(i, i ^ 1) for i in range(n_col)])

    after = lax.optimization_barrier

    ids = jnp.transpose(tile_ids, (0, 2, 1))[0]
    parts = pack(sensitivity[0], weight_class, ids, counts, n_chip)
    to_row, to_chip = parts[:n_row], parts[n_row:]
    plane = [to_row[0]] + [flip_row(to_row[j], j) for j in range(1, n_row)]
    from_chip = [to_chip[0]] + [shift_chip(to_chip[s], s) for s in range(1, n_chip)]
    zeros = zero_upper(per_row * width, per_col * width, to_chip[0])
    plane, from_chip, zeros = after((plane, from_chip, zeros))
    rows = sensitivity.shape[-2]
    chip = jnp.stack(plane).reshape(-1, rows)
    near = {0: chip}
    for s in range(1, middle):
        near[s] = shift_chip(near[s - 1], 1)
        near[n_chip - s] = shift_chip(near[(n_chip - s + 1) % n_chip], -1)
    right = jnp.stack(from_chip)
    sides = [right] + [flip_row(right, j) for j in range(1, n_row)]
    far = shift_chip(jnp.pad(near[middle - 1], ((0, EXTRA), (0, 0))), 1)
    near = after(near)
    swapped = {s: flip_core(near[s]) for s in near}
    swapped, waiting = after((swapped, sides))
    other_sides = [flip_core(x) for x in waiting]
    left = [[near[s], swapped[s]] for s in sorted(near)]
    pieces = [(j, 0, n_chip) for j in range(n_row * CORES)]

    out, tail_right, slot, tile = main_part(
        left, sides + other_sides, pieces, zeros, n_row, per_row, per_col
    )
    far, slot = after((far, slot))
    return tail_part([far, flip_core(far)], tail_right, slot, tile, out, per_col)


def solution(mesh):
    in_specs = (
        P(("row", "col"), None, None, None, None),
        P(("row", "col"), None, None),
        P(("row", "col"), None),
        P(("row", "col"), None),
    )
    return jax.shard_map(
        local, mesh=mesh, in_specs=in_specs, out_specs=P("row", "col"), check_vma=False
    )
```

time: 78.9 us -> 67.2 us (0.85)
  Pallas kernels: 28.4 us -> 19.2 us
  waiting for transfers between devices: 21.7 us -> 26.2 us
  local copies, waits for them, and re-layouts: 3.62 us -> 0.04 us
  other arithmetic: 1.93 us -> 0.14 us
  starting transfers between devices: 22.9 us -> 21.3 us
    pallas_call x5 -> x3, Pallas kernels: 19.2 us -> 10.4 us  [the longest x1 6.03 us: zero_upper(): pl.pallas_call(zero_kernel, out_shape=jax.ShapeDtypeStruct((height, width...]
    ppermute x9 -> x6, waiting for transfers between devices: 16.4 us -> 19.4 us  [shift_chip(): return lax.ppermute(value, 'col', pairs)]
    unnamed x4, local copies, waits for them, and re-layouts: 2.29 us -> 0.01 us
    another operation x3 -> x2, other arithmetic: 1.93 us -> 0.14 us  [the longest x1 0.07 us: local(): right = jnp.stack(from_chip)]
    transpose x1 -> x0, local copies, waits for them, and re-layouts: 1.34 us -> none  [local(): ids = jnp.transpose(tile_ids, (1, 0, 2))]
    ppermute x12 -> x8, starting transfers between devices: 2.63 us -> 1.61 us  [flip_core(): return lax.ppermute(value, 'col', [(i, i ^ 1) for i in range(n_col)])]
    ppermute x12 -> x8, waiting for transfers between devices: 4.18 us -> 5.16 us  [flip_core(): return lax.ppermute(value, 'col', [(i, i ^ 1) for i in range(n_col)])]
    ppermute x9 -> x6, starting transfers between devices: 11.7 us -> 11 us  [shift_chip(): return lax.ppermute(value, 'col', pairs)]
  transfers between devices with their start and end apart: 27 -> 20, of which waited for: 9 -> 9; matrix products, arithmetic and copies ran while one was open for 2% -> 0% of each run, Pallas kernels for 29% -> 22%
where the time goes in v4:
time: 67.2 us; the launch traced here: 66.9 us
  waiting for transfers between devices  26.2 us (39%)
  starting transfers between devices  21.3 us (32%)
  Pallas kernels  19.2 us (29%)
    ppermute x6, waiting for transfers between devices, shift_chip(): return lax.ppermute(value, 'col', pairs)  19.4 us
    ppermute x6, starting transfers between devices, shift_chip(): return lax.ppermute(value, 'col', pairs)  11 us
    pallas_call x1, Pallas kernels, main_part(): pl.pallas_call(functools.partial(main_kernel, n_row, n_chip, slots, per_r...  8.75 us
    ppermute x6, starting transfers between devices, flip_row(): return lax.ppermute(value, 'row', [(i, i ^ j) for i in range(n_row)])  8.61 us
    pallas_call x1, Pallas kernels, zero_upper(): pl.pallas_call(zero_kernel, out_shape=jax.ShapeDtypeStruct((height, width...  6.03 us
    ppermute x8, waiting for transfers between devices, flip_core(): return lax.ppermute(value, 'col', [(i, i ^ 1) for i in range(n_col)])  5.16 us
    pallas_call x1, Pallas kernels, tail_part(): pl.pallas_call(functools.partial(tail_kernel, n_row, slots, per_col), out...  2.22 us
    pallas_call x1, Pallas kernels, pack(): pl.pallas_call(functools.partial(pack_kernel, n_row, n_chip, slots), out_...  2.16 us
  transfers between devices with their start and end apart: 20, of which 9 were waited for; matrix products, arithmetic and copies ran while one was open for 0% of the time, Pallas kernels for 22%

profile of v4, /device:TPU:0, one launch (start us, length us, event | category | flops | bytes accessed | tf_op | source)
XLA Modules:
  0.0 66.9 jit_solution(8144369117800276444)
XLA Ops:
  0.0 2.2 %shard_map.46 = (bf16[256,256]{1,0:T(8,128)(2,1)}, bf16[256,256]{1,0:T(8,128)(2,1)}, bf16[256,256]{1,0:T(8,128)(2,1)}, bf16[256,256]{1,0:T(8,128)(2,1)}, bf16[52...) custom-call(bf16[4,2,256,128]{3,2,1,0:T(8,128)(2,1)} %bitcast.18, ...), custom_call_target="tpu_custom_call" | custom-call | tf_op jit(solution)/shard_map/pallas_call | solution.py:51
  2.2 3.0 %collective-permute-start = (bf16[256,256]{1,0:T(8,128)(2,1)}, bf16[256,256]{1,0:T(8,128)(2,1)S(1)}, u32[]{:S(2)}, u32[]{:S(2)}) collective-permute-start(bf16[256,256]{1,0:T(8,128)(2,1)} %get-tuple-element.39), channel_id=1, source_target_pairs={{0,8},{8,0},{16,24},{24,16},{1,9},{9,1},{17,25},{25,17},{2,10},{10... | collective-permute-start | bytes 393224 | tf_op jit(solution)/shard_map/ppermute | solution.py:394
  5.2 1.6 %collective-permute-start.3 = (bf16[528,128]{1,0:T(8,128)(2,1)}, bf16[528,128]{1,0:T(8,128)(2,1)S(1)}, u32[]{:S(2)}, u32[]{:S(2)}) collective-permute-start(bf16[528,128]{1,0:T(8,128)(2,1)} %get-tuple-element.43), channel_id=1, source_target_pairs={{0,2},{1,3},{2,4},{3,5},{4,6},{5,7},{6,0},{7,1},{8,10},{9,11},{10,... | collective-permute-start | bytes 405512 | tf_op jit(solution)/shard_map/ppermute | solution.py:398
  6.7 2.6 %collective-permute-start.4 = (bf16[528,128]{1,0:T(8,128)(2,1)}, bf16[528,128]{1,0:T(8,128)(2,1)S(1)}, u32[]{:S(2)}, u32[]{:S(2)}) collective-permute-start(bf16[528,128]{1,0:T(8,128)(2,1)} %get-tuple-element.44), channel_id=1, source_target_pairs={{0,4},{1,5},{2,6},{3,7},{4,0},{5,1},{6,2},{7,3},{8,12},{9,13},{10,... | collective-permute-start | bytes 405512 | tf_op jit(solution)/shard_map/ppermute | solution.py:398
  9.3 1.3 %collective-permute-start.5 = (bf16[528,128]{1,0:T(8,128)(2,1)}, bf16[528,128]{1,0:T(8,128)(2,1)S(1)}, u32[]{:S(2)}, u32[]{:S(2)}) collective-permute-start(bf16[528,128]{1,0:T(8,128)(2,1)} %get-tuple-element.45), channel_id=1, source_target_pairs={{0,6},{1,7},{2,0},{3,1},{4,2},{5,3},{6,4},{7,5},{8,14},{9,15},{10,... | collective-permute-start | bytes 405512 | tf_op jit(solution)/shard_map/ppermute | solution.py:398
  10.7 1.5 %collective-permute-start.1 = (bf16[256,256]{1,0:T(8,128)(2,1)}, bf16[256,256]{1,0:T(8,128)(2,1)S(1)}, u32[]{:S(2)}, u32[]{:S(2)}) collective-permute-start(bf16[256,256]{1,0:T(8,128)(2,1)} %get-tuple-element.40), channel_id=1, source_target_pairs={{0,16},{8,24},{16,0},{24,8},{1,17},{9,25},{17,1},{25,9},{2,18},{10... | collective-permute-start | bytes 393224 | tf_op jit(solution)/shard_map/ppermute | solution.py:394
  12.7 6.0 %shard_map.47.refs_14_ = f32[4096,2048]{1,0:T(8,128)} custom-call(bf16[528,128]{1,0:T(8,128)(2,1)} %get-tuple-element.53.after_ref), custom_call_target="tpu_custom_call" | custom-call | bytes 16777216 | tf_op jit(solution)/shard_map/pallas_call | solution.py:369
  18.9 1.6 %collective-permute-start.12 = (bf16[4,528,128]{2,1,0:T(8,128)(2,1)S(1)}, bf16[4,528,128]{2,1,0:T(8,128)(2,1)S(1)}, u32[]{:S(2)}, u32[]{:S(2)}) collective-permute-start(bf16[4,528,128]{2,1,0:T(8,128)(2,1)S(1)} %pad_maximum_fusion.refs_6_), channel_id=1, source_target_pairs={{0,8},{8,0},{16,24},{24,16},{1,9},{9,1},{17,25},{25,17},{2,10},{10... | collective-permute-start | bytes 1622024 | tf_op jit(solution)/shard_map/ppermute | solution.py:394
  20.5 1.8 %collective-permute-start.6 = (bf16[1024,256]{1,0:T(8,128)(2,1)S(1)}, bf16[1024,256]{1,0:T(8,128)(2,1)S(1)}, u32[]{:S(2)}, u32[]{:S(2)}) collective-permute-start(bf16[1024,256]{1,0:T(8,128)(2,1)S(1)} %bitcast.13), channel_id=1, source_target_pairs={{0,2},{1,3},{2,4},{3,5},{4,6},{5,7},{6,0},{7,1},{8,10},{9,11},{10,... | collective-permute-start | bytes 1572872 | tf_op jit(solution)/shard_map/ppermute | solution.py:398
  22.3 2.0 %collective-permute-start.8 = (bf16[1024,256]{1,0:T(8,128)(2,1)S(1)}, bf16[1024,256]{1,0:T(8,128)(2,1)S(1)}, u32[]{:S(2)}, u32[]{:S(2)}) collective-permute-start(bf16[1024,256]{1,0:T(8,128)(2,1)S(1)} %bitcast.14), channel_id=1, source_target_pairs={{0,6},{1,7},{2,0},{3,1},{4,2},{5,3},{6,4},{7,5},{8,14},{9,15},{10,... | collective-permute-start | bytes 1572872 | tf_op jit(solution)/shard_map/ppermute | solution.py:398
  24.4 1.5 %collective-permute-start.13 = (bf16[4,528,128]{2,1,0:T(8,128)(2,1)S(1)}, bf16[4,528,128]{2,1,0:T(8,128)(2,1)S(1)}, u32[]{:S(2)}, u32[]{:S(2)}) collective-permute-start(bf16[4,528,128]{2,1,0:T(8,128)(2,1)S(1)} %pad_maximum_fusion.refs_6_), channel_id=1, source_target_pairs={{0,16},{8,24},{16,0},{24,8},{1,17},{9,25},{17,1},{25,9},{2,18},{10... | collective-permute-start | bytes 1622024 | tf_op jit(solution)/shard_map/ppermute | solution.py:394
  25.9 0.5 collective-permute-start.14
  26.4 10.8 %collective-permute-done.6.refs_2_ = bf16[1024,256]{1,0:T(8,128)(2,1)S(1)} collective-permute-done((bf16[1024,256]{1,0:T(8,128)(2,1)S(1)}, bf16[1024,256]{1,0:T(8,128)(2,1)S(1)}, u32[]{:S(2)}, u32[]{:S(2)}) %collective-permute-start.6) | collective-permute-done | bytes 524320 | tf_op jit(solution)/shard_map/ppermute | solution.py:398
  37.2 8.3 %collective-permute-done.8.refs_4_ = bf16[1024,256]{1,0:T(8,128)(2,1)S(1)} collective-permute-done((bf16[1024,256]{1,0:T(8,128)(2,1)S(1)}, bf16[1024,256]{1,0:T(8,128)(2,1)S(1)}, u32[]{:S(2)}, u32[]{:S(2)}) %collective-permute-start.8) | collective-permute-done | bytes 524320 | tf_op jit(solution)/shard_map/ppermute | solution.py:398
  45.5 0.5 collective-permute-start.11
  46.1 1.6 %collective-permute-done.13.refs_8_ = bf16[4,528,128]{2,1,0:T(8,128)(2,1)S(1)} collective-permute-done((bf16[4,528,128]{2,1,0:T(8,128)(2,1)S(1)}, bf16[4,528,128]{2,1,0:T(8,128)(2,1)S(1)}, u32[]{:S(2)}, u32[]{:S(2)}) %collective-permute-start.13) | collective-permute-done | bytes 540704 | tf_op jit(solution)/shard_map/ppermute | solution.py:394
  47.7 1.7 %collective-permute-start.7 = (bf16[1072,256]{1,0:T(8,128)(2,1)S(1)}, bf16[1072,256]{1,0:T(8,128)(2,1)S(1)}, u32[]{:S(2)}, u32[]{:S(2)}) collective-permute-start(bf16[1072,256]{1,0:T(8,128)(2,1)S(1)} %pad.4), channel_id=1, source_target_pairs={{0,2},{1,3},{2,4},{3,5},{4,6},{5,7},{6,0},{7,1},{8,10},{9,11},{10,... | collective-permute-start | bytes 1646600 | tf_op jit(solution)/shard_map/ppermute | solution.py:398
  50.4 0.9 %collective-permute-done.15.refs_10_ = bf16[4,528,128]{2,1,0:T(8,128)(2,1)S(1)} collective-permute-done((bf16[4,528,128]{2,1,0:T(8,128)(2,1)S(1)}, bf16[4,528,128]{2,1,0:T(8,128)(2,1)S(1)}, u32[]{:S(2)}, u32[]{:S(2)}) %collective-permute-start.15) | collective-permute-done | bytes 540704 | tf_op jit(solution)/shard_map/ppermute | solution.py:401
  51.3 0.8 %collective-permute-done.16.refs_11_ = bf16[4,528,128]{2,1,0:T(8,128)(2,1)S(1)} collective-permute-done((bf16[4,528,128]{2,1,0:T(8,128)(2,1)S(1)}, bf16[4,528,128]{2,1,0:T(8,128)(2,1)S(1)}, u32[]{:S(2)}, u32[]{:S(2)}) %collective-permute-start.16) | collective-permute-done | bytes 540704 | tf_op jit(solution)/shard_map/ppermute | solution.py:401
  52.1 0.8 %collective-permute-done.17.refs_12_ = bf16[4,528,128]{2,1,0:T(8,128)(2,1)S(1)} collective-permute-done((bf16[4,528,128]{2,1,0:T(8,128)(2,1)S(1)}, bf16[4,528,128]{2,1,0:T(8,128)(2,1)S(1)}, u32[]{:S(2)}, u32[]{:S(2)}) %collective-permute-start.17) | collective-permute-done | bytes 540704 | tf_op jit(solution)/shard_map/ppermute | solution.py:401
  52.9 0.8 %collective-permute-done.18.refs_13_ = bf16[4,528,128]{2,1,0:T(8,128)(2,1)S(1)} collective-permute-done((bf16[4,528,128]{2,1,0:T(8,128)(2,1)S(1)}, bf16[4,528,128]{2,1,0:T(8,128)(2,1)S(1)}, u32[]{:S(2)}, u32[]{:S(2)}) %collective-permute-start.18) | collective-permute-done | bytes 540704 | tf_op jit(solution)/shard_map/ppermute | solution.py:401
  53.7 8.8 %shard_map.48 = (f32[4096,2048]{1,0:T(8,128)}, bf16[8,512,128]{2,1,0:T(8,128)(2,1)S(1)}, s32[32]{0:T(128)S(1)}, s32[33]{0:T(128)S(1)}) custom-call(bf16[1024,256]{1,0:T(8,128)(2,1)S(1)} %bitcast.16, bf16[1024,256]{1,0:T(8,128)(2,1)S(1)} %collective-permute-done.9.refs_1_, ...), custom_call_target="tpu_custom_call", output_to_operand_aliasing={{0}: (14, {})} | custom-call | tf_op jit(solution)/shard_map/pallas_call | solution.py:247
  62.8 1.9 %collective-permute-done.19.refs_1_ = bf16[1072,256]{1,0:T(8,128)(2,1)S(1)} collective-permute-done((bf16[1072,256]{1,0:T(8,128)(2,1)S(1)}, bf16[1072,256]{1,0:T(8,128)(2,1)S(1)}, u32[]{:S(2)}, u32[]{:S(2)}) %collective-permute-start.19) | collective-permute-done | bytes 548896 | tf_op jit(solution)/shard_map/ppermute | solution.py:401
  64.7 2.2 %shard_map.49 = f32[4096,2048]{1,0:T(8,128)} custom-call(s32[32]{0:T(128)S(1)} %get-tuple-element.66.slot_ref, s32[33]{0:T(128)S(1)} %get-tuple-element.67.tile_ref, bf16[1072,256]{1,0:T(8,128)(2,1)S(1)} %collective-permute-done.7.refs_0_, bf16[1072,256]{1,0:T(8,128)(2,1)S(1)} %collective-permute-done.19.refs_1_, ...), custom_call_target="tpu_custom_call", output_to_operand_aliasing={{}: (5, {})} | custom-call | tf_op jit(solution)/shard_map/pallas_call | solution.py:336
  (27 shorter events, 2.2 us)
Async XLA Ops:
  2.2 16.6 %copy-start = (bf16[528,128]{1,0:T(8,128)(2,1)S(1)}, bf16[528,128]{1,0:T(8,128)(2,1)}, u32[]{:S(2)}) copy-start(bf16[528,128]{1,0:T(8,128)(2,1)} %get-tuple-element.53.after_ref) | copy-start | bytes 405508
  2.2 18.3 %copy-start.1 = (bf16[256,256]{1,0:T(8,128)(2,1)S(1)}, bf16[256,256]{1,0:T(8,128)(2,1)}, u32[]{:S(2)}) copy-start(bf16[256,256]{1,0:T(8,128)(2,1)} %get-tuple-element.46) | copy-start | bytes 393220
  2.2 10.0 %collective-permute-start = (bf16[256,256]{1,0:T(8,128)(2,1)}, bf16[256,256]{1,0:T(8,128)(2,1)S(1)}, u32[]{:S(2)}, u32[]{:S(2)}) collective-permute-start(bf16[256,256]{1,0:T(8,128)(2,1)} %get-tuple-element.39), channel_id=1, source_target_pairs={{0,8},{8,0},{16,24},{24,16},{1,9},{9,1},{17,25},{25,17},{2,10},{10... | collective-permute-start | bytes 393224 | tf_op jit(solution)/shard_map/ppermute | solution.py:394
  5.2 13.6 %collective-permute-start.3 = (bf16[528,128]{1,0:T(8,128)(2,1)}, bf16[528,128]{1,0:T(8,128)(2,1)S(1)}, u32[]{:S(2)}, u32[]{:S(2)}) collective-permute-start(bf16[528,128]{1,0:T(8,128)(2,1)} %get-tuple-element.43), channel_id=1, source_target_pairs={{0,2},{1,3},{2,4},{3,5},{4,6},{5,7},{6,0},{7,1},{8,10},{9,11},{10,... | collective-permute-start | bytes 405512 | tf_op jit(solution)/shard_map/ppermute | solution.py:398
  6.7 12.0 %collective-permute-start.4 = (bf16[528,128]{1,0:T(8,128)(2,1)}, bf16[528,128]{1,0:T(8,128)(2,1)S(1)}, u32[]{:S(2)}, u32[]{:S(2)}) collective-permute-start(bf16[528,128]{1,0:T(8,128)(2,1)} %get-tuple-element.44), channel_id=1, source_target_pairs={{0,4},{1,5},{2,6},{3,7},{4,0},{5,1},{6,2},{7,3},{8,12},{9,13},{10,... | collective-permute-start | bytes 405512 | tf_op jit(solution)/shard_map/ppermute | solution.py:398
  9.3 9.4 %collective-permute-start.5 = (bf16[528,128]{1,0:T(8,128)(2,1)}, bf16[528,128]{1,0:T(8,128)(2,1)S(1)}, u32[]{:S(2)}, u32[]{:S(2)}) collective-permute-start(bf16[528,128]{1,0:T(8,128)(2,1)} %get-tuple-element.45), channel_id=1, source_target_pairs={{0,6},{1,7},{2,0},{3,1},{4,2},{5,3},{6,4},{7,5},{8,14},{9,15},{10,... | collective-permute-start | bytes 405512 | tf_op jit(solution)/shard_map/ppermute | solution.py:398
  10.7 8.0 %collective-permute-start.1 = (bf16[256,256]{1,0:T(8,128)(2,1)}, bf16[256,256]{1,0:T(8,128)(2,1)S(1)}, u32[]{:S(2)}, u32[]{:S(2)}) collective-permute-start(bf16[256,256]{1,0:T(8,128)(2,1)} %get-tuple-element.40), channel_id=1, source_target_pairs={{0,16},{8,24},{16,0},{24,8},{1,17},{9,25},{17,1},{25,9},{2,18},{10... | collective-permute-start | bytes 393224 | tf_op jit(solution)/shard_map/ppermute | solution.py:394
  12.2 6.5 %collective-permute-start.2 = (bf16[256,256]{1,0:T(8,128)(2,1)}, bf16[256,256]{1,0:T(8,128)(2,1)S(1)}, u32[]{:S(2)}, u32[]{:S(2)}) collective-permute-start(bf16[256,256]{1,0:T(8,128)(2,1)} %get-tuple-element.41), channel_id=1, source_target_pairs={{0,24},{8,16},{16,8},{24,0},{1,25},{9,17},{17,9},{25,1},{2,26},{10... | collective-permute-start | bytes 393224 | tf_op jit(solution)/shard_map/ppermute | solution.py:394
  18.9 27.2 %collective-permute-start.12 = (bf16[4,528,128]{2,1,0:T(8,128)(2,1)S(1)}, bf16[4,528,128]{2,1,0:T(8,128)(2,1)S(1)}, u32[]{:S(2)}, u32[]{:S(2)}) collective-permute-start(bf16[4,528,128]{2,1,0:T(8,128)(2,1)S(1)} %pad_maximum_fusion.refs_6_), channel_id=1, source_target_pairs={{0,8},{8,0},{16,24},{24,16},{1,9},{9,1},{17,25},{25,17},{2,10},{10... | collective-permute-start | bytes 1622024 | tf_op jit(solution)/shard_map/ppermute | solution.py:394
  20.5 16.7 %collective-permute-start.6 = (bf16[1024,256]{1,0:T(8,128)(2,1)S(1)}, bf16[1024,256]{1,0:T(8,128)(2,1)S(1)}, u32[]{:S(2)}, u32[]{:S(2)}) collective-permute-start(bf16[1024,256]{1,0:T(8,128)(2,1)S(1)} %bitcast.13), channel_id=1, source_target_pairs={{0,2},{1,3},{2,4},{3,5},{4,6},{5,7},{6,0},{7,1},{8,10},{9,11},{10,... | collective-permute-start | bytes 1572872 | tf_op jit(solution)/shard_map/ppermute | solution.py:398
  22.3 23.2 %collective-permute-start.8 = (bf16[1024,256]{1,0:T(8,128)(2,1)S(1)}, bf16[1024,256]{1,0:T(8,128)(2,1)S(1)}, u32[]{:S(2)}, u32[]{:S(2)}) collective-permute-start(bf16[1024,256]{1,0:T(8,128)(2,1)S(1)} %bitcast.14), channel_id=1, source_target_pairs={{0,6},{1,7},{2,0},{3,1},{4,2},{5,3},{6,4},{7,5},{8,14},{9,15},{10,... | collective-permute-start | bytes 1572872 | tf_op jit(solution)/shard_map/ppermute | solution.py:398
  24.4 23.3 %collective-permute-start.13 = (bf16[4,528,128]{2,1,0:T(8,128)(2,1)S(1)}, bf16[4,528,128]{2,1,0:T(8,128)(2,1)S(1)}, u32[]{:S(2)}, u32[]{:S(2)}) collective-permute-start(bf16[4,528,128]{2,1,0:T(8,128)(2,1)S(1)} %pad_maximum_fusion.refs_6_), channel_id=1, source_target_pairs={{0,16},{8,24},{16,0},{24,8},{1,17},{9,25},{17,1},{25,9},{2,18},{10... | collective-permute-start | bytes 1622024 | tf_op jit(solution)/shard_map/ppermute | solution.py:394
  25.9 23.4 %collective-permute-start.14 = (bf16[4,528,128]{2,1,0:T(8,128)(2,1)S(1)}, bf16[4,528,128]{2,1,0:T(8,128)(2,1)S(1)}, u32[]{:S(2)}, u32[]{:S(2)}) collective-permute-start(bf16[4,528,128]{2,1,0:T(8,128)(2,1)S(1)} %pad_maximum_fusion.refs_6_), channel_id=1, source_target_pairs={{0,24},{8,16},{16,8},{24,0},{1,25},{9,17},{17,9},{25,1},{2,26},{10... | collective-permute-start | bytes 1622024 | tf_op jit(solution)/shard_map/ppermute | solution.py:394
  45.5 3.8 %collective-permute-start.10 = (bf16[1024,256]{1,0:T(8,128)(2,1)S(1)}, bf16[1024,256]{1,0:T(8,128)(2,1)S(1)}, u32[]{:S(2)}, u32[]{:S(2)}) collective-permute-start(bf16[1024,256]{1,0:T(8,128)(2,1)S(1)} %collective-permute-done.6.refs_2_), channel_id=1, source_target_pairs={{0,1},{1,0},{2,3},{3,2},{4,5},{5,4},{6,7},{7,6},{8,9},{9,8},{10,11... | collective-permute-start | bytes 1572872 | tf_op jit(solution)/shard_map/ppermute | solution.py:401
  45.5 3.8 %collective-permute-start.11 = (bf16[1024,256]{1,0:T(8,128)(2,1)S(1)}, bf16[1024,256]{1,0:T(8,128)(2,1)S(1)}, u32[]{:S(2)}, u32[]{:S(2)}) collective-permute-start(bf16[1024,256]{1,0:T(8,128)(2,1)S(1)} %collective-permute-done.8.refs_4_), channel_id=1, source_target_pairs={{0,1},{1,0},{2,3},{3,2},{4,5},{5,4},{6,7},{7,6},{8,9},{9,8},{10,11... | collective-permute-start | bytes 1572872 | tf_op jit(solution)/shard_map/ppermute | solution.py:401
  46.0 3.3 %collective-permute-start.9 = (bf16[1024,256]{1,0:T(8,128)(2,1)S(1)}, bf16[1024,256]{1,0:T(8,128)(2,1)S(1)}, u32[]{:S(2)}, u32[]{:S(2)}) collective-permute-start(bf16[1024,256]{1,0:T(8,128)(2,1)S(1)} %bitcast.15), channel_id=1, source_target_pairs={{0,1},{1,0},{2,3},{3,2},{4,5},{5,4},{6,7},{7,6},{8,9},{9,8},{10,11... | collective-permute-start | bytes 1572872 | tf_op jit(solution)/shard_map/ppermute | solution.py:401
  47.7 15.1 %collective-permute-start.7 = (bf16[1072,256]{1,0:T(8,128)(2,1)S(1)}, bf16[1072,256]{1,0:T(8,128)(2,1)S(1)}, u32[]{:S(2)}, u32[]{:S(2)}) collective-permute-start(bf16[1072,256]{1,0:T(8,128)(2,1)S(1)} %pad.4), channel_id=1, source_target_pairs={{0,2},{1,3},{2,4},{3,5},{4,6},{5,7},{6,0},{7,1},{8,10},{9,11},{10,... | collective-permute-start | bytes 1646600 | tf_op jit(solution)/shard_map/ppermute | solution.py:398
  49.3 2.0 %collective-permute-start.15 = (bf16[4,528,128]{2,1,0:T(8,128)(2,1)S(1)}, bf16[4,528,128]{2,1,0:T(8,128)(2,1)S(1)}, u32[]{:S(2)}, u32[]{:S(2)}) collective-permute-start(bf16[4,528,128]{2,1,0:T(8,128)(2,1)S(1)} %pad_maximum_fusion.refs_6_), channel_id=1, source_target_pairs={{0,1},{1,0},{2,3},{3,2},{4,5},{5,4},{6,7},{7,6},{8,9},{9,8},{10,11... | collective-permute-start | bytes 1622024 | tf_op jit(solution)/shard_map/ppermute | solution.py:401
  49.4 2.7 %collective-permute-start.16 = (bf16[4,528,128]{2,1,0:T(8,128)(2,1)S(1)}, bf16[4,528,128]{2,1,0:T(8,128)(2,1)S(1)}, u32[]{:S(2)}, u32[]{:S(2)}) collective-permute-start(bf16[4,528,128]{2,1,0:T(8,128)(2,1)S(1)} %collective-permute-done.12.refs_7_), channel_id=1, source_target_pairs={{0,1},{1,0},{2,3},{3,2},{4,5},{5,4},{6,7},{7,6},{8,9},{9,8},{10,11... | collective-permute-start | bytes 1622024 | tf_op jit(solution)/shard_map/ppermute | solution.py:401
  49.9 3.0 %collective-permute-start.17 = (bf16[4,528,128]{2,1,0:T(8,128)(2,1)S(1)}, bf16[4,528,128]{2,1,0:T(8,128)(2,1)S(1)}, u32[]{:S(2)}, u32[]{:S(2)}) collective-permute-start(bf16[4,528,128]{2,1,0:T(8,128)(2,1)S(1)} %collective-permute-done.13.refs_8_), channel_id=1, source_target_pairs={{0,1},{1,0},{2,3},{3,2},{4,5},{5,4},{6,7},{7,6},{8,9},{9,8},{10,11... | collective-permute-start | bytes 1622024 | tf_op jit(solution)/shard_map/ppermute | solution.py:401
  50.0 3.7 %collective-permute-start.18 = (bf16[4,528,128]{2,1,0:T(8,128)(2,1)S(1)}, bf16[4,528,128]{2,1,0:T(8,128)(2,1)S(1)}, u32[]{:S(2)}, u32[]{:S(2)}) collective-permute-start(bf16[4,528,128]{2,1,0:T(8,128)(2,1)S(1)} %collective-permute-done.14.refs_9_), channel_id=1, source_target_pairs={{0,1},{1,0},{2,3},{3,2},{4,5},{5,4},{6,7},{7,6},{8,9},{9,8},{10,11... | collective-permute-start | bytes 1622024 | tf_op jit(solution)/shard_map/ppermute | solution.py:401
  62.8 1.9 %collective-permute-start.19 = (bf16[1072,256]{1,0:T(8,128)(2,1)S(1)}, bf16[1072,256]{1,0:T(8,128)(2,1)S(1)}, u32[]{:S(2)}, u32[]{:S(2)}) collective-permute-start(bf16[1072,256]{1,0:T(8,128)(2,1)S(1)} %collective-permute-done.7.refs_0_), channel_id=1, source_target_pairs={{0,1},{1,0},{2,3},{3,2},{4,5},{5,4},{6,7},{7,6},{8,9},{9,8},{10,11... | collective-permute-start | bytes 1646600 | tf_op jit(solution)/shard_map/ppermute | solution.py:401

commit v5 on v4

--- a/solution.py
+++ b/solution.py
@@ -10,7 +10,6 @@
 TILES = 128
 CORES = 2
 META = 16
-EXTRA = 48
 MIB = 1024 * 1024
 
 
@@ -59,13 +58,41 @@
     )(sensitivity, weight_class, ids, counts)
 
 
-def tile_of(place, station, r, z, core, i, j, slots, per_col, none):
-    base = (slots + 1) * station
-    left = place[base + i, r]
-    right = place[base + j, z] - core * per_col
-    used = (i < place[base + slots, r]) & (j < place[base + slots, z])
-    inside = used & (right >= 0) & (right < per_col)
-    return jnp.where(inside, left * per_col + right, none)
+def plan_of(facts, r, z, core, n_chip, slots, per_col, none):
+    _, stations, width = facts.shape
+    lane = lax.broadcasted_iota(jnp.int32, (stations, width), 1)
+
+    def pick(row, owner):
+        return jnp.sum(jnp.where(lane == owner, facts[row], 0.0), axis=1, keepdims=True)
+
+    used_left, used_right = pick(slots, r), pick(slots, z)
+    lefts = [pick(i, r) for i in range(slots)]
+    rights = [pick(j, z) - (core * per_col).astype(jnp.float32) for j in range(slots)]
+    column = []
+    for i in range(slots):
+        for j in range(slots):
+            met = (i < used_left) & (j < used_right) & (rights[j] >= 0) & (rights[j] < per_col)
+            column.append(jnp.where(met, lefts[i] * per_col + rights[j], float(none)))
+    count = len(column) * stations
+    tile = jnp.broadcast_to(jnp.concatenate(column, axis=0), (count, count))
+    other = tile.T
+
+    def facts_of(axis):
+        pair = lax.broadcasted_iota(jnp.int32, (count, count), axis)
+        station = lax.rem(pair, stations)
+        far = lax.rem(station, n_chip) == n_chip // 2
+        order = jnp.where(far, lax.div(station, n_chip), station) * len(column)
+        return far, (order + lax.div(pair, stations)).astype(jnp.float32)
+
+    far_down, order_down = facts_of(0)
+    far_across, order_across = facts_of(1)
+    same = (tile == other) & (far_down == far_across)
+    first = jnp.min(jnp.where(same, order_down, 1e6), axis=0, keepdims=True)
+    fresh = (first == order_across[:1]).astype(jnp.float32)
+    real = (other[:1] < none).astype(jnp.float32)
+    place = jnp.where(far_across[:1], first, other[:1])
+    code = 4.0 * place + 2.0 * fresh * real + fresh
+    return code.astype(jnp.int32), other[:1].astype(jnp.int32)
 
 
 def block_of(out_ref, tile, per_col, width):
@@ -81,22 +108,24 @@
     n_right = n_row * CORES
     n_source = n_left + len(pieces)
     sources = refs[:n_source]
-    out_ref, right_ref, slot_ref, tile_ref = refs[n_source + 1 :][:4]
-    (acc, left_buf, right_buf, fact_buf, zero_buf, blank, place, touches, owner, plan,
-     load_sem, fact_sem, zero_sem, blank_sem, store_sem) = refs[n_source + 5 :]
+    out_ref, right_ref, plan = refs[n_source + 1 :][:3]
+    (acc, left_buf, right_buf, fact_buf, code_buf, blank,
+     load_sem, code_sem, blank_sem, store_sem) = refs[n_source + 4 :]
     r = lax.axis_index("row")
     c = lax.axis_index("col")
     z, core = lax.div(c, CORES), lax.rem(c, CORES)
     width = acc.shape[-1]
     rows = left_buf.shape[-1]
     tiles = per_row * per_col
-    facts = slots + 1
+    stations = n_right * n_chip
     pairs = [(i, j) for i in range(slots) for j in range(slots)]
 
     def load(index):
         if index < n_left:
             target = left_buf.at[index]
-            source = sources[index].at[pl.ds(0, target.shape[0])]
+            source = sources[index]
+            if len(source.shape) == 2:
+                source = source.at[pl.ds(0, target.shape[0])]
         else:
             which, first, number = pieces[index - n_left]
             target = right_buf.at[which, pl.ds(first, number)]
@@ -105,13 +134,6 @@
 
     for index in [*range(n_left, n_source), *range(n_left)]:
         load(index).start()
-    zero_buf[...] = jnp.zeros_like(zero_buf)
-    clears = [
-        pltpu.make_async_copy(zero_buf, touches, zero_sem.at[0]),
-        pltpu.make_async_copy(zero_buf, owner, zero_sem.at[1]),
-    ]
-    for copy in clears:
-        copy.start()
     blank[...] = jnp.zeros_like(blank)
     step = blank.shape[0]
     top = out_ref.shape[0] // 2
@@ -125,53 +147,18 @@
     for index, (which, first, number) in enumerate(pieces):
         load(n_left + index).wait()
         for s in range(first, first + number):
-            base = (which * n_chip + s) * facts
+            station = which * n_chip + s
             meta = right_buf[which, s, slots * rows :].astype(jnp.float32)
-            fact_buf[base : base + facts, :] = meta[:facts].astype(jnp.int32)
-    to_smem = pltpu.make_async_copy(fact_buf, place, fact_sem)
+            for i in range(slots + 1):
+                fact_buf[i, station : station + 1, :] = meta[i : i + 1]
+    code, tile_row = plan_of(fact_buf, r, z, core, n_chip, slots, per_col, tiles)
+    code_buf[0:1, :] = code
+    code_buf[1:2, :] = tile_row
+    to_smem = pltpu.make_async_copy(code_buf, plan, code_sem)
     to_smem.start()
     for index in range(n_right):
         right_ref[index] = right_buf[index, last, : slots * rows]
-    for copy in clears:
-        copy.wait()
     to_smem.wait()
-
-    def at(tile):
-        return lax.div(tile, width), lax.rem(tile, width)
-
-    def find(station, i, j):
-        return tile_of(place, station, r, z, core, i, j, slots, per_col, tiles)
-
-    none = len(pairs) * n_right
-
-    def number_step(index, used):
-        for n, (i, j) in enumerate(pairs):
-            tile = find(index * n_chip + last, i, j)
-            held = owner[at(tile)]
-            fresh = (held == 0) & (tile < tiles)
-            spot = jnp.where(tile == tiles, none, jnp.where(fresh, used, held - 1))
-            slot_ref[index * len(pairs) + n] = 2 * spot + fresh.astype(jnp.int32)
-            owner[at(tile)] = jnp.where(tile == tiles, 0, spot + 1)
-            tile_ref[jnp.where(fresh, used, none)] = tile
-            used = used + fresh.astype(jnp.int32)
-        return used
-
-    used = lax.fori_loop(0, n_right, number_step, 0)
-    tile_ref[none] = used
-
-    def plan_step(index, stored):
-        for m, s in enumerate(others):
-            for n, (i, j) in enumerate(pairs):
-                tile = find(index * n_chip + s, i, j)
-                fresh = touches[at(tile)] == 0
-                touches[at(tile)] = 1
-                own = fresh & (tile < tiles)
-                code = 4 * tile + 2 * own.astype(jnp.int32) + fresh.astype(jnp.int32)
-                plan[(index * len(others) + m) * len(pairs) + n] = code
-                stored = stored + own.astype(jnp.int32)
-        return stored
-
-    stored = lax.fori_loop(0, n_right, plan_step, 0)
 
     for index in range(n_left):
         load(index).wait()
@@ -185,7 +172,7 @@
             )
             gram = jnp.dot(left, right, preferred_element_type=jnp.float32)
             for n, (i, j) in enumerate(pairs):
-                code = plan[(index * len(others) + m) * len(pairs) + n]
+                code = plan[0, n * stations + index * n_chip + s]
                 tile, fresh = lax.shift_right_logical(code, 2), code & 1
                 part = gram[i * width : (i + 1) * width, j * width : (j + 1) * width]
                 acc[tile] = jnp.where(fresh == 1, part, acc[tile] + part)
@@ -201,17 +188,19 @@
             acc.at[tile], block_of(out_ref, tile, per_col, width), store_sem
         )
 
-    def store_step(index, carry):
-        for n in range(len(others) * len(pairs)):
-            code = plan[index * len(others) * len(pairs) + n]
-
-            @pl.when(code & 2 != 0)
-            def _():
-                store(lax.shift_right_logical(code, 2)).start()
-
-        return carry
-
-    lax.fori_loop(0, n_right, store_step, 0)
+    def store_step(index, stored):
+        for s in others:
+            for n in range(len(pairs)):
+                code = plan[0, n * stations + index * n_chip + s]
+
+                @pl.when(code & 2 != 0)
+                def _():
+                    store(lax.shift_right_logical(code, 2)).start()
+
+                stored = stored + (lax.shift_right_logical(code, 1) & 1)
+        return stored
+
+    stored = lax.fori_loop(0, n_right, store_step, 0)
 
     def drain_store(index, carry):
         store(0).wait()
@@ -231,14 +220,15 @@
     chunks = len(flat) + len(right)
     tiles = per_row * per_col
     pairs = slots * slots * n_right
-    facts = (n_chip * n_right * (slots + 1), width)
-    state = (tiles // width + 1, width)
+    facts = (slots + 1, n_chip * n_right, width)
+    plan = (8, pairs * n_chip)
     step = width
     held = (
         (tiles + 1) * width * width * 4
         + len(flat) * height * rows * 2
         + n_right * (n_chip + 1) * (slots * rows + META) * width * 2
-        + facts[0] * width * 4
+        + facts[0] * facts[1] * width * 4
+        + 8 * plan[1] * plan[1] * 4
         + step * zeros.shape[1] * 4
     )
     anywhere = pl.BlockSpec(memory_space=pl.ANY)
@@ -249,25 +239,19 @@
         out_shape=[
             jax.ShapeDtypeStruct(zeros.shape, zeros.dtype),
             jax.ShapeDtypeStruct((n_right, slots * rows, width), jnp.bfloat16),
-            jax.ShapeDtypeStruct((pairs,), jnp.int32),
-            jax.ShapeDtypeStruct((pairs + 1,), jnp.int32),
+            jax.ShapeDtypeStruct(plan, jnp.int32),
         ],
         in_specs=[anywhere] * (chunks + 1),
-        out_specs=[anywhere, vmem, smem, smem],
+        out_specs=[anywhere, vmem, smem],
         scratch_shapes=[
             pltpu.VMEM((tiles + 1, width, width), jnp.float32),
             pltpu.VMEM((len(flat), height, rows), jnp.bfloat16),
             pltpu.VMEM((n_right, n_chip, slots * rows + META, width), jnp.bfloat16),
-            pltpu.VMEM(facts, jnp.int32),
-            pltpu.VMEM(state, jnp.int32),
+            pltpu.VMEM(facts, jnp.float32),
+            pltpu.VMEM(plan, jnp.int32),
             pltpu.VMEM((step, zeros.shape[1]), jnp.float32),
-            pltpu.SMEM(facts, jnp.int32),
-            pltpu.SMEM(state, jnp.int32),
-            pltpu.SMEM(state, jnp.int32),
-            pltpu.SMEM((pairs * len(left),), jnp.int32),
             pltpu.SemaphoreType.DMA((chunks,)),
             pltpu.SemaphoreType.DMA,
-            pltpu.SemaphoreType.DMA((2,)),
             pltpu.SemaphoreType.DMA((zeros.shape[0] // 2 // step,)),
             pltpu.SemaphoreType.DMA,
         ],
@@ -277,27 +261,38 @@
     )(*flat, *right, zeros)
 
 
-def tail_kernel(n_row, slots, per_col, slot_ref, tile_ref, *refs):
+def tail_kernel(n_row, n_chip, slots, per_col, plan, *refs):
     lefts, right_ref = refs[:CORES], refs[CORES]
     out_ref, held, acc, load_sem, store_sem = refs[CORES + 2 :]
     rows, width = lefts[0].shape[-1], acc.shape[-1]
+    stations = CORES * n_row * n_chip
     pairs = [(i, j) for i in range(slots) for j in range(slots)]
-    used = tile_ref[len(pairs) * CORES * n_row]
-
-    def load(spot):
-        tile = block_of(out_ref, tile_ref[spot], per_col, width)
-        return pltpu.make_async_copy(tile, held.at[spot], load_sem)
-
-    def store(spot):
-        tile = block_of(out_ref, tile_ref[spot], per_col, width)
-        return pltpu.make_async_copy(acc.at[spot], tile, store_sem)
-
-    def each(act):
-        def step(spot, carry):
-            act(spot)
-            return carry
-
-        lax.fori_loop(0, used, step, 0)
+
+    def at(index, n):
+        return n * stations + index * n_chip + n_chip // 2
+
+    def block(column):
+        return block_of(out_ref, plan[1, column], per_col, width)
+
+    def each_tile(act):
+        def step(index, number):
+            for n in range(len(pairs)):
+                code = plan[0, at(index, n)]
+
+                @pl.when(code & 2 != 0)
+                def _():
+                    act(lax.shift_right_logical(code, 2), at(index, n))
+
+                number = number + (lax.shift_right_logical(code, 1) & 1)
+            return number
+
+        return lax.fori_loop(0, CORES * n_row, step, 0)
+
+    def load(spot, column):
+        return pltpu.make_async_copy(block(column), held.at[spot], load_sem)
+
+    def store(spot, column):
+        return pltpu.make_async_copy(acc.at[spot], block(column), store_sem)
 
     def gram_of(index):
         first = index % n_row * slots * width
@@ -307,47 +302,56 @@
         )
         return jnp.dot(left, right, preferred_element_type=jnp.float32)
 
-    each(lambda spot: load(spot).start())
+    number = each_tile(lambda spot, column: load(spot, column).start())
     for index in range(CORES * n_row):
         gram = gram_of(index)
         for n, (i, j) in enumerate(pairs):
-            code = slot_ref[index * len(pairs) + n]
-            spot, fresh = lax.shift_right_logical(code, 1), code & 1
+            code = plan[0, at(index, n)]
+            spot, fresh = lax.shift_right_logical(code, 2), code & 1
             part = gram[i * width : (i + 1) * width, j * width : (j + 1) * width]
             acc[spot] = jnp.where(fresh == 1, part, acc[spot] + part)
-    each(lambda spot: load(spot).wait())
-
-    def add_store(spot):
+
+    def wait_load(index, carry):
+        pltpu.make_async_copy(held.at[0], held.at[0], load_sem).wait()
+        return carry
+
+    def wait_store(index, carry):
+        pltpu.make_async_copy(held.at[0], held.at[0], store_sem).wait()
+        return carry
+
+    lax.fori_loop(0, number, wait_load, 0)
+
+    def add_store(spot, column):
         acc[spot] = acc[spot] + held[spot]
-        store(spot).start()
-
-    each(add_store)
-    each(lambda spot: store(spot).wait())
-
-
-def tail_part(left, right, slot, tile, out, per_col):
+        store(spot, column).start()
+
+    each_tile(add_store)
+    lax.fori_loop(0, number, wait_store, 0)
+
+
+def tail_part(left, right, plan, out, per_col):
     rows = left[0].shape[1]
     n_row = right.shape[0] // CORES
     slots, width = right.shape[1] // rows, right.shape[2]
-    spots = (slot.shape[0] + 1, width, width)
+    pairs = slots * slots * CORES * n_row
     anywhere = pl.BlockSpec(memory_space=pl.ANY)
     vmem = pl.BlockSpec(memory_space=pltpu.VMEM)
     smem = pl.BlockSpec(memory_space=pltpu.SMEM)
     return pl.pallas_call(
-        functools.partial(tail_kernel, n_row, slots, per_col),
+        functools.partial(tail_kernel, n_row, plan.shape[1] // pairs, slots, per_col),
         out_shape=jax.ShapeDtypeStruct(out.shape, out.dtype),
-        in_specs=[smem, smem] + [vmem] * (len(left) + 1) + [anywhere],
+        in_specs=[smem] + [vmem] * (len(left) + 1) + [anywhere],
         out_specs=anywhere,
         scratch_shapes=[
-            pltpu.VMEM(spots, jnp.float32),
-            pltpu.VMEM(spots, jnp.float32),
+            pltpu.VMEM((pairs, width, width), jnp.float32),
+            pltpu.VMEM((pairs, width, width), jnp.float32),
             pltpu.SemaphoreType.DMA,
             pltpu.SemaphoreType.DMA,
         ],
-        input_output_aliases={len(left) + 3: 0},
+        input_output_aliases={len(left) + 2: 0},
         compiler_params=pltpu.CompilerParams(vmem_limit_bytes=24 * MIB),
         cost_estimate=pl.CostEstimate(flops=0, bytes_accessed=0, transcendentals=0),
-    )(slot, tile, *left, right, out)
+    )(plan, *left, right, out)
 
 
 def zero_kernel(after_ref, out_ref, block, sem):
@@ -400,6 +404,9 @@
     def flip_core(value):
         return lax.ppermute(value, "col", [(i, i ^ 1) for i in range(n_col)])
 
+    def pad(value, extra):
+        return jnp.pad(value, ((0, extra), (0, 0)))
+
     after = lax.optimization_barrier
 
     ids = jnp.transpose(tile_ids, (0, 2, 1))[0]
@@ -414,22 +421,28 @@
     near = {0: chip}
     for s in range(1, middle):
         near[s] = shift_chip(near[s - 1], 1)
-        near[n_chip - s] = shift_chip(near[(n_chip - s + 1) % n_chip], -1)
+        near[n_chip - s] = shift_chip(pad(chip, 48) if s == 1 else near[n_chip - s + 1], -1)
     right = jnp.stack(from_chip)
-    sides = [right] + [flip_row(right, j) for j in range(1, n_row)]
-    far = shift_chip(jnp.pad(near[middle - 1], ((0, EXTRA), (0, 0))), 1)
-    near = after(near)
-    swapped = {s: flip_core(near[s]) for s in near}
-    swapped, waiting = after((swapped, sides))
-    other_sides = [flip_core(x) for x in waiting]
+    own = [flip_core(chip), flip_core(right)]
+    *own, again = after((*own, right))
+    sides = [right] + [flip_row(right if j == 1 else again, j) for j in range(1, n_row)]
+    far = shift_chip(pad(near[middle - 1], 64), 1)
+    early = [s for s in near if 0 < s < middle]
+    swapped = {s: flip_core(near[s]) for s in early}
+    swapped, late, waiting = after(
+        (swapped, {s: near[s] for s in near if s > middle}, sides[1:])
+    )
+    swapped |= {s: flip_core(late[s]) for s in late}
+    swapped[0] = own[0]
+    other_sides = [own[1]] + [flip_core(x) for x in waiting]
     left = [[near[s], swapped[s]] for s in sorted(near)]
     pieces = [(j, 0, n_chip) for j in range(n_row * CORES)]
 
-    out, tail_right, slot, tile = main_part(
+    out, tail_right, plan = main_part(
         left, sides + other_sides, pieces, zeros, n_row, per_row, per_col
     )
-    far, slot = after((far, slot))
-    return tail_part([far, flip_core(far)], tail_right, slot, tile, out, per_col)
+    far, plan = after((far, plan))
+    return tail_part([far, flip_core(far)], tail_right, plan, out, per_col)
 
 
 def solution(mesh):

time: 67.2 us -> 67.7 us (level)
  waiting for transfers between devices: 26.2 us -> 27.1 us
  starting transfers between devices: 21.3 us -> 20.6 us
    ppermute x6, waiting for transfers between devices: 1.61 us -> 4.62 us  [flip_row(): return lax.ppermute(value, 'row', [(i, i ^ j) for i in range(n_row)])]
    ppermute x6, waiting for transfers between devices: 19.4 us -> 17.4 us  [shift_chip(): return lax.ppermute(value, 'col', pairs)]
  transfers between devices with their start and end apart: 20 -> 20, of which waited for: 9 -> 9; matrix products, arithmetic and copies ran while one was open for 0% -> 0% of each run, Pallas kernels for 22% -> 21%
where the time goes in v5:
time: 67.7 us; the launch traced here: 67.6 us
  waiting for transfers between devices  27.1 us (40%)
  starting transfers between devices  20.6 us (30%)
  Pallas kernels  19.4 us (29%)
    ppermute x6, waiting for transfers between devices, shift_chip(): return lax.ppermute(value, 'col', pairs)  17.4 us
    ppermute x6, starting transfers between devices, shift_chip(): return lax.ppermute(value, 'col', pairs)  10.4 us
    ppermute x6, starting transfers between devices, flip_row(): return lax.ppermute(value, 'row', [(i, i ^ j) for i in range(n_row)])  8.49 us
    pallas_call x1, Pallas kernels, main_part(): pl.pallas_call(functools.partial(main_kernel, n_row, n_chip, slots, per_r...  8.45 us
    pallas_call x1, Pallas kernels, zero_upper(): pl.pallas_call(zero_kernel, out_shape=jax.ShapeDtypeStruct((height, width...  6.03 us
    ppermute x8, waiting for transfers between devices, flip_core(): return lax.ppermute(value, 'col', [(i, i ^ 1) for i in range(n_col)])  5.16 us
    ppermute x6, waiting for transfers between devices, flip_row(): return lax.ppermute(value, 'row', [(i, i ^ j) for i in range(n_row)])  4.62 us
    pallas_call x1, Pallas kernels, tail_part(): pl.pallas_call(functools.partial(tail_kernel, n_row, plan.shape[1] // pai...  2.81 us
  transfers between devices with their start and end apart: 20, of which 9 were waited for; matrix products, arithmetic and copies ran while one was open for 0% of the time, Pallas kernels for 21%

profile of v5, /device:TPU:0, one launch (start us, length us, event | category | flops | bytes accessed | tf_op | source)
XLA Modules:
  0.0 67.6 jit_solution(16556010593875258447)
XLA Ops:
  0.0 2.2 %shard_map.46 = (bf16[256,256]{1,0:T(8,128)(2,1)}, bf16[256,256]{1,0:T(8,128)(2,1)}, bf16[256,256]{1,0:T(8,128)(2,1)}, bf16[256,256]{1,0:T(8,128)(2,1)}, bf16[52...) custom-call(bf16[4,2,256,128]{3,2,1,0:T(8,128)(2,1)} %bitcast.18, ...), custom_call_target="tpu_custom_call" | custom-call | tf_op jit(solution)/shard_map/pallas_call | solution.py:50
  2.2 3.0 %collective-permute-start = (bf16[256,256]{1,0:T(8,128)(2,1)}, bf16[256,256]{1,0:T(8,128)(2,1)S(1)}, u32[]{:S(2)}, u32[]{:S(2)}) collective-permute-start(bf16[256,256]{1,0:T(8,128)(2,1)} %get-tuple-element.36), channel_id=1, source_target_pairs={{0,8},{8,0},{16,24},{24,16},{1,9},{9,1},{17,25},{25,17},{2,10},{10... | collective-permute-start | bytes 393224 | tf_op jit(solution)/shard_map/ppermute | solution.py:398
  5.2 1.6 %collective-permute-start.3 = (bf16[528,128]{1,0:T(8,128)(2,1)}, bf16[528,128]{1,0:T(8,128)(2,1)S(1)}, u32[]{:S(2)}, u32[]{:S(2)}) collective-permute-start(bf16[528,128]{1,0:T(8,128)(2,1)} %get-tuple-element.40), channel_id=1, source_target_pairs={{0,2},{1,3},{2,4},{3,5},{4,6},{5,7},{6,0},{7,1},{8,10},{9,11},{10,... | collective-permute-start | bytes 405512 | tf_op jit(solution)/shard_map/ppermute | solution.py:402
  6.7 2.6 %collective-permute-start.4 = (bf16[528,128]{1,0:T(8,128)(2,1)}, bf16[528,128]{1,0:T(8,128)(2,1)S(1)}, u32[]{:S(2)}, u32[]{:S(2)}) collective-permute-start(bf16[528,128]{1,0:T(8,128)(2,1)} %get-tuple-element.41), channel_id=1, source_target_pairs={{0,4},{1,5},{2,6},{3,7},{4,0},{5,1},{6,2},{7,3},{8,12},{9,13},{10,... | collective-permute-start | bytes 405512 | tf_op jit(solution)/shard_map/ppermute | solution.py:402
  9.3 1.3 %collective-permute-start.5 = (bf16[528,128]{1,0:T(8,128)(2,1)}, bf16[528,128]{1,0:T(8,128)(2,1)S(1)}, u32[]{:S(2)}, u32[]{:S(2)}) collective-permute-start(bf16[528,128]{1,0:T(8,128)(2,1)} %get-tuple-element.42), channel_id=1, source_target_pairs={{0,6},{1,7},{2,0},{3,1},{4,2},{5,3},{6,4},{7,5},{8,14},{9,15},{10,... | collective-permute-start | bytes 405512 | tf_op jit(solution)/shard_map/ppermute | solution.py:402
  10.7 1.5 %collective-permute-start.1 = (bf16[256,256]{1,0:T(8,128)(2,1)}, bf16[256,256]{1,0:T(8,128)(2,1)S(1)}, u32[]{:S(2)}, u32[]{:S(2)}) collective-permute-start(bf16[256,256]{1,0:T(8,128)(2,1)} %get-tuple-element.37), channel_id=1, source_target_pairs={{0,16},{8,24},{16,0},{24,8},{1,17},{9,25},{17,1},{25,9},{2,18},{10... | collective-permute-start | bytes 393224 | tf_op jit(solution)/shard_map/ppermute | solution.py:398
  12.7 6.0 %shard_map.47.refs_14_ = f32[4096,2048]{1,0:T(8,128)} custom-call(bf16[528,128]{1,0:T(8,128)(2,1)} %get-tuple-element.47.after_ref), custom_call_target="tpu_custom_call" | custom-call | bytes 16777216 | tf_op jit(solution)/shard_map/pallas_call | solution.py:373
  19.0 0.5 collective-permute-start.8
  19.6 2.8 %collective-permute-start.6 = (bf16[1024,256]{1,0:T(8,128)(2,1)S(1)}, bf16[1024,256]{1,0:T(8,128)(2,1)S(1)}, u32[]{:S(2)}, u32[]{:S(2)}) collective-permute-start(bf16[1024,256]{1,0:T(8,128)(2,1)S(1)} %bitcast.14), channel_id=1, source_target_pairs={{0,2},{1,3},{2,4},{3,5},{4,6},{5,7},{6,0},{7,1},{8,10},{9,11},{10,... | collective-permute-start | bytes 1572872 | tf_op jit(solution)/shard_map/ppermute | solution.py:402
  22.4 1.1 %collective-permute-start.11 = (bf16[1072,256]{1,0:T(8,128)(2,1)S(1)}, bf16[1072,256]{1,0:T(8,128)(2,1)S(1)}, u32[]{:S(2)}, u32[]{:S(2)}) collective-permute-start(bf16[1072,256]{1,0:T(8,128)(2,1)S(1)} %pad.9), channel_id=1, source_target_pairs={{0,6},{1,7},{2,0},{3,1},{4,2},{5,3},{6,4},{7,5},{8,14},{9,15},{10,... | collective-permute-start | bytes 1646600 | tf_op jit(solution)/shard_map/ppermute | solution.py:402
  23.5 1.5 %collective-permute-start.12 = (bf16[4,528,128]{2,1,0:T(8,128)(2,1)S(1)}, bf16[4,528,128]{2,1,0:T(8,128)(2,1)S(1)}, u32[]{:S(2)}, u32[]{:S(2)}) collective-permute-start(bf16[4,528,128]{2,1,0:T(8,128)(2,1)S(1)} %pad_maximum_fusion.refs_6_), channel_id=1, source_target_pairs={{0,8},{8,0},{16,24},{24,16},{1,9},{9,1},{17,25},{25,17},{2,10},{10... | collective-permute-start | bytes 1622024 | tf_op jit(solution)/shard_map/ppermute | solution.py:398
  25.0 1.5 %collective-permute-start.13 = (bf16[4,528,128]{2,1,0:T(8,128)(2,1)S(1)}, bf16[4,528,128]{2,1,0:T(8,128)(2,1)S(1)}, u32[]{:S(2)}, u32[]{:S(2)}) collective-permute-start(bf16[4,528,128]{2,1,0:T(8,128)(2,1)S(1)} %pad_maximum_fusion.refs_6_), channel_id=1, source_target_pairs={{0,16},{8,24},{16,0},{24,8},{1,17},{9,25},{17,1},{25,9},{2,18},{10... | collective-permute-start | bytes 1622024 | tf_op jit(solution)/shard_map/ppermute | solution.py:398
  27.0 9.2 %collective-permute-done.6.refs_2_ = bf16[1024,256]{1,0:T(8,128)(2,1)S(1)} collective-permute-done((bf16[1024,256]{1,0:T(8,128)(2,1)S(1)}, bf16[1024,256]{1,0:T(8,128)(2,1)S(1)}, u32[]{:S(2)}, u32[]{:S(2)}) %collective-permute-start.6) | collective-permute-done | bytes 524320 | tf_op jit(solution)/shard_map/ppermute | solution.py:402
  36.2 2.5 %collective-permute-done.12.refs_7_ = bf16[4,528,128]{2,1,0:T(8,128)(2,1)S(1)} collective-permute-done((bf16[4,528,128]{2,1,0:T(8,128)(2,1)S(1)}, bf16[4,528,128]{2,1,0:T(8,128)(2,1)S(1)}, u32[]{:S(2)}, u32[]{:S(2)}) %collective-permute-start.12) | collective-permute-done | bytes 540704 | tf_op jit(solution)/shard_map/ppermute | solution.py:398
  38.7 1.0 %collective-permute-start.7 = (bf16[1088,256]{1,0:T(8,128)(2,1)S(1)}, bf16[1088,256]{1,0:T(8,128)(2,1)S(1)}, u32[]{:S(2)}, u32[]{:S(2)}) collective-permute-start(bf16[1088,256]{1,0:T(8,128)(2,1)S(1)} %pad.8), channel_id=1, source_target_pairs={{0,2},{1,3},{2,4},{3,5},{4,6},{5,7},{6,0},{7,1},{8,10},{9,11},{10,... | collective-permute-start | bytes 1671176 | tf_op jit(solution)/shard_map/ppermute | solution.py:402
  39.7 8.2 %collective-permute-done.11.refs_4_ = bf16[1072,256]{1,0:T(8,128)(2,1)S(1)} collective-permute-done((bf16[1072,256]{1,0:T(8,128)(2,1)S(1)}, bf16[1072,256]{1,0:T(8,128)(2,1)S(1)}, u32[]{:S(2)}, u32[]{:S(2)}) %collective-permute-start.11) | collective-permute-done | bytes 548896 | tf_op jit(solution)/shard_map/ppermute | solution.py:402
  47.9 1.2 %collective-permute-done.13.refs_8_ = bf16[4,528,128]{2,1,0:T(8,128)(2,1)S(1)} collective-permute-done((bf16[4,528,128]{2,1,0:T(8,128)(2,1)S(1)}, bf16[4,528,128]{2,1,0:T(8,128)(2,1)S(1)}, u32[]{:S(2)}, u32[]{:S(2)}) %collective-permute-start.13) | collective-permute-done | bytes 540704 | tf_op jit(solution)/shard_map/ppermute | solution.py:398
  49.0 1.0 %collective-permute-done.14.refs_9_ = bf16[4,528,128]{2,1,0:T(8,128)(2,1)S(1)} collective-permute-done((bf16[4,528,128]{2,1,0:T(8,128)(2,1)S(1)}, bf16[4,528,128]{2,1,0:T(8,128)(2,1)S(1)}, u32[]{:S(2)}, u32[]{:S(2)}) %collective-permute-start.14) | collective-permute-done | bytes 540704 | tf_op jit(solution)/shard_map/ppermute | solution.py:398
  51.0 1.7 %collective-permute-done.16.refs_11_ = bf16[4,528,128]{2,1,0:T(8,128)(2,1)S(1)} collective-permute-done((bf16[4,528,128]{2,1,0:T(8,128)(2,1)S(1)}, bf16[4,528,128]{2,1,0:T(8,128)(2,1)S(1)}, u32[]{:S(2)}, u32[]{:S(2)}) %collective-permute-start.16) | collective-permute-done | bytes 540704 | tf_op jit(solution)/shard_map/ppermute | solution.py:405
  52.7 0.8 %collective-permute-done.17.refs_12_ = bf16[4,528,128]{2,1,0:T(8,128)(2,1)S(1)} collective-permute-done((bf16[4,528,128]{2,1,0:T(8,128)(2,1)S(1)}, bf16[4,528,128]{2,1,0:T(8,128)(2,1)S(1)}, u32[]{:S(2)}, u32[]{:S(2)}) %collective-permute-start.17) | collective-permute-done | bytes 540704 | tf_op jit(solution)/shard_map/ppermute | solution.py:405
  53.5 0.8 %collective-permute-done.18.refs_13_ = bf16[4,528,128]{2,1,0:T(8,128)(2,1)S(1)} collective-permute-done((bf16[4,528,128]{2,1,0:T(8,128)(2,1)S(1)}, bf16[4,528,128]{2,1,0:T(8,128)(2,1)S(1)}, u32[]{:S(2)}, u32[]{:S(2)}) %collective-permute-start.18) | collective-permute-done | bytes 540704 | tf_op jit(solution)/shard_map/ppermute | solution.py:405
  54.3 8.4 %shard_map.48 = (f32[4096,2048]{1,0:T(8,128)}, bf16[8,512,128]{2,1,0:T(8,128)(2,1)S(1)}, s32[8,128]{1,0:T(8,128)S(1)}) custom-call(bf16[1024,256]{1,0:T(8,128)(2,1)S(1)} %bitcast.16, bf16[1024,256]{1,0:T(8,128)(2,1)S(1)} %collective-permute-done.8.refs_1_, bf16[1024,256]{1,0:T(8,128)(2,1)S(1)} %collective-permute-done.6.refs_2_, ...), custom_call_target="tpu_custom_call", output_to_operand_aliasing={{0}: (14, {})} | custom-call | tf_op jit(solution)/shard_map/pallas_call | solution.py:237
  62.9 1.9 %collective-permute-done.19.refs_1_ = bf16[1088,256]{1,0:T(8,128)(2,1)S(1)} collective-permute-done((bf16[1088,256]{1,0:T(8,128)(2,1)S(1)}, bf16[1088,256]{1,0:T(8,128)(2,1)S(1)}, u32[]{:S(2)}, u32[]{:S(2)}) %collective-permute-start.19) | collective-permute-done | bytes 557088 | tf_op jit(solution)/shard_map/ppermute | solution.py:405
  64.8 2.8 %shard_map.49 = f32[4096,2048]{1,0:T(8,128)} custom-call(s32[8,128]{1,0:T(8,128)S(1)} %get-tuple-element.61.plan, bf16[1088,256]{1,0:T(8,128)(2,1)S(1)} %collective-permute-done.7.refs_0_, bf16[1088,256]{1,0:T(8,128)(2,1)S(1)} %collective-permute-done.19.refs_1_, bf16[8,512,128]{2,1,0:T(8,128)(2,1)S(1)} %get-tuple-element.63.refs_2_, ...), custom_call_target="tpu_custom_call", output_to_operand_aliasing={{}: (4, {})} | custom-call | tf_op jit(solution)/shard_map/pallas_call | solution.py:340
  (28 shorter events, 2.4 us)
Async XLA Ops:
  2.2 16.6 %copy-start = (bf16[528,128]{1,0:T(8,128)(2,1)S(1)}, bf16[528,128]{1,0:T(8,128)(2,1)}, u32[]{:S(2)}) copy-start(bf16[528,128]{1,0:T(8,128)(2,1)} %get-tuple-element.47.after_ref) | copy-start | bytes 405508
  2.2 16.8 %copy-start.1 = (bf16[256,256]{1,0:T(8,128)(2,1)S(1)}, bf16[256,256]{1,0:T(8,128)(2,1)}, u32[]{:S(2)}) copy-start(bf16[256,256]{1,0:T(8,128)(2,1)} %get-tuple-element.43) | copy-start | bytes 393220
  2.2 10.0 %collective-permute-start = (bf16[256,256]{1,0:T(8,128)(2,1)}, bf16[256,256]{1,0:T(8,128)(2,1)S(1)}, u32[]{:S(2)}, u32[]{:S(2)}) collective-permute-start(bf16[256,256]{1,0:T(8,128)(2,1)} %get-tuple-element.36), channel_id=1, source_target_pairs={{0,8},{8,0},{16,24},{24,16},{1,9},{9,1},{17,25},{25,17},{2,10},{10... | collective-permute-start | bytes 393224 | tf_op jit(solution)/shard_map/ppermute | solution.py:398
  5.2 13.6 %collective-permute-start.3 = (bf16[528,128]{1,0:T(8,128)(2,1)}, bf16[528,128]{1,0:T(8,128)(2,1)S(1)}, u32[]{:S(2)}, u32[]{:S(2)}) collective-permute-start(bf16[528,128]{1,0:T(8,128)(2,1)} %get-tuple-element.40), channel_id=1, source_target_pairs={{0,2},{1,3},{2,4},{3,5},{4,6},{5,7},{6,0},{7,1},{8,10},{9,11},{10,... | collective-permute-start | bytes 405512 | tf_op jit(solution)/shard_map/ppermute | solution.py:402
  6.7 12.0 %collective-permute-start.4 = (bf16[528,128]{1,0:T(8,128)(2,1)}, bf16[528,128]{1,0:T(8,128)(2,1)S(1)}, u32[]{:S(2)}, u32[]{:S(2)}) collective-permute-start(bf16[528,128]{1,0:T(8,128)(2,1)} %get-tuple-element.41), channel_id=1, source_target_pairs={{0,4},{1,5},{2,6},{3,7},{4,0},{5,1},{6,2},{7,3},{8,12},{9,13},{10,... | collective-permute-start | bytes 405512 | tf_op jit(solution)/shard_map/ppermute | solution.py:402
  9.3 9.4 %collective-permute-start.5 = (bf16[528,128]{1,0:T(8,128)(2,1)}, bf16[528,128]{1,0:T(8,128)(2,1)S(1)}, u32[]{:S(2)}, u32[]{:S(2)}) collective-permute-start(bf16[528,128]{1,0:T(8,128)(2,1)} %get-tuple-element.42), channel_id=1, source_target_pairs={{0,6},{1,7},{2,0},{3,1},{4,2},{5,3},{6,4},{7,5},{8,14},{9,15},{10,... | collective-permute-start | bytes 405512 | tf_op jit(solution)/shard_map/ppermute | solution.py:402
  10.7 8.0 %collective-permute-start.1 = (bf16[256,256]{1,0:T(8,128)(2,1)}, bf16[256,256]{1,0:T(8,128)(2,1)S(1)}, u32[]{:S(2)}, u32[]{:S(2)}) collective-permute-start(bf16[256,256]{1,0:T(8,128)(2,1)} %get-tuple-element.37), channel_id=1, source_target_pairs={{0,16},{8,24},{16,0},{24,8},{1,17},{9,25},{17,1},{25,9},{2,18},{10... | collective-permute-start | bytes 393224 | tf_op jit(solution)/shard_map/ppermute | solution.py:398
  12.2 6.5 %collective-permute-start.2 = (bf16[256,256]{1,0:T(8,128)(2,1)}, bf16[256,256]{1,0:T(8,128)(2,1)S(1)}, u32[]{:S(2)}, u32[]{:S(2)}) collective-permute-start(bf16[256,256]{1,0:T(8,128)(2,1)} %get-tuple-element.38), channel_id=1, source_target_pairs={{0,24},{8,16},{16,8},{24,0},{1,25},{9,17},{17,9},{25,1},{2,26},{10... | collective-permute-start | bytes 393224 | tf_op jit(solution)/shard_map/ppermute | solution.py:398
  18.9 6.1 %collective-permute-start.9 = (bf16[4,528,128]{2,1,0:T(8,128)(2,1)S(1)}, bf16[4,528,128]{2,1,0:T(8,128)(2,1)S(1)}, u32[]{:S(2)}, u32[]{:S(2)}) collective-permute-start(bf16[4,528,128]{2,1,0:T(8,128)(2,1)S(1)} %pad_maximum_fusion.refs_6_), channel_id=1, source_target_pairs={{0,1},{1,0},{2,3},{3,2},{4,5},{5,4},{6,7},{7,6},{8,9},{9,8},{10,11... | collective-permute-start | bytes 1622024 | tf_op jit(solution)/shard_map/ppermute | solution.py:405
  19.0 6.0 %collective-permute-start.8 = (bf16[1024,256]{1,0:T(8,128)(2,1)S(1)}, bf16[1024,256]{1,0:T(8,128)(2,1)S(1)}, u32[]{:S(2)}, u32[]{:S(2)}) collective-permute-start(bf16[1024,256]{1,0:T(8,128)(2,1)S(1)} %bitcast.13), channel_id=1, source_target_pairs={{0,1},{1,0},{2,3},{3,2},{4,5},{5,4},{6,7},{7,6},{8,9},{9,8},{10,11... | collective-permute-start | bytes 1572872 | tf_op jit(solution)/shard_map/ppermute | solution.py:405
  19.6 16.6 %collective-permute-start.6 = (bf16[1024,256]{1,0:T(8,128)(2,1)S(1)}, bf16[1024,256]{1,0:T(8,128)(2,1)S(1)}, u32[]{:S(2)}, u32[]{:S(2)}) collective-permute-start(bf16[1024,256]{1,0:T(8,128)(2,1)S(1)} %bitcast.14), channel_id=1, source_target_pairs={{0,2},{1,3},{2,4},{3,5},{4,6},{5,7},{6,0},{7,1},{8,10},{9,11},{10,... | collective-permute-start | bytes 1572872 | tf_op jit(solution)/shard_map/ppermute | solution.py:402
  22.4 25.5 %collective-permute-start.11 = (bf16[1072,256]{1,0:T(8,128)(2,1)S(1)}, bf16[1072,256]{1,0:T(8,128)(2,1)S(1)}, u32[]{:S(2)}, u32[]{:S(2)}) collective-permute-start(bf16[1072,256]{1,0:T(8,128)(2,1)S(1)} %pad.9), channel_id=1, source_target_pairs={{0,6},{1,7},{2,0},{3,1},{4,2},{5,3},{6,4},{7,5},{8,14},{9,15},{10,... | collective-permute-start | bytes 1646600 | tf_op jit(solution)/shard_map/ppermute | solution.py:402
  23.5 15.2 %collective-permute-start.12 = (bf16[4,528,128]{2,1,0:T(8,128)(2,1)S(1)}, bf16[4,528,128]{2,1,0:T(8,128)(2,1)S(1)}, u32[]{:S(2)}, u32[]{:S(2)}) collective-permute-start(bf16[4,528,128]{2,1,0:T(8,128)(2,1)S(1)} %pad_maximum_fusion.refs_6_), channel_id=1, source_target_pairs={{0,8},{8,0},{16,24},{24,16},{1,9},{9,1},{17,25},{25,17},{2,10},{10... | collective-permute-start | bytes 1622024 | tf_op jit(solution)/shard_map/ppermute | solution.py:398
  25.0 24.0 %collective-permute-start.13 = (bf16[4,528,128]{2,1,0:T(8,128)(2,1)S(1)}, bf16[4,528,128]{2,1,0:T(8,128)(2,1)S(1)}, u32[]{:S(2)}, u32[]{:S(2)}) collective-permute-start(bf16[4,528,128]{2,1,0:T(8,128)(2,1)S(1)} %pad_maximum_fusion.refs_6_), channel_id=1, source_target_pairs={{0,16},{8,24},{16,0},{24,8},{1,17},{9,25},{17,1},{25,9},{2,18},{10... | collective-permute-start | bytes 1622024 | tf_op jit(solution)/shard_map/ppermute | solution.py:398
  26.5 23.5 %collective-permute-start.14 = (bf16[4,528,128]{2,1,0:T(8,128)(2,1)S(1)}, bf16[4,528,128]{2,1,0:T(8,128)(2,1)S(1)}, u32[]{:S(2)}, u32[]{:S(2)}) collective-permute-start(bf16[4,528,128]{2,1,0:T(8,128)(2,1)S(1)} %pad_maximum_fusion.refs_6_), channel_id=1, source_target_pairs={{0,24},{8,16},{16,8},{24,0},{1,25},{9,17},{17,9},{25,1},{2,26},{10... | collective-permute-start | bytes 1622024 | tf_op jit(solution)/shard_map/ppermute | solution.py:398
  36.2 11.7 %collective-permute-start.10 = (bf16[1024,256]{1,0:T(8,128)(2,1)S(1)}, bf16[1024,256]{1,0:T(8,128)(2,1)S(1)}, u32[]{:S(2)}, u32[]{:S(2)}) collective-permute-start(bf16[1024,256]{1,0:T(8,128)(2,1)S(1)} %collective-permute-done.6.refs_2_), channel_id=1, source_target_pairs={{0,1},{1,0},{2,3},{3,2},{4,5},{5,4},{6,7},{7,6},{8,9},{9,8},{10,11... | collective-permute-start | bytes 1572872 | tf_op jit(solution)/shard_map/ppermute | solution.py:405
  38.7 24.1 %collective-permute-start.7 = (bf16[1088,256]{1,0:T(8,128)(2,1)S(1)}, bf16[1088,256]{1,0:T(8,128)(2,1)S(1)}, u32[]{:S(2)}, u32[]{:S(2)}) collective-permute-start(bf16[1088,256]{1,0:T(8,128)(2,1)S(1)} %pad.8), channel_id=1, source_target_pairs={{0,2},{1,3},{2,4},{3,5},{4,6},{5,7},{6,0},{7,1},{8,10},{9,11},{10,... | collective-permute-start | bytes 1671176 | tf_op jit(solution)/shard_map/ppermute | solution.py:402
  50.0 4.3 %collective-permute-start.15 = (bf16[1072,256]{1,0:T(8,128)(2,1)S(1)}, bf16[1072,256]{1,0:T(8,128)(2,1)S(1)}, u32[]{:S(2)}, u32[]{:S(2)}) collective-permute-start(bf16[1072,256]{1,0:T(8,128)(2,1)S(1)} %collective-permute-done.11.refs_4_), channel_id=1, source_target_pairs={{0,1},{1,0},{2,3},{3,2},{4,5},{5,4},{6,7},{7,6},{8,9},{9,8},{10,11... | collective-permute-start | bytes 1646600 | tf_op jit(solution)/shard_map/ppermute | solution.py:405
  50.0 2.7 %collective-permute-start.16 = (bf16[4,528,128]{2,1,0:T(8,128)(2,1)S(1)}, bf16[4,528,128]{2,1,0:T(8,128)(2,1)S(1)}, u32[]{:S(2)}, u32[]{:S(2)}) collective-permute-start(bf16[4,528,128]{2,1,0:T(8,128)(2,1)S(1)} %collective-permute-done.12.refs_7_), channel_id=1, source_target_pairs={{0,1},{1,0},{2,3},{3,2},{4,5},{5,4},{6,7},{7,6},{8,9},{9,8},{10,11... | collective-permute-start | bytes 1622024 | tf_op jit(solution)/shard_map/ppermute | solution.py:405
  50.5 3.0 %collective-permute-start.17 = (bf16[4,528,128]{2,1,0:T(8,128)(2,1)S(1)}, bf16[4,528,128]{2,1,0:T(8,128)(2,1)S(1)}, u32[]{:S(2)}, u32[]{:S(2)}) collective-permute-start(bf16[4,528,128]{2,1,0:T(8,128)(2,1)S(1)} %collective-permute-done.13.refs_8_), channel_id=1, source_target_pairs={{0,1},{1,0},{2,3},{3,2},{4,5},{5,4},{6,7},{7,6},{8,9},{9,8},{10,11... | collective-permute-start | bytes 1622024 | tf_op jit(solution)/shard_map/ppermute | solution.py:405
  50.5 3.8 %collective-permute-start.18 = (bf16[4,528,128]{2,1,0:T(8,128)(2,1)S(1)}, bf16[4,528,128]{2,1,0:T(8,128)(2,1)S(1)}, u32[]{:S(2)}, u32[]{:S(2)}) collective-permute-start(bf16[4,528,128]{2,1,0:T(8,128)(2,1)S(1)} %collective-permute-done.14.refs_9_), channel_id=1, source_target_pairs={{0,1},{1,0},{2,3},{3,2},{4,5},{5,4},{6,7},{7,6},{8,9},{9,8},{10,11... | collective-permute-start | bytes 1622024 | tf_op jit(solution)/shard_map/ppermute | solution.py:405
  62.8 2.0 %collective-permute-start.19 = (bf16[1088,256]{1,0:T(8,128)(2,1)S(1)}, bf16[1088,256]{1,0:T(8,128)(2,1)S(1)}, u32[]{:S(2)}, u32[]{:S(2)}) collective-permute-start(bf16[1088,256]{1,0:T(8,128)(2,1)S(1)} %collective-permute-done.7.refs_0_), channel_id=1, source_target_pairs={{0,1},{1,0},{2,3},{3,2},{4,5},{5,4},{6,7},{7,6},{8,9},{9,8},{10,11... | collective-permute-start | bytes 1671176 | tf_op jit(solution)/shard_map/ppermute | solution.py:405

commit v6 on v5

v6 whole, which is shorter than its diff:
```python
import functools

import jax
import jax.numpy as jnp
from jax import lax
from jax.experimental import pallas as pl
from jax.experimental.pallas import tpu as pltpu
from jax.sharding import PartitionSpec as P

TILES = 128
CORES = 2
META = 16
ZERO_EARLY = 6
MIB = 1024 * 1024


def scale_of(class_ref):
    classes = class_ref[...]
    return jnp.where(
        classes == 0, 1.0, jnp.where(classes == 1, 0.5, jnp.where(classes == 2, 0.25, 0.125))
    ).astype(jnp.float32)


def pack_kernel(n_row, n_chip, slots, sens_ref, class_ref, ids_ref, counts_ref, *refs):
    outs, meta_ref = refs[:-1], refs[-1]
    r = lax.axis_index("row")
    z = lax.div(lax.axis_index("col"), CORES)
    rows, width = sens_ref.shape[2:]
    scale = scale_of(class_ref)
    for j in range(n_row):
        for i in range(slots):
            tile = sens_ref[r ^ j, i].T.astype(jnp.float32) * scale
            outs[j][i * width : (i + 1) * width] = tile.astype(jnp.bfloat16)
    scale = jnp.broadcast_to(scale, (width, rows)).T
    meta_ref[...] = jnp.zeros_like(meta_ref)
    meta_ref[:slots, :n_row] = ids_ref[...].astype(jnp.float32)
    meta_ref[slots : slots + 1, :n_row] = counts_ref[...].astype(jnp.float32)
    meta = meta_ref[...].astype(jnp.bfloat16)
    for s in range(n_chip):
        owner = lax.rem(z + s, n_chip)
        out = outs[n_row + s]
        for i in range(slots):
            tile = sens_ref[owner, i].astype(jnp.float32) * scale
            out[i * rows : (i + 1) * rows] = tile.astype(jnp.bfloat16)
        out[slots * rows :] = meta


def pack(sensitivity, weight_class, ids, counts, n_chip):
    n_row, slots, rows, width = sensitivity.shape
    vmem = pl.BlockSpec(memory_space=pltpu.VMEM)
    return pl.pallas_call(
        functools.partial(pack_kernel, n_row, n_chip, slots),
        out_shape=[jax.ShapeDtypeStruct((slots * width, rows), jnp.bfloat16)] * n_row
        + [jax.ShapeDtypeStruct((slots * rows + META, width), jnp.bfloat16)] * n_chip,
        in_specs=[vmem] * 4,
        out_specs=[vmem] * (n_row + n_chip),
        scratch_shapes=[pltpu.VMEM((META, width), jnp.float32)],
        cost_estimate=pl.CostEstimate(flops=0, bytes_accessed=0, transcendentals=0),
    )(sensitivity, weight_class, ids, counts)


def plan_of(facts, r, z, core, n_row, n_chip, slots, per_col, none, by_tile):
    _, stations, width = facts.shape
    lane = lax.broadcasted_iota(jnp.int32, (stations, width), 1)

    def pick(row, owner):
        return jnp.sum(jnp.where(lane == owner, facts[row], 0.0), axis=1, keepdims=True)

    used_left, used_right = pick(slots, r), pick(slots, z)
    lefts = [pick(i, r) for i in range(slots)]
    rights = [pick(j, z) - (core * per_col).astype(jnp.float32) for j in range(slots)]
    column = []
    for i in range(slots):
        for j in range(slots):
            met = (i < used_left) & (j < used_right) & (rights[j] >= 0) & (rights[j] < per_col)
            column.append(jnp.where(met, lefts[i] * per_col + rights[j], float(none)))
    count = len(column) * stations
    tile = jnp.broadcast_to(jnp.concatenate(column, axis=0), (count, count))
    other = tile.T

    def part_of(axis):
        pair = lax.broadcasted_iota(jnp.int32, (count, count), axis)
        station = lax.rem(pair, stations)
        s = lax.rem(station, n_chip)
        number = station * len(column) + lax.div(pair, stations)
        return s == n_chip // 2, number.astype(jnp.float32)

    tail_down, number_down = part_of(0)
    tail_across, number_across = part_of(1)
    same = (tile == other) & (tail_down == tail_across)
    first = jnp.min(jnp.where(same, number_down, 1e6), axis=0, keepdims=True)
    fresh = (first == number_across[:1]).astype(jnp.float32)
    last = jnp.max(jnp.where(same, number_down, -1.0), axis=0, keepdims=True)
    final = (last == number_across[:1]).astype(jnp.float32)
    real = (other[:1] < none).astype(jnp.float32)
    place = other[:1] if by_tile else first
    code = 8.0 * place + 4.0 * final * real + 2.0 * fresh * real + fresh
    return code.astype(jnp.int32), other[:1].astype(jnp.int32)


def settle(plan, groups, stations, slots, acc, held, out_ref, per_col, load_sem, store_sem):
    width = acc.shape[-1]
    pairs = slots * slots

    def copy(place, column, back):
        block = block_of(out_ref, plan[1, column], per_col, width)
        if back:
            return pltpu.make_async_copy(acc.at[place], block, store_sem)
        return pltpu.make_async_copy(block, held.at[place], load_sem)

    def each(columns, flag, act):
        number = 0
        for column in columns:
            for n in range(pairs):
                code = plan[0, column + n * stations]
                hit = lax.shift_right_logical(code, flag) & 1

                @pl.when(hit == 1)
                def _():
                    act(lax.shift_right_logical(code, 3), column + n * stations)

                number = number + hit
        return number

    def wait(number, sem):
        def step(index, carry):
            pltpu.make_async_copy(acc.at[0], acc.at[0], sem).wait()
            return carry

        lax.fori_loop(0, number, step, 0)

    def add(column, left, right):
        gram = jnp.dot(left(), right(), preferred_element_type=jnp.float32)
        for n in range(pairs):
            code = plan[0, column + n * stations]
            place, fresh = lax.shift_right_logical(code, 3), code & 1
            i, j = divmod(n, slots)
            part = gram[i * width : (i + 1) * width, j * width : (j + 1) * width]
            acc[place] = jnp.where(fresh == 1, part, acc[place] + part)

    def walk(act):
        total = 0
        for steps, stations_of in groups:
            if steps == 1:
                total = total + act(stations_of(0))
            else:
                total = lax.fori_loop(
                    0, steps, lambda step, sofar: sofar + act(stations_of(step)), total
                )
        return total

    def columns_of(found):
        return [column for column, _, _ in found]

    def start_loads(found):
        return each(columns_of(found), 1, lambda place, at: copy(place, at, False).start())

    def add_all(found):
        for column, left, right in found:
            add(column, left, right)
        return 0

    def add_store(found):
        add_all(found)
        return each(columns_of(found), 2, lambda place, at: copy(place, at, True).start())

    def finish(place, column):
        acc[place] = acc[place] + held[place]
        copy(place, column, True).start()

    if held is None:
        number = walk(add_store)
    else:
        number = walk(start_loads)
        walk(add_all)
        wait(number, load_sem)
        walk(lambda found: each(columns_of(found), 1, finish))
    wait(number, store_sem)


def parts_of(n_chip):
    far = n_chip // 2
    near = [s for s in range(n_chip) if s != far]
    return [near] * CORES, [[far]] * CORES


def block_of(out_ref, tile, per_col, width):
    rows = pl.ds(pl.multiple_of(lax.div(tile, per_col) * width, width), width)
    columns = pl.ds(pl.multiple_of(lax.rem(tile, per_col) * width, width), width)
    return out_ref.at[rows, columns]


def main_kernel(n_row, n_chip, slots, per_row, per_col, pieces, *refs):
    early, late = parts_of(n_chip)
    n_left = sum(map(len, early))
    n_source = n_left + len(pieces)
    sources = refs[:n_source]
    out_ref, right_ref, plan = refs[n_source + 1 :][:3]
    acc, left_buf, right_buf, fact_buf, code_buf = refs[n_source + 4 :][:5]
    load_sem, code_sem, store_sem = refs[n_source + 9 :]
    r = lax.axis_index("row")
    c = lax.axis_index("col")
    z, core = lax.div(c, CORES), lax.rem(c, CORES)
    rows, width = left_buf.shape[-1], acc.shape[-1]
    tiles = per_row * per_col
    stations = CORES * n_row * n_chip

    def load(index):
        if index < n_left:
            target = left_buf.at[index]
            source = sources[index].at[pl.ds(0, target.shape[0])]
        else:
            which, first, number = pieces[index - n_left]
            target = right_buf.at[which, pl.ds(first, number)]
            source = sources[index]
        return pltpu.make_async_copy(source, target, load_sem.at[index])

    for index in [*range(n_left, n_source), *range(n_left)]:
        load(index).start()
    for index, (which, first, number) in enumerate(pieces):
        load(n_left + index).wait()
        for s in range(first, first + number):
            station = which * n_chip + s
            meta = right_buf[which, s, slots * rows :].astype(jnp.float32)
            for i in range(slots + 1):
                fact_buf[i, station : station + 1, :] = meta[i : i + 1]
    code, tile_row = plan_of(
        fact_buf, r, z, core, n_row, n_chip, slots, per_col, tiles, acc.shape[0] > tiles
    )
    code_buf[0:1, :] = code
    code_buf[1:2, :] = tile_row
    to_smem = pltpu.make_async_copy(code_buf, plan, code_sem)
    to_smem.start()
    kept = 0
    for other in range(CORES):
        for j in range(n_row):
            for s in late[other]:
                right_ref[kept] = right_buf[other * n_row + j, s, : slots * rows]
                kept += 1
    for index in range(n_left):
        load(index).wait()
    to_smem.wait()

    def group(other):
        base = len(early[0]) * other

        def stations_of(j):
            index = other * n_row + j

            def station(m, s):
                def left():
                    return left_buf[base + m, pl.ds(j * slots * width, slots * width)]

                def right():
                    tiles = [right_buf[index, s, i * rows : (i + 1) * rows] for i in range(slots)]
                    return jnp.concatenate(tiles, axis=1)

                return index * n_chip + s, left, right

            return [station(m, s) for m, s in enumerate(early[other])]

        return n_row, stations_of

    groups = [group(other) for other in range(CORES)]
    settle(plan, groups, stations, slots, acc, None, out_ref, per_col, None, store_sem)


def main_part(left, right, pieces, out, n_row, per_row, per_col):
    n_chip = len(left[0]) + 1
    early, late = parts_of(n_chip)
    flat = [*left[0], *left[1]]
    rows, width = flat[0].shape[1], right[0].shape[2]
    slots = right[0].shape[1] // rows
    height = n_row * slots * width
    tiles = per_row * per_col
    stations = CORES * n_row * n_chip
    pairs = slots * slots * stations
    places = min(tiles + 1, pairs)
    plan = (8, pairs)
    sources = [*flat, *right]
    anywhere = pl.BlockSpec(memory_space=pl.ANY)
    held = (
        places * width * width * 4
        + len(flat) * height * rows * 2
        + (stations + n_row * sum(map(len, late))) * (slots * rows + META) * width * 2
        + (slots + 1) * stations * width * 4
        + 8 * pairs * pairs * 4
    )
    return pl.pallas_call(
        functools.partial(main_kernel, n_row, n_chip, slots, per_row, per_col, pieces),
        out_shape=[
            jax.ShapeDtypeStruct(out.shape, out.dtype),
            jax.ShapeDtypeStruct(
                (n_row * sum(map(len, late)), slots * rows, width), jnp.bfloat16
            ),
            jax.ShapeDtypeStruct(plan, jnp.int32),
        ],
        in_specs=[anywhere] * (len(sources) + 1),
        out_specs=[
            anywhere,
            pl.BlockSpec(memory_space=pltpu.VMEM),
            pl.BlockSpec(memory_space=pltpu.SMEM),
        ],
        scratch_shapes=[
            pltpu.VMEM((places, width, width), jnp.float32),
            pltpu.VMEM((len(flat), height, rows), jnp.bfloat16),
            pltpu.VMEM((CORES * n_row, n_chip, slots * rows + META, width), jnp.bfloat16),
            pltpu.VMEM((slots + 1, stations, width), jnp.float32),
            pltpu.VMEM(plan, jnp.int32),
            pltpu.SemaphoreType.DMA((len(sources),)),
            pltpu.SemaphoreType.DMA,
            pltpu.SemaphoreType.DMA,
        ],
        input_output_aliases={len(sources): 0},
        compiler_params=pltpu.CompilerParams(vmem_limit_bytes=held + 3 * MIB),
        cost_estimate=pl.CostEstimate(flops=0, bytes_accessed=0, transcendentals=0),
    )(*sources, out)


def tail_kernel(n_row, n_chip, slots, per_col, plan, *refs):
    _, late = parts_of(n_chip)
    n_left = sum(map(len, late))
    lefts, right_ref = refs[:n_left], refs[n_left]
    out_ref, acc, held, load_sem, store_sem = refs[n_left + 2 :]
    rows, width = lefts[0].shape[-1], acc.shape[-1]
    stations = CORES * n_row * n_chip

    found = []
    for other in range(CORES):
        for j in range(n_row):
            for m, s in enumerate(late[other]):
                source = lefts[len(late[0]) * other + m]

                def left(source=source, j=j):
                    return source[j * slots * width : (j + 1) * slots * width]

                def right(kept=len(found)):
                    tiles = [right_ref[kept, i * rows : (i + 1) * rows] for i in range(slots)]
                    return jnp.concatenate(tiles, axis=1)

                found.append(((other * n_row + j) * n_chip + s, left, right))
    groups = [(1, lambda step: found)]
    settle(plan, groups, stations, slots, acc, held, out_ref, per_col, load_sem, store_sem)


def tail_part(left, right, plan, out, n_row, per_row, per_col):
    flat = [*left[0], *left[1]]
    _, depth, width = right.shape
    slots = depth // flat[0].shape[1]
    stations = plan.shape[1] // slots**2
    n_chip = stations // (CORES * n_row)
    places = (min(per_row * per_col + 1, plan.shape[1]), width, width)
    anywhere = pl.BlockSpec(memory_space=pl.ANY)
    vmem = pl.BlockSpec(memory_space=pltpu.VMEM)
    smem = pl.BlockSpec(memory_space=pltpu.SMEM)
    held = 2 * places[0] * width * width * 4 + 2 * right.size * 2 + 2 * MIB * len(flat)
    return pl.pallas_call(
        functools.partial(tail_kernel, n_row, n_chip, slots, per_col),
        out_shape=jax.ShapeDtypeStruct(out.shape, out.dtype),
        in_specs=[smem] + [vmem] * (len(flat) + 1) + [anywhere],
        out_specs=anywhere,
        scratch_shapes=[
            pltpu.VMEM(places, jnp.float32),
            pltpu.VMEM(places, jnp.float32),
            pltpu.SemaphoreType.DMA,
            pltpu.SemaphoreType.DMA,
        ],
        input_output_aliases={len(flat) + 2: 0},
        compiler_params=pltpu.CompilerParams(vmem_limit_bytes=held + 4 * MIB),
        cost_estimate=pl.CostEstimate(flops=0, bytes_accessed=0, transcendentals=0),
    )(plan, *flat, right, out)


def zero_kernel(first, count, *refs):
    out_ref, block, sem = refs[-3:]
    block[...] = jnp.zeros_like(block)
    height = block.shape[0]
    copies = [
        pltpu.make_async_copy(block, out_ref.at[pl.ds((first + n) * height, height)], sem.at[n])
        for n in range(count)
    ]
    for copy in copies:
        copy.start()
    for copy in copies:
        copy.wait()


def zero_part(height, width, part, after, out=None):
    step = 128
    count = height // step
    early = count * ZERO_EARLY // 16
    first, number = ((0, early), (early, count - early))[part]
    anywhere = pl.BlockSpec(memory_space=pl.ANY)
    inputs = [after] if out is None else [after, out]
    return pl.pallas_call(
        functools.partial(zero_kernel, first, number),
        out_shape=jax.ShapeDtypeStruct((height, width), jnp.float32),
        in_specs=[anywhere] * len(inputs),
        out_specs=anywhere,
        scratch_shapes=[
            pltpu.VMEM((step, width), jnp.float32),
            pltpu.SemaphoreType.DMA((number,)),
        ],
        input_output_aliases={} if out is None else {1: 0},
        compiler_params=pltpu.CompilerParams(vmem_limit_bytes=4 * MIB),
        cost_estimate=pl.CostEstimate(
            flops=0, bytes_accessed=height * width * 2, transcendentals=0
        ),
    )(*inputs)


def local(sensitivity, tile_ids, counts, weight_class):
    n_row = lax.axis_size("row")
    n_col = lax.axis_size("col")
    n_chip = n_col // CORES
    width = sensitivity.shape[-1]
    per_row = TILES // n_row
    per_col = TILES // n_col
    middle = n_chip // 2

    def flip_row(value, j):
        return lax.ppermute(value, "row", [(i, i ^ j) for i in range(n_row)])

    def shift_chip(value, s):
        pairs = [(i, (i + CORES * s) % n_col) for i in range(n_col)]
        return lax.ppermute(value, "col", pairs)

    def flip_core(value):
        return lax.ppermute(value, "col", [(i, i ^ 1) for i in range(n_col)])

    def pad(value, extra):
        return jnp.pad(value, ((0, extra), (0, 0)))

    after = lax.optimization_barrier

    ids = jnp.transpose(tile_ids, (0, 2, 1))[0]
    parts = pack(sensitivity[0], weight_class, ids, counts, n_chip)
    to_row, to_chip = parts[:n_row], parts[n_row:]
    plane = [to_row[0]] + [flip_row(to_row[j], j) for j in range(1, n_row)]
    from_chip = [to_chip[0]] + [shift_chip(to_chip[s], s) for s in range(1, n_chip)]
    height, breadth = per_row * width, per_col * width
    zeros = zero_part(height, breadth, 0, to_chip[0])
    plane, from_chip, zeros = after((plane, from_chip, zeros))
    rows = sensitivity.shape[-2]
    chip = jnp.stack(plane).reshape(-1, rows)
    near = {0: chip}
    for s in range(1, middle):
        near[s] = shift_chip(near[s - 1], 1)
        near[n_chip - s] = shift_chip(pad(chip, 48) if s == 1 else near[n_chip - s + 1], -1)
    right = jnp.stack(from_chip)
    own = [flip_core(chip), flip_core(right)]
    *own, again, token = after((*own, right, to_chip[0]))
    sides = [right] + [flip_row(right if j == 1 else again, j) for j in range(1, n_row)]
    far = shift_chip(pad(near[middle - 1], 64), 1)
    swapped = {s: flip_core(near[s]) for s in range(1, middle)}
    zeros = zero_part(height, breadth, 1, token, zeros)
    swapped, late, waiting, zeros = after(
        (swapped, {s: near[s] for s in near if s > middle}, sides[1:], zeros)
    )
    swapped |= {s: flip_core(late[s]) for s in late} | {0: own[0]}
    sides += [own[1]] + [flip_core(x) for x in waiting]
    pieces = [(index, 0, n_chip) for index in range(CORES * n_row)]
    early = [[near[s] for s in sorted(near)], [swapped[s] for s in sorted(swapped)]]
    out, tail_right, plan = main_part(early, sides, pieces, zeros, n_row, per_row, per_col)
    far, plan = after((far, plan))
    return tail_part([[far], [flip_core(far)]], tail_right, plan, out, n_row, per_row, per_col)


def solution(mesh):
    in_specs = (
        P(("row", "col"), None, None, None, None),
        P(("row", "col"), None, None),
        P(("row", "col"), None),
        P(("row", "col"), None),
    )
    return jax.shard_map(
        local, mesh=mesh, in_specs=in_specs, out_specs=P("row", "col"), check_vma=False
    )
```

time: 67.7 us -> 65.3 us (0.965)
  waiting for transfers between devices: 27.1 us -> 19.7 us
  Pallas kernels: 19.4 us -> 23.1 us
  local copies, waits for them, and re-layouts: 0.08 us -> 0.99 us
    ppermute x6, waiting for transfers between devices: 17.4 us -> 10 us  [shift_chip(): return lax.ppermute(value, 'col', pairs)]
    pallas_call x2 -> x3, Pallas kernels: 8.83 us -> 15.4 us  [the longest x2 12.1 us: zero_part(): pl.pallas_call(functools.partial(zero_kernel, first, number), out_shape=j...]
    pallas_call x1, Pallas kernels: 8.45 us -> 5.57 us  [main_part(): pl.pallas_call(functools.partial(main_kernel, n_row, n_chip, slots, per_r...]
    unnamed x4 -> x6, local copies, waits for them, and re-layouts: 0.01 us -> 0.91 us
  transfers between devices with their start and end apart: 20 -> 20, of which waited for: 9 -> 10; matrix products, arithmetic and copies ran while one was open for 0% -> 0% of each run, Pallas kernels for 21% -> 27%
where the time goes in v6:
time: 65.3 us; the launch traced here: 65.2 us
  Pallas kernels  23.1 us (35%)
  starting transfers between devices  21.1 us (32%)
  waiting for transfers between devices  19.7 us (30%)
  local copies, waits for them, and re-layouts  0.99 us (2%)
    pallas_call x2, Pallas kernels, zero_part(): pl.pallas_call(functools.partial(zero_kernel, first, number), out_shape=j...  12.1 us
    ppermute x6, starting transfers between devices, shift_chip(): return lax.ppermute(value, 'col', pairs)  10.6 us
    ppermute x6, waiting for transfers between devices, shift_chip(): return lax.ppermute(value, 'col', pairs)  10 us
    ppermute x6, starting transfers between devices, flip_row(): return lax.ppermute(value, 'row', [(i, i ^ j) for i in range(n_row)])  8.43 us
    pallas_call x1, Pallas kernels, main_part(): pl.pallas_call(functools.partial(main_kernel, n_row, n_chip, slots, per_r...  5.57 us
    ppermute x6, waiting for transfers between devices, flip_row(): return lax.ppermute(value, 'row', [(i, i ^ j) for i in range(n_row)])  4.84 us
    ppermute x8, waiting for transfers between devices, flip_core(): return lax.ppermute(value, 'col', [(i, i ^ 1) for i in range(n_col)])  4.84 us
    pallas_call x1, Pallas kernels, tail_part(): pl.pallas_call(functools.partial(tail_kernel, n_row, n_chip, slots, per_c...  3.33 us
  transfers between devices with their start and end apart: 20, of which 10 were waited for; matrix products, arithmetic and copies ran while one was open for 0% of the time, Pallas kernels for 27%

profile of v6, /device:TPU:0, one launch (start us, length us, event | category | flops | bytes accessed | tf_op | source)
XLA Modules:
  0.0 65.2 jit_solution(16868272765279728491)
XLA Ops:
  0.0 2.1 %shard_map.46 = (bf16[256,256]{1,0:T(8,128)(2,1)}, bf16[256,256]{1,0:T(8,128)(2,1)}, bf16[256,256]{1,0:T(8,128)(2,1)}, bf16[256,256]{1,0:T(8,128)(2,1)}, bf16[52...) custom-call(bf16[4,2,256,128]{3,2,1,0:T(8,128)(2,1)} %bitcast.18, ...), custom_call_target="tpu_custom_call" | custom-call | tf_op jit(solution)/shard_map/pallas_call | solution.py:51
  2.2 2.9 %collective-permute-start = (bf16[256,256]{1,0:T(8,128)(2,1)}, bf16[256,256]{1,0:T(8,128)(2,1)S(1)}, u32[]{:S(2)}, u32[]{:S(2)}) collective-permute-start(bf16[256,256]{1,0:T(8,128)(2,1)} %get-tuple-element.38), channel_id=1, source_target_pairs={{0,8},{8,0},{16,24},{24,16},{1,9},{9,1},{17,25},{25,17},{2,10},{10... | collective-permute-start | bytes 393224 | tf_op jit(solution)/shard_map/ppermute | solution.py:422
  5.1 1.6 %collective-permute-start.3 = (bf16[528,128]{1,0:T(8,128)(2,1)}, bf16[528,128]{1,0:T(8,128)(2,1)S(1)}, u32[]{:S(2)}, u32[]{:S(2)}) collective-permute-start(bf16[528,128]{1,0:T(8,128)(2,1)} %get-tuple-element.42), channel_id=1, source_target_pairs={{0,2},{1,3},{2,4},{3,5},{4,6},{5,7},{6,0},{7,1},{8,10},{9,11},{10,... | collective-permute-start | bytes 405512 | tf_op jit(solution)/shard_map/ppermute | solution.py:426
  6.7 2.6 %collective-permute-start.4 = (bf16[528,128]{1,0:T(8,128)(2,1)}, bf16[528,128]{1,0:T(8,128)(2,1)S(1)}, u32[]{:S(2)}, u32[]{:S(2)}) collective-permute-start(bf16[528,128]{1,0:T(8,128)(2,1)} %get-tuple-element.43), channel_id=1, source_target_pairs={{0,4},{1,5},{2,6},{3,7},{4,0},{5,1},{6,2},{7,3},{8,12},{9,13},{10,... | collective-permute-start | bytes 405512 | tf_op jit(solution)/shard_map/ppermute | solution.py:426
  9.3 1.3 %collective-permute-start.5 = (bf16[528,128]{1,0:T(8,128)(2,1)}, bf16[528,128]{1,0:T(8,128)(2,1)S(1)}, u32[]{:S(2)}, u32[]{:S(2)}) collective-permute-start(bf16[528,128]{1,0:T(8,128)(2,1)} %get-tuple-element.44), channel_id=1, source_target_pairs={{0,6},{1,7},{2,0},{3,1},{4,2},{5,3},{6,4},{7,5},{8,14},{9,15},{10,... | collective-permute-start | bytes 405512 | tf_op jit(solution)/shard_map/ppermute | solution.py:426
  10.6 1.5 %collective-permute-start.1 = (bf16[256,256]{1,0:T(8,128)(2,1)}, bf16[256,256]{1,0:T(8,128)(2,1)S(1)}, u32[]{:S(2)}, u32[]{:S(2)}) collective-permute-start(bf16[256,256]{1,0:T(8,128)(2,1)} %get-tuple-element.39), channel_id=1, source_target_pairs={{0,16},{8,24},{16,0},{24,8},{1,17},{9,25},{17,1},{25,9},{2,18},{10... | collective-permute-start | bytes 393224 | tf_op jit(solution)/shard_map/ppermute | solution.py:422
  12.6 0.9 %copy-done = bf16[528,128]{1,0:T(8,128)(2,1)S(1)} copy-done((bf16[528,128]{1,0:T(8,128)(2,1)S(1)}, bf16[528,128]{1,0:T(8,128)(2,1)}, u32[]{:S(2)}) %copy-start) | copy-done | bytes 135192
  13.5 4.7 %shard_map.47.refs_1_ = f32[4096,2048]{1,0:T(8,128)} custom-call(bf16[528,128]{1,0:T(8,128)(2,1)S(1)} %copy-done), custom_call_target="tpu_custom_call" | custom-call | bytes 16777216 | tf_op jit(solution)/shard_map/pallas_call | solution.py:395
  19.3 3.0 %collective-permute-start.6 = (bf16[1024,256]{1,0:T(8,128)(2,1)S(1)}, bf16[1024,256]{1,0:T(8,128)(2,1)S(1)}, u32[]{:S(2)}, u32[]{:S(2)}) collective-permute-start(bf16[1024,256]{1,0:T(8,128)(2,1)S(1)} %bitcast.14), channel_id=1, source_target_pairs={{0,2},{1,3},{2,4},{3,5},{4,6},{5,7},{6,0},{7,1},{8,10},{9,11},{10,... | collective-permute-start | bytes 1572872 | tf_op jit(solution)/shard_map/ppermute | solution.py:426
  22.3 1.1 %collective-permute-start.8 = (bf16[1072,256]{1,0:T(8,128)(2,1)S(1)}, bf16[1072,256]{1,0:T(8,128)(2,1)S(1)}, u32[]{:S(2)}, u32[]{:S(2)}) collective-permute-start(bf16[1072,256]{1,0:T(8,128)(2,1)S(1)} %pad.9), channel_id=1, source_target_pairs={{0,6},{1,7},{2,0},{3,1},{4,2},{5,3},{6,4},{7,5},{8,14},{9,15},{10,... | collective-permute-start | bytes 1646600 | tf_op jit(solution)/shard_map/ppermute | solution.py:426
  23.4 1.1 %collective-permute-start.12 = (bf16[4,528,128]{2,1,0:T(8,128)(2,1)S(1)}, bf16[4,528,128]{2,1,0:T(8,128)(2,1)S(1)}, u32[]{:S(2)}, u32[]{:S(2)}) collective-permute-start(bf16[4,528,128]{2,1,0:T(8,128)(2,1)S(1)} %pad_maximum_fusion.refs_6_), channel_id=1, source_target_pairs={{0,8},{8,0},{16,24},{24,16},{1,9},{9,1},{17,25},{25,17},{2,10},{10... | collective-permute-start | bytes 1622024 | tf_op jit(solution)/shard_map/ppermute | solution.py:422
  24.5 1.5 %collective-permute-start.13 = (bf16[4,528,128]{2,1,0:T(8,128)(2,1)S(1)}, bf16[4,528,128]{2,1,0:T(8,128)(2,1)S(1)}, u32[]{:S(2)}, u32[]{:S(2)}) collective-permute-start(bf16[4,528,128]{2,1,0:T(8,128)(2,1)S(1)} %pad_maximum_fusion.refs_6_), channel_id=1, source_target_pairs={{0,16},{8,24},{16,0},{24,8},{1,17},{9,25},{17,1},{25,9},{2,18},{10... | collective-permute-start | bytes 1622024 | tf_op jit(solution)/shard_map/ppermute | solution.py:422
  26.0 0.9 %collective-permute-start.14 = (bf16[4,528,128]{2,1,0:T(8,128)(2,1)S(1)}, bf16[4,528,128]{2,1,0:T(8,128)(2,1)S(1)}, u32[]{:S(2)}, u32[]{:S(2)}) collective-permute-start(bf16[4,528,128]{2,1,0:T(8,128)(2,1)S(1)} %pad_maximum_fusion.refs_6_), channel_id=1, source_target_pairs={{0,24},{8,16},{16,8},{24,0},{1,25},{9,17},{17,9},{25,1},{2,26},{10... | collective-permute-start | bytes 1622024 | tf_op jit(solution)/shard_map/ppermute | solution.py:422
  26.9 9.2 %collective-permute-done.6.refs_1_ = bf16[1024,256]{1,0:T(8,128)(2,1)S(1)} collective-permute-done((bf16[1024,256]{1,0:T(8,128)(2,1)S(1)}, bf16[1024,256]{1,0:T(8,128)(2,1)S(1)}, u32[]{:S(2)}, u32[]{:S(2)}) %collective-permute-start.6) | collective-permute-done | bytes 524320 | tf_op jit(solution)/shard_map/ppermute | solution.py:426
  36.1 2.5 %collective-permute-done.12.refs_7_ = bf16[4,528,128]{2,1,0:T(8,128)(2,1)S(1)} collective-permute-done((bf16[4,528,128]{2,1,0:T(8,128)(2,1)S(1)}, bf16[4,528,128]{2,1,0:T(8,128)(2,1)S(1)}, u32[]{:S(2)}, u32[]{:S(2)}) %collective-permute-start.12) | collective-permute-done | bytes 540704 | tf_op jit(solution)/shard_map/ppermute | solution.py:422
  38.6 1.0 %collective-permute-start.7 = (bf16[1088,256]{1,0:T(8,128)(2,1)S(1)}, bf16[1088,256]{1,0:T(8,128)(2,1)S(1)}, u32[]{:S(2)}, u32[]{:S(2)}) collective-permute-start(bf16[1088,256]{1,0:T(8,128)(2,1)S(1)} %pad.8), channel_id=1, source_target_pairs={{0,2},{1,3},{2,4},{3,5},{4,6},{5,7},{6,0},{7,1},{8,10},{9,11},{10,... | collective-permute-start | bytes 1671176 | tf_op jit(solution)/shard_map/ppermute | solution.py:426
  39.6 7.3 %shard_map.48.refs_14_ = f32[4096,2048]{1,0:T(8,128)} custom-call(bf16[528,128]{1,0:T(8,128)(2,1)S(1)} %copy-done.1, f32[4096,2048]{1,0:T(8,128)} %shard_map.47.refs_1_), custom_call_target="tpu_custom_call", output_to_operand_aliasing={{}: (1, {})} | custom-call | bytes 16777216 | tf_op jit(solution)/shard_map/pallas_call | solution.py:395
  46.9 0.9 %collective-permute-done.8.refs_2_ = bf16[1072,256]{1,0:T(8,128)(2,1)S(1)} collective-permute-done((bf16[1072,256]{1,0:T(8,128)(2,1)S(1)}, bf16[1072,256]{1,0:T(8,128)(2,1)S(1)}, u32[]{:S(2)}, u32[]{:S(2)}) %collective-permute-start.8) | collective-permute-done | bytes 548896 | tf_op jit(solution)/shard_map/ppermute | solution.py:426
  47.8 0.8 %collective-permute-done.13.refs_8_ = bf16[4,528,128]{2,1,0:T(8,128)(2,1)S(1)} collective-permute-done((bf16[4,528,128]{2,1,0:T(8,128)(2,1)S(1)}, bf16[4,528,128]{2,1,0:T(8,128)(2,1)S(1)}, u32[]{:S(2)}, u32[]{:S(2)}) %collective-permute-start.13) | collective-permute-done | bytes 540704 | tf_op jit(solution)/shard_map/ppermute | solution.py:422
  48.6 1.3 %collective-permute-done.14.refs_9_ = bf16[4,528,128]{2,1,0:T(8,128)(2,1)S(1)} collective-permute-done((bf16[4,528,128]{2,1,0:T(8,128)(2,1)S(1)}, bf16[4,528,128]{2,1,0:T(8,128)(2,1)S(1)}, u32[]{:S(2)}, u32[]{:S(2)}) %collective-permute-start.14) | collective-permute-done | bytes 540704 | tf_op jit(solution)/shard_map/ppermute | solution.py:422
  51.0 1.7 %collective-permute-done.16.refs_11_ = bf16[4,528,128]{2,1,0:T(8,128)(2,1)S(1)} collective-permute-done((bf16[4,528,128]{2,1,0:T(8,128)(2,1)S(1)}, bf16[4,528,128]{2,1,0:T(8,128)(2,1)S(1)}, u32[]{:S(2)}, u32[]{:S(2)}) %collective-permute-start.16) | collective-permute-done | bytes 540704 | tf_op jit(solution)/shard_map/ppermute | solution.py:429
  54.2 5.6 %shard_map.49 = (f32[4096,2048]{1,0:T(8,128)}, bf16[8,512,128]{2,1,0:T(8,128)(2,1)S(1)}, s32[8,128]{1,0:T(8,128)S(1)}) custom-call(bf16[1024,256]{1,0:T(8,128)(2,1)S(1)} %bitcast.16, bf16[1024,256]{1,0:T(8,128)(2,1)S(1)} %collective-permute-done.6.refs_1_, bf16[1072,256]{1,0:T(8,128)(2,1)S(1)} %collective-permute-done.8.refs_2_, ...), custom_call_target="tpu_custom_call", output_to_operand_aliasing={{0}: (14, {})} | custom-call | tf_op jit(solution)/shard_map/pallas_call | solution.py:289
  60.2 1.6 %collective-permute-done.19.refs_1_ = bf16[1088,256]{1,0:T(8,128)(2,1)S(1)} collective-permute-done((bf16[1088,256]{1,0:T(8,128)(2,1)S(1)}, bf16[1088,256]{1,0:T(8,128)(2,1)S(1)}, u32[]{:S(2)}, u32[]{:S(2)}) %collective-permute-start.19) | collective-permute-done | bytes 557088 | tf_op jit(solution)/shard_map/ppermute | solution.py:429
  61.8 3.3 %shard_map.50 = f32[4096,2048]{1,0:T(8,128)} custom-call(s32[8,128]{1,0:T(8,128)S(1)} %get-tuple-element.65.plan, bf16[1088,256]{1,0:T(8,128)(2,1)S(1)} %collective-permute-done.7.refs_0_, bf16[1088,256]{1,0:T(8,128)(2,1)S(1)} %collective-permute-done.19.refs_1_, bf16[8,512,128]{2,1,0:T(8,128)(2,1)S(1)} %get-tuple-element.67.refs_2_, ...), custom_call_target="tpu_custom_call", output_to_operand_aliasing={{}: (4, {})} | custom-call | tf_op jit(solution)/shard_map/pallas_call | solution.py:357
  (31 shorter events, 4.6 us)
Async XLA Ops:
  2.2 10.0 %collective-permute-start = (bf16[256,256]{1,0:T(8,128)(2,1)}, bf16[256,256]{1,0:T(8,128)(2,1)S(1)}, u32[]{:S(2)}, u32[]{:S(2)}) collective-permute-start(bf16[256,256]{1,0:T(8,128)(2,1)} %get-tuple-element.38), channel_id=1, source_target_pairs={{0,8},{8,0},{16,24},{24,16},{1,9},{9,1},{17,25},{25,17},{2,10},{10... | collective-permute-start | bytes 393224 | tf_op jit(solution)/shard_map/ppermute | solution.py:422
  5.1 13.4 %collective-permute-start.3 = (bf16[528,128]{1,0:T(8,128)(2,1)}, bf16[528,128]{1,0:T(8,128)(2,1)S(1)}, u32[]{:S(2)}, u32[]{:S(2)}) collective-permute-start(bf16[528,128]{1,0:T(8,128)(2,1)} %get-tuple-element.42), channel_id=1, source_target_pairs={{0,2},{1,3},{2,4},{3,5},{4,6},{5,7},{6,0},{7,1},{8,10},{9,11},{10,... | collective-permute-start | bytes 405512 | tf_op jit(solution)/shard_map/ppermute | solution.py:426
  6.7 11.8 %collective-permute-start.4 = (bf16[528,128]{1,0:T(8,128)(2,1)}, bf16[528,128]{1,0:T(8,128)(2,1)S(1)}, u32[]{:S(2)}, u32[]{:S(2)}) collective-permute-start(bf16[528,128]{1,0:T(8,128)(2,1)} %get-tuple-element.43), channel_id=1, source_target_pairs={{0,4},{1,5},{2,6},{3,7},{4,0},{5,1},{6,2},{7,3},{8,12},{9,13},{10,... | collective-permute-start | bytes 405512 | tf_op jit(solution)/shard_map/ppermute | solution.py:426
  9.3 9.2 %collective-permute-start.5 = (bf16[528,128]{1,0:T(8,128)(2,1)}, bf16[528,128]{1,0:T(8,128)(2,1)S(1)}, u32[]{:S(2)}, u32[]{:S(2)}) collective-permute-start(bf16[528,128]{1,0:T(8,128)(2,1)} %get-tuple-element.44), channel_id=1, source_target_pairs={{0,6},{1,7},{2,0},{3,1},{4,2},{5,3},{6,4},{7,5},{8,14},{9,15},{10,... | collective-permute-start | bytes 405512 | tf_op jit(solution)/shard_map/ppermute | solution.py:426
  10.6 7.9 %collective-permute-start.1 = (bf16[256,256]{1,0:T(8,128)(2,1)}, bf16[256,256]{1,0:T(8,128)(2,1)S(1)}, u32[]{:S(2)}, u32[]{:S(2)}) collective-permute-start(bf16[256,256]{1,0:T(8,128)(2,1)} %get-tuple-element.39), channel_id=1, source_target_pairs={{0,16},{8,24},{16,0},{24,8},{1,17},{9,25},{17,1},{25,9},{2,18},{10... | collective-permute-start | bytes 393224 | tf_op jit(solution)/shard_map/ppermute | solution.py:422
  12.1 6.4 %collective-permute-start.2 = (bf16[256,256]{1,0:T(8,128)(2,1)}, bf16[256,256]{1,0:T(8,128)(2,1)S(1)}, u32[]{:S(2)}, u32[]{:S(2)}) collective-permute-start(bf16[256,256]{1,0:T(8,128)(2,1)} %get-tuple-element.40), channel_id=1, source_target_pairs={{0,24},{8,16},{16,8},{24,0},{1,25},{9,17},{17,9},{25,1},{2,26},{10... | collective-permute-start | bytes 393224 | tf_op jit(solution)/shard_map/ppermute | solution.py:422
  12.6 0.9 %copy-start = (bf16[528,128]{1,0:T(8,128)(2,1)S(1)}, bf16[528,128]{1,0:T(8,128)(2,1)}, u32[]{:S(2)}) copy-start(bf16[528,128]{1,0:T(8,128)(2,1)} %get-tuple-element.55.refs_0_) | copy-start | bytes 405508
  13.5 5.0 %copy-start.1 = (bf16[528,128]{1,0:T(8,128)(2,1)S(1)}, bf16[528,128]{1,0:T(8,128)(2,1)}, u32[]{:S(2)}) copy-start(bf16[528,128]{1,0:T(8,128)(2,1)} %get-tuple-element.55.refs_0_) | copy-start | bytes 405508
  13.5 5.2 %copy-start.2 = (bf16[256,256]{1,0:T(8,128)(2,1)S(1)}, bf16[256,256]{1,0:T(8,128)(2,1)}, u32[]{:S(2)}) copy-start(bf16[256,256]{1,0:T(8,128)(2,1)} %get-tuple-element.45) | copy-start | bytes 393220
  18.6 5.9 %collective-permute-start.10 = (bf16[4,528,128]{2,1,0:T(8,128)(2,1)S(1)}, bf16[4,528,128]{2,1,0:T(8,128)(2,1)S(1)}, u32[]{:S(2)}, u32[]{:S(2)}) collective-permute-start(bf16[4,528,128]{2,1,0:T(8,128)(2,1)S(1)} %pad_maximum_fusion.refs_6_), channel_id=1, source_target_pairs={{0,1},{1,0},{2,3},{3,2},{4,5},{5,4},{6,7},{7,6},{8,9},{9,8},{10,11... | collective-permute-start | bytes 1622024 | tf_op jit(solution)/shard_map/ppermute | solution.py:429
  18.8 5.8 %collective-permute-start.9 = (bf16[1024,256]{1,0:T(8,128)(2,1)S(1)}, bf16[1024,256]{1,0:T(8,128)(2,1)S(1)}, u32[]{:S(2)}, u32[]{:S(2)}) collective-permute-start(bf16[1024,256]{1,0:T(8,128)(2,1)S(1)} %bitcast.13), channel_id=1, source_target_pairs={{0,1},{1,0},{2,3},{3,2},{4,5},{5,4},{6,7},{7,6},{8,9},{9,8},{10,11... | collective-permute-start | bytes 1572872 | tf_op jit(solution)/shard_map/ppermute | solution.py:429
  19.3 16.8 %collective-permute-start.6 = (bf16[1024,256]{1,0:T(8,128)(2,1)S(1)}, bf16[1024,256]{1,0:T(8,128)(2,1)S(1)}, u32[]{:S(2)}, u32[]{:S(2)}) collective-permute-start(bf16[1024,256]{1,0:T(8,128)(2,1)S(1)} %bitcast.14), channel_id=1, source_target_pairs={{0,2},{1,3},{2,4},{3,5},{4,6},{5,7},{6,0},{7,1},{8,10},{9,11},{10,... | collective-permute-start | bytes 1572872 | tf_op jit(solution)/shard_map/ppermute | solution.py:426
  22.3 25.5 %collective-permute-start.8 = (bf16[1072,256]{1,0:T(8,128)(2,1)S(1)}, bf16[1072,256]{1,0:T(8,128)(2,1)S(1)}, u32[]{:S(2)}, u32[]{:S(2)}) collective-permute-start(bf16[1072,256]{1,0:T(8,128)(2,1)S(1)} %pad.9), channel_id=1, source_target_pairs={{0,6},{1,7},{2,0},{3,1},{4,2},{5,3},{6,4},{7,5},{8,14},{9,15},{10,... | collective-permute-start | bytes 1646600 | tf_op jit(solution)/shard_map/ppermute | solution.py:426
  23.4 15.2 %collective-permute-start.12 = (bf16[4,528,128]{2,1,0:T(8,128)(2,1)S(1)}, bf16[4,528,128]{2,1,0:T(8,128)(2,1)S(1)}, u32[]{:S(2)}, u32[]{:S(2)}) collective-permute-start(bf16[4,528,128]{2,1,0:T(8,128)(2,1)S(1)} %pad_maximum_fusion.refs_6_), channel_id=1, source_target_pairs={{0,8},{8,0},{16,24},{24,16},{1,9},{9,1},{17,25},{25,17},{2,10},{10... | collective-permute-start | bytes 1622024 | tf_op jit(solution)/shard_map/ppermute | solution.py:422
  24.5 24.1 %collective-permute-start.13 = (bf16[4,528,128]{2,1,0:T(8,128)(2,1)S(1)}, bf16[4,528,128]{2,1,0:T(8,128)(2,1)S(1)}, u32[]{:S(2)}, u32[]{:S(2)}) collective-permute-start(bf16[4,528,128]{2,1,0:T(8,128)(2,1)S(1)} %pad_maximum_fusion.refs_6_), channel_id=1, source_target_pairs={{0,16},{8,24},{16,0},{24,8},{1,17},{9,25},{17,1},{25,9},{2,18},{10... | collective-permute-start | bytes 1622024 | tf_op jit(solution)/shard_map/ppermute | solution.py:422
  26.0 23.9 %collective-permute-start.14 = (bf16[4,528,128]{2,1,0:T(8,128)(2,1)S(1)}, bf16[4,528,128]{2,1,0:T(8,128)(2,1)S(1)}, u32[]{:S(2)}, u32[]{:S(2)}) collective-permute-start(bf16[4,528,128]{2,1,0:T(8,128)(2,1)S(1)} %pad_maximum_fusion.refs_6_), channel_id=1, source_target_pairs={{0,24},{8,16},{16,8},{24,0},{1,25},{9,17},{17,9},{25,1},{2,26},{10... | collective-permute-start | bytes 1622024 | tf_op jit(solution)/shard_map/ppermute | solution.py:422
  36.1 11.7 %collective-permute-start.11 = (bf16[1024,256]{1,0:T(8,128)(2,1)S(1)}, bf16[1024,256]{1,0:T(8,128)(2,1)S(1)}, u32[]{:S(2)}, u32[]{:S(2)}) collective-permute-start(bf16[1024,256]{1,0:T(8,128)(2,1)S(1)} %collective-permute-done.6.refs_1_), channel_id=1, source_target_pairs={{0,1},{1,0},{2,3},{3,2},{4,5},{5,4},{6,7},{7,6},{8,9},{9,8},{10,11... | collective-permute-start | bytes 1572872 | tf_op jit(solution)/shard_map/ppermute | solution.py:429
  38.6 21.2 %collective-permute-start.7 = (bf16[1088,256]{1,0:T(8,128)(2,1)S(1)}, bf16[1088,256]{1,0:T(8,128)(2,1)S(1)}, u32[]{:S(2)}, u32[]{:S(2)}) collective-permute-start(bf16[1088,256]{1,0:T(8,128)(2,1)S(1)} %pad.8), channel_id=1, source_target_pairs={{0,2},{1,3},{2,4},{3,5},{4,6},{5,7},{6,0},{7,1},{8,10},{9,11},{10,... | collective-permute-start | bytes 1671176 | tf_op jit(solution)/shard_map/ppermute | solution.py:426
  49.9 4.3 %collective-permute-start.15 = (bf16[1072,256]{1,0:T(8,128)(2,1)S(1)}, bf16[1072,256]{1,0:T(8,128)(2,1)S(1)}, u32[]{:S(2)}, u32[]{:S(2)}) collective-permute-start(bf16[1072,256]{1,0:T(8,128)(2,1)S(1)} %collective-permute-done.8.refs_2_), channel_id=1, source_target_pairs={{0,1},{1,0},{2,3},{3,2},{4,5},{5,4},{6,7},{7,6},{8,9},{9,8},{10,11... | collective-permute-start | bytes 1646600 | tf_op jit(solution)/shard_map/ppermute | solution.py:429
  49.9 2.7 %collective-permute-start.16 = (bf16[4,528,128]{2,1,0:T(8,128)(2,1)S(1)}, bf16[4,528,128]{2,1,0:T(8,128)(2,1)S(1)}, u32[]{:S(2)}, u32[]{:S(2)}) collective-permute-start(bf16[4,528,128]{2,1,0:T(8,128)(2,1)S(1)} %collective-permute-done.12.refs_7_), channel_id=1, source_target_pairs={{0,1},{1,0},{2,3},{3,2},{4,5},{5,4},{6,7},{7,6},{8,9},{9,8},{10,11... | collective-permute-start | bytes 1622024 | tf_op jit(solution)/shard_map/ppermute | solution.py:429
  50.5 3.0 %collective-permute-start.17 = (bf16[4,528,128]{2,1,0:T(8,128)(2,1)S(1)}, bf16[4,528,128]{2,1,0:T(8,128)(2,1)S(1)}, u32[]{:S(2)}, u32[]{:S(2)}) collective-permute-start(bf16[4,528,128]{2,1,0:T(8,128)(2,1)S(1)} %collective-permute-done.13.refs_8_), channel_id=1, source_target_pairs={{0,1},{1,0},{2,3},{3,2},{4,5},{5,4},{6,7},{7,6},{8,9},{9,8},{10,11... | collective-permute-start | bytes 1622024 | tf_op jit(solution)/shard_map/ppermute | solution.py:429
  50.5 3.8 %collective-permute-start.18 = (bf16[4,528,128]{2,1,0:T(8,128)(2,1)S(1)}, bf16[4,528,128]{2,1,0:T(8,128)(2,1)S(1)}, u32[]{:S(2)}, u32[]{:S(2)}) collective-permute-start(bf16[4,528,128]{2,1,0:T(8,128)(2,1)S(1)} %collective-permute-done.14.refs_9_), channel_id=1, source_target_pairs={{0,1},{1,0},{2,3},{3,2},{4,5},{5,4},{6,7},{7,6},{8,9},{9,8},{10,11... | collective-permute-start | bytes 1622024 | tf_op jit(solution)/shard_map/ppermute | solution.py:429
  59.8 2.0 %collective-permute-start.19 = (bf16[1088,256]{1,0:T(8,128)(2,1)S(1)}, bf16[1088,256]{1,0:T(8,128)(2,1)S(1)}, u32[]{:S(2)}, u32[]{:S(2)}) collective-permute-start(bf16[1088,256]{1,0:T(8,128)(2,1)S(1)} %collective-permute-done.7.refs_0_), channel_id=1, source_target_pairs={{0,1},{1,0},{2,3},{3,2},{4,5},{5,4},{6,7},{7,6},{8,9},{9,8},{10,11... | collective-permute-start | bytes 1671176 | tf_op jit(solution)/shard_map/ppermute | solution.py:429

commit v7 on v6

--- a/solution.py
+++ b/solution.py
@@ -446,18 +446,16 @@
     near = {0: chip}
     for s in range(1, middle):
         near[s] = shift_chip(near[s - 1], 1)
-        near[n_chip - s] = shift_chip(pad(chip, 48) if s == 1 else near[n_chip - s + 1], -1)
+        near[n_chip - s] = shift_chip(pad(chip, 32) if s == 1 else near[n_chip - s + 1], -1)
     right = jnp.stack(from_chip)
     own = [flip_core(chip), flip_core(right)]
     *own, again, token = after((*own, right, to_chip[0]))
     sides = [right] + [flip_row(right if j == 1 else again, j) for j in range(1, n_row)]
-    far = shift_chip(pad(near[middle - 1], 64), 1)
+    far = shift_chip(pad(near[middle - 1], 48), 1)
     swapped = {s: flip_core(near[s]) for s in range(1, middle)}
     zeros = zero_part(height, breadth, 1, token, zeros)
-    swapped, late, waiting, zeros = after(
-        (swapped, {s: near[s] for s in near if s > middle}, sides[1:], zeros)
-    )
-    swapped |= {s: flip_core(late[s]) for s in late} | {0: own[0]}
+    swapped, waiting, zeros = after((swapped, sides[1:], zeros))
+    swapped |= {s: flip_core(near[s]) for s in near if s > middle} | {0: own[0]}
     sides += [own[1]] + [flip_core(x) for x in waiting]
     pieces = [(index, 0, n_chip) for index in range(CORES * n_row)]
     early = [[near[s] for s in sorted(near)], [swapped[s] for s in sorted(swapped)]]

time: 65.3 us -> 64 us (0.980)
  starting transfers between devices: 21.1 us -> 19.3 us
    ppermute x6, waiting for transfers between devices: 10 us -> 12 us  [shift_chip(): return lax.ppermute(value, 'col', pairs)]
    ppermute x6, waiting for transfers between devices: 4.84 us -> 3.47 us  [flip_row(): return lax.ppermute(value, 'row', [(i, i ^ j) for i in range(n_row)])]
    ppermute x8, starting transfers between devices: 2.09 us -> 1.31 us  [flip_core(): return lax.ppermute(value, 'col', [(i, i ^ 1) for i in range(n_col)])]
  transfers between devices with their start and end apart: 20 -> 20, of which waited for: 10 -> 9; matrix products, arithmetic and copies ran while one was open for 0% -> 0% of each run, Pallas kernels for 27% -> 28%
where the time goes in v7:
time: 64 us; the launch traced here: 63.6 us
  Pallas kernels  22.7 us (35%)
  waiting for transfers between devices  20.3 us (32%)
  starting transfers between devices  19.3 us (30%)
  local copies, waits for them, and re-layouts  0.98 us (2%)
    pallas_call x2, Pallas kernels, zero_part(): pl.pallas_call(functools.partial(zero_kernel, first, number), out_shape=j...  12.1 us
    ppermute x6, waiting for transfers between devices, shift_chip(): return lax.ppermute(value, 'col', pairs)  12 us
    ppermute x6, starting transfers between devices, shift_chip(): return lax.ppermute(value, 'col', pairs)  10.2 us
    ppermute x6, starting transfers between devices, flip_row(): return lax.ppermute(value, 'row', [(i, i ^ j) for i in range(n_row)])  7.83 us
    pallas_call x1, Pallas kernels, main_part(): pl.pallas_call(functools.partial(main_kernel, n_row, n_chip, slots, per_r...  5.81 us
    ppermute x8, waiting for transfers between devices, flip_core(): return lax.ppermute(value, 'col', [(i, i ^ 1) for i in range(n_col)])  4.78 us
    ppermute x6, waiting for transfers between devices, flip_row(): return lax.ppermute(value, 'row', [(i, i ^ j) for i in range(n_row)])  3.47 us
    pallas_call x1, Pallas kernels, tail_part(): pl.pallas_call(functools.partial(tail_kernel, n_row, n_chip, slots, per_c...  2.72 us
  transfers between devices with their start and end apart: 20, of which 9 were waited for; matrix products, arithmetic and copies ran while one was open for 0% of the time, Pallas kernels for 28%

profile of v7, /device:TPU:0, one launch (start us, length us, event | category | flops | bytes accessed | tf_op | source)
XLA Modules:
  0.0 63.6 jit_solution(15053932990672494021)
XLA Ops:
  0.0 2.1 %shard_map.46 = (bf16[256,256]{1,0:T(8,128)(2,1)}, bf16[256,256]{1,0:T(8,128)(2,1)}, bf16[256,256]{1,0:T(8,128)(2,1)}, bf16[256,256]{1,0:T(8,128)(2,1)}, bf16[52...) custom-call(bf16[4,2,256,128]{3,2,1,0:T(8,128)(2,1)} %bitcast.18, ...), custom_call_target="tpu_custom_call" | custom-call | tf_op jit(solution)/shard_map/pallas_call | solution.py:51
  2.2 2.9 %collective-permute-start = (bf16[256,256]{1,0:T(8,128)(2,1)}, bf16[256,256]{1,0:T(8,128)(2,1)S(1)}, u32[]{:S(2)}, u32[]{:S(2)}) collective-permute-start(bf16[256,256]{1,0:T(8,128)(2,1)} %get-tuple-element.37), channel_id=1, source_target_pairs={{0,8},{8,0},{16,24},{24,16},{1,9},{9,1},{17,25},{25,17},{2,10},{10... | collective-permute-start | bytes 393224 | tf_op jit(solution)/shard_map/ppermute | solution.py:422
  5.1 1.6 %collective-permute-start.3 = (bf16[528,128]{1,0:T(8,128)(2,1)}, bf16[528,128]{1,0:T(8,128)(2,1)S(1)}, u32[]{:S(2)}, u32[]{:S(2)}) collective-permute-start(bf16[528,128]{1,0:T(8,128)(2,1)} %get-tuple-element.41), channel_id=1, source_target_pairs={{0,2},{1,3},{2,4},{3,5},{4,6},{5,7},{6,0},{7,1},{8,10},{9,11},{10,... | collective-permute-start | bytes 405512 | tf_op jit(solution)/shard_map/ppermute | solution.py:426
  6.7 2.6 %collective-permute-start.4 = (bf16[528,128]{1,0:T(8,128)(2,1)}, bf16[528,128]{1,0:T(8,128)(2,1)S(1)}, u32[]{:S(2)}, u32[]{:S(2)}) collective-permute-start(bf16[528,128]{1,0:T(8,128)(2,1)} %get-tuple-element.42), channel_id=1, source_target_pairs={{0,4},{1,5},{2,6},{3,7},{4,0},{5,1},{6,2},{7,3},{8,12},{9,13},{10,... | collective-permute-start | bytes 405512 | tf_op jit(solution)/shard_map/ppermute | solution.py:426
  9.3 1.3 %collective-permute-start.5 = (bf16[528,128]{1,0:T(8,128)(2,1)}, bf16[528,128]{1,0:T(8,128)(2,1)S(1)}, u32[]{:S(2)}, u32[]{:S(2)}) collective-permute-start(bf16[528,128]{1,0:T(8,128)(2,1)} %get-tuple-element.43), channel_id=1, source_target_pairs={{0,6},{1,7},{2,0},{3,1},{4,2},{5,3},{6,4},{7,5},{8,14},{9,15},{10,... | collective-permute-start | bytes 405512 | tf_op jit(solution)/shard_map/ppermute | solution.py:426
  10.6 1.5 %collective-permute-start.1 = (bf16[256,256]{1,0:T(8,128)(2,1)}, bf16[256,256]{1,0:T(8,128)(2,1)S(1)}, u32[]{:S(2)}, u32[]{:S(2)}) collective-permute-start(bf16[256,256]{1,0:T(8,128)(2,1)} %get-tuple-element.38), channel_id=1, source_target_pairs={{0,16},{8,24},{16,0},{24,8},{1,17},{9,25},{17,1},{25,9},{2,18},{10... | collective-permute-start | bytes 393224 | tf_op jit(solution)/shard_map/ppermute | solution.py:422
  12.6 0.9 %copy-done = bf16[528,128]{1,0:T(8,128)(2,1)S(1)} copy-done((bf16[528,128]{1,0:T(8,128)(2,1)S(1)}, bf16[528,128]{1,0:T(8,128)(2,1)}, u32[]{:S(2)}) %copy-start) | copy-done | bytes 135192
  13.5 4.7 %shard_map.47.refs_1_ = f32[4096,2048]{1,0:T(8,128)} custom-call(bf16[528,128]{1,0:T(8,128)(2,1)S(1)} %copy-done), custom_call_target="tpu_custom_call" | custom-call | bytes 16777216 | tf_op jit(solution)/shard_map/pallas_call | solution.py:395
  18.8 0.5 collective-permute-start.9
  19.3 3.0 %collective-permute-start.6 = (bf16[1024,256]{1,0:T(8,128)(2,1)S(1)}, bf16[1024,256]{1,0:T(8,128)(2,1)S(1)}, u32[]{:S(2)}, u32[]{:S(2)}) collective-permute-start(bf16[1024,256]{1,0:T(8,128)(2,1)S(1)} %bitcast.14), channel_id=1, source_target_pairs={{0,2},{1,3},{2,4},{3,5},{4,6},{5,7},{6,0},{7,1},{8,10},{9,11},{10,... | collective-permute-start | bytes 1572872 | tf_op jit(solution)/shard_map/ppermute | solution.py:426
  22.8 1.7 %collective-permute-start.8 = (bf16[1056,256]{1,0:T(8,128)(2,1)S(1)}, bf16[1056,256]{1,0:T(8,128)(2,1)S(1)}, u32[]{:S(2)}, u32[]{:S(2)}) collective-permute-start(bf16[1056,256]{1,0:T(8,128)(2,1)S(1)} %pad.9), channel_id=1, source_target_pairs={{0,6},{1,7},{2,0},{3,1},{4,2},{5,3},{6,4},{7,5},{8,14},{9,15},{10,... | collective-permute-start | bytes 1622024 | tf_op jit(solution)/shard_map/ppermute | solution.py:426
  24.5 1.5 %collective-permute-start.13 = (bf16[4,528,128]{2,1,0:T(8,128)(2,1)S(1)}, bf16[4,528,128]{2,1,0:T(8,128)(2,1)S(1)}, u32[]{:S(2)}, u32[]{:S(2)}) collective-permute-start(bf16[4,528,128]{2,1,0:T(8,128)(2,1)S(1)} %pad_maximum_fusion.refs_6_), channel_id=1, source_target_pairs={{0,16},{8,24},{16,0},{24,8},{1,17},{9,25},{17,1},{25,9},{2,18},{10... | collective-permute-start | bytes 1622024 | tf_op jit(solution)/shard_map/ppermute | solution.py:422
  26.0 0.9 %collective-permute-start.14 = (bf16[4,528,128]{2,1,0:T(8,128)(2,1)S(1)}, bf16[4,528,128]{2,1,0:T(8,128)(2,1)S(1)}, u32[]{:S(2)}, u32[]{:S(2)}) collective-permute-start(bf16[4,528,128]{2,1,0:T(8,128)(2,1)S(1)} %pad_maximum_fusion.refs_6_), channel_id=1, source_target_pairs={{0,24},{8,16},{16,8},{24,0},{1,25},{9,17},{17,9},{25,1},{2,26},{10... | collective-permute-start | bytes 1622024 | tf_op jit(solution)/shard_map/ppermute | solution.py:422
  26.9 9.2 %collective-permute-done.6.refs_1_ = bf16[1024,256]{1,0:T(8,128)(2,1)S(1)} collective-permute-done((bf16[1024,256]{1,0:T(8,128)(2,1)S(1)}, bf16[1024,256]{1,0:T(8,128)(2,1)S(1)}, u32[]{:S(2)}, u32[]{:S(2)}) %collective-permute-start.6) | collective-permute-done | bytes 524320 | tf_op jit(solution)/shard_map/ppermute | solution.py:426
  36.1 1.3 %collective-permute-done.12.refs_7_ = bf16[4,528,128]{2,1,0:T(8,128)(2,1)S(1)} collective-permute-done((bf16[4,528,128]{2,1,0:T(8,128)(2,1)S(1)}, bf16[4,528,128]{2,1,0:T(8,128)(2,1)S(1)}, u32[]{:S(2)}, u32[]{:S(2)}) %collective-permute-start.12) | collective-permute-done | bytes 540704 | tf_op jit(solution)/shard_map/ppermute | solution.py:422
  37.4 7.3 %shard_map.48.refs_14_ = f32[4096,2048]{1,0:T(8,128)} custom-call(bf16[528,128]{1,0:T(8,128)(2,1)S(1)} %copy-done.1, f32[4096,2048]{1,0:T(8,128)} %shard_map.47.refs_1_), custom_call_target="tpu_custom_call", output_to_operand_aliasing={{}: (1, {})} | custom-call | bytes 16777216 | tf_op jit(solution)/shard_map/pallas_call | solution.py:395
  44.8 2.8 %collective-permute-done.8.refs_2_ = bf16[1056,256]{1,0:T(8,128)(2,1)S(1)} collective-permute-done((bf16[1056,256]{1,0:T(8,128)(2,1)S(1)}, bf16[1056,256]{1,0:T(8,128)(2,1)S(1)}, u32[]{:S(2)}, u32[]{:S(2)}) %collective-permute-start.8) | collective-permute-done | bytes 540704 | tf_op jit(solution)/shard_map/ppermute | solution.py:426
  47.6 1.9 %collective-permute-done.13.refs_8_ = bf16[4,528,128]{2,1,0:T(8,128)(2,1)S(1)} collective-permute-done((bf16[4,528,128]{2,1,0:T(8,128)(2,1)S(1)}, bf16[4,528,128]{2,1,0:T(8,128)(2,1)S(1)}, u32[]{:S(2)}, u32[]{:S(2)}) %collective-permute-start.13) | collective-permute-done | bytes 540704 | tf_op jit(solution)/shard_map/ppermute | solution.py:422
  50.0 1.4 %collective-permute-done.16.refs_11_ = bf16[4,528,128]{2,1,0:T(8,128)(2,1)S(1)} collective-permute-done((bf16[4,528,128]{2,1,0:T(8,128)(2,1)S(1)}, bf16[4,528,128]{2,1,0:T(8,128)(2,1)S(1)}, u32[]{:S(2)}, u32[]{:S(2)}) %collective-permute-start.16) | collective-permute-done | bytes 540704 | tf_op jit(solution)/shard_map/ppermute | solution.py:429
  51.5 0.8 %collective-permute-done.17.refs_12_ = bf16[4,528,128]{2,1,0:T(8,128)(2,1)S(1)} collective-permute-done((bf16[4,528,128]{2,1,0:T(8,128)(2,1)S(1)}, bf16[4,528,128]{2,1,0:T(8,128)(2,1)S(1)}, u32[]{:S(2)}, u32[]{:S(2)}) %collective-permute-start.17) | collective-permute-done | bytes 540704 | tf_op jit(solution)/shard_map/ppermute | solution.py:429
  52.2 0.8 %collective-permute-done.18.refs_13_ = bf16[4,528,128]{2,1,0:T(8,128)(2,1)S(1)} collective-permute-done((bf16[4,528,128]{2,1,0:T(8,128)(2,1)S(1)}, bf16[4,528,128]{2,1,0:T(8,128)(2,1)S(1)}, u32[]{:S(2)}, u32[]{:S(2)}) %collective-permute-start.18) | collective-permute-done | bytes 540704 | tf_op jit(solution)/shard_map/ppermute | solution.py:429
  53.0 5.8 %shard_map.49 = (f32[4096,2048]{1,0:T(8,128)}, bf16[8,512,128]{2,1,0:T(8,128)(2,1)S(1)}, s32[8,128]{1,0:T(8,128)S(1)}) custom-call(bf16[1024,256]{1,0:T(8,128)(2,1)S(1)} %bitcast.16, bf16[1024,256]{1,0:T(8,128)(2,1)S(1)} %collective-permute-done.6.refs_1_, bf16[1056,256]{1,0:T(8,128)(2,1)S(1)} %collective-permute-done.8.refs_2_, ...), custom_call_target="tpu_custom_call", output_to_operand_aliasing={{0}: (14, {})} | custom-call | tf_op jit(solution)/shard_map/pallas_call | solution.py:289
  59.0 1.8 %collective-permute-done.19.refs_1_ = bf16[1072,256]{1,0:T(8,128)(2,1)S(1)} collective-permute-done((bf16[1072,256]{1,0:T(8,128)(2,1)S(1)}, bf16[1072,256]{1,0:T(8,128)(2,1)S(1)}, u32[]{:S(2)}, u32[]{:S(2)}) %collective-permute-start.19) | collective-permute-done | bytes 548896 | tf_op jit(solution)/shard_map/ppermute | solution.py:429
  60.8 2.7 %shard_map.50 = f32[4096,2048]{1,0:T(8,128)} custom-call(s32[8,128]{1,0:T(8,128)S(1)} %get-tuple-element.63.plan, bf16[1072,256]{1,0:T(8,128)(2,1)S(1)} %collective-permute-done.7.refs_0_, bf16[1072,256]{1,0:T(8,128)(2,1)S(1)} %collective-permute-done.19.refs_1_, bf16[8,512,128]{2,1,0:T(8,128)(2,1)S(1)} %get-tuple-element.65.refs_2_, ...), custom_call_target="tpu_custom_call", output_to_operand_aliasing={{}: (4, {})} | custom-call | tf_op jit(solution)/shard_map/pallas_call | solution.py:357
  (31 shorter events, 2.3 us)
Async XLA Ops:
  2.2 10.0 %collective-permute-start = (bf16[256,256]{1,0:T(8,128)(2,1)}, bf16[256,256]{1,0:T(8,128)(2,1)S(1)}, u32[]{:S(2)}, u32[]{:S(2)}) collective-permute-start(bf16[256,256]{1,0:T(8,128)(2,1)} %get-tuple-element.37), channel_id=1, source_target_pairs={{0,8},{8,0},{16,24},{24,16},{1,9},{9,1},{17,25},{25,17},{2,10},{10... | collective-permute-start | bytes 393224 | tf_op jit(solution)/shard_map/ppermute | solution.py:422
  5.1 13.4 %collective-permute-start.3 = (bf16[528,128]{1,0:T(8,128)(2,1)}, bf16[528,128]{1,0:T(8,128)(2,1)S(1)}, u32[]{:S(2)}, u32[]{:S(2)}) collective-permute-start(bf16[528,128]{1,0:T(8,128)(2,1)} %get-tuple-element.41), channel_id=1, source_target_pairs={{0,2},{1,3},{2,4},{3,5},{4,6},{5,7},{6,0},{7,1},{8,10},{9,11},{10,... | collective-permute-start | bytes 405512 | tf_op jit(solution)/shard_map/ppermute | solution.py:426
  6.7 11.8 %collective-permute-start.4 = (bf16[528,128]{1,0:T(8,128)(2,1)}, bf16[528,128]{1,0:T(8,128)(2,1)S(1)}, u32[]{:S(2)}, u32[]{:S(2)}) collective-permute-start(bf16[528,128]{1,0:T(8,128)(2,1)} %get-tuple-element.42), channel_id=1, source_target_pairs={{0,4},{1,5},{2,6},{3,7},{4,0},{5,1},{6,2},{7,3},{8,12},{9,13},{10,... | collective-permute-start | bytes 405512 | tf_op jit(solution)/shard_map/ppermute | solution.py:426
  9.3 9.2 %collective-permute-start.5 = (bf16[528,128]{1,0:T(8,128)(2,1)}, bf16[528,128]{1,0:T(8,128)(2,1)S(1)}, u32[]{:S(2)}, u32[]{:S(2)}) collective-permute-start(bf16[528,128]{1,0:T(8,128)(2,1)} %get-tuple-element.43), channel_id=1, source_target_pairs={{0,6},{1,7},{2,0},{3,1},{4,2},{5,3},{6,4},{7,5},{8,14},{9,15},{10,... | collective-permute-start | bytes 405512 | tf_op jit(solution)/shard_map/ppermute | solution.py:426
  10.6 7.9 %collective-permute-start.1 = (bf16[256,256]{1,0:T(8,128)(2,1)}, bf16[256,256]{1,0:T(8,128)(2,1)S(1)}, u32[]{:S(2)}, u32[]{:S(2)}) collective-permute-start(bf16[256,256]{1,0:T(8,128)(2,1)} %get-tuple-element.38), channel_id=1, source_target_pairs={{0,16},{8,24},{16,0},{24,8},{1,17},{9,25},{17,1},{25,9},{2,18},{10... | collective-permute-start | bytes 393224 | tf_op jit(solution)/shard_map/ppermute | solution.py:422
  12.1 6.4 %collective-permute-start.2 = (bf16[256,256]{1,0:T(8,128)(2,1)}, bf16[256,256]{1,0:T(8,128)(2,1)S(1)}, u32[]{:S(2)}, u32[]{:S(2)}) collective-permute-start(bf16[256,256]{1,0:T(8,128)(2,1)} %get-tuple-element.39), channel_id=1, source_target_pairs={{0,24},{8,16},{16,8},{24,0},{1,25},{9,17},{17,9},{25,1},{2,26},{10... | collective-permute-start | bytes 393224 | tf_op jit(solution)/shard_map/ppermute | solution.py:422
  12.6 0.9 %copy-start = (bf16[528,128]{1,0:T(8,128)(2,1)S(1)}, bf16[528,128]{1,0:T(8,128)(2,1)}, u32[]{:S(2)}) copy-start(bf16[528,128]{1,0:T(8,128)(2,1)} %get-tuple-element.54.refs_0_) | copy-start | bytes 405508
  13.5 5.0 %copy-start.1 = (bf16[528,128]{1,0:T(8,128)(2,1)S(1)}, bf16[528,128]{1,0:T(8,128)(2,1)}, u32[]{:S(2)}) copy-start(bf16[528,128]{1,0:T(8,128)(2,1)} %get-tuple-element.54.refs_0_) | copy-start | bytes 405508
  13.5 5.2 %copy-start.2 = (bf16[256,256]{1,0:T(8,128)(2,1)S(1)}, bf16[256,256]{1,0:T(8,128)(2,1)}, u32[]{:S(2)}) copy-start(bf16[256,256]{1,0:T(8,128)(2,1)} %get-tuple-element.44) | copy-start | bytes 393220
  18.6 5.9 %collective-permute-start.10 = (bf16[4,528,128]{2,1,0:T(8,128)(2,1)S(1)}, bf16[4,528,128]{2,1,0:T(8,128)(2,1)S(1)}, u32[]{:S(2)}, u32[]{:S(2)}) collective-permute-start(bf16[4,528,128]{2,1,0:T(8,128)(2,1)S(1)} %pad_maximum_fusion.refs_6_), channel_id=1, source_target_pairs={{0,1},{1,0},{2,3},{3,2},{4,5},{5,4},{6,7},{7,6},{8,9},{9,8},{10,11... | collective-permute-start | bytes 1622024 | tf_op jit(solution)/shard_map/ppermute | solution.py:429
  18.8 5.8 %collective-permute-start.9 = (bf16[1024,256]{1,0:T(8,128)(2,1)S(1)}, bf16[1024,256]{1,0:T(8,128)(2,1)S(1)}, u32[]{:S(2)}, u32[]{:S(2)}) collective-permute-start(bf16[1024,256]{1,0:T(8,128)(2,1)S(1)} %bitcast.13), channel_id=1, source_target_pairs={{0,1},{1,0},{2,3},{3,2},{4,5},{5,4},{6,7},{7,6},{8,9},{9,8},{10,11... | collective-permute-start | bytes 1572872 | tf_op jit(solution)/shard_map/ppermute | solution.py:429
  19.3 16.8 %collective-permute-start.6 = (bf16[1024,256]{1,0:T(8,128)(2,1)S(1)}, bf16[1024,256]{1,0:T(8,128)(2,1)S(1)}, u32[]{:S(2)}, u32[]{:S(2)}) collective-permute-start(bf16[1024,256]{1,0:T(8,128)(2,1)S(1)} %bitcast.14), channel_id=1, source_target_pairs={{0,2},{1,3},{2,4},{3,5},{4,6},{5,7},{6,0},{7,1},{8,10},{9,11},{10,... | collective-permute-start | bytes 1572872 | tf_op jit(solution)/shard_map/ppermute | solution.py:426
  22.3 15.2 %collective-permute-start.12 = (bf16[4,528,128]{2,1,0:T(8,128)(2,1)S(1)}, bf16[4,528,128]{2,1,0:T(8,128)(2,1)S(1)}, u32[]{:S(2)}, u32[]{:S(2)}) collective-permute-start(bf16[4,528,128]{2,1,0:T(8,128)(2,1)S(1)} %pad_maximum_fusion.refs_6_), channel_id=1, source_target_pairs={{0,8},{8,0},{16,24},{24,16},{1,9},{9,1},{17,25},{25,17},{2,10},{10... | collective-permute-start | bytes 1622024 | tf_op jit(solution)/shard_map/ppermute | solution.py:422
  22.8 24.8 %collective-permute-start.8 = (bf16[1056,256]{1,0:T(8,128)(2,1)S(1)}, bf16[1056,256]{1,0:T(8,128)(2,1)S(1)}, u32[]{:S(2)}, u32[]{:S(2)}) collective-permute-start(bf16[1056,256]{1,0:T(8,128)(2,1)S(1)} %pad.9), channel_id=1, source_target_pairs={{0,6},{1,7},{2,0},{3,1},{4,2},{5,3},{6,4},{7,5},{8,14},{9,15},{10,... | collective-permute-start | bytes 1622024 | tf_op jit(solution)/shard_map/ppermute | solution.py:426
  24.5 25.0 %collective-permute-start.13 = (bf16[4,528,128]{2,1,0:T(8,128)(2,1)S(1)}, bf16[4,528,128]{2,1,0:T(8,128)(2,1)S(1)}, u32[]{:S(2)}, u32[]{:S(2)}) collective-permute-start(bf16[4,528,128]{2,1,0:T(8,128)(2,1)S(1)} %pad_maximum_fusion.refs_6_), channel_id=1, source_target_pairs={{0,16},{8,24},{16,0},{24,8},{1,17},{9,25},{17,1},{25,9},{2,18},{10... | collective-permute-start | bytes 1622024 | tf_op jit(solution)/shard_map/ppermute | solution.py:422
  26.0 23.5 %collective-permute-start.14 = (bf16[4,528,128]{2,1,0:T(8,128)(2,1)S(1)}, bf16[4,528,128]{2,1,0:T(8,128)(2,1)S(1)}, u32[]{:S(2)}, u32[]{:S(2)}) collective-permute-start(bf16[4,528,128]{2,1,0:T(8,128)(2,1)S(1)} %pad_maximum_fusion.refs_6_), channel_id=1, source_target_pairs={{0,24},{8,16},{16,8},{24,0},{1,25},{9,17},{17,9},{25,1},{2,26},{10... | collective-permute-start | bytes 1622024 | tf_op jit(solution)/shard_map/ppermute | solution.py:422
  36.1 11.5 %collective-permute-start.11 = (bf16[1024,256]{1,0:T(8,128)(2,1)S(1)}, bf16[1024,256]{1,0:T(8,128)(2,1)S(1)}, u32[]{:S(2)}, u32[]{:S(2)}) collective-permute-start(bf16[1024,256]{1,0:T(8,128)(2,1)S(1)} %collective-permute-done.6.refs_1_), channel_id=1, source_target_pairs={{0,1},{1,0},{2,3},{3,2},{4,5},{5,4},{6,7},{7,6},{8,9},{9,8},{10,11... | collective-permute-start | bytes 1572872 | tf_op jit(solution)/shard_map/ppermute | solution.py:429
  37.4 21.4 %collective-permute-start.7 = (bf16[1072,256]{1,0:T(8,128)(2,1)S(1)}, bf16[1072,256]{1,0:T(8,128)(2,1)S(1)}, u32[]{:S(2)}, u32[]{:S(2)}) collective-permute-start(bf16[1072,256]{1,0:T(8,128)(2,1)S(1)} %pad.8), channel_id=1, source_target_pairs={{0,2},{1,3},{2,4},{3,5},{4,6},{5,7},{6,0},{7,1},{8,10},{9,11},{10,... | collective-permute-start | bytes 1646600 | tf_op jit(solution)/shard_map/ppermute | solution.py:426
  47.6 2.4 %collective-permute-start.15 = (bf16[1056,256]{1,0:T(8,128)(2,1)S(1)}, bf16[1056,256]{1,0:T(8,128)(2,1)S(1)}, u32[]{:S(2)}, u32[]{:S(2)}) collective-permute-start(bf16[1056,256]{1,0:T(8,128)(2,1)S(1)} %collective-permute-done.8.refs_2_), channel_id=1, source_target_pairs={{0,1},{1,0},{2,3},{3,2},{4,5},{5,4},{6,7},{7,6},{8,9},{9,8},{10,11... | collective-permute-start | bytes 1622024 | tf_op jit(solution)/shard_map/ppermute | solution.py:429
  49.5 1.9 %collective-permute-start.16 = (bf16[4,528,128]{2,1,0:T(8,128)(2,1)S(1)}, bf16[4,528,128]{2,1,0:T(8,128)(2,1)S(1)}, u32[]{:S(2)}, u32[]{:S(2)}) collective-permute-start(bf16[4,528,128]{2,1,0:T(8,128)(2,1)S(1)} %collective-permute-done.12.refs_7_), channel_id=1, source_target_pairs={{0,1},{1,0},{2,3},{3,2},{4,5},{5,4},{6,7},{7,6},{8,9},{9,8},{10,11... | collective-permute-start | bytes 1622024 | tf_op jit(solution)/shard_map/ppermute | solution.py:429
  49.5 2.7 %collective-permute-start.17 = (bf16[4,528,128]{2,1,0:T(8,128)(2,1)S(1)}, bf16[4,528,128]{2,1,0:T(8,128)(2,1)S(1)}, u32[]{:S(2)}, u32[]{:S(2)}) collective-permute-start(bf16[4,528,128]{2,1,0:T(8,128)(2,1)S(1)} %collective-permute-done.13.refs_8_), channel_id=1, source_target_pairs={{0,1},{1,0},{2,3},{3,2},{4,5},{5,4},{6,7},{7,6},{8,9},{9,8},{10,11... | collective-permute-start | bytes 1622024 | tf_op jit(solution)/shard_map/ppermute | solution.py:429
  50.0 3.0 %collective-permute-start.18 = (bf16[4,528,128]{2,1,0:T(8,128)(2,1)S(1)}, bf16[4,528,128]{2,1,0:T(8,128)(2,1)S(1)}, u32[]{:S(2)}, u32[]{:S(2)}) collective-permute-start(bf16[4,528,128]{2,1,0:T(8,128)(2,1)S(1)} %collective-permute-done.14.refs_9_), channel_id=1, source_target_pairs={{0,1},{1,0},{2,3},{3,2},{4,5},{5,4},{6,7},{7,6},{8,9},{9,8},{10,11... | collective-permute-start | bytes 1622024 | tf_op jit(solution)/shard_map/ppermute | solution.py:429
  58.9 2.0 %collective-permute-start.19 = (bf16[1072,256]{1,0:T(8,128)(2,1)S(1)}, bf16[1072,256]{1,0:T(8,128)(2,1)S(1)}, u32[]{:S(2)}, u32[]{:S(2)}) collective-permute-start(bf16[1072,256]{1,0:T(8,128)(2,1)S(1)} %collective-permute-done.7.refs_0_), channel_id=1, source_target_pairs={{0,1},{1,0},{2,3},{3,2},{4,5},{5,4},{6,7},{7,6},{8,9},{9,8},{10,11... | collective-permute-start | bytes 1646600 | tf_op jit(solution)/shard_map/ppermute | solution.py:429

commit v8 on v7

--- a/solution.py
+++ b/solution.py
@@ -82,8 +82,9 @@
         pair = lax.broadcasted_iota(jnp.int32, (count, count), axis)
         station = lax.rem(pair, stations)
         s = lax.rem(station, n_chip)
-        number = station * len(column) + lax.div(pair, stations)
-        return s == n_chip // 2, number.astype(jnp.float32)
+        tail = s == n_chip // 2
+        number = jnp.where(tail, lax.div(station, n_chip), station) * len(column)
+        return tail, (number + lax.div(pair, stations)).astype(jnp.float32)
 
     tail_down, number_down = part_of(0)
     tail_across, number_across = part_of(1)
@@ -94,40 +95,34 @@
     final = (last == number_across[:1]).astype(jnp.float32)
     real = (other[:1] < none).astype(jnp.float32)
     place = other[:1] if by_tile else first
+    met = (tile == other) & jnp.logical_not(tail_down)
+    met = jnp.min(jnp.where(met, number_down, 1e6), axis=0, keepdims=True)
+    before = jnp.where(met < 1e6, other[:1] if by_tile else met, -1.0)
     code = 8.0 * place + 4.0 * final * real + 2.0 * fresh * real + fresh
-    return code.astype(jnp.int32), other[:1].astype(jnp.int32)
-
-
-def settle(plan, groups, stations, slots, acc, held, out_ref, per_col, load_sem, store_sem):
+    return [row.astype(jnp.int32) for row in (code, other[:1], before)]
+
+
+def each_hit(plan, columns, flag, act):
+    number = 0
+    for column in columns:
+        code = plan[0, column]
+        hit = lax.shift_right_logical(code, flag) & 1
+
+        @pl.when(hit == 1)
+        def _():
+            act(lax.shift_right_logical(code, 3), column)
+
+        number = number + hit
+    return number
+
+
+def settle(plan, groups, stations, slots, acc, base, out_ref, per_col, store_sem):
     width = acc.shape[-1]
     pairs = slots * slots
 
-    def copy(place, column, back):
+    def store(place, column):
         block = block_of(out_ref, plan[1, column], per_col, width)
-        if back:
-            return pltpu.make_async_copy(acc.at[place], block, store_sem)
-        return pltpu.make_async_copy(block, held.at[place], load_sem)
-
-    def each(columns, flag, act):
-        number = 0
-        for column in columns:
-            for n in range(pairs):
-                code = plan[0, column + n * stations]
-                hit = lax.shift_right_logical(code, flag) & 1
-
-                @pl.when(hit == 1)
-                def _():
-                    act(lax.shift_right_logical(code, 3), column + n * stations)
-
-                number = number + hit
-        return number
-
-    def wait(number, sem):
-        def step(index, carry):
-            pltpu.make_async_copy(acc.at[0], acc.at[0], sem).wait()
-            return carry
-
-        lax.fori_loop(0, number, step, 0)
+        pltpu.make_async_copy(acc.at[place], block, store_sem).start()
 
     def add(column, left, right):
         gram = jnp.dot(left(), right(), preferred_element_type=jnp.float32)
@@ -136,46 +131,32 @@
             place, fresh = lax.shift_right_logical(code, 3), code & 1
             i, j = divmod(n, slots)
             part = gram[i * width : (i + 1) * width, j * width : (j + 1) * width]
-            acc[place] = jnp.where(fresh == 1, part, acc[place] + part)
-
-    def walk(act):
-        total = 0
-        for steps, stations_of in groups:
-            if steps == 1:
-                total = total + act(stations_of(0))
-            else:
-                total = lax.fori_loop(
-                    0, steps, lambda step, sofar: sofar + act(stations_of(step)), total
-                )
-        return total
-
-    def columns_of(found):
-        return [column for column, _, _ in found]
-
-    def start_loads(found):
-        return each(columns_of(found), 1, lambda place, at: copy(place, at, False).start())
-
-    def add_all(found):
+            start = part if base is None else base[place] + part
+            acc[place] = jnp.where(fresh == 1, start, acc[place] + part)
+
+    def add_store(found):
         for column, left, right in found:
             add(column, left, right)
-        return 0
-
-    def add_store(found):
-        add_all(found)
-        return each(columns_of(found), 2, lambda place, at: copy(place, at, True).start())
-
-    def finish(place, column):
-        acc[place] = acc[place] + held[place]
-        copy(place, column, True).start()
-
-    if held is None:
-        number = walk(add_store)
-    else:
-        number = walk(start_loads)
-        walk(add_all)
-        wait(number, load_sem)
-        walk(lambda found: each(columns_of(found), 1, finish))
-    wait(number, store_sem)
+        columns = [column + n * stations for column, _, _ in found for n in range(pairs)]
+        return each_hit(plan, columns, 2, store)
+
+    total = 0
+    for steps, stations_of in groups:
+        if steps == 1:
+            total = total + add_store(stations_of(0))
+        else:
+            total = lax.fori_loop(
+                0, steps, lambda step, sofar: sofar + add_store(stations_of(step)), total
+            )
+    return total
+
+
+def drain(number, acc, sem):
+    def step(index, carry):
+        pltpu.make_async_copy(acc.at[0], acc.at[0], sem).wait()
+        return carry
+
+    lax.fori_loop(0, number, step, 0)
 
 
 def parts_of(n_chip):
@@ -195,9 +176,9 @@
     n_left = sum(map(len, early))
     n_source = n_left + len(pieces)
     sources = refs[:n_source]
-    out_ref, right_ref, plan = refs[n_source + 1 :][:3]
-    acc, left_buf, right_buf, fact_buf, code_buf = refs[n_source + 4 :][:5]
-    load_sem, code_sem, store_sem = refs[n_source + 9 :]
+    out_ref, right_ref, carry_ref, plan = refs[n_source + 1 :][:4]
+    acc, left_buf, right_buf, fact_buf, code_buf = refs[n_source + 5 :][:5]
+    load_sem, code_sem, store_sem = refs[n_source + 10 :]
     r = lax.axis_index("row")
     c = lax.axis_index("col")
     z, core = lax.div(c, CORES), lax.rem(c, CORES)
@@ -224,11 +205,10 @@
             meta = right_buf[which, s, slots * rows :].astype(jnp.float32)
             for i in range(slots + 1):
                 fact_buf[i, station : station + 1, :] = meta[i : i + 1]
-    code, tile_row = plan_of(
-        fact_buf, r, z, core, n_row, n_chip, slots, per_col, tiles, acc.shape[0] > tiles
-    )
-    code_buf[0:1, :] = code
-    code_buf[1:2, :] = tile_row
+    by_tile = acc.shape[0] > tiles
+    lines = plan_of(fact_buf, r, z, core, n_row, n_chip, slots, per_col, tiles, by_tile)
+    for n, line in enumerate(lines):
+        code_buf[n : n + 1, :] = line
     to_smem = pltpu.make_async_copy(code_buf, plan, code_sem)
     to_smem.start()
     kept = 0
@@ -262,7 +242,19 @@
         return n_row, stations_of
 
     groups = [group(other) for other in range(CORES)]
-    settle(plan, groups, stations, slots, acc, None, out_ref, per_col, None, store_sem)
+    number = settle(plan, groups, stations, slots, acc, None, out_ref, per_col, store_sem)
+
+    def hand_on(place, column):
+        before = plan[2, column]
+        carry_ref[place] = jnp.where(before < 0, 0.0, acc[jnp.maximum(before, 0)])
+
+    def hand_step(index, carry):
+        column = index * n_chip + n_chip // 2
+        each_hit(plan, [column + n * stations for n in range(slots * slots)], 1, hand_on)
+        return carry
+
+    lax.fori_loop(0, CORES * n_row, hand_step, 0)
+    drain(number, acc, store_sem)
 
 
 def main_part(left, right, pieces, out, n_row, per_row, per_col):
@@ -276,11 +268,13 @@
     stations = CORES * n_row * n_chip
     pairs = slots * slots * stations
     places = min(tiles + 1, pairs)
+    by_tile = places > tiles
+    tail_places = (places if by_tile else slots * slots * CORES * n_row, width, width)
     plan = (8, pairs)
     sources = [*flat, *right]
     anywhere = pl.BlockSpec(memory_space=pl.ANY)
     held = (
-        places * width * width * 4
+        (places + tail_places[0]) * width * width * 4
         + len(flat) * height * rows * 2
         + (stations + n_row * sum(map(len, late))) * (slots * rows + META) * width * 2
         + (slots + 1) * stations * width * 4
@@ -293,11 +287,13 @@
             jax.ShapeDtypeStruct(
                 (n_row * sum(map(len, late)), slots * rows, width), jnp.bfloat16
             ),
+            jax.ShapeDtypeStruct(tail_places, jnp.float32),
             jax.ShapeDtypeStruct(plan, jnp.int32),
         ],
         in_specs=[anywhere] * (len(sources) + 1),
         out_specs=[
             anywhere,
+            pl.BlockSpec(memory_space=pltpu.VMEM),
             pl.BlockSpec(memory_space=pltpu.VMEM),
             pl.BlockSpec(memory_space=pltpu.SMEM),
         ],
@@ -320,8 +316,8 @@
 def tail_kernel(n_row, n_chip, slots, per_col, plan, *refs):
     _, late = parts_of(n_chip)
     n_left = sum(map(len, late))
-    lefts, right_ref = refs[:n_left], refs[n_left]
-    out_ref, acc, held, load_sem, store_sem = refs[n_left + 2 :]
+    lefts, right_ref, base_ref = refs[:n_left], refs[n_left], refs[n_left + 1]
+    out_ref, acc, store_sem = refs[n_left + 3 :]
     rows, width = lefts[0].shape[-1], acc.shape[-1]
     stations = CORES * n_row * n_chip
 
@@ -340,35 +336,33 @@
 
                 found.append(((other * n_row + j) * n_chip + s, left, right))
     groups = [(1, lambda step: found)]
-    settle(plan, groups, stations, slots, acc, held, out_ref, per_col, load_sem, store_sem)
-
-
-def tail_part(left, right, plan, out, n_row, per_row, per_col):
+    number = settle(plan, groups, stations, slots, acc, base_ref, out_ref, per_col, store_sem)
+    drain(number, acc, store_sem)
+
+
+def tail_part(left, right, base, plan, out, n_row, per_row, per_col):
     flat = [*left[0], *left[1]]
     _, depth, width = right.shape
     slots = depth // flat[0].shape[1]
     stations = plan.shape[1] // slots**2
     n_chip = stations // (CORES * n_row)
-    places = (min(per_row * per_col + 1, plan.shape[1]), width, width)
     anywhere = pl.BlockSpec(memory_space=pl.ANY)
     vmem = pl.BlockSpec(memory_space=pltpu.VMEM)
     smem = pl.BlockSpec(memory_space=pltpu.SMEM)
-    held = 2 * places[0] * width * width * 4 + 2 * right.size * 2 + 2 * MIB * len(flat)
+    held = 3 * base.size * 4 + 2 * right.size * 2 + 2 * MIB * len(flat)
     return pl.pallas_call(
         functools.partial(tail_kernel, n_row, n_chip, slots, per_col),
         out_shape=jax.ShapeDtypeStruct(out.shape, out.dtype),
-        in_specs=[smem] + [vmem] * (len(flat) + 1) + [anywhere],
+        in_specs=[smem] + [vmem] * (len(flat) + 2) + [anywhere],
         out_specs=anywhere,
         scratch_shapes=[
-            pltpu.VMEM(places, jnp.float32),
-            pltpu.VMEM(places, jnp.float32),
-            pltpu.SemaphoreType.DMA,
+            pltpu.VMEM(base.shape, jnp.float32),
             pltpu.SemaphoreType.DMA,
         ],
-        input_output_aliases={len(flat) + 2: 0},
+        input_output_aliases={len(flat) + 3: 0},
         compiler_params=pltpu.CompilerParams(vmem_limit_bytes=held + 4 * MIB),
         cost_estimate=pl.CostEstimate(flops=0, bytes_accessed=0, transcendentals=0),
-    )(plan, *flat, right, out)
+    )(plan, *flat, right, base, out)
 
 
 def zero_kernel(first, count, *refs):
@@ -459,9 +453,11 @@
     sides += [own[1]] + [flip_core(x) for x in waiting]
     pieces = [(index, 0, n_chip) for index in range(CORES * n_row)]
     early = [[near[s] for s in sorted(near)], [swapped[s] for s in sorted(swapped)]]
-    out, tail_right, plan = main_part(early, sides, pieces, zeros, n_row, per_row, per_col)
+    out, tail_right, base, plan = main_part(early, sides, pieces, zeros, n_row, per_row, per_col)
     far, plan = after((far, plan))
-    return tail_part([[far], [flip_core(far)]], tail_right, plan, out, n_row, per_row, per_col)
+    return tail_part(
+        [[far], [flip_core(far)]], tail_right, base, plan, out, n_row, per_row, per_col
+    )
 
 
 def solution(mesh):

time: 64 us -> 63.1 us (0.986)
  Pallas kernels: 22.7 us -> 22 us
    pallas_call x1, Pallas kernels: 2.72 us -> 2.03 us  [tail_part(): pl.pallas_call(functools.partial(tail_kernel, n_row, n_chip, slots, per_c...]
  transfers between devices with their start and end apart: 20 -> 20, of which waited for: 9 -> 10; matrix products, arithmetic and copies ran while one was open for 0% -> 0% of each run, Pallas kernels for 28% -> 28%
where the time goes in v8:
time: 63.1 us; the launch traced here: 62.8 us
  Pallas kernels  22 us (35%)
  waiting for transfers between devices  20.3 us (32%)
  starting transfers between devices  19.3 us (31%)
  local copies, waits for them, and re-layouts  0.98 us (2%)
    ppermute x6, waiting for transfers between devices, shift_chip(): return lax.ppermute(value, 'col', pairs)  12.1 us
    pallas_call x2, Pallas kernels, zero_part(): pl.pallas_call(functools.partial(zero_kernel, first, number), out_shape=j...  12.1 us
    ppermute x6, starting transfers between devices, shift_chip(): return lax.ppermute(value, 'col', pairs)  10.2 us
    ppermute x6, starting transfers between devices, flip_row(): return lax.ppermute(value, 'row', [(i, i ^ j) for i in range(n_row)])  7.83 us
    pallas_call x1, Pallas kernels, main_part(): pl.pallas_call(functools.partial(main_kernel, n_row, n_chip, slots, per_r...  5.75 us
    ppermute x8, waiting for transfers between devices, flip_core(): return lax.ppermute(value, 'col', [(i, i ^ 1) for i in range(n_col)])  4.78 us
    ppermute x6, waiting for transfers between devices, flip_row(): return lax.ppermute(value, 'row', [(i, i ^ j) for i in range(n_row)])  3.47 us
    pallas_call x1, Pallas kernels, pack(): pl.pallas_call(functools.partial(pack_kernel, n_row, n_chip, slots), out_...  2.15 us
  transfers between devices with their start and end apart: 20, of which 10 were waited for; matrix products, arithmetic and copies ran while one was open for 0% of the time, Pallas kernels for 28%

profile of v8, /device:TPU:0, one launch (start us, length us, event | category | flops | bytes accessed | tf_op | source)
XLA Modules:
  0.0 62.8 jit_solution(15305083483907877520)
XLA Ops:
  0.0 2.1 %shard_map.46 = (bf16[256,256]{1,0:T(8,128)(2,1)}, bf16[256,256]{1,0:T(8,128)(2,1)}, bf16[256,256]{1,0:T(8,128)(2,1)}, bf16[256,256]{1,0:T(8,128)(2,1)}, bf16[52...) custom-call(bf16[4,2,256,128]{3,2,1,0:T(8,128)(2,1)} %bitcast.18, ...), custom_call_target="tpu_custom_call" | custom-call | tf_op jit(solution)/shard_map/pallas_call | solution.py:51
  2.2 2.9 %collective-permute-start = (bf16[256,256]{1,0:T(8,128)(2,1)}, bf16[256,256]{1,0:T(8,128)(2,1)S(1)}, u32[]{:S(2)}, u32[]{:S(2)}) collective-permute-start(bf16[256,256]{1,0:T(8,128)(2,1)} %get-tuple-element.38), channel_id=1, source_target_pairs={{0,8},{8,0},{16,24},{24,16},{1,9},{9,1},{17,25},{25,17},{2,10},{10... | collective-permute-start | bytes 393224 | tf_op jit(solution)/shard_map/ppermute | solution.py:416
  5.1 1.6 %collective-permute-start.3 = (bf16[528,128]{1,0:T(8,128)(2,1)}, bf16[528,128]{1,0:T(8,128)(2,1)S(1)}, u32[]{:S(2)}, u32[]{:S(2)}) collective-permute-start(bf16[528,128]{1,0:T(8,128)(2,1)} %get-tuple-element.42), channel_id=1, source_target_pairs={{0,2},{1,3},{2,4},{3,5},{4,6},{5,7},{6,0},{7,1},{8,10},{9,11},{10,... | collective-permute-start | bytes 405512 | tf_op jit(solution)/shard_map/ppermute | solution.py:420
  6.7 2.6 %collective-permute-start.4 = (bf16[528,128]{1,0:T(8,128)(2,1)}, bf16[528,128]{1,0:T(8,128)(2,1)S(1)}, u32[]{:S(2)}, u32[]{:S(2)}) collective-permute-start(bf16[528,128]{1,0:T(8,128)(2,1)} %get-tuple-element.43), channel_id=1, source_target_pairs={{0,4},{1,5},{2,6},{3,7},{4,0},{5,1},{6,2},{7,3},{8,12},{9,13},{10,... | collective-permute-start | bytes 405512 | tf_op jit(solution)/shard_map/ppermute | solution.py:420
  9.3 1.3 %collective-permute-start.5 = (bf16[528,128]{1,0:T(8,128)(2,1)}, bf16[528,128]{1,0:T(8,128)(2,1)S(1)}, u32[]{:S(2)}, u32[]{:S(2)}) collective-permute-start(bf16[528,128]{1,0:T(8,128)(2,1)} %get-tuple-element.44), channel_id=1, source_target_pairs={{0,6},{1,7},{2,0},{3,1},{4,2},{5,3},{6,4},{7,5},{8,14},{9,15},{10,... | collective-permute-start | bytes 405512 | tf_op jit(solution)/shard_map/ppermute | solution.py:420
  10.6 1.5 %collective-permute-start.1 = (bf16[256,256]{1,0:T(8,128)(2,1)}, bf16[256,256]{1,0:T(8,128)(2,1)S(1)}, u32[]{:S(2)}, u32[]{:S(2)}) collective-permute-start(bf16[256,256]{1,0:T(8,128)(2,1)} %get-tuple-element.39), channel_id=1, source_target_pairs={{0,16},{8,24},{16,0},{24,8},{1,17},{9,25},{17,1},{25,9},{2,18},{10... | collective-permute-start | bytes 393224 | tf_op jit(solution)/shard_map/ppermute | solution.py:416
  12.6 0.9 %copy-done = bf16[528,128]{1,0:T(8,128)(2,1)S(1)} copy-done((bf16[528,128]{1,0:T(8,128)(2,1)S(1)}, bf16[528,128]{1,0:T(8,128)(2,1)}, u32[]{:S(2)}) %copy-start) | copy-done | bytes 135192
  13.5 4.7 %shard_map.47.refs_1_ = f32[4096,2048]{1,0:T(8,128)} custom-call(bf16[528,128]{1,0:T(8,128)(2,1)S(1)} %copy-done), custom_call_target="tpu_custom_call" | custom-call | bytes 16777216 | tf_op jit(solution)/shard_map/pallas_call | solution.py:389
  18.8 0.5 collective-permute-start.9
  19.3 3.0 %collective-permute-start.6 = (bf16[1024,256]{1,0:T(8,128)(2,1)S(1)}, bf16[1024,256]{1,0:T(8,128)(2,1)S(1)}, u32[]{:S(2)}, u32[]{:S(2)}) collective-permute-start(bf16[1024,256]{1,0:T(8,128)(2,1)S(1)} %bitcast.14), channel_id=1, source_target_pairs={{0,2},{1,3},{2,4},{3,5},{4,6},{5,7},{6,0},{7,1},{8,10},{9,11},{10,... | collective-permute-start | bytes 1572872 | tf_op jit(solution)/shard_map/ppermute | solution.py:420
  22.8 1.7 %collective-permute-start.8 = (bf16[1056,256]{1,0:T(8,128)(2,1)S(1)}, bf16[1056,256]{1,0:T(8,128)(2,1)S(1)}, u32[]{:S(2)}, u32[]{:S(2)}) collective-permute-start(bf16[1056,256]{1,0:T(8,128)(2,1)S(1)} %pad.9), channel_id=1, source_target_pairs={{0,6},{1,7},{2,0},{3,1},{4,2},{5,3},{6,4},{7,5},{8,14},{9,15},{10,... | collective-permute-start | bytes 1622024 | tf_op jit(solution)/shard_map/ppermute | solution.py:420
  24.5 1.5 %collective-permute-start.13 = (bf16[4,528,128]{2,1,0:T(8,128)(2,1)S(1)}, bf16[4,528,128]{2,1,0:T(8,128)(2,1)S(1)}, u32[]{:S(2)}, u32[]{:S(2)}) collective-permute-start(bf16[4,528,128]{2,1,0:T(8,128)(2,1)S(1)} %pad_maximum_fusion.refs_6_), channel_id=1, source_target_pairs={{0,16},{8,24},{16,0},{24,8},{1,17},{9,25},{17,1},{25,9},{2,18},{10... | collective-permute-start | bytes 1622024 | tf_op jit(solution)/shard_map/ppermute | solution.py:416
  26.0 0.9 %collective-permute-start.14 = (bf16[4,528,128]{2,1,0:T(8,128)(2,1)S(1)}, bf16[4,528,128]{2,1,0:T(8,128)(2,1)S(1)}, u32[]{:S(2)}, u32[]{:S(2)}) collective-permute-start(bf16[4,528,128]{2,1,0:T(8,128)(2,1)S(1)} %pad_maximum_fusion.refs_6_), channel_id=1, source_target_pairs={{0,24},{8,16},{16,8},{24,0},{1,25},{9,17},{17,9},{25,1},{2,26},{10... | collective-permute-start | bytes 1622024 | tf_op jit(solution)/shard_map/ppermute | solution.py:416
  26.9 9.2 %collective-permute-done.6.refs_1_ = bf16[1024,256]{1,0:T(8,128)(2,1)S(1)} collective-permute-done((bf16[1024,256]{1,0:T(8,128)(2,1)S(1)}, bf16[1024,256]{1,0:T(8,128)(2,1)S(1)}, u32[]{:S(2)}, u32[]{:S(2)}) %collective-permute-start.6) | collective-permute-done | bytes 524320 | tf_op jit(solution)/shard_map/ppermute | solution.py:420
  36.1 1.3 %collective-permute-done.12.refs_7_ = bf16[4,528,128]{2,1,0:T(8,128)(2,1)S(1)} collective-permute-done((bf16[4,528,128]{2,1,0:T(8,128)(2,1)S(1)}, bf16[4,528,128]{2,1,0:T(8,128)(2,1)S(1)}, u32[]{:S(2)}, u32[]{:S(2)}) %collective-permute-start.12) | collective-permute-done | bytes 540704 | tf_op jit(solution)/shard_map/ppermute | solution.py:416
  37.4 7.3 %shard_map.48.refs_14_ = f32[4096,2048]{1,0:T(8,128)} custom-call(bf16[528,128]{1,0:T(8,128)(2,1)S(1)} %copy-done.1, f32[4096,2048]{1,0:T(8,128)} %shard_map.47.refs_1_), custom_call_target="tpu_custom_call", output_to_operand_aliasing={{}: (1, {})} | custom-call | bytes 16777216 | tf_op jit(solution)/shard_map/pallas_call | solution.py:389
  44.8 2.8 %collective-permute-done.8.refs_2_ = bf16[1056,256]{1,0:T(8,128)(2,1)S(1)} collective-permute-done((bf16[1056,256]{1,0:T(8,128)(2,1)S(1)}, bf16[1056,256]{1,0:T(8,128)(2,1)S(1)}, u32[]{:S(2)}, u32[]{:S(2)}) %collective-permute-start.8) | collective-permute-done | bytes 540704 | tf_op jit(solution)/shard_map/ppermute | solution.py:420
  47.6 1.9 %collective-permute-done.13.refs_8_ = bf16[4,528,128]{2,1,0:T(8,128)(2,1)S(1)} collective-permute-done((bf16[4,528,128]{2,1,0:T(8,128)(2,1)S(1)}, bf16[4,528,128]{2,1,0:T(8,128)(2,1)S(1)}, u32[]{:S(2)}, u32[]{:S(2)}) %collective-permute-start.13) | collective-permute-done | bytes 540704 | tf_op jit(solution)/shard_map/ppermute | solution.py:416
  50.0 1.4 %collective-permute-done.16.refs_11_ = bf16[4,528,128]{2,1,0:T(8,128)(2,1)S(1)} collective-permute-done((bf16[4,528,128]{2,1,0:T(8,128)(2,1)S(1)}, bf16[4,528,128]{2,1,0:T(8,128)(2,1)S(1)}, u32[]{:S(2)}, u32[]{:S(2)}) %collective-permute-start.16) | collective-permute-done | bytes 540704 | tf_op jit(solution)/shard_map/ppermute | solution.py:423
  51.5 0.8 %collective-permute-done.17.refs_12_ = bf16[4,528,128]{2,1,0:T(8,128)(2,1)S(1)} collective-permute-done((bf16[4,528,128]{2,1,0:T(8,128)(2,1)S(1)}, bf16[4,528,128]{2,1,0:T(8,128)(2,1)S(1)}, u32[]{:S(2)}, u32[]{:S(2)}) %collective-permute-start.17) | collective-permute-done | bytes 540704 | tf_op jit(solution)/shard_map/ppermute | solution.py:423
  52.2 0.8 %collective-permute-done.18.refs_13_ = bf16[4,528,128]{2,1,0:T(8,128)(2,1)S(1)} collective-permute-done((bf16[4,528,128]{2,1,0:T(8,128)(2,1)S(1)}, bf16[4,528,128]{2,1,0:T(8,128)(2,1)S(1)}, u32[]{:S(2)}, u32[]{:S(2)}) %collective-permute-start.18) | collective-permute-done | bytes 540704 | tf_op jit(solution)/shard_map/ppermute | solution.py:423
  53.0 5.8 %shard_map.49 = (f32[4096,2048]{1,0:T(8,128)}, bf16[8,512,128]{2,1,0:T(8,128)(2,1)S(1)}, f32[32,128,128]{2,1,0:T(8,128)S(1)}, s32[8,128]{1,0:T(8,128)S(1)}) custom-call(bf16[1024,256]{1,0:T(8,128)(2,1)S(1)} %bitcast.16, bf16[1024,256]{1,0:T(8,128)(2,1)S(1)} %collective-permute-done.6.refs_1_, ...), custom_call_target="tpu_custom_call", output_to_operand_aliasing={{0}: (14, {})} | custom-call | tf_op jit(solution)/shard_map/pallas_call | solution.py:283
  59.0 1.8 %collective-permute-done.19.refs_1_ = bf16[1072,256]{1,0:T(8,128)(2,1)S(1)} collective-permute-done((bf16[1072,256]{1,0:T(8,128)(2,1)S(1)}, bf16[1072,256]{1,0:T(8,128)(2,1)S(1)}, u32[]{:S(2)}, u32[]{:S(2)}) %collective-permute-start.19) | collective-permute-done | bytes 548896 | tf_op jit(solution)/shard_map/ppermute | solution.py:423
  60.8 2.0 %shard_map.50 = f32[4096,2048]{1,0:T(8,128)} custom-call(s32[8,128]{1,0:T(8,128)S(1)} %get-tuple-element.64.plan, bf16[1072,256]{1,0:T(8,128)(2,1)S(1)} %collective-permute-done.7.refs_0_, bf16[1072,256]{1,0:T(8,128)(2,1)S(1)} %collective-permute-done.19.refs_1_, bf16[8,512,128]{2,1,0:T(8,128)(2,1)S(1)} %get-tuple-element.66.refs_2_, ...), custom_call_target="tpu_custom_call", output_to_operand_aliasing={{}: (5, {})} | custom-call | tf_op jit(solution)/shard_map/pallas_call | solution.py:353
  (31 shorter events, 2.3 us)
Async XLA Ops:
  2.2 10.0 %collective-permute-start = (bf16[256,256]{1,0:T(8,128)(2,1)}, bf16[256,256]{1,0:T(8,128)(2,1)S(1)}, u32[]{:S(2)}, u32[]{:S(2)}) collective-permute-start(bf16[256,256]{1,0:T(8,128)(2,1)} %get-tuple-element.38), channel_id=1, source_target_pairs={{0,8},{8,0},{16,24},{24,16},{1,9},{9,1},{17,25},{25,17},{2,10},{10... | collective-permute-start | bytes 393224 | tf_op jit(solution)/shard_map/ppermute | solution.py:416
  5.1 13.4 %collective-permute-start.3 = (bf16[528,128]{1,0:T(8,128)(2,1)}, bf16[528,128]{1,0:T(8,128)(2,1)S(1)}, u32[]{:S(2)}, u32[]{:S(2)}) collective-permute-start(bf16[528,128]{1,0:T(8,128)(2,1)} %get-tuple-element.42), channel_id=1, source_target_pairs={{0,2},{1,3},{2,4},{3,5},{4,6},{5,7},{6,0},{7,1},{8,10},{9,11},{10,... | collective-permute-start | bytes 405512 | tf_op jit(solution)/shard_map/ppermute | solution.py:420
  6.7 11.8 %collective-permute-start.4 = (bf16[528,128]{1,0:T(8,128)(2,1)}, bf16[528,128]{1,0:T(8,128)(2,1)S(1)}, u32[]{:S(2)}, u32[]{:S(2)}) collective-permute-start(bf16[528,128]{1,0:T(8,128)(2,1)} %get-tuple-element.43), channel_id=1, source_target_pairs={{0,4},{1,5},{2,6},{3,7},{4,0},{5,1},{6,2},{7,3},{8,12},{9,13},{10,... | collective-permute-start | bytes 405512 | tf_op jit(solution)/shard_map/ppermute | solution.py:420
  9.3 9.2 %collective-permute-start.5 = (bf16[528,128]{1,0:T(8,128)(2,1)}, bf16[528,128]{1,0:T(8,128)(2,1)S(1)}, u32[]{:S(2)}, u32[]{:S(2)}) collective-permute-start(bf16[528,128]{1,0:T(8,128)(2,1)} %get-tuple-element.44), channel_id=1, source_target_pairs={{0,6},{1,7},{2,0},{3,1},{4,2},{5,3},{6,4},{7,5},{8,14},{9,15},{10,... | collective-permute-start | bytes 405512 | tf_op jit(solution)/shard_map/ppermute | solution.py:420
  10.6 7.9 %collective-permute-start.1 = (bf16[256,256]{1,0:T(8,128)(2,1)}, bf16[256,256]{1,0:T(8,128)(2,1)S(1)}, u32[]{:S(2)}, u32[]{:S(2)}) collective-permute-start(bf16[256,256]{1,0:T(8,128)(2,1)} %get-tuple-element.39), channel_id=1, source_target_pairs={{0,16},{8,24},{16,0},{24,8},{1,17},{9,25},{17,1},{25,9},{2,18},{10... | collective-permute-start | bytes 393224 | tf_op jit(solution)/shard_map/ppermute | solution.py:416
  12.1 6.4 %collective-permute-start.2 = (bf16[256,256]{1,0:T(8,128)(2,1)}, bf16[256,256]{1,0:T(8,128)(2,1)S(1)}, u32[]{:S(2)}, u32[]{:S(2)}) collective-permute-start(bf16[256,256]{1,0:T(8,128)(2,1)} %get-tuple-element.40), channel_id=1, source_target_pairs={{0,24},{8,16},{16,8},{24,0},{1,25},{9,17},{17,9},{25,1},{2,26},{10... | collective-permute-start | bytes 393224 | tf_op jit(solution)/shard_map/ppermute | solution.py:416
  12.6 0.9 %copy-start = (bf16[528,128]{1,0:T(8,128)(2,1)S(1)}, bf16[528,128]{1,0:T(8,128)(2,1)}, u32[]{:S(2)}) copy-start(bf16[528,128]{1,0:T(8,128)(2,1)} %get-tuple-element.55.refs_0_) | copy-start | bytes 405508
  13.5 5.0 %copy-start.1 = (bf16[528,128]{1,0:T(8,128)(2,1)S(1)}, bf16[528,128]{1,0:T(8,128)(2,1)}, u32[]{:S(2)}) copy-start(bf16[528,128]{1,0:T(8,128)(2,1)} %get-tuple-element.55.refs_0_) | copy-start | bytes 405508
  13.5 5.2 %copy-start.2 = (bf16[256,256]{1,0:T(8,128)(2,1)S(1)}, bf16[256,256]{1,0:T(8,128)(2,1)}, u32[]{:S(2)}) copy-start(bf16[256,256]{1,0:T(8,128)(2,1)} %get-tuple-element.45) | copy-start | bytes 393220
  18.6 5.9 %collective-permute-start.10 = (bf16[4,528,128]{2,1,0:T(8,128)(2,1)S(1)}, bf16[4,528,128]{2,1,0:T(8,128)(2,1)S(1)}, u32[]{:S(2)}, u32[]{:S(2)}) collective-permute-start(bf16[4,528,128]{2,1,0:T(8,128)(2,1)S(1)} %pad_maximum_fusion.refs_6_), channel_id=1, source_target_pairs={{0,1},{1,0},{2,3},{3,2},{4,5},{5,4},{6,7},{7,6},{8,9},{9,8},{10,11... | collective-permute-start | bytes 1622024 | tf_op jit(solution)/shard_map/ppermute | solution.py:423
  18.8 5.8 %collective-permute-start.9 = (bf16[1024,256]{1,0:T(8,128)(2,1)S(1)}, bf16[1024,256]{1,0:T(8,128)(2,1)S(1)}, u32[]{:S(2)}, u32[]{:S(2)}) collective-permute-start(bf16[1024,256]{1,0:T(8,128)(2,1)S(1)} %bitcast.13), channel_id=1, source_target_pairs={{0,1},{1,0},{2,3},{3,2},{4,5},{5,4},{6,7},{7,6},{8,9},{9,8},{10,11... | collective-permute-start | bytes 1572872 | tf_op jit(solution)/shard_map/ppermute | solution.py:423
  19.3 16.8 %collective-permute-start.6 = (bf16[1024,256]{1,0:T(8,128)(2,1)S(1)}, bf16[1024,256]{1,0:T(8,128)(2,1)S(1)}, u32[]{:S(2)}, u32[]{:S(2)}) collective-permute-start(bf16[1024,256]{1,0:T(8,128)(2,1)S(1)} %bitcast.14), channel_id=1, source_target_pairs={{0,2},{1,3},{2,4},{3,5},{4,6},{5,7},{6,0},{7,1},{8,10},{9,11},{10,... | collective-permute-start | bytes 1572872 | tf_op jit(solution)/shard_map/ppermute | solution.py:420
  22.3 15.2 %collective-permute-start.12 = (bf16[4,528,128]{2,1,0:T(8,128)(2,1)S(1)}, bf16[4,528,128]{2,1,0:T(8,128)(2,1)S(1)}, u32[]{:S(2)}, u32[]{:S(2)}) collective-permute-start(bf16[4,528,128]{2,1,0:T(8,128)(2,1)S(1)} %pad_maximum_fusion.refs_6_), channel_id=1, source_target_pairs={{0,8},{8,0},{16,24},{24,16},{1,9},{9,1},{17,25},{25,17},{2,10},{10... | collective-permute-start | bytes 1622024 | tf_op jit(solution)/shard_map/ppermute | solution.py:416
  22.8 24.8 %collective-permute-start.8 = (bf16[1056,256]{1,0:T(8,128)(2,1)S(1)}, bf16[1056,256]{1,0:T(8,128)(2,1)S(1)}, u32[]{:S(2)}, u32[]{:S(2)}) collective-permute-start(bf16[1056,256]{1,0:T(8,128)(2,1)S(1)} %pad.9), channel_id=1, source_target_pairs={{0,6},{1,7},{2,0},{3,1},{4,2},{5,3},{6,4},{7,5},{8,14},{9,15},{10,... | collective-permute-start | bytes 1622024 | tf_op jit(solution)/shard_map/ppermute | solution.py:420
  24.5 25.0 %collective-permute-start.13 = (bf16[4,528,128]{2,1,0:T(8,128)(2,1)S(1)}, bf16[4,528,128]{2,1,0:T(8,128)(2,1)S(1)}, u32[]{:S(2)}, u32[]{:S(2)}) collective-permute-start(bf16[4,528,128]{2,1,0:T(8,128)(2,1)S(1)} %pad_maximum_fusion.refs_6_), channel_id=1, source_target_pairs={{0,16},{8,24},{16,0},{24,8},{1,17},{9,25},{17,1},{25,9},{2,18},{10... | collective-permute-start | bytes 1622024 | tf_op jit(solution)/shard_map/ppermute | solution.py:416
  26.0 23.5 %collective-permute-start.14 = (bf16[4,528,128]{2,1,0:T(8,128)(2,1)S(1)}, bf16[4,528,128]{2,1,0:T(8,128)(2,1)S(1)}, u32[]{:S(2)}, u32[]{:S(2)}) collective-permute-start(bf16[4,528,128]{2,1,0:T(8,128)(2,1)S(1)} %pad_maximum_fusion.refs_6_), channel_id=1, source_target_pairs={{0,24},{8,16},{16,8},{24,0},{1,25},{9,17},{17,9},{25,1},{2,26},{10... | collective-permute-start | bytes 1622024 | tf_op jit(solution)/shard_map/ppermute | solution.py:416
  36.1 11.5 %collective-permute-start.11 = (bf16[1024,256]{1,0:T(8,128)(2,1)S(1)}, bf16[1024,256]{1,0:T(8,128)(2,1)S(1)}, u32[]{:S(2)}, u32[]{:S(2)}) collective-permute-start(bf16[1024,256]{1,0:T(8,128)(2,1)S(1)} %collective-permute-done.6.refs_1_), channel_id=1, source_target_pairs={{0,1},{1,0},{2,3},{3,2},{4,5},{5,4},{6,7},{7,6},{8,9},{9,8},{10,11... | collective-permute-start | bytes 1572872 | tf_op jit(solution)/shard_map/ppermute | solution.py:423
  37.4 21.4 %collective-permute-start.7 = (bf16[1072,256]{1,0:T(8,128)(2,1)S(1)}, bf16[1072,256]{1,0:T(8,128)(2,1)S(1)}, u32[]{:S(2)}, u32[]{:S(2)}) collective-permute-start(bf16[1072,256]{1,0:T(8,128)(2,1)S(1)} %pad.8), channel_id=1, source_target_pairs={{0,2},{1,3},{2,4},{3,5},{4,6},{5,7},{6,0},{7,1},{8,10},{9,11},{10,... | collective-permute-start | bytes 1646600 | tf_op jit(solution)/shard_map/ppermute | solution.py:420
  47.6 2.4 %collective-permute-start.15 = (bf16[1056,256]{1,0:T(8,128)(2,1)S(1)}, bf16[1056,256]{1,0:T(8,128)(2,1)S(1)}, u32[]{:S(2)}, u32[]{:S(2)}) collective-permute-start(bf16[1056,256]{1,0:T(8,128)(2,1)S(1)} %collective-permute-done.8.refs_2_), channel_id=1, source_target_pairs={{0,1},{1,0},{2,3},{3,2},{4,5},{5,4},{6,7},{7,6},{8,9},{9,8},{10,11... | collective-permute-start | bytes 1622024 | tf_op jit(solution)/shard_map/ppermute | solution.py:423
  49.5 1.9 %collective-permute-start.16 = (bf16[4,528,128]{2,1,0:T(8,128)(2,1)S(1)}, bf16[4,528,128]{2,1,0:T(8,128)(2,1)S(1)}, u32[]{:S(2)}, u32[]{:S(2)}) collective-permute-start(bf16[4,528,128]{2,1,0:T(8,128)(2,1)S(1)} %collective-permute-done.12.refs_7_), channel_id=1, source_target_pairs={{0,1},{1,0},{2,3},{3,2},{4,5},{5,4},{6,7},{7,6},{8,9},{9,8},{10,11... | collective-permute-start | bytes 1622024 | tf_op jit(solution)/shard_map/ppermute | solution.py:423
  49.5 2.7 %collective-permute-start.17 = (bf16[4,528,128]{2,1,0:T(8,128)(2,1)S(1)}, bf16[4,528,128]{2,1,0:T(8,128)(2,1)S(1)}, u32[]{:S(2)}, u32[]{:S(2)}) collective-permute-start(bf16[4,528,128]{2,1,0:T(8,128)(2,1)S(1)} %collective-permute-done.13.refs_8_), channel_id=1, source_target_pairs={{0,1},{1,0},{2,3},{3,2},{4,5},{5,4},{6,7},{7,6},{8,9},{9,8},{10,11... | collective-permute-start | bytes 1622024 | tf_op jit(solution)/shard_map/ppermute | solution.py:423
  50.0 3.0 %collective-permute-start.18 = (bf16[4,528,128]{2,1,0:T(8,128)(2,1)S(1)}, bf16[4,528,128]{2,1,0:T(8,128)(2,1)S(1)}, u32[]{:S(2)}, u32[]{:S(2)}) collective-permute-start(bf16[4,528,128]{2,1,0:T(8,128)(2,1)S(1)} %collective-permute-done.14.refs_9_), channel_id=1, source_target_pairs={{0,1},{1,0},{2,3},{3,2},{4,5},{5,4},{6,7},{7,6},{8,9},{9,8},{10,11... | collective-permute-start | bytes 1622024 | tf_op jit(solution)/shard_map/ppermute | solution.py:423
  58.9 1.9 %collective-permute-start.19 = (bf16[1072,256]{1,0:T(8,128)(2,1)S(1)}, bf16[1072,256]{1,0:T(8,128)(2,1)S(1)}, u32[]{:S(2)}, u32[]{:S(2)}) collective-permute-start(bf16[1072,256]{1,0:T(8,128)(2,1)S(1)} %collective-permute-done.7.refs_0_), channel_id=1, source_target_pairs={{0,1},{1,0},{2,3},{3,2},{4,5},{5,4},{6,7},{7,6},{8,9},{9,8},{10,11... | collective-permute-start | bytes 1646600 | tf_op jit(solution)/shard_map/ppermute | solution.py:423

commit v9 on v8

--- a/solution.py
+++ b/solution.py
@@ -171,38 +171,25 @@
     return out_ref.at[rows, columns]
 
 
-def main_kernel(n_row, n_chip, slots, per_row, per_col, pieces, *refs):
+def main_kernel(n_row, n_chip, slots, per_row, per_col, *refs):
     early, late = parts_of(n_chip)
     n_left = sum(map(len, early))
-    n_source = n_left + len(pieces)
+    n_source = n_left + CORES * n_row
     sources = refs[:n_source]
     out_ref, right_ref, carry_ref, plan = refs[n_source + 1 :][:4]
-    acc, left_buf, right_buf, fact_buf, code_buf = refs[n_source + 5 :][:5]
-    load_sem, code_sem, store_sem = refs[n_source + 10 :]
+    acc, fact_buf, code_buf, code_sem, store_sem = refs[n_source + 5 :]
     r = lax.axis_index("row")
     c = lax.axis_index("col")
     z, core = lax.div(c, CORES), lax.rem(c, CORES)
-    rows, width = left_buf.shape[-1], acc.shape[-1]
+    lefts, rights = sources[:n_left], sources[n_left:]
+    rows, width = lefts[0].shape[-1], acc.shape[-1]
     tiles = per_row * per_col
     stations = CORES * n_row * n_chip
 
-    def load(index):
-        if index < n_left:
-            target = left_buf.at[index]
-            source = sources[index].at[pl.ds(0, target.shape[0])]
-        else:
-            which, first, number = pieces[index - n_left]
-            target = right_buf.at[which, pl.ds(first, number)]
-            source = sources[index]
-        return pltpu.make_async_copy(source, target, load_sem.at[index])
-
-    for index in [*range(n_left, n_source), *range(n_left)]:
-        load(index).start()
-    for index, (which, first, number) in enumerate(pieces):
-        load(n_left + index).wait()
-        for s in range(first, first + number):
-            station = which * n_chip + s
-            meta = right_buf[which, s, slots * rows :].astype(jnp.float32)
+    for index in range(CORES * n_row):
+        for s in range(n_chip):
+            station = index * n_chip + s
+            meta = rights[index][s, slots * rows :].astype(jnp.float32)
             for i in range(slots + 1):
                 fact_buf[i, station : station + 1, :] = meta[i : i + 1]
     by_tile = acc.shape[0] > tiles
@@ -215,33 +202,29 @@
     for other in range(CORES):
         for j in range(n_row):
             for s in late[other]:
-                right_ref[kept] = right_buf[other * n_row + j, s, : slots * rows]
+                right_ref[kept] = rights[other * n_row + j][s, : slots * rows]
                 kept += 1
-    for index in range(n_left):
-        load(index).wait()
     to_smem.wait()
 
-    def group(other):
-        base = len(early[0]) * other
-
-        def stations_of(j):
-            index = other * n_row + j
-
-            def station(m, s):
-                def left():
-                    return left_buf[base + m, pl.ds(j * slots * width, slots * width)]
-
-                def right():
-                    tiles = [right_buf[index, s, i * rows : (i + 1) * rows] for i in range(slots)]
-                    return jnp.concatenate(tiles, axis=1)
-
-                return index * n_chip + s, left, right
-
-            return [station(m, s) for m, s in enumerate(early[other])]
-
-        return n_row, stations_of
-
-    groups = [group(other) for other in range(CORES)]
+    def group(other, j):
+        index = other * n_row + j
+
+        def station(m, s):
+            first = j * slots * width
+
+            def left():
+                return lefts[len(early[0]) * other + m][first : first + slots * width]
+
+            def right():
+                tiles = [rights[index][s, i * rows : (i + 1) * rows] for i in range(slots)]
+                return jnp.concatenate(tiles, axis=1)
+
+            return index * n_chip + s, left, right
+
+        found = [station(m, s) for m, s in enumerate(early[other])]
+        return 1, lambda step: found
+
+    groups = [group(other, j) for other in range(CORES) for j in range(n_row)]
     number = settle(plan, groups, stations, slots, acc, None, out_ref, per_col, store_sem)
 
     def hand_on(place, column):
@@ -257,13 +240,12 @@
     drain(number, acc, store_sem)
 
 
-def main_part(left, right, pieces, out, n_row, per_row, per_col):
+def main_part(left, right, out, n_row, per_row, per_col):
     n_chip = len(left[0]) + 1
     early, late = parts_of(n_chip)
     flat = [*left[0], *left[1]]
     rows, width = flat[0].shape[1], right[0].shape[2]
     slots = right[0].shape[1] // rows
-    height = n_row * slots * width
     tiles = per_row * per_col
     stations = CORES * n_row * n_chip
     pairs = slots * slots * stations
@@ -275,13 +257,13 @@
     anywhere = pl.BlockSpec(memory_space=pl.ANY)
     held = (
         (places + tail_places[0]) * width * width * 4
-        + len(flat) * height * rows * 2
-        + (stations + n_row * sum(map(len, late))) * (slots * rows + META) * width * 2
+        + sum(x.size for x in sources) * 2
+        + n_row * sum(map(len, late)) * (slots * rows + META) * width * 2
         + (slots + 1) * stations * width * 4
         + 8 * pairs * pairs * 4
     )
     return pl.pallas_call(
-        functools.partial(main_kernel, n_row, n_chip, slots, per_row, per_col, pieces),
+        functools.partial(main_kernel, n_row, n_chip, slots, per_row, per_col),
         out_shape=[
             jax.ShapeDtypeStruct(out.shape, out.dtype),
             jax.ShapeDtypeStruct(
@@ -290,7 +272,7 @@
             jax.ShapeDtypeStruct(tail_places, jnp.float32),
             jax.ShapeDtypeStruct(plan, jnp.int32),
         ],
-        in_specs=[anywhere] * (len(sources) + 1),
+        in_specs=[pl.BlockSpec(memory_space=pltpu.VMEM)] * len(sources) + [anywhere],
         out_specs=[
             anywhere,
             pl.BlockSpec(memory_space=pltpu.VMEM),
@@ -299,11 +281,8 @@
         ],
         scratch_shapes=[
             pltpu.VMEM((places, width, width), jnp.float32),
-            pltpu.VMEM((len(flat), height, rows), jnp.bfloat16),
-            pltpu.VMEM((CORES * n_row, n_chip, slots * rows + META, width), jnp.bfloat16),
             pltpu.VMEM((slots + 1, stations, width), jnp.float32),
             pltpu.VMEM(plan, jnp.int32),
-            pltpu.SemaphoreType.DMA((len(sources),)),
             pltpu.SemaphoreType.DMA,
             pltpu.SemaphoreType.DMA,
         ],
@@ -451,9 +430,8 @@
     swapped, waiting, zeros = after((swapped, sides[1:], zeros))
     swapped |= {s: flip_core(near[s]) for s in near if s > middle} | {0: own[0]}
     sides += [own[1]] + [flip_core(x) for x in waiting]
-    pieces = [(index, 0, n_chip) for index in range(CORES * n_row)]
     early = [[near[s] for s in sorted(near)], [swapped[s] for s in sorted(swapped)]]
-    out, tail_right, base, plan = main_part(early, sides, pieces, zeros, n_row, per_row, per_col)
+    out, tail_right, base, plan = main_part(early, sides, zeros, n_row, per_row, per_col)
     far, plan = after((far, plan))
     return tail_part(
         [[far], [flip_core(far)]], tail_right, base, plan, out, n_row, per_row, per_col

time: 63.1 us -> 63 us (level)
  waiting for transfers between devices: 20.3 us -> 22.4 us
  Pallas kernels: 22 us -> 20.1 us
    pallas_call x1, Pallas kernels: 5.75 us -> 3.86 us  [main_part(): pl.pallas_call(functools.partial(main_kernel, n_row, n_chip, slots, per_r...]
    ppermute x6, waiting for transfers between devices: 12.1 us -> 14 us  [shift_chip(): return lax.ppermute(value, 'col', pairs)]
  transfers between devices with their start and end apart: 20 -> 20, of which waited for: 10 -> 10; matrix products, arithmetic and copies ran while one was open for 0% -> 0% of each run, Pallas kernels for 28% -> 25%
where the time goes in v9:
time: 63 us; the launch traced here: 62.8 us
  waiting for transfers between devices  22.4 us (36%)
  Pallas kernels  20.1 us (32%)
  starting transfers between devices  19.1 us (30%)
  local copies, waits for them, and re-layouts  0.98 us (2%)
    ppermute x6, waiting for transfers between devices, shift_chip(): return lax.ppermute(value, 'col', pairs)  14 us
    pallas_call x2, Pallas kernels, zero_part(): pl.pallas_call(functools.partial(zero_kernel, first, number), out_shape=j...  12.1 us
    ppermute x6, starting transfers between devices, shift_chip(): return lax.ppermute(value, 'col', pairs)  10.2 us
    ppermute x6, starting transfers between devices, flip_row(): return lax.ppermute(value, 'row', [(i, i ^ j) for i in range(n_row)])  7.83 us
    ppermute x8, waiting for transfers between devices, flip_core(): return lax.ppermute(value, 'col', [(i, i ^ 1) for i in range(n_col)])  4.91 us
    pallas_call x1, Pallas kernels, main_part(): pl.pallas_call(functools.partial(main_kernel, n_row, n_chip, slots, per_r...  3.86 us
    ppermute x6, waiting for transfers between devices, flip_row(): return lax.ppermute(value, 'row', [(i, i ^ j) for i in range(n_row)])  3.47 us
    pallas_call x1, Pallas kernels, pack(): pl.pallas_call(functools.partial(pack_kernel, n_row, n_chip, slots), out_...  2.15 us
  transfers between devices with their start and end apart: 20, of which 10 were waited for; matrix products, arithmetic and copies ran while one was open for 0% of the time, Pallas kernels for 25%

profile of v9, /device:TPU:0, one launch (start us, length us, event | category | flops | bytes accessed | tf_op | source)
XLA Modules:
  0.0 62.8 jit_solution(9207827463435631855)
XLA Ops:
  0.0 2.1 %shard_map.46 = (bf16[256,256]{1,0:T(8,128)(2,1)}, bf16[256,256]{1,0:T(8,128)(2,1)}, bf16[256,256]{1,0:T(8,128)(2,1)}, bf16[256,256]{1,0:T(8,128)(2,1)}, bf16[52...) custom-call(bf16[4,2,256,128]{3,2,1,0:T(8,128)(2,1)} %bitcast.18, ...), custom_call_target="tpu_custom_call" | custom-call | tf_op jit(solution)/shard_map/pallas_call | solution.py:51
  2.2 2.9 %collective-permute-start = (bf16[256,256]{1,0:T(8,128)(2,1)}, bf16[256,256]{1,0:T(8,128)(2,1)S(1)}, u32[]{:S(2)}, u32[]{:S(2)}) collective-permute-start(bf16[256,256]{1,0:T(8,128)(2,1)} %get-tuple-element.38), channel_id=1, source_target_pairs={{0,8},{8,0},{16,24},{24,16},{1,9},{9,1},{17,25},{25,17},{2,10},{10... | collective-permute-start | bytes 393224 | tf_op jit(solution)/shard_map/ppermute | solution.py:395
  5.1 1.6 %collective-permute-start.3 = (bf16[528,128]{1,0:T(8,128)(2,1)}, bf16[528,128]{1,0:T(8,128)(2,1)S(1)}, u32[]{:S(2)}, u32[]{:S(2)}) collective-permute-start(bf16[528,128]{1,0:T(8,128)(2,1)} %get-tuple-element.42), channel_id=1, source_target_pairs={{0,2},{1,3},{2,4},{3,5},{4,6},{5,7},{6,0},{7,1},{8,10},{9,11},{10,... | collective-permute-start | bytes 405512 | tf_op jit(solution)/shard_map/ppermute | solution.py:399
  6.7 2.6 %collective-permute-start.4 = (bf16[528,128]{1,0:T(8,128)(2,1)}, bf16[528,128]{1,0:T(8,128)(2,1)S(1)}, u32[]{:S(2)}, u32[]{:S(2)}) collective-permute-start(bf16[528,128]{1,0:T(8,128)(2,1)} %get-tuple-element.43), channel_id=1, source_target_pairs={{0,4},{1,5},{2,6},{3,7},{4,0},{5,1},{6,2},{7,3},{8,12},{9,13},{10,... | collective-permute-start | bytes 405512 | tf_op jit(solution)/shard_map/ppermute | solution.py:399
  9.3 1.3 %collective-permute-start.5 = (bf16[528,128]{1,0:T(8,128)(2,1)}, bf16[528,128]{1,0:T(8,128)(2,1)S(1)}, u32[]{:S(2)}, u32[]{:S(2)}) collective-permute-start(bf16[528,128]{1,0:T(8,128)(2,1)} %get-tuple-element.44), channel_id=1, source_target_pairs={{0,6},{1,7},{2,0},{3,1},{4,2},{5,3},{6,4},{7,5},{8,14},{9,15},{10,... | collective-permute-start | bytes 405512 | tf_op jit(solution)/shard_map/ppermute | solution.py:399
  10.6 1.5 %collective-permute-start.1 = (bf16[256,256]{1,0:T(8,128)(2,1)}, bf16[256,256]{1,0:T(8,128)(2,1)S(1)}, u32[]{:S(2)}, u32[]{:S(2)}) collective-permute-start(bf16[256,256]{1,0:T(8,128)(2,1)} %get-tuple-element.39), channel_id=1, source_target_pairs={{0,16},{8,24},{16,0},{24,8},{1,17},{9,25},{17,1},{25,9},{2,18},{10... | collective-permute-start | bytes 393224 | tf_op jit(solution)/shard_map/ppermute | solution.py:395
  12.6 0.9 %copy-done = bf16[528,128]{1,0:T(8,128)(2,1)S(1)} copy-done((bf16[528,128]{1,0:T(8,128)(2,1)S(1)}, bf16[528,128]{1,0:T(8,128)(2,1)}, u32[]{:S(2)}) %copy-start) | copy-done | bytes 135192
  13.5 4.7 %shard_map.47.refs_1_ = f32[4096,2048]{1,0:T(8,128)} custom-call(bf16[528,128]{1,0:T(8,128)(2,1)S(1)} %copy-done), custom_call_target="tpu_custom_call" | custom-call | bytes 16777216 | tf_op jit(solution)/shard_map/pallas_call | solution.py:368
  19.3 3.0 %collective-permute-start.6 = (bf16[1024,256]{1,0:T(8,128)(2,1)S(1)}, bf16[1024,256]{1,0:T(8,128)(2,1)S(1)}, u32[]{:S(2)}, u32[]{:S(2)}) collective-permute-start(bf16[1024,256]{1,0:T(8,128)(2,1)S(1)} %bitcast.14), channel_id=1, source_target_pairs={{0,2},{1,3},{2,4},{3,5},{4,6},{5,7},{6,0},{7,1},{8,10},{9,11},{10,... | collective-permute-start | bytes 1572872 | tf_op jit(solution)/shard_map/ppermute | solution.py:399
  22.8 1.7 %collective-permute-start.8 = (bf16[1056,256]{1,0:T(8,128)(2,1)S(1)}, bf16[1056,256]{1,0:T(8,128)(2,1)S(1)}, u32[]{:S(2)}, u32[]{:S(2)}) collective-permute-start(bf16[1056,256]{1,0:T(8,128)(2,1)S(1)} %pad.9), channel_id=1, source_target_pairs={{0,6},{1,7},{2,0},{3,1},{4,2},{5,3},{6,4},{7,5},{8,14},{9,15},{10,... | collective-permute-start | bytes 1622024 | tf_op jit(solution)/shard_map/ppermute | solution.py:399
  24.5 1.5 %collective-permute-start.13 = (bf16[4,528,128]{2,1,0:T(8,128)(2,1)S(1)}, bf16[4,528,128]{2,1,0:T(8,128)(2,1)S(1)}, u32[]{:S(2)}, u32[]{:S(2)}) collective-permute-start(bf16[4,528,128]{2,1,0:T(8,128)(2,1)S(1)} %pad_maximum_fusion.refs_6_), channel_id=1, source_target_pairs={{0,16},{8,24},{16,0},{24,8},{1,17},{9,25},{17,1},{25,9},{2,18},{10... | collective-permute-start | bytes 1622024 | tf_op jit(solution)/shard_map/ppermute | solution.py:395
  26.0 0.9 %collective-permute-start.14 = (bf16[4,528,128]{2,1,0:T(8,128)(2,1)S(1)}, bf16[4,528,128]{2,1,0:T(8,128)(2,1)S(1)}, u32[]{:S(2)}, u32[]{:S(2)}) collective-permute-start(bf16[4,528,128]{2,1,0:T(8,128)(2,1)S(1)} %pad_maximum_fusion.refs_6_), channel_id=1, source_target_pairs={{0,24},{8,16},{16,8},{24,0},{1,25},{9,17},{17,9},{25,1},{2,26},{10... | collective-permute-start | bytes 1622024 | tf_op jit(solution)/shard_map/ppermute | solution.py:395
  26.9 9.2 %collective-permute-done.6.refs_1_ = bf16[1024,256]{1,0:T(8,128)(2,1)S(1)} collective-permute-done((bf16[1024,256]{1,0:T(8,128)(2,1)S(1)}, bf16[1024,256]{1,0:T(8,128)(2,1)S(1)}, u32[]{:S(2)}, u32[]{:S(2)}) %collective-permute-start.6) | collective-permute-done | bytes 524320 | tf_op jit(solution)/shard_map/ppermute | solution.py:399
  36.1 1.3 %collective-permute-done.12.refs_7_ = bf16[4,528,128]{2,1,0:T(8,128)(2,1)S(1)} collective-permute-done((bf16[4,528,128]{2,1,0:T(8,128)(2,1)S(1)}, bf16[4,528,128]{2,1,0:T(8,128)(2,1)S(1)}, u32[]{:S(2)}, u32[]{:S(2)}) %collective-permute-start.12) | collective-permute-done | bytes 540704 | tf_op jit(solution)/shard_map/ppermute | solution.py:395
  37.4 7.3 %shard_map.48.refs_14_ = f32[4096,2048]{1,0:T(8,128)} custom-call(bf16[528,128]{1,0:T(8,128)(2,1)S(1)} %copy-done.1, f32[4096,2048]{1,0:T(8,128)} %shard_map.47.refs_1_), custom_call_target="tpu_custom_call", output_to_operand_aliasing={{}: (1, {})} | custom-call | bytes 16777216 | tf_op jit(solution)/shard_map/pallas_call | solution.py:368
  44.8 2.8 %collective-permute-done.8.refs_2_ = bf16[1056,256]{1,0:T(8,128)(2,1)S(1)} collective-permute-done((bf16[1056,256]{1,0:T(8,128)(2,1)S(1)}, bf16[1056,256]{1,0:T(8,128)(2,1)S(1)}, u32[]{:S(2)}, u32[]{:S(2)}) %collective-permute-start.8) | collective-permute-done | bytes 540704 | tf_op jit(solution)/shard_map/ppermute | solution.py:399
  47.6 1.9 %collective-permute-done.13.refs_8_ = bf16[4,528,128]{2,1,0:T(8,128)(2,1)S(1)} collective-permute-done((bf16[4,528,128]{2,1,0:T(8,128)(2,1)S(1)}, bf16[4,528,128]{2,1,0:T(8,128)(2,1)S(1)}, u32[]{:S(2)}, u32[]{:S(2)}) %collective-permute-start.13) | collective-permute-done | bytes 540704 | tf_op jit(solution)/shard_map/ppermute | solution.py:395
  50.0 1.4 %collective-permute-done.16.refs_11_ = bf16[4,528,128]{2,1,0:T(8,128)(2,1)S(1)} collective-permute-done((bf16[4,528,128]{2,1,0:T(8,128)(2,1)S(1)}, bf16[4,528,128]{2,1,0:T(8,128)(2,1)S(1)}, u32[]{:S(2)}, u32[]{:S(2)}) %collective-permute-start.16) | collective-permute-done | bytes 540704 | tf_op jit(solution)/shard_map/ppermute | solution.py:402
  51.5 0.8 %collective-permute-done.17.refs_12_ = bf16[4,528,128]{2,1,0:T(8,128)(2,1)S(1)} collective-permute-done((bf16[4,528,128]{2,1,0:T(8,128)(2,1)S(1)}, bf16[4,528,128]{2,1,0:T(8,128)(2,1)S(1)}, u32[]{:S(2)}, u32[]{:S(2)}) %collective-permute-start.17) | collective-permute-done | bytes 540704 | tf_op jit(solution)/shard_map/ppermute | solution.py:402
  52.2 0.8 %collective-permute-done.18.refs_13_ = bf16[4,528,128]{2,1,0:T(8,128)(2,1)S(1)} collective-permute-done((bf16[4,528,128]{2,1,0:T(8,128)(2,1)S(1)}, bf16[4,528,128]{2,1,0:T(8,128)(2,1)S(1)}, u32[]{:S(2)}, u32[]{:S(2)}) %collective-permute-start.18) | collective-permute-done | bytes 540704 | tf_op jit(solution)/shard_map/ppermute | solution.py:402
  53.0 3.9 %shard_map.49 = (f32[4096,2048]{1,0:T(8,128)}, bf16[8,512,128]{2,1,0:T(8,128)(2,1)S(1)}, f32[32,128,128]{2,1,0:T(8,128)S(1)}, s32[8,128]{1,0:T(8,128)S(1)}) custom-call(bf16[1024,256]{1,0:T(8,128)(2,1)S(1)} %bitcast.16, bf16[1024,256]{1,0:T(8,128)(2,1)S(1)} %collective-permute-done.6.refs_1_, ...), custom_call_target="tpu_custom_call", output_to_operand_aliasing={{0}: (14, {})} | custom-call | tf_op jit(solution)/shard_map/pallas_call | solution.py:265
  56.9 2.0 %collective-permute-done.7.refs_0_ = bf16[1072,256]{1,0:T(8,128)(2,1)S(1)} collective-permute-done((bf16[1072,256]{1,0:T(8,128)(2,1)S(1)}, bf16[1072,256]{1,0:T(8,128)(2,1)S(1)}, u32[]{:S(2)}, u32[]{:S(2)}) %collective-permute-start.7) | collective-permute-done | bytes 548896 | tf_op jit(solution)/shard_map/ppermute | solution.py:399
  58.9 1.9 %collective-permute-done.19.refs_1_ = bf16[1072,256]{1,0:T(8,128)(2,1)S(1)} collective-permute-done((bf16[1072,256]{1,0:T(8,128)(2,1)S(1)}, bf16[1072,256]{1,0:T(8,128)(2,1)S(1)}, u32[]{:S(2)}, u32[]{:S(2)}) %collective-permute-start.19) | collective-permute-done | bytes 548896 | tf_op jit(solution)/shard_map/ppermute | solution.py:402
  60.8 2.0 %shard_map.50 = f32[4096,2048]{1,0:T(8,128)} custom-call(s32[8,128]{1,0:T(8,128)S(1)} %get-tuple-element.64.plan, bf16[1072,256]{1,0:T(8,128)(2,1)S(1)} %collective-permute-done.7.refs_0_, bf16[1072,256]{1,0:T(8,128)(2,1)S(1)} %collective-permute-done.19.refs_1_, bf16[8,512,128]{2,1,0:T(8,128)(2,1)S(1)} %get-tuple-element.66.refs_2_, ...), custom_call_target="tpu_custom_call", output_to_operand_aliasing={{}: (5, {})} | custom-call | tf_op jit(solution)/shard_map/pallas_call | solution.py:332
  (31 shorter events, 2.6 us)
Async XLA Ops:
  2.2 10.0 %collective-permute-start = (bf16[256,256]{1,0:T(8,128)(2,1)}, bf16[256,256]{1,0:T(8,128)(2,1)S(1)}, u32[]{:S(2)}, u32[]{:S(2)}) collective-permute-start(bf16[256,256]{1,0:T(8,128)(2,1)} %get-tuple-element.38), channel_id=1, source_target_pairs={{0,8},{8,0},{16,24},{24,16},{1,9},{9,1},{17,25},{25,17},{2,10},{10... | collective-permute-start | bytes 393224 | tf_op jit(solution)/shard_map/ppermute | solution.py:395
  5.1 13.4 %collective-permute-start.3 = (bf16[528,128]{1,0:T(8,128)(2,1)}, bf16[528,128]{1,0:T(8,128)(2,1)S(1)}, u32[]{:S(2)}, u32[]{:S(2)}) collective-permute-start(bf16[528,128]{1,0:T(8,128)(2,1)} %get-tuple-element.42), channel_id=1, source_target_pairs={{0,2},{1,3},{2,4},{3,5},{4,6},{5,7},{6,0},{7,1},{8,10},{9,11},{10,... | collective-permute-start | bytes 405512 | tf_op jit(solution)/shard_map/ppermute | solution.py:399
  6.7 11.8 %collective-permute-start.4 = (bf16[528,128]{1,0:T(8,128)(2,1)}, bf16[528,128]{1,0:T(8,128)(2,1)S(1)}, u32[]{:S(2)}, u32[]{:S(2)}) collective-permute-start(bf16[528,128]{1,0:T(8,128)(2,1)} %get-tuple-element.43), channel_id=1, source_target_pairs={{0,4},{1,5},{2,6},{3,7},{4,0},{5,1},{6,2},{7,3},{8,12},{9,13},{10,... | collective-permute-start | bytes 405512 | tf_op jit(solution)/shard_map/ppermute | solution.py:399
  9.3 9.2 %collective-permute-start.5 = (bf16[528,128]{1,0:T(8,128)(2,1)}, bf16[528,128]{1,0:T(8,128)(2,1)S(1)}, u32[]{:S(2)}, u32[]{:S(2)}) collective-permute-start(bf16[528,128]{1,0:T(8,128)(2,1)} %get-tuple-element.44), channel_id=1, source_target_pairs={{0,6},{1,7},{2,0},{3,1},{4,2},{5,3},{6,4},{7,5},{8,14},{9,15},{10,... | collective-permute-start | bytes 405512 | tf_op jit(solution)/shard_map/ppermute | solution.py:399
  10.6 7.9 %collective-permute-start.1 = (bf16[256,256]{1,0:T(8,128)(2,1)}, bf16[256,256]{1,0:T(8,128)(2,1)S(1)}, u32[]{:S(2)}, u32[]{:S(2)}) collective-permute-start(bf16[256,256]{1,0:T(8,128)(2,1)} %get-tuple-element.39), channel_id=1, source_target_pairs={{0,16},{8,24},{16,0},{24,8},{1,17},{9,25},{17,1},{25,9},{2,18},{10... | collective-permute-start | bytes 393224 | tf_op jit(solution)/shard_map/ppermute | solution.py:395
  12.1 6.4 %collective-permute-start.2 = (bf16[256,256]{1,0:T(8,128)(2,1)}, bf16[256,256]{1,0:T(8,128)(2,1)S(1)}, u32[]{:S(2)}, u32[]{:S(2)}) collective-permute-start(bf16[256,256]{1,0:T(8,128)(2,1)} %get-tuple-element.40), channel_id=1, source_target_pairs={{0,24},{8,16},{16,8},{24,0},{1,25},{9,17},{17,9},{25,1},{2,26},{10... | collective-permute-start | bytes 393224 | tf_op jit(solution)/shard_map/ppermute | solution.py:395
  12.6 0.9 %copy-start = (bf16[528,128]{1,0:T(8,128)(2,1)S(1)}, bf16[528,128]{1,0:T(8,128)(2,1)}, u32[]{:S(2)}) copy-start(bf16[528,128]{1,0:T(8,128)(2,1)} %get-tuple-element.55.refs_0_) | copy-start | bytes 405508
  13.5 5.0 %copy-start.1 = (bf16[528,128]{1,0:T(8,128)(2,1)S(1)}, bf16[528,128]{1,0:T(8,128)(2,1)}, u32[]{:S(2)}) copy-start(bf16[528,128]{1,0:T(8,128)(2,1)} %get-tuple-element.55.refs_0_) | copy-start | bytes 405508
  13.5 5.2 %copy-start.2 = (bf16[256,256]{1,0:T(8,128)(2,1)S(1)}, bf16[256,256]{1,0:T(8,128)(2,1)}, u32[]{:S(2)}) copy-start(bf16[256,256]{1,0:T(8,128)(2,1)} %get-tuple-element.45) | copy-start | bytes 393220
  18.6 5.9 %collective-permute-start.10 = (bf16[4,528,128]{2,1,0:T(8,128)(2,1)S(1)}, bf16[4,528,128]{2,1,0:T(8,128)(2,1)S(1)}, u32[]{:S(2)}, u32[]{:S(2)}) collective-permute-start(bf16[4,528,128]{2,1,0:T(8,128)(2,1)S(1)} %pad_maximum_fusion.refs_6_), channel_id=1, source_target_pairs={{0,1},{1,0},{2,3},{3,2},{4,5},{5,4},{6,7},{7,6},{8,9},{9,8},{10,11... | collective-permute-start | bytes 1622024 | tf_op jit(solution)/shard_map/ppermute | solution.py:402
  18.8 5.8 %collective-permute-start.9 = (bf16[1024,256]{1,0:T(8,128)(2,1)S(1)}, bf16[1024,256]{1,0:T(8,128)(2,1)S(1)}, u32[]{:S(2)}, u32[]{:S(2)}) collective-permute-start(bf16[1024,256]{1,0:T(8,128)(2,1)S(1)} %bitcast.13), channel_id=1, source_target_pairs={{0,1},{1,0},{2,3},{3,2},{4,5},{5,4},{6,7},{7,6},{8,9},{9,8},{10,11... | collective-permute-start | bytes 1572872 | tf_op jit(solution)/shard_map/ppermute | solution.py:402
  19.3 16.8 %collective-permute-start.6 = (bf16[1024,256]{1,0:T(8,128)(2,1)S(1)}, bf16[1024,256]{1,0:T(8,128)(2,1)S(1)}, u32[]{:S(2)}, u32[]{:S(2)}) collective-permute-start(bf16[1024,256]{1,0:T(8,128)(2,1)S(1)} %bitcast.14), channel_id=1, source_target_pairs={{0,2},{1,3},{2,4},{3,5},{4,6},{5,7},{6,0},{7,1},{8,10},{9,11},{10,... | collective-permute-start | bytes 1572872 | tf_op jit(solution)/shard_map/ppermute | solution.py:399
  22.3 15.2 %collective-permute-start.12 = (bf16[4,528,128]{2,1,0:T(8,128)(2,1)S(1)}, bf16[4,528,128]{2,1,0:T(8,128)(2,1)S(1)}, u32[]{:S(2)}, u32[]{:S(2)}) collective-permute-start(bf16[4,528,128]{2,1,0:T(8,128)(2,1)S(1)} %pad_maximum_fusion.refs_6_), channel_id=1, source_target_pairs={{0,8},{8,0},{16,24},{24,16},{1,9},{9,1},{17,25},{25,17},{2,10},{10... | collective-permute-start | bytes 1622024 | tf_op jit(solution)/shard_map/ppermute | solution.py:395
  22.8 24.8 %collective-permute-start.8 = (bf16[1056,256]{1,0:T(8,128)(2,1)S(1)}, bf16[1056,256]{1,0:T(8,128)(2,1)S(1)}, u32[]{:S(2)}, u32[]{:S(2)}) collective-permute-start(bf16[1056,256]{1,0:T(8,128)(2,1)S(1)} %pad.9), channel_id=1, source_target_pairs={{0,6},{1,7},{2,0},{3,1},{4,2},{5,3},{6,4},{7,5},{8,14},{9,15},{10,... | collective-permute-start | bytes 1622024 | tf_op jit(solution)/shard_map/ppermute | solution.py:399
  24.5 25.0 %collective-permute-start.13 = (bf16[4,528,128]{2,1,0:T(8,128)(2,1)S(1)}, bf16[4,528,128]{2,1,0:T(8,128)(2,1)S(1)}, u32[]{:S(2)}, u32[]{:S(2)}) collective-permute-start(bf16[4,528,128]{2,1,0:T(8,128)(2,1)S(1)} %pad_maximum_fusion.refs_6_), channel_id=1, source_target_pairs={{0,16},{8,24},{16,0},{24,8},{1,17},{9,25},{17,1},{25,9},{2,18},{10... | collective-permute-start | bytes 1622024 | tf_op jit(solution)/shard_map/ppermute | solution.py:395
  26.0 23.5 %collective-permute-start.14 = (bf16[4,528,128]{2,1,0:T(8,128)(2,1)S(1)}, bf16[4,528,128]{2,1,0:T(8,128)(2,1)S(1)}, u32[]{:S(2)}, u32[]{:S(2)}) collective-permute-start(bf16[4,528,128]{2,1,0:T(8,128)(2,1)S(1)} %pad_maximum_fusion.refs_6_), channel_id=1, source_target_pairs={{0,24},{8,16},{16,8},{24,0},{1,25},{9,17},{17,9},{25,1},{2,26},{10... | collective-permute-start | bytes 1622024 | tf_op jit(solution)/shard_map/ppermute | solution.py:395
  36.1 11.5 %collective-permute-start.11 = (bf16[1024,256]{1,0:T(8,128)(2,1)S(1)}, bf16[1024,256]{1,0:T(8,128)(2,1)S(1)}, u32[]{:S(2)}, u32[]{:S(2)}) collective-permute-start(bf16[1024,256]{1,0:T(8,128)(2,1)S(1)} %collective-permute-done.6.refs_1_), channel_id=1, source_target_pairs={{0,1},{1,0},{2,3},{3,2},{4,5},{5,4},{6,7},{7,6},{8,9},{9,8},{10,11... | collective-permute-start | bytes 1572872 | tf_op jit(solution)/shard_map/ppermute | solution.py:402
  37.4 21.4 %collective-permute-start.7 = (bf16[1072,256]{1,0:T(8,128)(2,1)S(1)}, bf16[1072,256]{1,0:T(8,128)(2,1)S(1)}, u32[]{:S(2)}, u32[]{:S(2)}) collective-permute-start(bf16[1072,256]{1,0:T(8,128)(2,1)S(1)} %pad.8), channel_id=1, source_target_pairs={{0,2},{1,3},{2,4},{3,5},{4,6},{5,7},{6,0},{7,1},{8,10},{9,11},{10,... | collective-permute-start | bytes 1646600 | tf_op jit(solution)/shard_map/ppermute | solution.py:399
  47.6 2.4 %collective-permute-start.15 = (bf16[1056,256]{1,0:T(8,128)(2,1)S(1)}, bf16[1056,256]{1,0:T(8,128)(2,1)S(1)}, u32[]{:S(2)}, u32[]{:S(2)}) collective-permute-start(bf16[1056,256]{1,0:T(8,128)(2,1)S(1)} %collective-permute-done.8.refs_2_), channel_id=1, source_target_pairs={{0,1},{1,0},{2,3},{3,2},{4,5},{5,4},{6,7},{7,6},{8,9},{9,8},{10,11... | collective-permute-start | bytes 1622024 | tf_op jit(solution)/shard_map/ppermute | solution.py:402
  49.5 1.9 %collective-permute-start.16 = (bf16[4,528,128]{2,1,0:T(8,128)(2,1)S(1)}, bf16[4,528,128]{2,1,0:T(8,128)(2,1)S(1)}, u32[]{:S(2)}, u32[]{:S(2)}) collective-permute-start(bf16[4,528,128]{2,1,0:T(8,128)(2,1)S(1)} %collective-permute-done.12.refs_7_), channel_id=1, source_target_pairs={{0,1},{1,0},{2,3},{3,2},{4,5},{5,4},{6,7},{7,6},{8,9},{9,8},{10,11... | collective-permute-start | bytes 1622024 | tf_op jit(solution)/shard_map/ppermute | solution.py:402
  49.5 2.7 %collective-permute-start.17 = (bf16[4,528,128]{2,1,0:T(8,128)(2,1)S(1)}, bf16[4,528,128]{2,1,0:T(8,128)(2,1)S(1)}, u32[]{:S(2)}, u32[]{:S(2)}) collective-permute-start(bf16[4,528,128]{2,1,0:T(8,128)(2,1)S(1)} %collective-permute-done.13.refs_8_), channel_id=1, source_target_pairs={{0,1},{1,0},{2,3},{3,2},{4,5},{5,4},{6,7},{7,6},{8,9},{9,8},{10,11... | collective-permute-start | bytes 1622024 | tf_op jit(solution)/shard_map/ppermute | solution.py:402
  50.0 3.0 %collective-permute-start.18 = (bf16[4,528,128]{2,1,0:T(8,128)(2,1)S(1)}, bf16[4,528,128]{2,1,0:T(8,128)(2,1)S(1)}, u32[]{:S(2)}, u32[]{:S(2)}) collective-permute-start(bf16[4,528,128]{2,1,0:T(8,128)(2,1)S(1)} %collective-permute-done.14.refs_9_), channel_id=1, source_target_pairs={{0,1},{1,0},{2,3},{3,2},{4,5},{5,4},{6,7},{7,6},{8,9},{9,8},{10,11... | collective-permute-start | bytes 1622024 | tf_op jit(solution)/shard_map/ppermute | solution.py:402
  58.9 1.9 %collective-permute-start.19 = (bf16[1072,256]{1,0:T(8,128)(2,1)S(1)}, bf16[1072,256]{1,0:T(8,128)(2,1)S(1)}, u32[]{:S(2)}, u32[]{:S(2)}) collective-permute-start(bf16[1072,256]{1,0:T(8,128)(2,1)S(1)} %collective-permute-done.7.refs_0_), channel_id=1, source_target_pairs={{0,1},{1,0},{2,3},{3,2},{4,5},{5,4},{6,7},{7,6},{8,9},{9,8},{10,11... | collective-permute-start | bytes 1646600 | tf_op jit(solution)/shard_map/ppermute | solution.py:402

commit v10 on v9

--- a/solution.py
+++ b/solution.py
@@ -10,6 +10,7 @@
 TILES = 128
 CORES = 2
 META = 16
+TAIL_GROUP = 2
 ZERO_EARLY = 6
 MIB = 1024 * 1024
 
@@ -314,7 +315,10 @@
                     return jnp.concatenate(tiles, axis=1)
 
                 found.append(((other * n_row + j) * n_chip + s, left, right))
-    groups = [(1, lambda step: found)]
+    groups = [
+        (1, lambda step, first=first: found[first : first + TAIL_GROUP])
+        for first in range(0, len(found), TAIL_GROUP)
+    ]
     number = settle(plan, groups, stations, slots, acc, base_ref, out_ref, per_col, store_sem)
     drain(number, acc, store_sem)
 

time: 63 us -> 62.9 us (level)
  no operation moved by 1% of the time
where the time goes in v10:
time: 62.9 us; the launch traced here: 62.7 us
  waiting for transfers between devices  22.3 us (35%)
  Pallas kernels  20 us (32%)
  starting transfers between devices  19.1 us (30%)
  local copies, waits for them, and re-layouts  0.98 us (2%)
    ppermute x6, waiting for transfers between devices, shift_chip(): return lax.ppermute(value, 'col', pairs)  13.9 us
    pallas_call x2, Pallas kernels, zero_part(): pl.pallas_call(functools.partial(zero_kernel, first, number), out_shape=j...  12.1 us
    ppermute x6, starting transfers between devices, shift_chip(): return lax.ppermute(value, 'col', pairs)  10.2 us
    ppermute x6, starting transfers between devices, flip_row(): return lax.ppermute(value, 'row', [(i, i ^ j) for i in range(n_row)])  7.83 us
    ppermute x8, waiting for transfers between devices, flip_core(): return lax.ppermute(value, 'col', [(i, i ^ 1) for i in range(n_col)])  4.91 us
    pallas_call x1, Pallas kernels, main_part(): pl.pallas_call(functools.partial(main_kernel, n_row, n_chip, slots, per_r...  3.91 us
    ppermute x6, waiting for transfers between devices, flip_row(): return lax.ppermute(value, 'row', [(i, i ^ j) for i in range(n_row)])  3.47 us
    pallas_call x1, Pallas kernels, pack(): pl.pallas_call(functools.partial(pack_kernel, n_row, n_chip, slots), out_...  2.15 us
  transfers between devices with their start and end apart: 20, of which 10 were waited for; matrix products, arithmetic and copies ran while one was open for 0% of the time, Pallas kernels for 25%

profile of v10, /device:TPU:0, one launch (start us, length us, event | category | flops | bytes accessed | tf_op | source)
XLA Modules:
  0.0 62.7 jit_solution(9211081408748711162)
XLA Ops:
  0.0 2.1 %shard_map.46 = (bf16[256,256]{1,0:T(8,128)(2,1)}, bf16[256,256]{1,0:T(8,128)(2,1)}, bf16[256,256]{1,0:T(8,128)(2,1)}, bf16[256,256]{1,0:T(8,128)(2,1)}, bf16[52...) custom-call(bf16[4,2,256,128]{3,2,1,0:T(8,128)(2,1)} %bitcast.18, ...), custom_call_target="tpu_custom_call" | custom-call | tf_op jit(solution)/shard_map/pallas_call | solution.py:52
  2.2 2.9 %collective-permute-start = (bf16[256,256]{1,0:T(8,128)(2,1)}, bf16[256,256]{1,0:T(8,128)(2,1)S(1)}, u32[]{:S(2)}, u32[]{:S(2)}) collective-permute-start(bf16[256,256]{1,0:T(8,128)(2,1)} %get-tuple-element.38), channel_id=1, source_target_pairs={{0,8},{8,0},{16,24},{24,16},{1,9},{9,1},{17,25},{25,17},{2,10},{10... | collective-permute-start | bytes 393224 | tf_op jit(solution)/shard_map/ppermute | solution.py:399
  5.1 1.6 %collective-permute-start.3 = (bf16[528,128]{1,0:T(8,128)(2,1)}, bf16[528,128]{1,0:T(8,128)(2,1)S(1)}, u32[]{:S(2)}, u32[]{:S(2)}) collective-permute-start(bf16[528,128]{1,0:T(8,128)(2,1)} %get-tuple-element.42), channel_id=1, source_target_pairs={{0,2},{1,3},{2,4},{3,5},{4,6},{5,7},{6,0},{7,1},{8,10},{9,11},{10,... | collective-permute-start | bytes 405512 | tf_op jit(solution)/shard_map/ppermute | solution.py:403
  6.7 2.6 %collective-permute-start.4 = (bf16[528,128]{1,0:T(8,128)(2,1)}, bf16[528,128]{1,0:T(8,128)(2,1)S(1)}, u32[]{:S(2)}, u32[]{:S(2)}) collective-permute-start(bf16[528,128]{1,0:T(8,128)(2,1)} %get-tuple-element.43), channel_id=1, source_target_pairs={{0,4},{1,5},{2,6},{3,7},{4,0},{5,1},{6,2},{7,3},{8,12},{9,13},{10,... | collective-permute-start | bytes 405512 | tf_op jit(solution)/shard_map/ppermute | solution.py:403
  9.3 1.3 %collective-permute-start.5 = (bf16[528,128]{1,0:T(8,128)(2,1)}, bf16[528,128]{1,0:T(8,128)(2,1)S(1)}, u32[]{:S(2)}, u32[]{:S(2)}) collective-permute-start(bf16[528,128]{1,0:T(8,128)(2,1)} %get-tuple-element.44), channel_id=1, source_target_pairs={{0,6},{1,7},{2,0},{3,1},{4,2},{5,3},{6,4},{7,5},{8,14},{9,15},{10,... | collective-permute-start | bytes 405512 | tf_op jit(solution)/shard_map/ppermute | solution.py:403
  10.6 1.5 %collective-permute-start.1 = (bf16[256,256]{1,0:T(8,128)(2,1)}, bf16[256,256]{1,0:T(8,128)(2,1)S(1)}, u32[]{:S(2)}, u32[]{:S(2)}) collective-permute-start(bf16[256,256]{1,0:T(8,128)(2,1)} %get-tuple-element.39), channel_id=1, source_target_pairs={{0,16},{8,24},{16,0},{24,8},{1,17},{9,25},{17,1},{25,9},{2,18},{10... | collective-permute-start | bytes 393224 | tf_op jit(solution)/shard_map/ppermute | solution.py:399
  12.6 0.9 %copy-done = bf16[528,128]{1,0:T(8,128)(2,1)S(1)} copy-done((bf16[528,128]{1,0:T(8,128)(2,1)S(1)}, bf16[528,128]{1,0:T(8,128)(2,1)}, u32[]{:S(2)}) %copy-start) | copy-done | bytes 135192
  13.5 4.7 %shard_map.47.refs_1_ = f32[4096,2048]{1,0:T(8,128)} custom-call(bf16[528,128]{1,0:T(8,128)(2,1)S(1)} %copy-done), custom_call_target="tpu_custom_call" | custom-call | bytes 16777216 | tf_op jit(solution)/shard_map/pallas_call | solution.py:372
  19.3 3.0 %collective-permute-start.6 = (bf16[1024,256]{1,0:T(8,128)(2,1)S(1)}, bf16[1024,256]{1,0:T(8,128)(2,1)S(1)}, u32[]{:S(2)}, u32[]{:S(2)}) collective-permute-start(bf16[1024,256]{1,0:T(8,128)(2,1)S(1)} %bitcast.14), channel_id=1, source_target_pairs={{0,2},{1,3},{2,4},{3,5},{4,6},{5,7},{6,0},{7,1},{8,10},{9,11},{10,... | collective-permute-start | bytes 1572872 | tf_op jit(solution)/shard_map/ppermute | solution.py:403
  22.8 1.7 %collective-permute-start.8 = (bf16[1056,256]{1,0:T(8,128)(2,1)S(1)}, bf16[1056,256]{1,0:T(8,128)(2,1)S(1)}, u32[]{:S(2)}, u32[]{:S(2)}) collective-permute-start(bf16[1056,256]{1,0:T(8,128)(2,1)S(1)} %pad.9), channel_id=1, source_target_pairs={{0,6},{1,7},{2,0},{3,1},{4,2},{5,3},{6,4},{7,5},{8,14},{9,15},{10,... | collective-permute-start | bytes 1622024 | tf_op jit(solution)/shard_map/ppermute | solution.py:403
  24.5 1.5 %collective-permute-start.13 = (bf16[4,528,128]{2,1,0:T(8,128)(2,1)S(1)}, bf16[4,528,128]{2,1,0:T(8,128)(2,1)S(1)}, u32[]{:S(2)}, u32[]{:S(2)}) collective-permute-start(bf16[4,528,128]{2,1,0:T(8,128)(2,1)S(1)} %pad_maximum_fusion.refs_6_), channel_id=1, source_target_pairs={{0,16},{8,24},{16,0},{24,8},{1,17},{9,25},{17,1},{25,9},{2,18},{10... | collective-permute-start | bytes 1622024 | tf_op jit(solution)/shard_map/ppermute | solution.py:399
  26.0 0.9 %collective-permute-start.14 = (bf16[4,528,128]{2,1,0:T(8,128)(2,1)S(1)}, bf16[4,528,128]{2,1,0:T(8,128)(2,1)S(1)}, u32[]{:S(2)}, u32[]{:S(2)}) collective-permute-start(bf16[4,528,128]{2,1,0:T(8,128)(2,1)S(1)} %pad_maximum_fusion.refs_6_), channel_id=1, source_target_pairs={{0,24},{8,16},{16,8},{24,0},{1,25},{9,17},{17,9},{25,1},{2,26},{10... | collective-permute-start | bytes 1622024 | tf_op jit(solution)/shard_map/ppermute | solution.py:399
  26.9 9.2 %collective-permute-done.6.refs_1_ = bf16[1024,256]{1,0:T(8,128)(2,1)S(1)} collective-permute-done((bf16[1024,256]{1,0:T(8,128)(2,1)S(1)}, bf16[1024,256]{1,0:T(8,128)(2,1)S(1)}, u32[]{:S(2)}, u32[]{:S(2)}) %collective-permute-start.6) | collective-permute-done | bytes 524320 | tf_op jit(solution)/shard_map/ppermute | solution.py:403
  36.1 1.3 %collective-permute-done.12.refs_7_ = bf16[4,528,128]{2,1,0:T(8,128)(2,1)S(1)} collective-permute-done((bf16[4,528,128]{2,1,0:T(8,128)(2,1)S(1)}, bf16[4,528,128]{2,1,0:T(8,128)(2,1)S(1)}, u32[]{:S(2)}, u32[]{:S(2)}) %collective-permute-start.12) | collective-permute-done | bytes 540704 | tf_op jit(solution)/shard_map/ppermute | solution.py:399
  37.4 7.3 %shard_map.48.refs_14_ = f32[4096,2048]{1,0:T(8,128)} custom-call(bf16[528,128]{1,0:T(8,128)(2,1)S(1)} %copy-done.1, f32[4096,2048]{1,0:T(8,128)} %shard_map.47.refs_1_), custom_call_target="tpu_custom_call", output_to_operand_aliasing={{}: (1, {})} | custom-call | bytes 16777216 | tf_op jit(solution)/shard_map/pallas_call | solution.py:372
  44.8 2.8 %collective-permute-done.8.refs_2_ = bf16[1056,256]{1,0:T(8,128)(2,1)S(1)} collective-permute-done((bf16[1056,256]{1,0:T(8,128)(2,1)S(1)}, bf16[1056,256]{1,0:T(8,128)(2,1)S(1)}, u32[]{:S(2)}, u32[]{:S(2)}) %collective-permute-start.8) | collective-permute-done | bytes 540704 | tf_op jit(solution)/shard_map/ppermute | solution.py:403
  47.6 1.9 %collective-permute-done.13.refs_8_ = bf16[4,528,128]{2,1,0:T(8,128)(2,1)S(1)} collective-permute-done((bf16[4,528,128]{2,1,0:T(8,128)(2,1)S(1)}, bf16[4,528,128]{2,1,0:T(8,128)(2,1)S(1)}, u32[]{:S(2)}, u32[]{:S(2)}) %collective-permute-start.13) | collective-permute-done | bytes 540704 | tf_op jit(solution)/shard_map/ppermute | solution.py:399
  50.0 1.4 %collective-permute-done.16.refs_11_ = bf16[4,528,128]{2,1,0:T(8,128)(2,1)S(1)} collective-permute-done((bf16[4,528,128]{2,1,0:T(8,128)(2,1)S(1)}, bf16[4,528,128]{2,1,0:T(8,128)(2,1)S(1)}, u32[]{:S(2)}, u32[]{:S(2)}) %collective-permute-start.16) | collective-permute-done | bytes 540704 | tf_op jit(solution)/shard_map/ppermute | solution.py:406
  51.5 0.8 %collective-permute-done.17.refs_12_ = bf16[4,528,128]{2,1,0:T(8,128)(2,1)S(1)} collective-permute-done((bf16[4,528,128]{2,1,0:T(8,128)(2,1)S(1)}, bf16[4,528,128]{2,1,0:T(8,128)(2,1)S(1)}, u32[]{:S(2)}, u32[]{:S(2)}) %collective-permute-start.17) | collective-permute-done | bytes 540704 | tf_op jit(solution)/shard_map/ppermute | solution.py:406
  52.2 0.8 %collective-permute-done.18.refs_13_ = bf16[4,528,128]{2,1,0:T(8,128)(2,1)S(1)} collective-permute-done((bf16[4,528,128]{2,1,0:T(8,128)(2,1)S(1)}, bf16[4,528,128]{2,1,0:T(8,128)(2,1)S(1)}, u32[]{:S(2)}, u32[]{:S(2)}) %collective-permute-start.18) | collective-permute-done | bytes 540704 | tf_op jit(solution)/shard_map/ppermute | solution.py:406
  53.0 3.9 %shard_map.49 = (f32[4096,2048]{1,0:T(8,128)}, bf16[8,512,128]{2,1,0:T(8,128)(2,1)S(1)}, f32[32,128,128]{2,1,0:T(8,128)S(1)}, s32[8,128]{1,0:T(8,128)S(1)}) custom-call(bf16[1024,256]{1,0:T(8,128)(2,1)S(1)} %bitcast.16, bf16[1024,256]{1,0:T(8,128)(2,1)S(1)} %collective-permute-done.6.refs_1_, ...), custom_call_target="tpu_custom_call", output_to_operand_aliasing={{0}: (14, {})} | custom-call | tf_op jit(solution)/shard_map/pallas_call | solution.py:266
  56.9 1.9 %collective-permute-done.7.refs_0_ = bf16[1072,256]{1,0:T(8,128)(2,1)S(1)} collective-permute-done((bf16[1072,256]{1,0:T(8,128)(2,1)S(1)}, bf16[1072,256]{1,0:T(8,128)(2,1)S(1)}, u32[]{:S(2)}, u32[]{:S(2)}) %collective-permute-start.7) | collective-permute-done | bytes 548896 | tf_op jit(solution)/shard_map/ppermute | solution.py:403
  58.9 1.9 %collective-permute-done.19.refs_1_ = bf16[1072,256]{1,0:T(8,128)(2,1)S(1)} collective-permute-done((bf16[1072,256]{1,0:T(8,128)(2,1)S(1)}, bf16[1072,256]{1,0:T(8,128)(2,1)S(1)}, u32[]{:S(2)}, u32[]{:S(2)}) %collective-permute-start.19) | collective-permute-done | bytes 548896 | tf_op jit(solution)/shard_map/ppermute | solution.py:406
  60.8 1.9 %shard_map.50 = f32[4096,2048]{1,0:T(8,128)} custom-call(s32[8,128]{1,0:T(8,128)S(1)} %get-tuple-element.64.plan, bf16[1072,256]{1,0:T(8,128)(2,1)S(1)} %collective-permute-done.7.refs_0_, bf16[1072,256]{1,0:T(8,128)(2,1)S(1)} %collective-permute-done.19.refs_1_, bf16[8,512,128]{2,1,0:T(8,128)(2,1)S(1)} %get-tuple-element.66.refs_2_, ...), custom_call_target="tpu_custom_call", output_to_operand_aliasing={{}: (5, {})} | custom-call | tf_op jit(solution)/shard_map/pallas_call | solution.py:336
  (31 shorter events, 2.6 us)
Async XLA Ops:
  2.2 10.0 %collective-permute-start = (bf16[256,256]{1,0:T(8,128)(2,1)}, bf16[256,256]{1,0:T(8,128)(2,1)S(1)}, u32[]{:S(2)}, u32[]{:S(2)}) collective-permute-start(bf16[256,256]{1,0:T(8,128)(2,1)} %get-tuple-element.38), channel_id=1, source_target_pairs={{0,8},{8,0},{16,24},{24,16},{1,9},{9,1},{17,25},{25,17},{2,10},{10... | collective-permute-start | bytes 393224 | tf_op jit(solution)/shard_map/ppermute | solution.py:399
  5.1 13.4 %collective-permute-start.3 = (bf16[528,128]{1,0:T(8,128)(2,1)}, bf16[528,128]{1,0:T(8,128)(2,1)S(1)}, u32[]{:S(2)}, u32[]{:S(2)}) collective-permute-start(bf16[528,128]{1,0:T(8,128)(2,1)} %get-tuple-element.42), channel_id=1, source_target_pairs={{0,2},{1,3},{2,4},{3,5},{4,6},{5,7},{6,0},{7,1},{8,10},{9,11},{10,... | collective-permute-start | bytes 405512 | tf_op jit(solution)/shard_map/ppermute | solution.py:403
  6.7 11.8 %collective-permute-start.4 = (bf16[528,128]{1,0:T(8,128)(2,1)}, bf16[528,128]{1,0:T(8,128)(2,1)S(1)}, u32[]{:S(2)}, u32[]{:S(2)}) collective-permute-start(bf16[528,128]{1,0:T(8,128)(2,1)} %get-tuple-element.43), channel_id=1, source_target_pairs={{0,4},{1,5},{2,6},{3,7},{4,0},{5,1},{6,2},{7,3},{8,12},{9,13},{10,... | collective-permute-start | bytes 405512 | tf_op jit(solution)/shard_map/ppermute | solution.py:403
  9.3 9.2 %collective-permute-start.5 = (bf16[528,128]{1,0:T(8,128)(2,1)}, bf16[528,128]{1,0:T(8,128)(2,1)S(1)}, u32[]{:S(2)}, u32[]{:S(2)}) collective-permute-start(bf16[528,128]{1,0:T(8,128)(2,1)} %get-tuple-element.44), channel_id=1, source_target_pairs={{0,6},{1,7},{2,0},{3,1},{4,2},{5,3},{6,4},{7,5},{8,14},{9,15},{10,... | collective-permute-start | bytes 405512 | tf_op jit(solution)/shard_map/ppermute | solution.py:403
  10.6 7.9 %collective-permute-start.1 = (bf16[256,256]{1,0:T(8,128)(2,1)}, bf16[256,256]{1,0:T(8,128)(2,1)S(1)}, u32[]{:S(2)}, u32[]{:S(2)}) collective-permute-start(bf16[256,256]{1,0:T(8,128)(2,1)} %get-tuple-element.39), channel_id=1, source_target_pairs={{0,16},{8,24},{16,0},{24,8},{1,17},{9,25},{17,1},{25,9},{2,18},{10... | collective-permute-start | bytes 393224 | tf_op jit(solution)/shard_map/ppermute | solution.py:399
  12.1 6.4 %collective-permute-start.2 = (bf16[256,256]{1,0:T(8,128)(2,1)}, bf16[256,256]{1,0:T(8,128)(2,1)S(1)}, u32[]{:S(2)}, u32[]{:S(2)}) collective-permute-start(bf16[256,256]{1,0:T(8,128)(2,1)} %get-tuple-element.40), channel_id=1, source_target_pairs={{0,24},{8,16},{16,8},{24,0},{1,25},{9,17},{17,9},{25,1},{2,26},{10... | collective-permute-start | bytes 393224 | tf_op jit(solution)/shard_map/ppermute | solution.py:399
  12.6 0.9 %copy-start = (bf16[528,128]{1,0:T(8,128)(2,1)S(1)}, bf16[528,128]{1,0:T(8,128)(2,1)}, u32[]{:S(2)}) copy-start(bf16[528,128]{1,0:T(8,128)(2,1)} %get-tuple-element.55.refs_0_) | copy-start | bytes 405508
  13.5 5.0 %copy-start.1 = (bf16[528,128]{1,0:T(8,128)(2,1)S(1)}, bf16[528,128]{1,0:T(8,128)(2,1)}, u32[]{:S(2)}) copy-start(bf16[528,128]{1,0:T(8,128)(2,1)} %get-tuple-element.55.refs_0_) | copy-start | bytes 405508
  13.5 5.2 %copy-start.2 = (bf16[256,256]{1,0:T(8,128)(2,1)S(1)}, bf16[256,256]{1,0:T(8,128)(2,1)}, u32[]{:S(2)}) copy-start(bf16[256,256]{1,0:T(8,128)(2,1)} %get-tuple-element.45) | copy-start | bytes 393220
  18.6 5.9 %collective-permute-start.10 = (bf16[4,528,128]{2,1,0:T(8,128)(2,1)S(1)}, bf16[4,528,128]{2,1,0:T(8,128)(2,1)S(1)}, u32[]{:S(2)}, u32[]{:S(2)}) collective-permute-start(bf16[4,528,128]{2,1,0:T(8,128)(2,1)S(1)} %pad_maximum_fusion.refs_6_), channel_id=1, source_target_pairs={{0,1},{1,0},{2,3},{3,2},{4,5},{5,4},{6,7},{7,6},{8,9},{9,8},{10,11... | collective-permute-start | bytes 1622024 | tf_op jit(solution)/shard_map/ppermute | solution.py:406
  18.8 5.8 %collective-permute-start.9 = (bf16[1024,256]{1,0:T(8,128)(2,1)S(1)}, bf16[1024,256]{1,0:T(8,128)(2,1)S(1)}, u32[]{:S(2)}, u32[]{:S(2)}) collective-permute-start(bf16[1024,256]{1,0:T(8,128)(2,1)S(1)} %bitcast.13), channel_id=1, source_target_pairs={{0,1},{1,0},{2,3},{3,2},{4,5},{5,4},{6,7},{7,6},{8,9},{9,8},{10,11... | collective-permute-start | bytes 1572872 | tf_op jit(solution)/shard_map/ppermute | solution.py:406
  19.3 16.8 %collective-permute-start.6 = (bf16[1024,256]{1,0:T(8,128)(2,1)S(1)}, bf16[1024,256]{1,0:T(8,128)(2,1)S(1)}, u32[]{:S(2)}, u32[]{:S(2)}) collective-permute-start(bf16[1024,256]{1,0:T(8,128)(2,1)S(1)} %bitcast.14), channel_id=1, source_target_pairs={{0,2},{1,3},{2,4},{3,5},{4,6},{5,7},{6,0},{7,1},{8,10},{9,11},{10,... | collective-permute-start | bytes 1572872 | tf_op jit(solution)/shard_map/ppermute | solution.py:403
  22.3 15.2 %collective-permute-start.12 = (bf16[4,528,128]{2,1,0:T(8,128)(2,1)S(1)}, bf16[4,528,128]{2,1,0:T(8,128)(2,1)S(1)}, u32[]{:S(2)}, u32[]{:S(2)}) collective-permute-start(bf16[4,528,128]{2,1,0:T(8,128)(2,1)S(1)} %pad_maximum_fusion.refs_6_), channel_id=1, source_target_pairs={{0,8},{8,0},{16,24},{24,16},{1,9},{9,1},{17,25},{25,17},{2,10},{10... | collective-permute-start | bytes 1622024 | tf_op jit(solution)/shard_map/ppermute | solution.py:399
  22.8 24.8 %collective-permute-start.8 = (bf16[1056,256]{1,0:T(8,128)(2,1)S(1)}, bf16[1056,256]{1,0:T(8,128)(2,1)S(1)}, u32[]{:S(2)}, u32[]{:S(2)}) collective-permute-start(bf16[1056,256]{1,0:T(8,128)(2,1)S(1)} %pad.9), channel_id=1, source_target_pairs={{0,6},{1,7},{2,0},{3,1},{4,2},{5,3},{6,4},{7,5},{8,14},{9,15},{10,... | collective-permute-start | bytes 1622024 | tf_op jit(solution)/shard_map/ppermute | solution.py:403
  24.5 25.0 %collective-permute-start.13 = (bf16[4,528,128]{2,1,0:T(8,128)(2,1)S(1)}, bf16[4,528,128]{2,1,0:T(8,128)(2,1)S(1)}, u32[]{:S(2)}, u32[]{:S(2)}) collective-permute-start(bf16[4,528,128]{2,1,0:T(8,128)(2,1)S(1)} %pad_maximum_fusion.refs_6_), channel_id=1, source_target_pairs={{0,16},{8,24},{16,0},{24,8},{1,17},{9,25},{17,1},{25,9},{2,18},{10... | collective-permute-start | bytes 1622024 | tf_op jit(solution)/shard_map/ppermute | solution.py:399
  26.0 23.5 %collective-permute-start.14 = (bf16[4,528,128]{2,1,0:T(8,128)(2,1)S(1)}, bf16[4,528,128]{2,1,0:T(8,128)(2,1)S(1)}, u32[]{:S(2)}, u32[]{:S(2)}) collective-permute-start(bf16[4,528,128]{2,1,0:T(8,128)(2,1)S(1)} %pad_maximum_fusion.refs_6_), channel_id=1, source_target_pairs={{0,24},{8,16},{16,8},{24,0},{1,25},{9,17},{17,9},{25,1},{2,26},{10... | collective-permute-start | bytes 1622024 | tf_op jit(solution)/shard_map/ppermute | solution.py:399
  36.1 11.5 %collective-permute-start.11 = (bf16[1024,256]{1,0:T(8,128)(2,1)S(1)}, bf16[1024,256]{1,0:T(8,128)(2,1)S(1)}, u32[]{:S(2)}, u32[]{:S(2)}) collective-permute-start(bf16[1024,256]{1,0:T(8,128)(2,1)S(1)} %collective-permute-done.6.refs_1_), channel_id=1, source_target_pairs={{0,1},{1,0},{2,3},{3,2},{4,5},{5,4},{6,7},{7,6},{8,9},{9,8},{10,11... | collective-permute-start | bytes 1572872 | tf_op jit(solution)/shard_map/ppermute | solution.py:406
  37.4 21.4 %collective-permute-start.7 = (bf16[1072,256]{1,0:T(8,128)(2,1)S(1)}, bf16[1072,256]{1,0:T(8,128)(2,1)S(1)}, u32[]{:S(2)}, u32[]{:S(2)}) collective-permute-start(bf16[1072,256]{1,0:T(8,128)(2,1)S(1)} %pad.8), channel_id=1, source_target_pairs={{0,2},{1,3},{2,4},{3,5},{4,6},{5,7},{6,0},{7,1},{8,10},{9,11},{10,... | collective-permute-start | bytes 1646600 | tf_op jit(solution)/shard_map/ppermute | solution.py:403
  47.6 2.4 %collective-permute-start.15 = (bf16[1056,256]{1,0:T(8,128)(2,1)S(1)}, bf16[1056,256]{1,0:T(8,128)(2,1)S(1)}, u32[]{:S(2)}, u32[]{:S(2)}) collective-permute-start(bf16[1056,256]{1,0:T(8,128)(2,1)S(1)} %collective-permute-done.8.refs_2_), channel_id=1, source_target_pairs={{0,1},{1,0},{2,3},{3,2},{4,5},{5,4},{6,7},{7,6},{8,9},{9,8},{10,11... | collective-permute-start | bytes 1622024 | tf_op jit(solution)/shard_map/ppermute | solution.py:406
  49.5 1.9 %collective-permute-start.16 = (bf16[4,528,128]{2,1,0:T(8,128)(2,1)S(1)}, bf16[4,528,128]{2,1,0:T(8,128)(2,1)S(1)}, u32[]{:S(2)}, u32[]{:S(2)}) collective-permute-start(bf16[4,528,128]{2,1,0:T(8,128)(2,1)S(1)} %collective-permute-done.12.refs_7_), channel_id=1, source_target_pairs={{0,1},{1,0},{2,3},{3,2},{4,5},{5,4},{6,7},{7,6},{8,9},{9,8},{10,11... | collective-permute-start | bytes 1622024 | tf_op jit(solution)/shard_map/ppermute | solution.py:406
  49.5 2.7 %collective-permute-start.17 = (bf16[4,528,128]{2,1,0:T(8,128)(2,1)S(1)}, bf16[4,528,128]{2,1,0:T(8,128)(2,1)S(1)}, u32[]{:S(2)}, u32[]{:S(2)}) collective-permute-start(bf16[4,528,128]{2,1,0:T(8,128)(2,1)S(1)} %collective-permute-done.13.refs_8_), channel_id=1, source_target_pairs={{0,1},{1,0},{2,3},{3,2},{4,5},{5,4},{6,7},{7,6},{8,9},{9,8},{10,11... | collective-permute-start | bytes 1622024 | tf_op jit(solution)/shard_map/ppermute | solution.py:406
  50.0 3.0 %collective-permute-start.18 = (bf16[4,528,128]{2,1,0:T(8,128)(2,1)S(1)}, bf16[4,528,128]{2,1,0:T(8,128)(2,1)S(1)}, u32[]{:S(2)}, u32[]{:S(2)}) collective-permute-start(bf16[4,528,128]{2,1,0:T(8,128)(2,1)S(1)} %collective-permute-done.14.refs_9_), channel_id=1, source_target_pairs={{0,1},{1,0},{2,3},{3,2},{4,5},{5,4},{6,7},{7,6},{8,9},{9,8},{10,11... | collective-permute-start | bytes 1622024 | tf_op jit(solution)/shard_map/ppermute | solution.py:406
  58.9 1.9 %collective-permute-start.19 = (bf16[1072,256]{1,0:T(8,128)(2,1)S(1)}, bf16[1072,256]{1,0:T(8,128)(2,1)S(1)}, u32[]{:S(2)}, u32[]{:S(2)}) collective-permute-start(bf16[1072,256]{1,0:T(8,128)(2,1)S(1)} %collective-permute-done.7.refs_0_), channel_id=1, source_target_pairs={{0,1},{1,0},{2,3},{3,2},{4,5},{5,4},{6,7},{7,6},{8,9},{9,8},{10,11... | collective-permute-start | bytes 1646600 | tf_op jit(solution)/shard_map/ppermute | solution.py:406

commit v11 on v10

--- a/solution.py
+++ b/solution.py
@@ -10,7 +10,7 @@
 TILES = 128
 CORES = 2
 META = 16
-TAIL_GROUP = 2
+TAIL_GROUP = 1
 ZERO_EARLY = 6
 MIB = 1024 * 1024
 
@@ -428,7 +428,7 @@
     own = [flip_core(chip), flip_core(right)]
     *own, again, token = after((*own, right, to_chip[0]))
     sides = [right] + [flip_row(right if j == 1 else again, j) for j in range(1, n_row)]
-    far = shift_chip(pad(near[middle - 1], 48), 1)
+    far = shift_chip(pad(near[middle - 1], 40), 1)
     swapped = {s: flip_core(near[s]) for s in range(1, middle)}
     zeros = zero_part(height, breadth, 1, token, zeros)
     swapped, waiting, zeros = after((swapped, sides[1:], zeros))

time: 62.9 us -> 62.7 us (level)
  transfers between devices with their start and end apart: 20 -> 20, of which waited for: 10 -> 10; matrix products, arithmetic and copies ran while one was open for 0% -> 0% of each run, Pallas kernels for 25% -> 26%
where the time goes in v11:
time: 62.7 us; the launch traced here: 62.6 us
  waiting for transfers between devices  22.2 us (35%)
  Pallas kernels  20 us (32%)
  starting transfers between devices  19.1 us (30%)
  local copies, waits for them, and re-layouts  0.98 us (2%)
    ppermute x6, waiting for transfers between devices, shift_chip(): return lax.ppermute(value, 'col', pairs)  13.8 us
    pallas_call x2, Pallas kernels, zero_part(): pl.pallas_call(functools.partial(zero_kernel, first, number), out_shape=j...  12.1 us
    ppermute x6, starting transfers between devices, shift_chip(): return lax.ppermute(value, 'col', pairs)  10.2 us
    ppermute x6, starting transfers between devices, flip_row(): return lax.ppermute(value, 'row', [(i, i ^ j) for i in range(n_row)])  7.83 us
    ppermute x8, waiting for transfers between devices, flip_core(): return lax.ppermute(value, 'col', [(i, i ^ 1) for i in range(n_col)])  4.91 us
    pallas_call x1, Pallas kernels, main_part(): pl.pallas_call(functools.partial(main_kernel, n_row, n_chip, slots, per_r...  3.91 us
    ppermute x6, waiting for transfers between devices, flip_row(): return lax.ppermute(value, 'row', [(i, i ^ j) for i in range(n_row)])  3.47 us
    pallas_call x1, Pallas kernels, pack(): pl.pallas_call(functools.partial(pack_kernel, n_row, n_chip, slots), out_...  2.15 us
  transfers between devices with their start and end apart: 20, of which 10 were waited for; matrix products, arithmetic and copies ran while one was open for 0% of the time, Pallas kernels for 26%

profile of v11, /device:TPU:0, one launch (start us, length us, event | category | flops | bytes accessed | tf_op | source)
XLA Modules:
  0.0 62.6 jit_solution(6530202323486459360)
XLA Ops:
  0.0 2.1 %shard_map.46 = (bf16[256,256]{1,0:T(8,128)(2,1)}, bf16[256,256]{1,0:T(8,128)(2,1)}, bf16[256,256]{1,0:T(8,128)(2,1)}, bf16[256,256]{1,0:T(8,128)(2,1)}, bf16[52...) custom-call(bf16[4,2,256,128]{3,2,1,0:T(8,128)(2,1)} %bitcast.18, ...), custom_call_target="tpu_custom_call" | custom-call | tf_op jit(solution)/shard_map/pallas_call | solution.py:52
  2.2 2.9 %collective-permute-start = (bf16[256,256]{1,0:T(8,128)(2,1)}, bf16[256,256]{1,0:T(8,128)(2,1)S(1)}, u32[]{:S(2)}, u32[]{:S(2)}) collective-permute-start(bf16[256,256]{1,0:T(8,128)(2,1)} %get-tuple-element.38), channel_id=1, source_target_pairs={{0,8},{8,0},{16,24},{24,16},{1,9},{9,1},{17,25},{25,17},{2,10},{10... | collective-permute-start | bytes 393224 | tf_op jit(solution)/shard_map/ppermute | solution.py:399
  5.1 1.6 %collective-permute-start.3 = (bf16[528,128]{1,0:T(8,128)(2,1)}, bf16[528,128]{1,0:T(8,128)(2,1)S(1)}, u32[]{:S(2)}, u32[]{:S(2)}) collective-permute-start(bf16[528,128]{1,0:T(8,128)(2,1)} %get-tuple-element.42), channel_id=1, source_target_pairs={{0,2},{1,3},{2,4},{3,5},{4,6},{5,7},{6,0},{7,1},{8,10},{9,11},{10,... | collective-permute-start | bytes 405512 | tf_op jit(solution)/shard_map/ppermute | solution.py:403
  6.7 2.6 %collective-permute-start.4 = (bf16[528,128]{1,0:T(8,128)(2,1)}, bf16[528,128]{1,0:T(8,128)(2,1)S(1)}, u32[]{:S(2)}, u32[]{:S(2)}) collective-permute-start(bf16[528,128]{1,0:T(8,128)(2,1)} %get-tuple-element.43), channel_id=1, source_target_pairs={{0,4},{1,5},{2,6},{3,7},{4,0},{5,1},{6,2},{7,3},{8,12},{9,13},{10,... | collective-permute-start | bytes 405512 | tf_op jit(solution)/shard_map/ppermute | solution.py:403
  9.3 1.3 %collective-permute-start.5 = (bf16[528,128]{1,0:T(8,128)(2,1)}, bf16[528,128]{1,0:T(8,128)(2,1)S(1)}, u32[]{:S(2)}, u32[]{:S(2)}) collective-permute-start(bf16[528,128]{1,0:T(8,128)(2,1)} %get-tuple-element.44), channel_id=1, source_target_pairs={{0,6},{1,7},{2,0},{3,1},{4,2},{5,3},{6,4},{7,5},{8,14},{9,15},{10,... | collective-permute-start | bytes 405512 | tf_op jit(solution)/shard_map/ppermute | solution.py:403
  10.6 1.5 %collective-permute-start.1 = (bf16[256,256]{1,0:T(8,128)(2,1)}, bf16[256,256]{1,0:T(8,128)(2,1)S(1)}, u32[]{:S(2)}, u32[]{:S(2)}) collective-permute-start(bf16[256,256]{1,0:T(8,128)(2,1)} %get-tuple-element.39), channel_id=1, source_target_pairs={{0,16},{8,24},{16,0},{24,8},{1,17},{9,25},{17,1},{25,9},{2,18},{10... | collective-permute-start | bytes 393224 | tf_op jit(solution)/shard_map/ppermute | solution.py:399
  12.6 0.9 %copy-done = bf16[528,128]{1,0:T(8,128)(2,1)S(1)} copy-done((bf16[528,128]{1,0:T(8,128)(2,1)S(1)}, bf16[528,128]{1,0:T(8,128)(2,1)}, u32[]{:S(2)}) %copy-start) | copy-done | bytes 135192
  13.5 4.7 %shard_map.47.refs_1_ = f32[4096,2048]{1,0:T(8,128)} custom-call(bf16[528,128]{1,0:T(8,128)(2,1)S(1)} %copy-done), custom_call_target="tpu_custom_call" | custom-call | bytes 16777216 | tf_op jit(solution)/shard_map/pallas_call | solution.py:372
  19.3 3.0 %collective-permute-start.6 = (bf16[1024,256]{1,0:T(8,128)(2,1)S(1)}, bf16[1024,256]{1,0:T(8,128)(2,1)S(1)}, u32[]{:S(2)}, u32[]{:S(2)}) collective-permute-start(bf16[1024,256]{1,0:T(8,128)(2,1)S(1)} %bitcast.14), channel_id=1, source_target_pairs={{0,2},{1,3},{2,4},{3,5},{4,6},{5,7},{6,0},{7,1},{8,10},{9,11},{10,... | collective-permute-start | bytes 1572872 | tf_op jit(solution)/shard_map/ppermute | solution.py:403
  22.8 1.7 %collective-permute-start.8 = (bf16[1056,256]{1,0:T(8,128)(2,1)S(1)}, bf16[1056,256]{1,0:T(8,128)(2,1)S(1)}, u32[]{:S(2)}, u32[]{:S(2)}) collective-permute-start(bf16[1056,256]{1,0:T(8,128)(2,1)S(1)} %pad.9), channel_id=1, source_target_pairs={{0,6},{1,7},{2,0},{3,1},{4,2},{5,3},{6,4},{7,5},{8,14},{9,15},{10,... | collective-permute-start | bytes 1622024 | tf_op jit(solution)/shard_map/ppermute | solution.py:403
  24.5 1.5 %collective-permute-start.13 = (bf16[4,528,128]{2,1,0:T(8,128)(2,1)S(1)}, bf16[4,528,128]{2,1,0:T(8,128)(2,1)S(1)}, u32[]{:S(2)}, u32[]{:S(2)}) collective-permute-start(bf16[4,528,128]{2,1,0:T(8,128)(2,1)S(1)} %pad_maximum_fusion.refs_6_), channel_id=1, source_target_pairs={{0,16},{8,24},{16,0},{24,8},{1,17},{9,25},{17,1},{25,9},{2,18},{10... | collective-permute-start | bytes 1622024 | tf_op jit(solution)/shard_map/ppermute | solution.py:399
  26.0 0.9 %collective-permute-start.14 = (bf16[4,528,128]{2,1,0:T(8,128)(2,1)S(1)}, bf16[4,528,128]{2,1,0:T(8,128)(2,1)S(1)}, u32[]{:S(2)}, u32[]{:S(2)}) collective-permute-start(bf16[4,528,128]{2,1,0:T(8,128)(2,1)S(1)} %pad_maximum_fusion.refs_6_), channel_id=1, source_target_pairs={{0,24},{8,16},{16,8},{24,0},{1,25},{9,17},{17,9},{25,1},{2,26},{10... | collective-permute-start | bytes 1622024 | tf_op jit(solution)/shard_map/ppermute | solution.py:399
  26.9 9.2 %collective-permute-done.6.refs_1_ = bf16[1024,256]{1,0:T(8,128)(2,1)S(1)} collective-permute-done((bf16[1024,256]{1,0:T(8,128)(2,1)S(1)}, bf16[1024,256]{1,0:T(8,128)(2,1)S(1)}, u32[]{:S(2)}, u32[]{:S(2)}) %collective-permute-start.6) | collective-permute-done | bytes 524320 | tf_op jit(solution)/shard_map/ppermute | solution.py:403
  36.1 1.3 %collective-permute-done.12.refs_7_ = bf16[4,528,128]{2,1,0:T(8,128)(2,1)S(1)} collective-permute-done((bf16[4,528,128]{2,1,0:T(8,128)(2,1)S(1)}, bf16[4,528,128]{2,1,0:T(8,128)(2,1)S(1)}, u32[]{:S(2)}, u32[]{:S(2)}) %collective-permute-start.12) | collective-permute-done | bytes 540704 | tf_op jit(solution)/shard_map/ppermute | solution.py:399
  37.4 7.3 %shard_map.48.refs_14_ = f32[4096,2048]{1,0:T(8,128)} custom-call(bf16[528,128]{1,0:T(8,128)(2,1)S(1)} %copy-done.1, f32[4096,2048]{1,0:T(8,128)} %shard_map.47.refs_1_), custom_call_target="tpu_custom_call", output_to_operand_aliasing={{}: (1, {})} | custom-call | bytes 16777216 | tf_op jit(solution)/shard_map/pallas_call | solution.py:372
  44.8 2.8 %collective-permute-done.8.refs_2_ = bf16[1056,256]{1,0:T(8,128)(2,1)S(1)} collective-permute-done((bf16[1056,256]{1,0:T(8,128)(2,1)S(1)}, bf16[1056,256]{1,0:T(8,128)(2,1)S(1)}, u32[]{:S(2)}, u32[]{:S(2)}) %collective-permute-start.8) | collective-permute-done | bytes 540704 | tf_op jit(solution)/shard_map/ppermute | solution.py:403
  47.6 1.9 %collective-permute-done.13.refs_8_ = bf16[4,528,128]{2,1,0:T(8,128)(2,1)S(1)} collective-permute-done((bf16[4,528,128]{2,1,0:T(8,128)(2,1)S(1)}, bf16[4,528,128]{2,1,0:T(8,128)(2,1)S(1)}, u32[]{:S(2)}, u32[]{:S(2)}) %collective-permute-start.13) | collective-permute-done | bytes 540704 | tf_op jit(solution)/shard_map/ppermute | solution.py:399
  50.0 1.4 %collective-permute-done.16.refs_11_ = bf16[4,528,128]{2,1,0:T(8,128)(2,1)S(1)} collective-permute-done((bf16[4,528,128]{2,1,0:T(8,128)(2,1)S(1)}, bf16[4,528,128]{2,1,0:T(8,128)(2,1)S(1)}, u32[]{:S(2)}, u32[]{:S(2)}) %collective-permute-start.16) | collective-permute-done | bytes 540704 | tf_op jit(solution)/shard_map/ppermute | solution.py:406
  51.5 0.8 %collective-permute-done.17.refs_12_ = bf16[4,528,128]{2,1,0:T(8,128)(2,1)S(1)} collective-permute-done((bf16[4,528,128]{2,1,0:T(8,128)(2,1)S(1)}, bf16[4,528,128]{2,1,0:T(8,128)(2,1)S(1)}, u32[]{:S(2)}, u32[]{:S(2)}) %collective-permute-start.17) | collective-permute-done | bytes 540704 | tf_op jit(solution)/shard_map/ppermute | solution.py:406
  52.2 0.8 %collective-permute-done.18.refs_13_ = bf16[4,528,128]{2,1,0:T(8,128)(2,1)S(1)} collective-permute-done((bf16[4,528,128]{2,1,0:T(8,128)(2,1)S(1)}, bf16[4,528,128]{2,1,0:T(8,128)(2,1)S(1)}, u32[]{:S(2)}, u32[]{:S(2)}) %collective-permute-start.18) | collective-permute-done | bytes 540704 | tf_op jit(solution)/shard_map/ppermute | solution.py:406
  53.0 3.9 %shard_map.49 = (f32[4096,2048]{1,0:T(8,128)}, bf16[8,512,128]{2,1,0:T(8,128)(2,1)S(1)}, f32[32,128,128]{2,1,0:T(8,128)S(1)}, s32[8,128]{1,0:T(8,128)S(1)}) custom-call(bf16[1024,256]{1,0:T(8,128)(2,1)S(1)} %bitcast.16, bf16[1024,256]{1,0:T(8,128)(2,1)S(1)} %collective-permute-done.6.refs_1_, ...), custom_call_target="tpu_custom_call", output_to_operand_aliasing={{0}: (14, {})} | custom-call | tf_op jit(solution)/shard_map/pallas_call | solution.py:266
  56.9 1.8 %collective-permute-done.7.refs_0_ = bf16[1064,256]{1,0:T(8,128)(2,1)S(1)} collective-permute-done((bf16[1064,256]{1,0:T(8,128)(2,1)S(1)}, bf16[1064,256]{1,0:T(8,128)(2,1)S(1)}, u32[]{:S(2)}, u32[]{:S(2)}) %collective-permute-start.7) | collective-permute-done | bytes 544800 | tf_op jit(solution)/shard_map/ppermute | solution.py:403
  58.8 1.9 %collective-permute-done.19.refs_1_ = bf16[1064,256]{1,0:T(8,128)(2,1)S(1)} collective-permute-done((bf16[1064,256]{1,0:T(8,128)(2,1)S(1)}, bf16[1064,256]{1,0:T(8,128)(2,1)S(1)}, u32[]{:S(2)}, u32[]{:S(2)}) %collective-permute-start.19) | collective-permute-done | bytes 544800 | tf_op jit(solution)/shard_map/ppermute | solution.py:406
  60.7 1.9 %shard_map.50 = f32[4096,2048]{1,0:T(8,128)} custom-call(s32[8,128]{1,0:T(8,128)S(1)} %get-tuple-element.64.plan, bf16[1064,256]{1,0:T(8,128)(2,1)S(1)} %collective-permute-done.7.refs_0_, bf16[1064,256]{1,0:T(8,128)(2,1)S(1)} %collective-permute-done.19.refs_1_, bf16[8,512,128]{2,1,0:T(8,128)(2,1)S(1)} %get-tuple-element.66.refs_2_, ...), custom_call_target="tpu_custom_call", output_to_operand_aliasing={{}: (5, {})} | custom-call | tf_op jit(solution)/shard_map/pallas_call | solution.py:336
  (31 shorter events, 2.6 us)
Async XLA Ops:
  2.2 10.0 %collective-permute-start = (bf16[256,256]{1,0:T(8,128)(2,1)}, bf16[256,256]{1,0:T(8,128)(2,1)S(1)}, u32[]{:S(2)}, u32[]{:S(2)}) collective-permute-start(bf16[256,256]{1,0:T(8,128)(2,1)} %get-tuple-element.38), channel_id=1, source_target_pairs={{0,8},{8,0},{16,24},{24,16},{1,9},{9,1},{17,25},{25,17},{2,10},{10... | collective-permute-start | bytes 393224 | tf_op jit(solution)/shard_map/ppermute | solution.py:399
  5.1 13.4 %collective-permute-start.3 = (bf16[528,128]{1,0:T(8,128)(2,1)}, bf16[528,128]{1,0:T(8,128)(2,1)S(1)}, u32[]{:S(2)}, u32[]{:S(2)}) collective-permute-start(bf16[528,128]{1,0:T(8,128)(2,1)} %get-tuple-element.42), channel_id=1, source_target_pairs={{0,2},{1,3},{2,4},{3,5},{4,6},{5,7},{6,0},{7,1},{8,10},{9,11},{10,... | collective-permute-start | bytes 405512 | tf_op jit(solution)/shard_map/ppermute | solution.py:403
  6.7 11.8 %collective-permute-start.4 = (bf16[528,128]{1,0:T(8,128)(2,1)}, bf16[528,128]{1,0:T(8,128)(2,1)S(1)}, u32[]{:S(2)}, u32[]{:S(2)}) collective-permute-start(bf16[528,128]{1,0:T(8,128)(2,1)} %get-tuple-element.43), channel_id=1, source_target_pairs={{0,4},{1,5},{2,6},{3,7},{4,0},{5,1},{6,2},{7,3},{8,12},{9,13},{10,... | collective-permute-start | bytes 405512 | tf_op jit(solution)/shard_map/ppermute | solution.py:403
  9.3 9.2 %collective-permute-start.5 = (bf16[528,128]{1,0:T(8,128)(2,1)}, bf16[528,128]{1,0:T(8,128)(2,1)S(1)}, u32[]{:S(2)}, u32[]{:S(2)}) collective-permute-start(bf16[528,128]{1,0:T(8,128)(2,1)} %get-tuple-element.44), channel_id=1, source_target_pairs={{0,6},{1,7},{2,0},{3,1},{4,2},{5,3},{6,4},{7,5},{8,14},{9,15},{10,... | collective-permute-start | bytes 405512 | tf_op jit(solution)/shard_map/ppermute | solution.py:403
  10.6 7.9 %collective-permute-start.1 = (bf16[256,256]{1,0:T(8,128)(2,1)}, bf16[256,256]{1,0:T(8,128)(2,1)S(1)}, u32[]{:S(2)}, u32[]{:S(2)}) collective-permute-start(bf16[256,256]{1,0:T(8,128)(2,1)} %get-tuple-element.39), channel_id=1, source_target_pairs={{0,16},{8,24},{16,0},{24,8},{1,17},{9,25},{17,1},{25,9},{2,18},{10... | collective-permute-start | bytes 393224 | tf_op jit(solution)/shard_map/ppermute | solution.py:399
  12.1 6.4 %collective-permute-start.2 = (bf16[256,256]{1,0:T(8,128)(2,1)}, bf16[256,256]{1,0:T(8,128)(2,1)S(1)}, u32[]{:S(2)}, u32[]{:S(2)}) collective-permute-start(bf16[256,256]{1,0:T(8,128)(2,1)} %get-tuple-element.40), channel_id=1, source_target_pairs={{0,24},{8,16},{16,8},{24,0},{1,25},{9,17},{17,9},{25,1},{2,26},{10... | collective-permute-start | bytes 393224 | tf_op jit(solution)/shard_map/ppermute | solution.py:399
  12.6 0.9 %copy-start = (bf16[528,128]{1,0:T(8,128)(2,1)S(1)}, bf16[528,128]{1,0:T(8,128)(2,1)}, u32[]{:S(2)}) copy-start(bf16[528,128]{1,0:T(8,128)(2,1)} %get-tuple-element.55.refs_0_) | copy-start | bytes 405508
  13.5 5.0 %copy-start.1 = (bf16[528,128]{1,0:T(8,128)(2,1)S(1)}, bf16[528,128]{1,0:T(8,128)(2,1)}, u32[]{:S(2)}) copy-start(bf16[528,128]{1,0:T(8,128)(2,1)} %get-tuple-element.55.refs_0_) | copy-start | bytes 405508
  13.5 5.2 %copy-start.2 = (bf16[256,256]{1,0:T(8,128)(2,1)S(1)}, bf16[256,256]{1,0:T(8,128)(2,1)}, u32[]{:S(2)}) copy-start(bf16[256,256]{1,0:T(8,128)(2,1)} %get-tuple-element.45) | copy-start | bytes 393220
  18.6 5.9 %collective-permute-start.10 = (bf16[4,528,128]{2,1,0:T(8,128)(2,1)S(1)}, bf16[4,528,128]{2,1,0:T(8,128)(2,1)S(1)}, u32[]{:S(2)}, u32[]{:S(2)}) collective-permute-start(bf16[4,528,128]{2,1,0:T(8,128)(2,1)S(1)} %pad_maximum_fusion.refs_6_), channel_id=1, source_target_pairs={{0,1},{1,0},{2,3},{3,2},{4,5},{5,4},{6,7},{7,6},{8,9},{9,8},{10,11... | collective-permute-start | bytes 1622024 | tf_op jit(solution)/shard_map/ppermute | solution.py:406
  18.8 5.8 %collective-permute-start.9 = (bf16[1024,256]{1,0:T(8,128)(2,1)S(1)}, bf16[1024,256]{1,0:T(8,128)(2,1)S(1)}, u32[]{:S(2)}, u32[]{:S(2)}) collective-permute-start(bf16[1024,256]{1,0:T(8,128)(2,1)S(1)} %bitcast.13), channel_id=1, source_target_pairs={{0,1},{1,0},{2,3},{3,2},{4,5},{5,4},{6,7},{7,6},{8,9},{9,8},{10,11... | collective-permute-start | bytes 1572872 | tf_op jit(solution)/shard_map/ppermute | solution.py:406
  19.3 16.8 %collective-permute-start.6 = (bf16[1024,256]{1,0:T(8,128)(2,1)S(1)}, bf16[1024,256]{1,0:T(8,128)(2,1)S(1)}, u32[]{:S(2)}, u32[]{:S(2)}) collective-permute-start(bf16[1024,256]{1,0:T(8,128)(2,1)S(1)} %bitcast.14), channel_id=1, source_target_pairs={{0,2},{1,3},{2,4},{3,5},{4,6},{5,7},{6,0},{7,1},{8,10},{9,11},{10,... | collective-permute-start | bytes 1572872 | tf_op jit(solution)/shard_map/ppermute | solution.py:403
  22.3 15.2 %collective-permute-start.12 = (bf16[4,528,128]{2,1,0:T(8,128)(2,1)S(1)}, bf16[4,528,128]{2,1,0:T(8,128)(2,1)S(1)}, u32[]{:S(2)}, u32[]{:S(2)}) collective-permute-start(bf16[4,528,128]{2,1,0:T(8,128)(2,1)S(1)} %pad_maximum_fusion.refs_6_), channel_id=1, source_target_pairs={{0,8},{8,0},{16,24},{24,16},{1,9},{9,1},{17,25},{25,17},{2,10},{10... | collective-permute-start | bytes 1622024 | tf_op jit(solution)/shard_map/ppermute | solution.py:399
  22.8 24.8 %collective-permute-start.8 = (bf16[1056,256]{1,0:T(8,128)(2,1)S(1)}, bf16[1056,256]{1,0:T(8,128)(2,1)S(1)}, u32[]{:S(2)}, u32[]{:S(2)}) collective-permute-start(bf16[1056,256]{1,0:T(8,128)(2,1)S(1)} %pad.9), channel_id=1, source_target_pairs={{0,6},{1,7},{2,0},{3,1},{4,2},{5,3},{6,4},{7,5},{8,14},{9,15},{10,... | collective-permute-start | bytes 1622024 | tf_op jit(solution)/shard_map/ppermute | solution.py:403
  24.5 25.0 %collective-permute-start.13 = (bf16[4,528,128]{2,1,0:T(8,128)(2,1)S(1)}, bf16[4,528,128]{2,1,0:T(8,128)(2,1)S(1)}, u32[]{:S(2)}, u32[]{:S(2)}) collective-permute-start(bf16[4,528,128]{2,1,0:T(8,128)(2,1)S(1)} %pad_maximum_fusion.refs_6_), channel_id=1, source_target_pairs={{0,16},{8,24},{16,0},{24,8},{1,17},{9,25},{17,1},{25,9},{2,18},{10... | collective-permute-start | bytes 1622024 | tf_op jit(solution)/shard_map/ppermute | solution.py:399
  26.0 23.5 %collective-permute-start.14 = (bf16[4,528,128]{2,1,0:T(8,128)(2,1)S(1)}, bf16[4,528,128]{2,1,0:T(8,128)(2,1)S(1)}, u32[]{:S(2)}, u32[]{:S(2)}) collective-permute-start(bf16[4,528,128]{2,1,0:T(8,128)(2,1)S(1)} %pad_maximum_fusion.refs_6_), channel_id=1, source_target_pairs={{0,24},{8,16},{16,8},{24,0},{1,25},{9,17},{17,9},{25,1},{2,26},{10... | collective-permute-start | bytes 1622024 | tf_op jit(solution)/shard_map/ppermute | solution.py:399
  36.1 11.5 %collective-permute-start.11 = (bf16[1024,256]{1,0:T(8,128)(2,1)S(1)}, bf16[1024,256]{1,0:T(8,128)(2,1)S(1)}, u32[]{:S(2)}, u32[]{:S(2)}) collective-permute-start(bf16[1024,256]{1,0:T(8,128)(2,1)S(1)} %collective-permute-done.6.refs_1_), channel_id=1, source_target_pairs={{0,1},{1,0},{2,3},{3,2},{4,5},{5,4},{6,7},{7,6},{8,9},{9,8},{10,11... | collective-permute-start | bytes 1572872 | tf_op jit(solution)/shard_map/ppermute | solution.py:406
  37.4 21.3 %collective-permute-start.7 = (bf16[1064,256]{1,0:T(8,128)(2,1)S(1)}, bf16[1064,256]{1,0:T(8,128)(2,1)S(1)}, u32[]{:S(2)}, u32[]{:S(2)}) collective-permute-start(bf16[1064,256]{1,0:T(8,128)(2,1)S(1)} %pad.8), channel_id=1, source_target_pairs={{0,2},{1,3},{2,4},{3,5},{4,6},{5,7},{6,0},{7,1},{8,10},{9,11},{10,... | collective-permute-start | bytes 1634312 | tf_op jit(solution)/shard_map/ppermute | solution.py:403
  47.6 2.4 %collective-permute-start.15 = (bf16[1056,256]{1,0:T(8,128)(2,1)S(1)}, bf16[1056,256]{1,0:T(8,128)(2,1)S(1)}, u32[]{:S(2)}, u32[]{:S(2)}) collective-permute-start(bf16[1056,256]{1,0:T(8,128)(2,1)S(1)} %collective-permute-done.8.refs_2_), channel_id=1, source_target_pairs={{0,1},{1,0},{2,3},{3,2},{4,5},{5,4},{6,7},{7,6},{8,9},{9,8},{10,11... | collective-permute-start | bytes 1622024 | tf_op jit(solution)/shard_map/ppermute | solution.py:406
  49.5 1.9 %collective-permute-start.16 = (bf16[4,528,128]{2,1,0:T(8,128)(2,1)S(1)}, bf16[4,528,128]{2,1,0:T(8,128)(2,1)S(1)}, u32[]{:S(2)}, u32[]{:S(2)}) collective-permute-start(bf16[4,528,128]{2,1,0:T(8,128)(2,1)S(1)} %collective-permute-done.12.refs_7_), channel_id=1, source_target_pairs={{0,1},{1,0},{2,3},{3,2},{4,5},{5,4},{6,7},{7,6},{8,9},{9,8},{10,11... | collective-permute-start | bytes 1622024 | tf_op jit(solution)/shard_map/ppermute | solution.py:406
  49.5 2.7 %collective-permute-start.17 = (bf16[4,528,128]{2,1,0:T(8,128)(2,1)S(1)}, bf16[4,528,128]{2,1,0:T(8,128)(2,1)S(1)}, u32[]{:S(2)}, u32[]{:S(2)}) collective-permute-start(bf16[4,528,128]{2,1,0:T(8,128)(2,1)S(1)} %collective-permute-done.13.refs_8_), channel_id=1, source_target_pairs={{0,1},{1,0},{2,3},{3,2},{4,5},{5,4},{6,7},{7,6},{8,9},{9,8},{10,11... | collective-permute-start | bytes 1622024 | tf_op jit(solution)/shard_map/ppermute | solution.py:406
  50.0 3.0 %collective-permute-start.18 = (bf16[4,528,128]{2,1,0:T(8,128)(2,1)S(1)}, bf16[4,528,128]{2,1,0:T(8,128)(2,1)S(1)}, u32[]{:S(2)}, u32[]{:S(2)}) collective-permute-start(bf16[4,528,128]{2,1,0:T(8,128)(2,1)S(1)} %collective-permute-done.14.refs_9_), channel_id=1, source_target_pairs={{0,1},{1,0},{2,3},{3,2},{4,5},{5,4},{6,7},{7,6},{8,9},{9,8},{10,11... | collective-permute-start | bytes 1622024 | tf_op jit(solution)/shard_map/ppermute | solution.py:406
  58.8 1.9 %collective-permute-start.19 = (bf16[1064,256]{1,0:T(8,128)(2,1)S(1)}, bf16[1064,256]{1,0:T(8,128)(2,1)S(1)}, u32[]{:S(2)}, u32[]{:S(2)}) collective-permute-start(bf16[1064,256]{1,0:T(8,128)(2,1)S(1)} %collective-permute-done.7.refs_0_), channel_id=1, source_target_pairs={{0,1},{1,0},{2,3},{3,2},{4,5},{5,4},{6,7},{7,6},{8,9},{9,8},{10,11... | collective-permute-start | bytes 1634312 | tf_op jit(solution)/shard_map/ppermute | solution.py:406
